TPU v7x, 32 devices: a whole 2x2x4 slice. The times are simulated.
32 devices in a mesh: groups: 2 (over x), expert: 16 (over z, y, core).
Axes of the slice: x: 2, y: 2, z: 4, core: 2. Of those that a mesh axis runs over, the one named last changes fastest.
Arguments:
- tokens_in: bfloat16 [4096, 1024], P(('groups', 'expert')), parts along dimension 0, may hold values from -6 to 6
- grad_out: bfloat16 [4096, 1024], P(('groups', 'expert')), parts along dimension 0, may hold values from -6 to 6
- gates: bfloat16 [4096, 8], P(('groups', 'expert')), parts along dimension 0, may hold values from 0.049804688 to 0.5
- expert_ids: int32 [4096, 8], P(('groups', 'expert')), parts along dimension 0, may hold values from 0 to 15, as said below
- replica_table: int32 [32], P('groups'), parts along dimension 0, may hold values from 0 to 15, as said below
- w_gate: bfloat16 [16, 1024, 384], P('expert'), may hold values from -0.1875 to 0.1875
- w_up: bfloat16 [16, 1024, 384], P('expert'), may hold values from -0.1875 to 0.1875
- w_down: bfloat16 [16, 384, 1024], P('expert'), may hold values from -0.3125 to 0.3125
Outputs:
- grad_tokens: bfloat16 [4096, 1024], P(('groups', 'expert')), parts along dimension 0
- grad_gates: bfloat16 [4096, 8], P(('groups', 'expert')), parts along dimension 0
- grad_w_gate: bfloat16 [32, 1024, 384], P(('groups', 'expert')), parts along dimension 0
- grad_w_up: bfloat16 [32, 1024, 384], P(('groups', 'expert')), parts along dimension 0
- grad_w_down: bfloat16 [32, 384, 1024], P(('groups', 'expert')), parts along dimension 0
There are 2 independent parts, one for each index of `groups`. A program takes and returns all parts, laid end to end along the dimension named above; an argument that names none is the same for every part. Nothing has to cross between parts.
Inputs may be any that keep to these rules, and one draw needn't show every extreme that they name: `expert_ids`: each row names 8 different experts. `replica_table`: entry d is the expert whose weights device d holds in its replica slot.
All inputs are finite; a program needn't handle non-finite values.
Results may differ from a plain program's by a relative error of at most 0.0057.
Values may be sent and summed in bfloat16 or wider, within the bound.
No kernel may reach another device: no remote copies, remote signals or barrier semaphores. Data moves between devices by JAX's collectives and lax.ppermute only.
A program may use at most 128 MiB of HBM per device.

v0:
```python
import jax
import jax.numpy as jnp
from jax import lax
from jax.sharding import PartitionSpec as P

TOP = 8


contract_rows = (((0,), (0,)), ((), ()))
contract_cols = (((1,), (1,)), ((), ()))


def plan_routes(row_ids, replica_table, source, devices, home_cap, rep_cap):
    flat_ids = row_ids.reshape(-1)
    expert_axis = jnp.arange(devices, dtype=jnp.int32)
    hosted = (replica_table[None, :] == expert_axis[:, None]).astype(jnp.int32)
    copies = 1 + jnp.sum(hosted, axis=1)
    replica_order = jnp.cumsum(hosted, axis=1) - hosted
    chosen = (flat_ids[:, None] == expert_axis[None, :]).astype(jnp.int32)
    row_rank = jnp.sum((jnp.cumsum(chosen, axis=0) - chosen) * chosen, axis=1)
    row_copies = jnp.take(copies, flat_ids, axis=0)
    copy_index = (row_rank + source) % row_copies
    at_home = copy_index == 0
    matched = (jnp.take(hosted, flat_ids, axis=0) == 1) & (
        jnp.take(replica_order, flat_ids, axis=0) == (copy_index - 1)[:, None]
    )
    replica_device = jnp.sum(jnp.where(matched, expert_axis[None, :], 0), axis=1)
    target = jnp.where(at_home, flat_ids, replica_device)
    bucket = target * 2 + jnp.where(at_home, 0, 1)
    bucket_hot = (bucket[:, None] == jnp.arange(2 * devices, dtype=jnp.int32)[None, :]).astype(
        jnp.int32
    )
    position = jnp.sum((jnp.cumsum(bucket_hot, axis=0) - bucket_hot) * bucket_hot, axis=1)
    slot_width = home_cap + rep_cap
    kept_rows = jnp.where(at_home, position < home_cap, position < rep_cap)
    slot_index = target * slot_width + jnp.where(at_home, position, home_cap + position)
    slot_index = jnp.where(kept_rows, slot_index, devices * slot_width)
    return (slot_index, kept_rows)


def expert_grads(rows_x, rows_dy, rows_gate, gate_w, up_w, down_w):
    pre_gate = jnp.dot(rows_x, gate_w, preferred_element_type=jnp.float32)
    pre_up = jnp.dot(rows_x, up_w, preferred_element_type=jnp.float32)
    sigmoid_gate = jax.nn.sigmoid(pre_gate)
    activated = pre_gate * sigmoid_gate
    product = activated * pre_up
    hidden = product.astype(jnp.bfloat16)
    back_hidden = lax.dot_general(
        rows_dy, down_w, contract_cols, preferred_element_type=jnp.float32
    )
    gate_grad = jnp.sum(
        lax.optimization_barrier(hidden).astype(jnp.float32) * back_hidden, axis=1
    ).astype(jnp.bfloat16)
    gate_value = rows_gate.astype(jnp.float32)[:, None]
    weighted = (gate_value * product).astype(jnp.bfloat16)
    down_grad = lax.dot_general(
        weighted, rows_dy, contract_rows, preferred_element_type=jnp.float32
    )
    scaled = gate_value * back_hidden
    grad_pre_gate = (
        scaled * pre_up * sigmoid_gate * (1.0 + pre_gate * (1.0 - sigmoid_gate))
    ).astype(jnp.bfloat16)
    grad_pre_up = (scaled * activated).astype(jnp.bfloat16)
    gate_w_grad = lax.dot_general(
        rows_x, grad_pre_gate, contract_rows, preferred_element_type=jnp.float32
    )
    up_w_grad = lax.dot_general(
        rows_x, grad_pre_up, contract_rows, preferred_element_type=jnp.float32
    )
    input_grad = lax.dot_general(
        grad_pre_gate, gate_w, contract_cols, preferred_element_type=jnp.float32
    )
    input_grad = input_grad + lax.dot_general(
        grad_pre_up, up_w, contract_cols, preferred_element_type=jnp.float32
    )
    return (input_grad.astype(jnp.bfloat16), gate_grad, gate_w_grad, up_w_grad, down_grad)


def on_device(tokens_in, grad_out, gates, expert_ids, replica_table, w_gate, w_up, w_down):
    devices = lax.axis_size("expert")
    source = lax.axis_index("expert")
    tok_rows = tokens_in.shape[0]
    home_cap = max(2, 5 * tok_rows * TOP // (4 * devices))
    rep_cap = max(2, tok_rows * TOP // (2 * devices))
    slot_width = home_cap + rep_cap
    model_width = tokens_in.shape[1]
    hidden_units = w_gate.shape[2]
    zero_bf = jnp.zeros((), jnp.bfloat16)
    slot_index, kept_rows = plan_routes(
        expert_ids, replica_table, source, devices, home_cap, rep_cap
    )
    routed = slot_index.shape[0]
    slot_fill = (
        jnp.full((devices * slot_width + 1,), -1, jnp.int32)
        .at[slot_index]
        .set(jnp.arange(routed, dtype=jnp.int32))[:-1]
    )
    filled = slot_fill >= 0
    clipped = jnp.maximum(slot_fill, 0)
    token_row = clipped // TOP
    top_index = clipped % TOP
    send_x = jnp.where(filled[:, None], jnp.take(tokens_in, token_row, axis=0), zero_bf).reshape(
        devices, slot_width, model_width
    )
    send_dy = jnp.where(filled[:, None], jnp.take(grad_out, token_row, axis=0), zero_bf).reshape(
        devices, slot_width, model_width
    )
    send_gate = jnp.where(filled, gates[token_row, top_index], zero_bf).reshape(devices, slot_width)
    piece_gate = w_gate.reshape(devices, model_width // devices, hidden_units)
    piece_up = w_up.reshape(devices, model_width // devices, hidden_units)
    piece_down = w_down.reshape(devices, hidden_units // devices, model_width)
    recv_x, recv_dy, recv_gate = (
        lax.all_to_all(send_x, "expert", split_axis=0, concat_axis=0, tiled=True),
        lax.all_to_all(send_dy, "expert", split_axis=0, concat_axis=0, tiled=True),
        lax.all_to_all(send_gate, "expert", split_axis=0, concat_axis=0, tiled=True),
    )
    spread_gate, spread_up, spread_down = (
        lax.all_to_all(piece_gate, "expert", split_axis=0, concat_axis=0, tiled=True),
        lax.all_to_all(piece_up, "expert", split_axis=0, concat_axis=0, tiled=True),
        lax.all_to_all(piece_down, "expert", split_axis=0, concat_axis=0, tiled=True),
    )
    copy_gate, copy_up, copy_down = (
        lax.all_to_all(
            jnp.take(spread_gate, replica_table, axis=0),
            "expert",
            split_axis=0,
            concat_axis=0,
            tiled=True,
        ),
        lax.all_to_all(
            jnp.take(spread_up, replica_table, axis=0),
            "expert",
            split_axis=0,
            concat_axis=0,
            tiled=True,
        ),
        lax.all_to_all(
            jnp.take(spread_down, replica_table, axis=0),
            "expert",
            split_axis=0,
            concat_axis=0,
            tiled=True,
        ),
    )
    home_grads = expert_grads(
        recv_x[:, :home_cap].reshape(-1, model_width),
        recv_dy[:, :home_cap].reshape(-1, model_width),
        recv_gate[:, :home_cap].reshape(-1),
        w_gate[0],
        w_up[0],
        w_down[0],
    )
    extra_grads = expert_grads(
        recv_x[:, home_cap:].reshape(-1, model_width),
        recv_dy[:, home_cap:].reshape(-1, model_width),
        recv_gate[:, home_cap:].reshape(-1),
        copy_gate.reshape(model_width, hidden_units),
        copy_up.reshape(model_width, hidden_units),
        copy_down.reshape(hidden_units, model_width),
    )
    back_x = jnp.concatenate(
        [
            home_grads[0].reshape(devices, home_cap, model_width),
            extra_grads[0].reshape(devices, rep_cap, model_width),
        ],
        axis=1,
    )
    back_gate = jnp.concatenate(
        [home_grads[1].reshape(devices, home_cap), extra_grads[1].reshape(devices, rep_cap)], axis=1
    )
    replica_gate = (
        extra_grads[2].astype(jnp.bfloat16).reshape(devices, model_width // devices, hidden_units)
    )
    replica_up = (
        extra_grads[3].astype(jnp.bfloat16).reshape(devices, model_width // devices, hidden_units)
    )
    replica_down = (
        extra_grads[4].astype(jnp.bfloat16).reshape(devices, hidden_units // devices, model_width)
    )
    returned_x, returned_gate, gate_partial_grad, up_partial_grad, down_partial_grad = (
        lax.all_to_all(back_x, "expert", split_axis=0, concat_axis=0, tiled=True),
        lax.all_to_all(back_gate, "expert", split_axis=0, concat_axis=0, tiled=True),
        lax.all_to_all(replica_gate, "expert", split_axis=0, concat_axis=0, tiled=True),
        lax.all_to_all(replica_up, "expert", split_axis=0, concat_axis=0, tiled=True),
        lax.all_to_all(replica_down, "expert", split_axis=0, concat_axis=0, tiled=True),
    )
    owner_device_table = (
        replica_table[None, :] == jnp.arange(devices, dtype=jnp.int32)[:, None]
    ).astype(jnp.bfloat16)
    summed_gate = jnp.einsum(
        "qt,tym->qym", owner_device_table, gate_partial_grad, preferred_element_type=jnp.float32
    ).astype(jnp.bfloat16)
    summed_up = jnp.einsum(
        "qt,tym->qym", owner_device_table, up_partial_grad, preferred_element_type=jnp.float32
    ).astype(jnp.bfloat16)
    summed_down = jnp.einsum(
        "qt,tym->qym", owner_device_table, down_partial_grad, preferred_element_type=jnp.float32
    ).astype(jnp.bfloat16)
    total_gate, total_up, total_down = (
        lax.all_to_all(summed_gate, "expert", split_axis=0, concat_axis=0, tiled=True),
        lax.all_to_all(summed_up, "expert", split_axis=0, concat_axis=0, tiled=True),
        lax.all_to_all(summed_down, "expert", split_axis=0, concat_axis=0, tiled=True),
    )
    grad_w_gate = (
        home_grads[2] + total_gate.reshape(model_width, hidden_units).astype(jnp.float32)
    ).astype(jnp.bfloat16)[None]
    grad_w_up = (
        home_grads[3] + total_up.reshape(model_width, hidden_units).astype(jnp.float32)
    ).astype(jnp.bfloat16)[None]
    grad_w_down = (
        home_grads[4] + total_down.reshape(hidden_units, model_width).astype(jnp.float32)
    ).astype(jnp.bfloat16)[None]
    clipped_slot = jnp.minimum(slot_index, devices * slot_width - 1)
    flat_back = returned_x.reshape(devices * slot_width, model_width)
    gathered_rows = jnp.where(
        kept_rows[:, None],
        jnp.take(flat_back, clipped_slot, axis=0).astype(jnp.float32),
        jnp.float32(0.0),
    )
    grad_tokens = jnp.sum(gathered_rows.reshape(-1, TOP, model_width), axis=1).astype(jnp.bfloat16)
    grad_gates = jnp.where(
        kept_rows, jnp.take(returned_gate.reshape(-1), clipped_slot, axis=0), zero_bf
    ).reshape(-1, TOP)
    return (grad_tokens, grad_gates, grad_w_gate, grad_w_up, grad_w_down)


def solution(mesh):
    return jax.shard_map(
        on_device,
        mesh=mesh,
        in_specs=(
            P(("groups", "expert"), None),
            P(("groups", "expert"), None),
            P(("groups", "expert"), None),
            P(("groups", "expert"), None),
            P("groups"),
            P("expert", None, None),
            P("expert", None, None),
            P("expert", None, None),
        ),
        out_specs=(
            P(("groups", "expert"), None),
            P(("groups", "expert"), None),
            P(("groups", "expert"), None, None),
            P(("groups", "expert"), None, None),
            P(("groups", "expert"), None, None),
        ),
        check_vma=False,
    )
```

profile of v0, /device:TPU:13, one launch (start us, length us, event | category | flops | bytes accessed | tf_op | source)
XLA Modules:
  0.0 647.2 jit_solution(17578999911705583110)
XLA Ops:
  4.1 4.4 compare_select_fusion.6
  8.6 4.5 reduce-window.14
  14.1 2.8 gather_fusion.4
  16.9 2.8 gather_fusion.5
  19.8 5.9 broadcast_add_fusion.2
  26.4 9.0 %reduce-window.16 = s32[32,8,128]{2,1,0:T(8,128)S(1)} reduce-window(s32[32,8,128]{2,1,0:T(8,128)S(1)} %fusion.30, s32[]{:T(128)} %constant.107.clone.1), window={size=1x1x128 pad=0_0x0_0x127_0}, to_apply=%region_6.8 | reduce-window | flops 4161536 | bytes 262148 | tf_op jit(solution)/shard_map/reduce-window.2
  36.4 4.3 scatter_custom_fusion
  40.8 13.4 %gather_fusion = bf16[1792]{0:T(1024)(128)(2,1)S(1)} fusion(bf16[128,8]{0,1:T(8,128)(2,1)S(1)} %copy-done.2, s32[1792]{0:T(1024)S(1)} %get-tuple-element.39), kind=kCustom, calls=%fused_computation.6 | custom fusion | bytes 21504 | tf_op jit(solution)/shard_map/gather | solution.py:108
  54.3 10.1 %all_to_all.93 = bf16[16,1,112]{2,1,0:T(2,128)(2,1)S(1)} all-to-all(bf16[16,1,112]{2,1,0:T(2,128)(2,1)S(1)} %select_n.440), channel_id=1, replica_groups=mesh['groups'=2,'expert'=16] {'expert'}, dimensions={0} | all-to-all | bytes 7168 | tf_op jit(solution)/shard_map/all_to_all | solution.py:115
  64.4 24.5 %all_to_all.94 = bf16[16,64,384]{2,1,0:T(8,128)(2,1)S(1)} all-to-all(bf16[16,64,384]{2,1,0:T(8,128)(2,1)S(1)} %bitcast.164), channel_id=1, replica_groups=mesh['groups'=2,'expert'=16] {'expert'}, dimensions={0} | all-to-all | bytes 1572864 | tf_op jit(solution)/shard_map/all_to_all | solution.py:119
  88.9 23.9 %all_to_all.95 = bf16[16,64,384]{2,1,0:T(8,128)(2,1)S(1)} all-to-all(bf16[16,64,384]{2,1,0:T(8,128)(2,1)S(1)} %bitcast.163), channel_id=1, replica_groups=mesh['groups'=2,'expert'=16] {'expert'}, dimensions={0} | all-to-all | bytes 1572864 | tf_op jit(solution)/shard_map/all_to_all | solution.py:118
  112.8 5.0 all-to-all-start.3
  117.9 1.5 gather_fusion.8
  119.4 1.5 gather_fusion.9
  120.9 2.3 broadcast_select_fusion.1
  123.2 13.9 %all-to-all-done.3 = bf16[16,24,1024]{2,1,0:T(8,128)(2,1)S(1)} async-done(((bf16[16,24,1024]{2,1,0:T(8,128)(2,1)}), bf16[16,24,1024]{2,1,0:T(8,128)(2,1)S(1)}, u32[]{:S(2)}, u32[]{:S(2)}) %all-to-all-start.3) | async-done | bytes 786464 | tf_op jit(solution)/shard_map/all_to_all | solution.py:120
  137.1 23.9 %all_to_all.96 = bf16[16,64,384]{2,1,0:T(8,128)(2,1)S(1)} all-to-all(bf16[16,64,384]{2,1,0:T(8,128)(2,1)S(1)} %get-tuple-element.55), channel_id=1, replica_groups=mesh['groups'=2,'expert'=16] {'expert'}, dimensions={0} | all-to-all | bytes 1572864 | tf_op jit(solution)/shard_map/all_to_all | solution.py:130
  161.0 5.0 all-to-all-start.8
  166.0 6.6 %gather_fusion.7 = bf16[1792,1024]{1,0:T(8,128)(2,1)} fusion(bf16[128,1024]{1,0:T(8,128)(2,1)S(1)} %copy-done, s32[2048]{0:T(1024)S(1)} %pad_clamp_fusion), kind=kCustom, calls=%fused_computation.4.clone | custom fusion | bytes 7347200 | tf_op jit(solution)/shard_map/jit(_take)/gather | solution.py:102
  172.7 6.6 %gather_fusion.6 = bf16[1792,1024]{1,0:T(8,128)(2,1)} fusion(bf16[128,1024]{1,0:T(8,128)(2,1)S(1)} %copy-done.3, s32[2048]{0:T(1024)S(1)} %pad_clamp_fusion), kind=kCustom, calls=%fused_computation.1.clone | custom fusion | bytes 7347200 | tf_op jit(solution)/shard_map/jit(_take)/gather | solution.py:105
  179.2 5.8 select_select_fusion.1
  185.2 87.0 %all_to_all.97 = bf16[16,112,1024]{2,1,0:T(8,128)(2,1)} all-to-all(bf16[16,112,1024]{2,1,0:T(8,128)(2,1)} %bitcast.152), channel_id=1, replica_groups=mesh['groups'=2,'expert'=16] {'expert'}, dimensions={0} | all-to-all | bytes 7340032 | tf_op jit(solution)/shard_map/all_to_all | solution.py:113
  272.2 5.2 all-to-all-start.1
  279.1 2.1 broadcast_select_fusion.2
  281.2 77.4 %all-to-all-done.1 = bf16[16,112,1024]{2,1,0:T(8,128)(2,1)} async-done(((bf16[16,112,1024]{2,1,0:T(8,128)(2,1)}), bf16[16,112,1024]{2,1,0:T(8,128)(2,1)}, u32[]{:S(2)}, u32[]{:S(2)}) %all-to-all-start.1) | async-done | bytes 3670048 | tf_op jit(solution)/shard_map/all_to_all | solution.py:114
  358.7 4.9 all-to-all-start.4
  365.0 2.0 slice.88
  367.0 3.1 slice.90
  373.1 2.6 fusion.11
  375.7 2.6 fusion.14
  378.3 4.6 all-to-all-done.4
  382.9 3.6 multiply_convert_fusion.6
  386.7 2.2 slice.87
  389.9 3.2 multiply_convert_fusion.1
  394.2 5.0 all-to-all-start.10
  399.1 3.2 convolution_convert_fusion.1
  402.8 6.8 %all-to-all-start.15 = ((bf16[16,24,1024]{2,1,0:T(8,128)(2,1)}), bf16[16,24,1024]{2,1,0:T(8,128)(2,1)}, u32[]{:S(2)}, u32[]{:S(2)}) async-start(bf16[16,24,1024]{2,1,0:T(8,128)(2,1)} %bitcast.175), calls=%async_computation.15 | async-start | bytes 1572864 | tf_op jit(solution)/shard_map/all_to_all | solution.py:185
  409.6 1.6 convolution_convert_fusion.3
  411.2 17.7 %all-to-all-done.15 = bf16[16,24,1024]{2,1,0:T(8,128)(2,1)} async-done(((bf16[16,24,1024]{2,1,0:T(8,128)(2,1)}), bf16[16,24,1024]{2,1,0:T(8,128)(2,1)}, u32[]{:S(2)}, u32[]{:S(2)}) %all-to-all-start.15) | async-done | bytes 786464 | tf_op jit(solution)/shard_map/all_to_all | solution.py:185
  429.0 4.9 all-to-all-start.13
  433.9 2.6 convolution_convert_fusion.5
  436.5 16.7 %all-to-all-done.13 = bf16[16,64,384]{2,1,0:T(8,128)(2,1)} async-done(((bf16[16,64,384]{2,1,0:T(8,128)(2,1)}), bf16[16,64,384]{2,1,0:T(8,128)(2,1)}, u32[]{:S(2)}, u32[]{:S(2)}) %all-to-all-start.13) | async-done | bytes 786464 | tf_op jit(solution)/shard_map/all_to_all | solution.py:184
  453.2 5.0 all-to-all-start.11
  458.2 1.8 convolution_convert_fusion
  461.3 16.2 %all-to-all-done.11 = bf16[16,64,384]{2,1,0:T(8,128)(2,1)S(1)} async-done(((bf16[16,64,384]{2,1,0:T(8,128)(2,1)}), bf16[16,64,384]{2,1,0:T(8,128)(2,1)S(1)}, u32[]{:S(2)}, u32[]{:S(2)}) %all-to-all-start.11) | async-done | bytes 786464 | tf_op jit(solution)/shard_map/all_to_all | solution.py:183
  477.4 5.0 all-to-all-start.16
  482.4 1.7 convolution_convert_fusion.2
  485.1 16.6 %all-to-all-done.16 = bf16[16,24,1024]{2,1,0:T(8,128)(2,1)} async-done(((bf16[16,24,1024]{2,1,0:T(8,128)(2,1)}), bf16[16,24,1024]{2,1,0:T(8,128)(2,1)}, u32[]{:S(2)}, u32[]{:S(2)}) %all-to-all-start.16) | async-done | bytes 786464 | tf_op jit(solution)/shard_map/all_to_all | solution.py:202
  501.7 5.0 all-to-all-start.14
  508.3 17.7 %all-to-all-done.14 = bf16[16,64,384]{2,1,0:T(8,128)(2,1)} async-done(((bf16[16,64,384]{2,1,0:T(8,128)(2,1)}), bf16[16,64,384]{2,1,0:T(8,128)(2,1)}, u32[]{:S(2)}, u32[]{:S(2)}) %all-to-all-start.14) | async-done | bytes 786464 | tf_op jit(solution)/shard_map/all_to_all | solution.py:201
  526.0 5.0 all-to-all-start.12
  531.0 1.7 fusion.63
  534.2 1.6 fusion.9
  535.8 1.6 add_convert_fusion
  537.4 2.3 pad_maximum_fusion
  539.6 10.6 %all-to-all-done.12 = bf16[16,64,384]{2,1,0:T(8,128)(2,1)S(1)} async-done(((bf16[16,64,384]{2,1,0:T(8,128)(2,1)}), bf16[16,64,384]{2,1,0:T(8,128)(2,1)S(1)}, u32[]{:S(2)}, u32[]{:S(2)}) %all-to-all-start.12) | async-done | bytes 786464 | tf_op jit(solution)/shard_map/all_to_all | solution.py:200
  551.1 5.0 all-to-all-start.9
  556.8 6.8 %gather_fusion.3 = bf16[1024]{0:T(1024)(128)(2,1)S(1)} fusion(bf16[1792]{0:T(1024)(128)(2,1)S(1)} %reshape.489, s32[1024]{0:T(1024)S(1)} %broadcast_clamp_fusion), kind=kCustom, calls=%fused_computation.9 | custom fusion | bytes 8192 | tf_op jit(solution)/shard_map/jit(_take)/gather | solution.py:222
  564.8 4.0 fusion.5
  568.9 2.5 fusion.4
  572.1 3.3 fusion.6
  575.4 61.9 %all-to-all-done.9 = bf16[16,112,1024]{2,1,0:T(8,128)(2,1)} async-done(((bf16[16,112,1024]{2,1,0:T(8,128)(2,1)}), bf16[16,112,1024]{2,1,0:T(8,128)(2,1)}, u32[]{:S(2)}, u32[]{:S(2)}) %all-to-all-start.9) | async-done | bytes 3670048 | tf_op jit(solution)/shard_map/all_to_all | solution.py:181
  637.3 7.5 %gather_fusion.2 = bf16[1024,1024]{1,0:T(8,128)(2,1)S(1)} fusion(bf16[1792,1024]{1,0:T(8,128)(2,1)} %bitcast.47, s32[1024]{0:T(1024)S(1)} %broadcast_clamp_fusion), kind=kCustom, calls=%fused_computation.8 | custom fusion | bytes 4198400 | tf_op jit(solution)/shard_map/jit(_take)/gather | solution.py:217
  644.8 2.3 select_reduce_fusion
  (134 shorter events, 24.3 us)
Async XLA Ops:
  0.6 165.4 %copy-start = (bf16[128,1024]{1,0:T(8,128)(2,1)S(1)}, bf16[128,1024]{1,0:T(8,128)(2,1)}, u32[]{:S(2)}) copy-start(bf16[128,1024]{1,0:T(8,128)(2,1)} %param.14) | copy-start | bytes 786436
  19.8 21.0 %copy-start.2 = (bf16[128,8]{0,1:T(8,128)(2,1)S(1)}, bf16[128,8]{0,1:T(8,128)(2,1)}, u32[]{:S(2)}) copy-start(bf16[128,8]{0,1:T(8,128)(2,1)} %param.16) | copy-start | bytes 6148
  40.7 23.7 %copy-start.7 = (bf16[1,1024,384]{2,1,0:T(8,128)(2,1)S(1)}, bf16[1,1024,384]{2,1,0:T(8,128)(2,1)}, u32[]{:S(2)}) copy-start(bf16[1,1024,384]{2,1,0:T(8,128)(2,1)} %param.20) | copy-start | bytes 2359300
  40.8 48.2 %copy-start.4 = (bf16[1,1024,384]{2,1,0:T(8,128)(2,1)S(1)}, bf16[1,1024,384]{2,1,0:T(8,128)(2,1)}, u32[]{:S(2)}) copy-start(bf16[1,1024,384]{2,1,0:T(8,128)(2,1)} %param.19) | copy-start | bytes 2359300
  64.4 53.4 %copy-start.22 = (s32[16]{0:T(128)S(1)}, s32[16]{0:T(128)}, u32[]{:S(2)}) copy-start(s32[16]{0:T(128)} %param.18) | copy-start | bytes 196
  112.8 24.2 %all-to-all-start.3 = ((bf16[16,24,1024]{2,1,0:T(8,128)(2,1)}), bf16[16,24,1024]{2,1,0:T(8,128)(2,1)S(1)}, u32[]{:S(2)}, u32[]{:S(2)}) async-start(bf16[16,24,1024]{2,1,0:T(8,128)(2,1)} %bitcast.173), calls=%async_computation.3 | async-start | bytes 1572864 | tf_op jit(solution)/shard_map/all_to_all | solution.py:120
  119.4 1.5 copy-start.10
  161.0 24.2 %all-to-all-start.8 = ((bf16[16,64,384]{2,1,0:T(8,128)(2,1)}), bf16[16,64,384]{2,1,0:T(8,128)(2,1)S(1)}, u32[]{:S(2)}, u32[]{:S(2)}) async-start(bf16[16,64,384]{2,1,0:T(8,128)(2,1)} %get-tuple-element.56), calls=%async_computation.8 | async-start | bytes 1572864 | tf_op jit(solution)/shard_map/all_to_all | solution.py:123
  166.0 6.7 %copy-start.3 = (bf16[128,1024]{1,0:T(8,128)(2,1)S(1)}, bf16[128,1024]{1,0:T(8,128)(2,1)}, u32[]{:S(2)}) copy-start(bf16[128,1024]{1,0:T(8,128)(2,1)} %param.15) | copy-start | bytes 786436
  272.2 86.5 %all-to-all-start.1 = ((bf16[16,112,1024]{2,1,0:T(8,128)(2,1)}), bf16[16,112,1024]{2,1,0:T(8,128)(2,1)}, u32[]{:S(2)}, u32[]{:S(2)}) async-start(bf16[16,112,1024]{2,1,0:T(8,128)(2,1)} %bitcast.151), calls=%async_computation.1 | async-start | bytes 7340032 | tf_op jit(solution)/shard_map/all_to_all | solution.py:114
  358.7 24.3 %all-to-all-start.4 = ((bf16[16,24,1024]{2,1,0:T(8,128)(2,1)}), bf16[16,24,1024]{2,1,0:T(8,128)(2,1)}, u32[]{:S(2)}, u32[]{:S(2)}) async-start(bf16[16,24,1024]{2,1,0:T(8,128)(2,1)} %broadcast_select_fusion.2), calls=%async_computation.4 | async-start | bytes 1572864 | tf_op jit(solution)/shard_map/all_to_all | solution.py:137
  367.0 8.7 %copy-start.11 = (bf16[16,80,1024]{2,1,0:T(8,128)(2,1)}, bf16[16,80,1024]{2,1,0:T(8,128)(2,1)S(1)}, u32[]{:S(2)}) copy-start(bf16[16,80,1024]{2,1,0:T(8,128)(2,1)S(1)} %slice.88) | copy-start | bytes 7864324
  370.1 3.0 copy-start.5
  373.1 2.6 copy-start.8
  386.7 2.2 copy-start.18
  386.7 2.6 copy-start.23
  386.7 3.2 copy-start.25
  388.9 4.2 copy-start.13
  394.2 8.7 %all-to-all-start.10 = ((bf16[16,1,112]{2,1,0:T(2,128)(2,1)}), bf16[16,1,112]{2,1,0:T(2,128)(2,1)S(1)}, u32[]{:S(2)}, u32[]{:S(2)}) async-start(bf16[16,1,112]{2,1,0:T(2,128)(2,1)} %copy.158), calls=%async_computation.10 | async-start | bytes 16384 | tf_op jit(solution)/shard_map/all_to_all | solution.py:182
  402.8 26.1 %all-to-all-start.15 = ((bf16[16,24,1024]{2,1,0:T(8,128)(2,1)}), bf16[16,24,1024]{2,1,0:T(8,128)(2,1)}, u32[]{:S(2)}, u32[]{:S(2)}) async-start(bf16[16,24,1024]{2,1,0:T(8,128)(2,1)} %bitcast.175), calls=%async_computation.15 | async-start | bytes 1572864 | tf_op jit(solution)/shard_map/all_to_all | solution.py:185
  429.0 24.3 %all-to-all-start.13 = ((bf16[16,64,384]{2,1,0:T(8,128)(2,1)}), bf16[16,64,384]{2,1,0:T(8,128)(2,1)}, u32[]{:S(2)}, u32[]{:S(2)}) async-start(bf16[16,64,384]{2,1,0:T(8,128)(2,1)} %bitcast.177), calls=%async_computation.13 | async-start | bytes 1572864 | tf_op jit(solution)/shard_map/all_to_all | solution.py:184
  453.2 24.2 %all-to-all-start.11 = ((bf16[16,64,384]{2,1,0:T(8,128)(2,1)}), bf16[16,64,384]{2,1,0:T(8,128)(2,1)S(1)}, u32[]{:S(2)}, u32[]{:S(2)}) async-start(bf16[16,64,384]{2,1,0:T(8,128)(2,1)} %bitcast.176), calls=%async_computation.11 | async-start | bytes 1572864 | tf_op jit(solution)/shard_map/all_to_all | solution.py:183
  477.4 24.3 %all-to-all-start.16 = ((bf16[16,24,1024]{2,1,0:T(8,128)(2,1)}), bf16[16,24,1024]{2,1,0:T(8,128)(2,1)}, u32[]{:S(2)}, u32[]{:S(2)}) async-start(bf16[16,24,1024]{2,1,0:T(8,128)(2,1)} %copy.165), calls=%async_computation.16 | async-start | bytes 1572864 | tf_op jit(solution)/shard_map/all_to_all | solution.py:202
  501.7 24.3 %all-to-all-start.14 = ((bf16[16,64,384]{2,1,0:T(8,128)(2,1)}), bf16[16,64,384]{2,1,0:T(8,128)(2,1)}, u32[]{:S(2)}, u32[]{:S(2)}) async-start(bf16[16,64,384]{2,1,0:T(8,128)(2,1)} %copy.163), calls=%async_computation.14 | async-start | bytes 1572864 | tf_op jit(solution)/shard_map/all_to_all | solution.py:201
  526.0 24.2 %all-to-all-start.12 = ((bf16[16,64,384]{2,1,0:T(8,128)(2,1)}), bf16[16,64,384]{2,1,0:T(8,128)(2,1)S(1)}, u32[]{:S(2)}, u32[]{:S(2)}) async-start(bf16[16,64,384]{2,1,0:T(8,128)(2,1)} %copy.161), calls=%async_computation.12 | async-start | bytes 1572864 | tf_op jit(solution)/shard_map/all_to_all | solution.py:200
  532.7 1.1 copy-start.6
  532.7 1.4 copy-start.15
  534.2 1.6 copy-start.9
  534.2 1.6 copy-start.17
  550.2 0.9 copy-start.19
  551.1 86.2 %all-to-all-start.9 = ((bf16[16,112,1024]{2,1,0:T(8,128)(2,1)}), bf16[16,112,1024]{2,1,0:T(8,128)(2,1)}, u32[]{:S(2)}, u32[]{:S(2)}) async-start(bf16[16,112,1024]{2,1,0:T(8,128)(2,1)} %pad_maximum_fusion), calls=%async_computation.9 | async-start | bytes 7340032 | tf_op jit(solution)/shard_map/all_to_all | solution.py:181
  556.0 7.7 %copy-start.21 = (s32[128,8]{0,1:T(8,128)S(1)}, s32[128,8]{0,1:T(8,128)}, u32[]{:S(2)}) copy-start(s32[128,8]{0,1:T(8,128)} %param.17) | copy-start | bytes 12292
  556.0 8.7 %copy-start.12 = (bf16[16,80,1024]{2,1,0:T(8,128)(2,1)S(1)}, bf16[16,80,1024]{2,1,0:T(8,128)(2,1)}, u32[]{:S(2)}) copy-start(bf16[16,80,1024]{2,1,0:T(8,128)(2,1)} %copy-done.11) | copy-start | bytes 7864324
  564.8 4.0 copy-start.16
  564.8 4.0 copy-start.20
  568.8 2.5 copy-start.14
  568.8 2.5 copy-start.24
  568.8 3.2 copy-start.26
  637.3 9.9 %copy-start.1 = (bf16[128,1024]{1,0:T(8,128)(2,1)S(1)}, bf16[128,1024]{1,0:T(8,128)(2,1)}, u32[]{:S(2)}) copy-start(bf16[128,1024]{1,0:T(8,128)(2,1)} %param.14) | copy-start | bytes 786436
where the time goes:
time: 649 us; the launch traced here: 647 us
  waiting for transfers between devices  254 us (39%)
  blocking collectives  170 us (26%)
  local copies, waits for them, and re-layouts  75.5 us (12%)
  starting transfers between devices  61.5 us (9%)
  other arithmetic  43.6 us (7%)
  matrix products  41.9 us (6%)
    all_to_all x1, blocking collectives, on_device(): lax.all_to_all(send_x, 'expert', split_axis=0, concat_axis=0, tiled=True)  87 us
    all_to_all x1, waiting for transfers between devices, on_device(): lax.all_to_all(send_dy, 'expert', split_axis=0, concat_axis=0, tiled=True)  77.4 us
    all_to_all x1, waiting for transfers between devices, on_device(): lax.all_to_all(back_x, 'expert', split_axis=0, concat_axis=0, tiled=True)  61.9 us
    all_to_all x1, blocking collectives, on_device(): lax.all_to_all(piece_up, 'expert', split_axis=0, concat_axis=0, tiled=True)  24.5 us
    all_to_all x1, blocking collectives, on_device(): lax.all_to_all(jnp.take(spread_up, replica_table, axis=0), 'expert', spli...  23.9 us
    all_to_all x1, blocking collectives, on_device(): lax.all_to_all(piece_gate, 'expert', split_axis=0, concat_axis=0, tiled=T...  23.9 us
    all_to_all x1, waiting for transfers between devices, on_device(): lax.all_to_all(replica_down, 'expert', split_axis=0, concat_axis=0, tiled...  17.7 us
    all_to_all x1, waiting for transfers between devices, on_device(): lax.all_to_all(summed_up, 'expert', split_axis=0, concat_axis=0, tiled=True)  17.7 us
  transfers between devices with their start and end apart: 12, of which 12 were waited for; matrix products, arithmetic and copies ran while one was open for 13% of the time, Pallas kernels for 0%

commit v1 on v0

v1 whole, which is shorter than its diff:
```python
import functools
import math

import jax
import jax.numpy as jnp
from jax import lax
from jax.experimental import pallas as pl
from jax.experimental.pallas import tpu as pltpu
from jax.sharding import PartitionSpec as P

TOP = 8
CORES = 2
LANES = 128
ROW_BLOCK = 256
W_ROWS = 1024

f32 = jnp.float32
bf16 = jnp.bfloat16
nt = (((1,), (1,)), ((), ()))
tn = (((0,), (0,)), ((), ()))
VMEM = pl.BlockSpec(memory_space=pltpu.VMEM)
SMEM = pl.BlockSpec(memory_space=pltpu.SMEM)
ANY = pl.BlockSpec(memory_space=pl.ANY)


def params(mib):
    return pltpu.CompilerParams(vmem_limit_bytes=mib * 1024 * 1024)


def lane_iota(rows, lanes):
    return lax.broadcasted_iota(jnp.int32, (rows, lanes), 1)


def plan_kernel(devices, home_cap, rep_cap, table, ids, gates, dy, dyg, kept_out):
    tokens, width = dy.shape
    lanes = dyg.shape[1] - width
    dyg[:, :width] = dy[...]
    lane = lane_iota(tokens, lanes)
    lane_row = lane_iota(8, lanes)

    def count(d, total):
        return total + jnp.where(lane_row == table[d], 1.0, 0.0)

    copies = lax.fori_loop(0, devices, count, jnp.ones((8, lanes), f32))[:1]
    named = jnp.zeros((tokens, lanes), f32)
    weight = jnp.zeros((tokens, lanes), f32)
    for k in range(TOP):
        hit = lane == ids[:, k : k + 1]
        named = jnp.where(hit, 1.0, named)
        weight = jnp.where(hit, gates[:, k : k + 1].astype(f32), weight)
    below = lax.broadcasted_iota(jnp.int32, (tokens, tokens), 0) > lane_iota(tokens, tokens)
    rank = jnp.dot(
        jnp.where(below, 1.0, 0.0).astype(bf16), named.astype(bf16), preferred_element_type=f32
    )
    turn = rank + lax.axis_index("expert").astype(f32)
    at_home = turn == copies * jnp.floor(turn / copies + 0.5)
    cap = jnp.where(at_home, float(home_cap), float(rep_cap))
    kept = jnp.where((named > 0.0) & (rank < cap * copies), 1.0, 0.0)
    dyg[:, width:] = (weight * kept).astype(bf16)
    kept_out[...] = kept


def plan(table, ids, gates, dy, devices, lanes):
    tokens, width = dy.shape
    home_cap = max(2, 5 * tokens * TOP // (4 * devices))
    rep_cap = max(2, tokens * TOP // (2 * devices))
    return pl.pallas_call(
        functools.partial(plan_kernel, devices, home_cap, rep_cap),
        out_shape=(
            jax.ShapeDtypeStruct((tokens, width + lanes), bf16),
            jax.ShapeDtypeStruct((tokens, lanes), f32),
        ),
        in_specs=[SMEM, VMEM, VMEM, VMEM],
        out_specs=(VMEM, VMEM),
        compiler_params=params(16),
        name="plan",
    )(table, ids, gates, dy)


def rows_kernel(slots, *refs):
    x_in, dyg_in = refs[:slots], refs[slots : 2 * slots]
    weights = refs[2 * slots : 2 * slots + 6]
    dxg, act = refs[2 * slots + 6 : 3 * slots + 6], refs[3 * slots + 6]
    x, dyg, w_gu, w_dn, sem = refs[3 * slots + 7 :]
    tokens, width = x_in[0].shape
    hidden = weights[2].shape[0]
    lanes = dyg.shape[1] - width
    copies = []

    def fetch(src, dst):
        copies.append(pltpu.make_async_copy(src, dst, sem.at[len(copies)]))
        copies[-1].start()
        return copies[-1]

    def fetch_weights(j):
        up = [
            fetch(weights[3 * j], w_gu.at[j, :, pl.ds(0, hidden)]),
            fetch(weights[3 * j + 1], w_gu.at[j, :, pl.ds(hidden, hidden)]),
        ]
        return up, [fetch(weights[3 * j + 2], w_dn.at[j])]

    got_x = [fetch(x_in[i], x.at[pl.ds(i * tokens, tokens)]) for i in range(slots)]
    own = fetch_weights(0)
    got_dy = [fetch(dyg_in[i], dyg.at[pl.ds(i * tokens, tokens)]) for i in range(slots)]
    sibling = fetch_weights(1)
    for c in got_x + own[0]:
        c.wait()

    rows = slots * tokens
    block = math.gcd(rows, max(ROW_BLOCK, tokens))
    me = lax.axis_index("expert")
    lane = lane_iota(block, lanes)

    def expert(j, at, after_up):
        here = pl.ds(at, block)
        pre = jnp.dot(x[here, :], w_gu[j], preferred_element_type=f32)
        after_up()
        back = lax.dot_general(dyg[here, :width], w_dn[j], nt, preferred_element_type=f32)
        column = lane == (me if j == 0 else me ^ 1)
        gate = jnp.sum(
            jnp.where(column, dyg[here, width:].astype(f32), 0.0), axis=1, keepdims=True
        )
        a, b = pre[:, :hidden], pre[:, hidden:]
        sig = jax.nn.sigmoid(a)
        silu = a * sig
        h = silu * b
        gg = jnp.sum(h.astype(bf16).astype(f32) * back, axis=1, keepdims=True)
        scaled = gate * back
        da = (scaled * b * sig * (1.0 + a * (1.0 - sig))).astype(bf16)
        db = (scaled * silu).astype(bf16)
        grads = jnp.concatenate([da, db], axis=1)
        first = j * 3 * hidden
        act[here, first : first + 2 * hidden] = grads
        act[here, first + 2 * hidden : first + 3 * hidden] = (gate * h).astype(bf16)
        dx = lax.dot_general(grads, w_gu[j], nt, preferred_element_type=f32)
        return dx, jnp.where(column, gg, 0.0)

    def wait_all(group):
        for c in group:
            c.wait()

    for at in range(0, rows, block):
        first = at == 0
        dx0, gg0 = expert(0, at, lambda: wait_all(got_dy + own[1]) if first else None)
        if first:
            wait_all(sibling[0] + sibling[1])
        dx1, gg1 = expert(1, at, lambda: None)
        dx = (dx0 + dx1).astype(bf16)
        gg = (gg0 + gg1).astype(bf16)
        for i in range(block // tokens):
            out = dxg[at // tokens + i]
            part = slice(i * tokens, (i + 1) * tokens)
            out[:, :width] = dx[part]
            out[:, width:] = gg[part]


def rows_grads(xs, dygs, weights):
    slots = len(xs)
    tokens, width = xs[0].shape
    full = dygs[0].shape[1]
    hidden = weights[2].shape[0]
    rows = slots * tokens
    flops = 2 * rows * 2 * 5 * width * hidden
    moved = 4 * rows * (width + full) + 12 * width * hidden + 4 * rows * full + 12 * rows * hidden
    return pl.pallas_call(
        functools.partial(rows_kernel, slots),
        out_shape=tuple(jax.ShapeDtypeStruct((tokens, full), bf16) for _ in xs)
        + (jax.ShapeDtypeStruct((rows, 6 * hidden), bf16),),
        in_specs=[ANY] * (2 * slots + 6),
        out_specs=(VMEM,) * (slots + 1),
        scratch_shapes=[
            pltpu.VMEM((rows, width), bf16),
            pltpu.VMEM((rows, full), bf16),
            pltpu.VMEM((2, width, 2 * hidden), bf16),
            pltpu.VMEM((2, hidden, width), bf16),
            pltpu.SemaphoreType.DMA((2 * slots + 6,)),
        ],
        compiler_params=params(40),
        cost_estimate=pl.CostEstimate(
            flops=flops, bytes_accessed=moved, transcendentals=2 * rows * hidden
        ),
        name="rows_grads",
    )(*xs, *dygs, *weights)


def weights_kernel(j, slots, steps, extra, *refs):
    x_in, dyg_in, act_in = refs[:slots], refs[slots : 2 * slots], refs[2 * slots : 2 * slots + steps]
    refs = refs[2 * slots + steps :]
    more, refs = refs[:extra], refs[extra:]
    gate_out, up_out, down_out = refs[:3]
    x, dy, act, sem = refs[3:]
    tokens, width = x_in[0].shape
    hidden = act.shape[1] // 3
    step_rows = act_in[0].shape[0]
    copies = []

    def fetch(src, dst):
        copies.append(pltpu.make_async_copy(src, dst, sem.at[len(copies)]))
        copies[-1].start()

    for i in range(steps):
        fetch(
            act_in[i].at[:, pl.ds(j * 3 * hidden, 3 * hidden)],
            act.at[pl.ds(i * step_rows, step_rows)],
        )
    for i in range(slots):
        fetch(x_in[i], x.at[pl.ds(i * tokens, tokens)])
    for i in range(slots):
        fetch(dyg_in[i].at[:, pl.ds(0, width)], dy.at[pl.ds(i * tokens, tokens)])
    for c in copies[: steps + slots]:
        c.wait()

    def put(out, here, value, k):
        if extra:
            value = value + more[k][here].astype(f32)
        if len(out.shape) == 3:
            out[0, here[0], here[1]] = value.astype(out.dtype)
        else:
            out[here[0], here[1]] = value.astype(out.dtype)

    part = math.gcd(width, 256)
    everything = slice(None)
    for m in range(0, width, part):
        here = (slice(m, m + part), everything)
        both = lax.dot_general(
            x[:, m : m + part], act[:, : 2 * hidden], tn, preferred_element_type=f32
        )
        put(gate_out, here, both[:, :hidden], 0)
        put(up_out, here, both[:, hidden:], 1)
    for c in copies[steps + slots :]:
        c.wait()
    part = math.gcd(hidden, 128)
    for m in range(0, hidden, part):
        here = (slice(m, m + part), everything)
        value = lax.dot_general(
            act[:, 2 * hidden + m : 2 * hidden + m + part], dy[...], tn, preferred_element_type=f32
        )
        put(down_out, here, value, 2)


def weights_grads(j, xs, dygs, acts, dtype, more=()):
    slots, steps = len(xs), len(acts)
    tokens, width = xs[0].shape
    hidden = acts[0].shape[1] // 6
    rows = slots * tokens
    lead = (1,) if more else ()
    return pl.pallas_call(
        functools.partial(weights_kernel, j, slots, steps, len(more)),
        out_shape=(
            jax.ShapeDtypeStruct(lead + (width, hidden), dtype),
            jax.ShapeDtypeStruct(lead + (width, hidden), dtype),
            jax.ShapeDtypeStruct(lead + (hidden, width), dtype),
        ),
        in_specs=[ANY] * (2 * slots + steps) + [VMEM] * len(more),
        out_specs=(VMEM,) * 3,
        scratch_shapes=[
            pltpu.VMEM((rows, width), bf16),
            pltpu.VMEM((rows, width), bf16),
            pltpu.VMEM((rows, 3 * hidden), bf16),
            pltpu.SemaphoreType.DMA((2 * slots + steps,)),
        ],
        compiler_params=params(40),
        cost_estimate=pl.CostEstimate(
            flops=6 * rows * width * hidden,
            bytes_accessed=rows * (4 * width + 6 * hidden) + 6 * width * hidden,
            transcendentals=0,
        ),
        name="weights_grads",
    )(*xs, *dygs, *acts, *more)


def finish_kernel(parts, ids, kept, *refs):
    pieces, (tokens_out, gates_out) = refs[:parts], refs[parts:]
    tokens, width = tokens_out.shape
    lanes = kept.shape[1]
    total = pieces[0][:, :width].astype(f32)
    gg = pieces[0][:, width:].astype(f32)
    for p in pieces[1:]:
        total = total + p[:, :width].astype(f32)
        gg = gg + p[:, width:].astype(f32)
    tokens_out[...] = total.astype(bf16)
    gg = gg * kept[...]
    lane = lane_iota(tokens, lanes)
    place = lane_iota(tokens, TOP)
    out = jnp.zeros((tokens, TOP), f32)
    for k in range(TOP):
        value = jnp.sum(jnp.where(lane == ids[:, k : k + 1], gg, 0.0), axis=1, keepdims=True)
        out = jnp.where(place == k, value, out)
    gates_out[...] = out.astype(bf16)


def finish(ids, kept, pieces, width):
    tokens = ids.shape[0]
    return pl.pallas_call(
        functools.partial(finish_kernel, len(pieces)),
        out_shape=(
            jax.ShapeDtypeStruct((tokens, width), bf16),
            jax.ShapeDtypeStruct((tokens, TOP), bf16),
        ),
        in_specs=[VMEM] * (2 + len(pieces)),
        out_specs=(VMEM, VMEM),
        compiler_params=params(16),
        name="finish",
    )(ids, kept, *pieces)


def add(*terms):
    total = terms[0].astype(f32)
    for t in terms[1:]:
        total = total + t.astype(f32)
    return total.astype(bf16)


def on_device(tokens_in, grad_out, gates, expert_ids, replica_table, w_gate, w_up, w_down):
    devices = lax.axis_size("expert")
    tokens, width = tokens_in.shape
    lanes = -(-devices // LANES) * LANES
    chips = devices // CORES
    inner = 2 ** (int(math.log2(chips)) // 2)
    outer = chips // inner

    def moved(i, dz, dy):
        core, chip = i % CORES, i // CORES
        z, y = chip // inner, chip % inner
        return (((z + dz) % outer) * inner + (y + dy) % inner) * CORES + core

    def send_z(v):
        return lax.ppermute(v, "expert", [(i, moved(i, 1, 0)) for i in range(devices)])

    def send_y(v):
        return lax.ppermute(v, "expert", [(i, moved(i, 0, 1)) for i in range(devices)])

    def send_core(v):
        return lax.ppermute(v, "expert", [(i, i ^ 1) for i in range(devices)])

    dyg, kept = plan(replica_table, expert_ids, gates, grad_out, devices, lanes)
    own = (w_gate[0], w_up[0], w_down[0])
    weights = own + tuple(send_core(w) for w in own)

    xs = [[tokens_in]]
    dygs = [[dyg]]
    for z in range(outer):
        if z:
            xs.append([send_z(xs[z - 1][0])])
            dygs.append([send_z(dygs[z - 1][0])])
        for y in range(1, inner):
            xs[z].append(send_y(xs[z][y - 1]))
            if z > 0 and z == outer - 1 and y == inner - 1:
                dygs[z].append(send_z(dygs[z - 1][y]))
            else:
                dygs[z].append(send_y(dygs[z][y - 1]))

    per = max(1, W_ROWS // (inner * tokens))
    groups = [range(z, min(outer, z + per)) for z in range(0, outer, per)]
    sums = [None, None]

    def partial(j, group, dtype, more=()):
        return weights_grads(
            j,
            [x for z in group for x in xs[z]],
            [d for z in group for d in dygs[z]],
            [acts[z] for z in group],
            dtype,
            more,
        )

    dxs, acts, across = [], [], []
    for z in range(outer):
        *dx, act = rows_grads(xs[z], dygs[z], weights)
        dxs.append(dx)
        acts.append(act)
        if inner > 1:
            total = dx[1]
            for y in range(2, inner):
                total = add(send_y(total), dx[y])
            across.append([send_y(total)])
        else:
            across.append([])
        if len(groups) > 1 and z == groups[z // per][-1]:
            for j in range(2):
                value = partial(j, groups[z // per], f32)
                sums[j] = value if z < per else [t + v for t, v in zip(sums[j], value)]
            if z + 1 < outer:
                sums, xs[z + 1] = lax.optimization_barrier((sums, xs[z + 1]))

    if len(groups) == 1:
        other = [send_core(v) for v in partial(1, groups[0], bf16)]
        grad_w = partial(0, groups[0], bf16, other)
    else:
        other = [send_core(v.astype(bf16)) for v in sums[1]]
        grad_w = [(v + o.astype(f32)).astype(bf16)[None] for v, o in zip(sums[0], other)]

    pieces = [dxs[0][0], *across[0]]
    if outer > 1:
        total = add(dxs[1][0], *across[1])
        for z in range(2, outer):
            total = add(send_z(total), dxs[z][0], *across[z])
        pieces.append(send_z(total))
    grad_tokens, grad_gates = finish(expert_ids, kept, pieces, width)
    return (grad_tokens, grad_gates, *grad_w)


def solution(mesh):
    both = ("groups", "expert")
    return jax.shard_map(
        on_device,
        mesh=mesh,
        in_specs=(
            P(both, None),
            P(both, None),
            P(both, None),
            P(both, None),
            P("groups"),
            P("expert", None, None),
            P("expert", None, None),
            P("expert", None, None),
        ),
        out_specs=(
            P(both, None),
            P(both, None),
            P(both, None, None),
            P(both, None, None),
            P(both, None, None),
        ),
        check_vma=False,
    )
```

time: 649 us -> 135 us (0.21)
  the two profiles are of different devices: /device:TPU:13 before, /device:TPU:0 now
where the time goes in v1:
time: 135 us; the launch traced here: 134 us
  waiting for transfers between devices  59.9 us (44%)
  Pallas kernels  29.2 us (22%)
  local copies, waits for them, and re-layouts  25.2 us (19%)
  starting transfers between devices  18.4 us (14%)
    ppermute x10, waiting for transfers between devices, send_z(): lax.ppermute(v, 'expert', [(i, moved(i, 1, 0)) for i in range(devices)])  39.6 us
    unnamed x87, local copies, waits for them, and re-layouts  25.2 us
    ppermute x11, waiting for transfers between devices, send_y(): lax.ppermute(v, 'expert', [(i, moved(i, 0, 1)) for i in range(devices)])  20.3 us
    pallas_call x4, Pallas kernels, rows_grads(): pl.pallas_call(functools.partial(rows_kernel, slots), out_shape=tuple((ja...  16 us
    ppermute x11, starting transfers between devices, send_y(): lax.ppermute(v, 'expert', [(i, moved(i, 0, 1)) for i in range(devices)])  11.8 us
    pallas_call x2, Pallas kernels, weights_grads(): pl.pallas_call(functools.partial(weights_kernel, j, slots, steps, len(mor...  10.5 us
    ppermute x10, starting transfers between devices, send_z(): lax.ppermute(v, 'expert', [(i, moved(i, 1, 0)) for i in range(devices)])  5.41 us
  transfers between devices with their start and end apart: 27, of which 11 were waited for; matrix products, arithmetic and copies ran while one was open for 1% of the time, Pallas kernels for 16%

profile of v1, /device:TPU:0, one launch (start us, length us, event | category | flops | bytes accessed | tf_op | source)
XLA Modules:
  0.0 134.0 jit_solution(17874433087956497746)
XLA Ops:
  0.6 0.8 copy.14.gates
  1.4 0.8 copy.15.ids
  2.2 0.9 copy-done.36
  3.2 0.7 copy-done.38
  3.8 1.1 plan.1
  4.9 3.1 %collective-permute-start.8 = (bf16[128,1152]{1,0:T(8,128)(2,1)S(1)}, bf16[128,1152]{1,0:T(8,128)(2,1)S(1)}, u32[]{:S(2)}, u32[]{:S(2)}) collective-permute-start(bf16[128,1152]{1,0:T(8,128)(2,1)S(1)} %get-tuple-element.28.refs_2_.refs_8_), channel_id=1, source_target_pairs={{0,4},{1,5},{2,6},{3,7},{4,8},{5,9},{6,10},{7,11},{8,12},{9,13},{1... | collective-permute-start | bytes 884744 | tf_op jit(solution)/shard_map/ppermute | solution.py:328
  8.0 1.6 %collective-permute-start.6 = (bf16[128,1024]{1,0:T(8,128)(2,1)}, bf16[128,1024]{1,0:T(8,128)(2,1)S(1)}, u32[]{:S(2)}, u32[]{:S(2)}) collective-permute-start(bf16[128,1024]{1,0:T(8,128)(2,1)} %refs_0_.5), channel_id=1, source_target_pairs={{0,4},{1,5},{2,6},{3,7},{4,8},{5,9},{6,10},{7,11},{8,12},{9,13},{1... | collective-permute-start | bytes 786440 | tf_op jit(solution)/shard_map/ppermute | solution.py:328
  9.6 0.5 collective-permute-start.3
  10.1 12.6 %collective-permute-done.6.refs_0_.refs_2_ = bf16[128,1024]{1,0:T(8,128)(2,1)S(1)} collective-permute-done((bf16[128,1024]{1,0:T(8,128)(2,1)}, bf16[128,1024]{1,0:T(8,128)(2,1)S(1)}, u32[]{:S(2)}, u32[]{:S(2)}) %collective-permute-start.6) | collective-permute-done | bytes 262176 | tf_op jit(solution)/shard_map/ppermute | solution.py:328
  22.7 1.6 %collective-permute-start.7 = (bf16[128,1024]{1,0:T(8,128)(2,1)S(1)}, bf16[128,1024]{1,0:T(8,128)(2,1)S(1)}, u32[]{:S(2)}, u32[]{:S(2)}) collective-permute-start(bf16[128,1024]{1,0:T(8,128)(2,1)S(1)} %collective-permute-done.6.refs_0_.refs_2_), channel_id=1, source_target_pairs={{0,2},{1,3},{2,0},{3,1},{4,6},{5,7},{6,4},{7,5},{8,10},{9,11},{10,... | collective-permute-start | bytes 786440 | tf_op jit(solution)/shard_map/ppermute | solution.py:331
  24.3 7.7 %collective-permute-done.12.refs_0_.refs_4_ = bf16[128,1024]{1,0:T(8,128)(2,1)S(1)} collective-permute-done((bf16[128,1024]{1,0:T(8,128)(2,1)S(1)}, bf16[128,1024]{1,0:T(8,128)(2,1)S(1)}, u32[]{:S(2)}, u32[]{:S(2)}) %collective-permute-start.12) | collective-permute-done | bytes 262176 | tf_op jit(solution)/shard_map/ppermute | solution.py:328
  32.0 1.3 collective-permute-start.9
  33.3 7.7 %collective-permute-done.14.refs_2_.refs_12_ = bf16[128,1152]{1,0:T(8,128)(2,1)S(1)} collective-permute-done((bf16[128,1152]{1,0:T(8,128)(2,1)S(1)}, bf16[128,1152]{1,0:T(8,128)(2,1)S(1)}, u32[]{:S(2)}, u32[]{:S(2)}) %collective-permute-start.14) | collective-permute-done | bytes 294944 | tf_op jit(solution)/shard_map/ppermute | solution.py:328
  41.0 1.1 collective-permute-start.13
  42.1 1.0 collective-permute-start.15
  43.2 1.1 copy-done.39
  44.3 1.1 copy-done.40
  45.4 1.1 copy-done.41
  46.6 4.0 %rows_grads.5 = (bf16[128,1152]{1,0:T(8,128)(2,1)S(1)}, bf16[128,1152]{1,0:T(8,128)(2,1)S(1)}, bf16[256,2304]{1,0:T(8,128)(2,1)S(1)}) custom-call(bf16[128,1024]{1,0:T(8,128)(2,1)S(1)} %collective-permute-done.6.refs_0_.refs_2_, bf16[128,1024]{1,0:T(8,128)(2,1)S(1)} %collective-permute-done.7.refs_1_.refs_3_, ...), custom_call_target="tpu_custom_call" | custom-call | flops 2013265920 | bytes 9306112 | tf_op jit(solution)/shard_map/rows_grads/pallas_call | solution.py:165
  50.6 1.1 collective-permute-start.10
  51.7 1.1 collective-permute-start.19
  52.7 3.2 %collective-permute-done.15.refs_3_.refs_13_ = bf16[128,1152]{1,0:T(8,128)(2,1)S(1)} collective-permute-done((bf16[128,1152]{1,0:T(8,128)(2,1)S(1)}, bf16[128,1152]{1,0:T(8,128)(2,1)S(1)}, u32[]{:S(2)}, u32[]{:S(2)}) %collective-permute-start.15) | collective-permute-done | bytes 294944 | tf_op jit(solution)/shard_map/ppermute | solution.py:331
  56.0 4.0 %rows_grads.6 = (bf16[128,1152]{1,0:T(8,128)(2,1)S(1)}, bf16[128,1152]{1,0:T(8,128)(2,1)S(1)}, bf16[256,2304]{1,0:T(8,128)(2,1)S(1)}) custom-call(bf16[128,1024]{1,0:T(8,128)(2,1)S(1)} %collective-permute-done.12.refs_0_.refs_4_, bf16[128,1024]{1,0:T(8,128)(2,1)S(1)} %collective-permute-done.13.refs_1_.refs_5_, ...), custom_call_target="tpu_custom_call" | custom-call | flops 2013265920 | bytes 9306112 | tf_op jit(solution)/shard_map/rows_grads/pallas_call | solution.py:165
  60.0 0.8 collective-permute-start.16
  60.8 1.5 %collective-permute-done.10 = bf16[128,1152]{1,0:T(8,128)(2,1)S(1)} collective-permute-done((bf16[128,1152]{1,0:T(8,128)(2,1)S(1)}, bf16[128,1152]{1,0:T(8,128)(2,1)S(1)}, u32[]{:S(2)}, u32[]{:S(2)}) %collective-permute-start.10) | collective-permute-done | bytes 294944 | tf_op jit(solution)/shard_map/ppermute | solution.py:331
  62.4 0.4 collective-permute-start.11
  62.8 1.1 collective-permute-start
  63.9 4.0 %collective-permute-done.19.refs_1_.refs_7_ = bf16[128,1024]{1,0:T(8,128)(2,1)S(1)} collective-permute-done((bf16[128,1024]{1,0:T(8,128)(2,1)S(1)}, bf16[128,1024]{1,0:T(8,128)(2,1)S(1)}, u32[]{:S(2)}, u32[]{:S(2)}) %collective-permute-start.19) | collective-permute-done | bytes 262176 | tf_op jit(solution)/shard_map/ppermute | solution.py:331
  67.9 0.8 collective-permute-start.1
  68.7 1.0 collective-permute-done.21.refs_3_.refs_15_
  69.7 4.0 %rows_grads.7 = (bf16[128,1152]{1,0:T(8,128)(2,1)S(1)}, bf16[128,1152]{1,0:T(8,128)(2,1)S(1)}, bf16[256,2304]{1,0:T(8,128)(2,1)S(1)}) custom-call(bf16[128,1024]{1,0:T(8,128)(2,1)S(1)} %collective-permute-done.18.refs_0_.refs_6_, bf16[128,1024]{1,0:T(8,128)(2,1)S(1)} %collective-permute-done.19.refs_1_.refs_7_, ...), custom_call_target="tpu_custom_call" | custom-call | flops 2013265920 | bytes 9306112 | tf_op jit(solution)/shard_map/rows_grads/pallas_call | solution.py:165
  73.7 1.1 collective-permute-start.22
  74.8 0.1 add_convert_fusion.1
  74.9 0.2 collective-permute-start.17
  75.1 4.7 %collective-permute-done.refs_1_ = bf16[128,1024]{1,0:T(8,128)(2,1)S(1)} collective-permute-done((bf16[128,1024]{1,0:T(8,128)(2,1)S(1)}, bf16[128,1024]{1,0:T(8,128)(2,1)S(1)}, u32[]{:S(2)}, u32[]{:S(2)}) %collective-permute-start) | collective-permute-done | bytes 262176 | tf_op jit(solution)/shard_map/ppermute | solution.py:331
  79.8 6.3 %collective-permute-done.1.refs_3_.refs_9_ = bf16[128,1152]{1,0:T(8,128)(2,1)S(1)} collective-permute-done((bf16[128,1152]{1,0:T(8,128)(2,1)S(1)}, bf16[128,1152]{1,0:T(8,128)(2,1)S(1)}, u32[]{:S(2)}, u32[]{:S(2)}) %collective-permute-start.1) | collective-permute-done | bytes 294944 | tf_op jit(solution)/shard_map/ppermute | solution.py:331
  86.2 4.0 %rows_grads.4 = (bf16[128,1152]{1,0:T(8,128)(2,1)S(1)}, bf16[128,1152]{1,0:T(8,128)(2,1)S(1)}, bf16[256,2304]{1,0:T(8,128)(2,1)S(1)}) custom-call(bf16[128,1024]{1,0:T(8,128)(2,1)S(1)} %copy-done.18, bf16[128,1024]{1,0:T(8,128)(2,1)S(1)} %collective-permute-done.refs_1_, bf16[128,1152]{1,0:T(8,128)(2,1)S(1)} %get-tuple-element.28.refs_2_.refs_8_, ...), custom_call_target="tpu_custom_call" | custom-call | flops 2013265920 | bytes 9306112 | tf_op jit(solution)/shard_map/rows_grads/pallas_call | solution.py:165
  90.2 0.8 collective-permute-start.5
  91.2 4.4 %weights_grads.2 = (bf16[1024,384]{1,0:T(8,128)(2,1)}, bf16[1024,384]{1,0:T(8,128)(2,1)}, bf16[384,1024]{1,0:T(8,128)(2,1)}) custom-call(bf16[128,1024]{1,0:T(8,128)(2,1)S(1)} %copy-done.18, bf16[128,1024]{1,0:T(8,128)(2,1)S(1)} %collective-permute-done.refs_1_, bf16[128,1024]{1,0:T(8,128)(2,1)S(1)} %collective-permute-done.6.refs_0_.refs_2_, ...), custom_call_target="tpu_custom_call" | custom-call | flops 2415919104 | bytes 8912896 | tf_op jit(solution)/shard_map/weights_grads/pallas_call | solution.py:247
  95.7 0.5 collective-permute-start.25
  96.3 0.1 add_convert_fusion
  96.5 0.5 collective-permute-done.5.refs_1_
  97.0 10.6 %collective-permute-done.23.refs_2_ = bf16[128,1152]{1,0:T(8,128)(2,1)S(1)} collective-permute-done((bf16[128,1152]{1,0:T(8,128)(2,1)S(1)}, bf16[128,1152]{1,0:T(8,128)(2,1)S(1)}, u32[]{:S(2)}, u32[]{:S(2)}) %collective-permute-start.23) | collective-permute-done | bytes 294944 | tf_op jit(solution)/shard_map/ppermute | solution.py:328
  107.6 1.6 %finish.1 = (bf16[128,1024]{1,0:T(8,128)(2,1)}, bf16[128,8]{1,0:T(8,128)(2,1)S(1)}) custom-call(s32[128,8]{1,0:T(8,128)S(1)} %copy-done.35, f32[128,128]{1,0:T(8,128)S(1)} %get-tuple-element.27.kept, bf16[128,1152]{1,0:T(8,128)(2,1)S(1)} %get-tuple-element.29.refs_0_, bf16[128,1152]{1,0:T(8,128)(2,1)S(1)} %collective-permute-done.5.refs_1_, ...), custom_call_target="tpu_custom_call" | custom-call | tf_op jit(solution)/shard_map/finish/pallas_call | solution.py:294
  109.3 0.6 copy-done.37
  109.9 1.4 %copy.16 = bf16[128,8]{0,1:T(8,128)(2,1)} copy(bf16[128,8]{1,0:T(8,128)(2,1)} %copy-done.37) | data formatting | bytes 4096
  111.3 1.3 copy-done.1
  112.6 1.0 copy-done.3
  113.5 1.0 copy-done.5
  114.5 1.0 copy-done.7
  115.4 1.0 copy-done.9
  116.4 1.0 copy-done.11
  117.4 1.0 copy-done.13
  118.3 1.0 copy-done.15
  119.3 1.0 copy-done.17
  120.3 0.9 copy-done.19
  121.2 0.9 copy-done.21
  122.2 0.9 copy-done.23
  123.1 0.9 copy-done.25
  124.1 0.9 copy-done.27
  125.0 0.9 copy-done.29
  126.0 0.9 copy-done.31
  126.9 0.9 copy-done.33
  127.9 6.0 %weights_grads.3 = (bf16[1,1024,384]{2,1,0:T(8,128)(2,1)}, bf16[1,1024,384]{2,1,0:T(8,128)(2,1)}, bf16[1,384,1024]{2,1,0:T(8,128)(2,1)}) custom-call(bf16[128,1024]{1,0:T(8,128)(2,1)S(1)} %copy-done.19, bf16[128,1024]{1,0:T(8,128)(2,1)S(1)} %copy-done.33, bf16[128,1024]{1,0:T(8,128)(2,1)S(1)} %copy-done.21, bf16[128,1024]{1,0:T(8,128)(2,1)S(1)} %copy-done.25, ...), custom_call_target="tpu_custom_call" | custom-call | flops 2415919104 | bytes 8912896 | tf_op jit(solution)/shard_map/weights_grads/pallas_call | solution.py:247
  (88 shorter events, 0.5 us)
Async XLA Ops:
  2.2 0.9 copy-start.36
  3.8 39.3 %copy-start.34 = (s32[128,8]{1,0:T(8,128)}, s32[128,8]{1,0:T(8,128)S(1)}, u32[]{:S(2)}) copy-start(s32[128,8]{1,0:T(8,128)S(1)} %copy.15.ids) | copy-start | bytes 12292
  4.9 86.1 %copy-start.2 = (bf16[128,1152]{1,0:T(8,128)(2,1)}, bf16[128,1152]{1,0:T(8,128)(2,1)S(1)}, u32[]{:S(2)}) copy-start(bf16[128,1152]{1,0:T(8,128)(2,1)S(1)} %get-tuple-element.28.refs_2_.refs_8_) | copy-start | bytes 884740
  4.9 17.7 %collective-permute-start.8 = (bf16[128,1152]{1,0:T(8,128)(2,1)S(1)}, bf16[128,1152]{1,0:T(8,128)(2,1)S(1)}, u32[]{:S(2)}, u32[]{:S(2)}) collective-permute-start(bf16[128,1152]{1,0:T(8,128)(2,1)S(1)} %get-tuple-element.28.refs_2_.refs_8_), channel_id=1, source_target_pairs={{0,4},{1,5},{2,6},{3,7},{4,8},{5,9},{6,10},{7,11},{8,12},{9,13},{1... | collective-permute-start | bytes 884744 | tf_op jit(solution)/shard_map/ppermute | solution.py:328
  8.0 14.7 %collective-permute-start.6 = (bf16[128,1024]{1,0:T(8,128)(2,1)}, bf16[128,1024]{1,0:T(8,128)(2,1)S(1)}, u32[]{:S(2)}, u32[]{:S(2)}) collective-permute-start(bf16[128,1024]{1,0:T(8,128)(2,1)} %refs_0_.5), channel_id=1, source_target_pairs={{0,4},{1,5},{2,6},{3,7},{4,8},{5,9},{6,10},{7,11},{8,12},{9,13},{1... | collective-permute-start | bytes 786440 | tf_op jit(solution)/shard_map/ppermute | solution.py:328
  9.6 32.6 %collective-permute-start.2 = (bf16[1024,384]{1,0:T(8,128)(2,1)}, bf16[1024,384]{1,0:T(8,128)(2,1)S(1)}, u32[]{:S(2)}, u32[]{:S(2)}) collective-permute-start(bf16[1024,384]{1,0:T(8,128)(2,1)} %bitcast.3), channel_id=1, source_target_pairs={{0,1},{1,0},{2,3},{3,2},{4,5},{5,4},{6,7},{7,6},{8,9},{9,8},{10,11... | collective-permute-start | bytes 2359304 | tf_op jit(solution)/shard_map/ppermute | solution.py:334
  9.6 33.6 %collective-permute-start.3 = (bf16[1024,384]{1,0:T(8,128)(2,1)}, bf16[1024,384]{1,0:T(8,128)(2,1)S(1)}, u32[]{:S(2)}, u32[]{:S(2)}) collective-permute-start(bf16[1024,384]{1,0:T(8,128)(2,1)} %bitcast.8), channel_id=1, source_target_pairs={{0,1},{1,0},{2,3},{3,2},{4,5},{5,4},{6,7},{7,6},{8,9},{9,8},{10,11... | collective-permute-start | bytes 2359304 | tf_op jit(solution)/shard_map/ppermute | solution.py:334
  10.1 33.1 %collective-permute-start.4 = (bf16[384,1024]{1,0:T(8,128)(2,1)}, bf16[384,1024]{1,0:T(8,128)(2,1)S(1)}, u32[]{:S(2)}, u32[]{:S(2)}) collective-permute-start(bf16[384,1024]{1,0:T(8,128)(2,1)} %bitcast.13), channel_id=1, source_target_pairs={{0,1},{1,0},{2,3},{3,2},{4,5},{5,4},{6,7},{7,6},{8,9},{9,8},{10,11... | collective-permute-start | bytes 2359304 | tf_op jit(solution)/shard_map/ppermute | solution.py:334
  22.7 68.4 %copy-start.20 = (bf16[128,1024]{1,0:T(8,128)(2,1)}, bf16[128,1024]{1,0:T(8,128)(2,1)S(1)}, u32[]{:S(2)}) copy-start(bf16[128,1024]{1,0:T(8,128)(2,1)S(1)} %collective-permute-done.6.refs_0_.refs_2_) | copy-start | bytes 786436
  22.7 9.3 %collective-permute-start.12 = (bf16[128,1024]{1,0:T(8,128)(2,1)S(1)}, bf16[128,1024]{1,0:T(8,128)(2,1)S(1)}, u32[]{:S(2)}, u32[]{:S(2)}) collective-permute-start(bf16[128,1024]{1,0:T(8,128)(2,1)S(1)} %collective-permute-done.6.refs_0_.refs_2_), channel_id=1, source_target_pairs={{0,4},{1,5},{2,6},{3,7},{4,8},{5,9},{6,10},{7,11},{8,12},{9,13},{1... | collective-permute-start | bytes 786440 | tf_op jit(solution)/shard_map/ppermute | solution.py:328
  22.7 68.4 %copy-start.4 = (bf16[128,1152]{1,0:T(8,128)(2,1)}, bf16[128,1152]{1,0:T(8,128)(2,1)S(1)}, u32[]{:S(2)}) copy-start(bf16[128,1152]{1,0:T(8,128)(2,1)S(1)} %collective-permute-done.8.refs_2_.refs_10_) | copy-start | bytes 884740
  22.7 9.3 %collective-permute-start.7 = (bf16[128,1024]{1,0:T(8,128)(2,1)S(1)}, bf16[128,1024]{1,0:T(8,128)(2,1)S(1)}, u32[]{:S(2)}, u32[]{:S(2)}) collective-permute-start(bf16[128,1024]{1,0:T(8,128)(2,1)S(1)} %collective-permute-done.6.refs_0_.refs_2_), channel_id=1, source_target_pairs={{0,2},{1,3},{2,0},{3,1},{4,6},{5,7},{6,4},{7,5},{8,10},{9,11},{10,... | collective-permute-start | bytes 786440 | tf_op jit(solution)/shard_map/ppermute | solution.py:331
  31.9 59.1 %copy-start.22 = (bf16[128,1024]{1,0:T(8,128)(2,1)}, bf16[128,1024]{1,0:T(8,128)(2,1)S(1)}, u32[]{:S(2)}) copy-start(bf16[128,1024]{1,0:T(8,128)(2,1)S(1)} %collective-permute-done.12.refs_0_.refs_4_) | copy-start | bytes 786436
  31.9 9.1 %collective-permute-start.14 = (bf16[128,1152]{1,0:T(8,128)(2,1)S(1)}, bf16[128,1152]{1,0:T(8,128)(2,1)S(1)}, u32[]{:S(2)}, u32[]{:S(2)}) collective-permute-start(bf16[128,1152]{1,0:T(8,128)(2,1)S(1)} %collective-permute-done.8.refs_2_.refs_10_), channel_id=1, source_target_pairs={{0,4},{1,5},{2,6},{3,7},{4,8},{5,9},{6,10},{7,11},{8,12},{9,13},{1... | collective-permute-start | bytes 884744 | tf_op jit(solution)/shard_map/ppermute | solution.py:328
  32.0 59.1 %copy-start.24 = (bf16[128,1024]{1,0:T(8,128)(2,1)}, bf16[128,1024]{1,0:T(8,128)(2,1)S(1)}, u32[]{:S(2)}) copy-start(bf16[128,1024]{1,0:T(8,128)(2,1)S(1)} %collective-permute-done.7.refs_1_.refs_3_) | copy-start | bytes 786436
  32.0 9.1 %collective-permute-start.9 = (bf16[128,1152]{1,0:T(8,128)(2,1)S(1)}, bf16[128,1152]{1,0:T(8,128)(2,1)S(1)}, u32[]{:S(2)}, u32[]{:S(2)}) collective-permute-start(bf16[128,1152]{1,0:T(8,128)(2,1)S(1)} %collective-permute-done.8.refs_2_.refs_10_), channel_id=1, source_target_pairs={{0,2},{1,3},{2,0},{3,1},{4,6},{5,7},{6,4},{7,5},{8,10},{9,11},{10,... | collective-permute-start | bytes 884744 | tf_op jit(solution)/shard_map/ppermute | solution.py:331
  41.0 50.0 %copy-start.6 = (bf16[128,1152]{1,0:T(8,128)(2,1)}, bf16[128,1152]{1,0:T(8,128)(2,1)S(1)}, u32[]{:S(2)}) copy-start(bf16[128,1152]{1,0:T(8,128)(2,1)S(1)} %collective-permute-done.14.refs_2_.refs_12_) | copy-start | bytes 884740
  41.0 10.7 %collective-permute-start.18 = (bf16[128,1024]{1,0:T(8,128)(2,1)S(1)}, bf16[128,1024]{1,0:T(8,128)(2,1)S(1)}, u32[]{:S(2)}, u32[]{:S(2)}) collective-permute-start(bf16[128,1024]{1,0:T(8,128)(2,1)S(1)} %collective-permute-done.12.refs_0_.refs_4_), channel_id=1, source_target_pairs={{0,4},{1,5},{2,6},{3,7},{4,8},{5,9},{6,10},{7,11},{8,12},{9,13},{1... | collective-permute-start | bytes 786440 | tf_op jit(solution)/shard_map/ppermute | solution.py:328
  41.0 50.0 %copy-start.8 = (bf16[128,1152]{1,0:T(8,128)(2,1)}, bf16[128,1152]{1,0:T(8,128)(2,1)S(1)}, u32[]{:S(2)}) copy-start(bf16[128,1152]{1,0:T(8,128)(2,1)S(1)} %collective-permute-done.9.refs_3_.refs_11_) | copy-start | bytes 884740
  41.0 11.7 %collective-permute-start.13 = (bf16[128,1024]{1,0:T(8,128)(2,1)S(1)}, bf16[128,1024]{1,0:T(8,128)(2,1)S(1)}, u32[]{:S(2)}, u32[]{:S(2)}) collective-permute-start(bf16[128,1024]{1,0:T(8,128)(2,1)S(1)} %collective-permute-done.12.refs_0_.refs_4_), channel_id=1, source_target_pairs={{0,2},{1,3},{2,0},{3,1},{4,6},{5,7},{6,4},{7,5},{8,10},{9,11},{10,... | collective-permute-start | bytes 786440 | tf_op jit(solution)/shard_map/ppermute | solution.py:331
  42.1 13.8 %collective-permute-start.15 = (bf16[128,1152]{1,0:T(8,128)(2,1)S(1)}, bf16[128,1152]{1,0:T(8,128)(2,1)S(1)}, u32[]{:S(2)}, u32[]{:S(2)}) collective-permute-start(bf16[128,1152]{1,0:T(8,128)(2,1)S(1)} %collective-permute-done.14.refs_2_.refs_12_), channel_id=1, source_target_pairs={{0,2},{1,3},{2,0},{3,1},{4,6},{5,7},{6,4},{7,5},{8,10},{9,11},{10,... | collective-permute-start | bytes 884744 | tf_op jit(solution)/shard_map/ppermute | solution.py:331
  43.1 1.1 copy-start.39
  44.3 1.1 copy-start.40
  45.4 1.1 copy-start.41
  50.6 12.3 %copy-start.18 = (bf16[128,1024]{1,0:T(8,128)(2,1)S(1)}, bf16[128,1024]{1,0:T(8,128)(2,1)}, u32[]{:S(2)}) copy-start(bf16[128,1024]{1,0:T(8,128)(2,1)} %refs_0_.5) | copy-start | bytes 786436
  50.6 11.7 %collective-permute-start.10 = (bf16[128,1152]{1,0:T(8,128)(2,1)S(1)}, bf16[128,1152]{1,0:T(8,128)(2,1)S(1)}, u32[]{:S(2)}, u32[]{:S(2)}) collective-permute-start(bf16[128,1152]{1,0:T(8,128)(2,1)S(1)} %get-tuple-element.32), channel_id=1, source_target_pairs={{0,2},{1,3},{2,0},{3,1},{4,6},{5,7},{6,4},{7,5},{8,10},{9,11},{10,... | collective-permute-start | bytes 884744 | tf_op jit(solution)/shard_map/ppermute | solution.py:331
  51.7 11.1 %collective-permute-start.20 = (bf16[128,1152]{1,0:T(8,128)(2,1)S(1)}, bf16[128,1152]{1,0:T(8,128)(2,1)S(1)}, u32[]{:S(2)}, u32[]{:S(2)}) collective-permute-start(bf16[128,1152]{1,0:T(8,128)(2,1)S(1)} %collective-permute-done.14.refs_2_.refs_12_), channel_id=1, source_target_pairs={{0,4},{1,5},{2,6},{3,7},{4,8},{5,9},{6,10},{7,11},{8,12},{9,13},{1... | collective-permute-start | bytes 884744 | tf_op jit(solution)/shard_map/ppermute | solution.py:328
  51.7 39.4 %copy-start.26 = (bf16[128,1024]{1,0:T(8,128)(2,1)}, bf16[128,1024]{1,0:T(8,128)(2,1)S(1)}, u32[]{:S(2)}) copy-start(bf16[128,1024]{1,0:T(8,128)(2,1)S(1)} %collective-permute-done.18.refs_0_.refs_6_) | copy-start | bytes 786436
  51.7 16.2 %collective-permute-start.19 = (bf16[128,1024]{1,0:T(8,128)(2,1)S(1)}, bf16[128,1024]{1,0:T(8,128)(2,1)S(1)}, u32[]{:S(2)}, u32[]{:S(2)}) collective-permute-start(bf16[128,1024]{1,0:T(8,128)(2,1)S(1)} %collective-permute-done.18.refs_0_.refs_6_), channel_id=1, source_target_pairs={{0,2},{1,3},{2,0},{3,1},{4,6},{5,7},{6,4},{7,5},{8,10},{9,11},{10,... | collective-permute-start | bytes 786440 | tf_op jit(solution)/shard_map/ppermute | solution.py:331
  52.7 38.3 %copy-start.28 = (bf16[128,1024]{1,0:T(8,128)(2,1)}, bf16[128,1024]{1,0:T(8,128)(2,1)S(1)}, u32[]{:S(2)}) copy-start(bf16[128,1024]{1,0:T(8,128)(2,1)S(1)} %collective-permute-done.13.refs_1_.refs_5_) | copy-start | bytes 786436
  56.0 35.1 %copy-start.10 = (bf16[128,1152]{1,0:T(8,128)(2,1)}, bf16[128,1152]{1,0:T(8,128)(2,1)S(1)}, u32[]{:S(2)}) copy-start(bf16[128,1152]{1,0:T(8,128)(2,1)S(1)} %collective-permute-done.15.refs_3_.refs_13_) | copy-start | bytes 884740
  60.0 14.8 %collective-permute-start.16 = (bf16[128,1152]{1,0:T(8,128)(2,1)S(1)}, bf16[128,1152]{1,0:T(8,128)(2,1)S(1)}, u32[]{:S(2)}, u32[]{:S(2)}) collective-permute-start(bf16[128,1152]{1,0:T(8,128)(2,1)S(1)} %get-tuple-element.34), channel_id=1, source_target_pairs={{0,2},{1,3},{2,0},{3,1},{4,6},{5,7},{6,4},{7,5},{8,10},{9,11},{10,... | collective-permute-start | bytes 884744 | tf_op jit(solution)/shard_map/ppermute | solution.py:331
  60.8 8.8 %collective-permute-start.21 = (bf16[128,1152]{1,0:T(8,128)(2,1)S(1)}, bf16[128,1152]{1,0:T(8,128)(2,1)S(1)}, u32[]{:S(2)}, u32[]{:S(2)}) collective-permute-start(bf16[128,1152]{1,0:T(8,128)(2,1)S(1)} %collective-permute-done.15.refs_3_.refs_13_), channel_id=1, source_target_pairs={{0,4},{1,5},{2,6},{3,7},{4,8},{5,9},{6,10},{7,11},{8,12},{9,13},{1... | collective-permute-start | bytes 884744 | tf_op jit(solution)/shard_map/ppermute | solution.py:328
  62.4 12.4 %collective-permute-start.11 = (bf16[128,1152]{1,0:T(8,128)(2,1)S(1)}, bf16[128,1152]{1,0:T(8,128)(2,1)S(1)}, u32[]{:S(2)}, u32[]{:S(2)}) collective-permute-start(bf16[128,1152]{1,0:T(8,128)(2,1)S(1)} %add_convert_fusion.2), channel_id=1, source_target_pairs={{0,4},{1,5},{2,6},{3,7},{4,8},{5,9},{6,10},{7,11},{8,12},{9,13},{1... | collective-permute-start | bytes 884744 | tf_op jit(solution)/shard_map/ppermute | solution.py:328
  62.8 28.3 %copy-start.12 = (bf16[128,1152]{1,0:T(8,128)(2,1)}, bf16[128,1152]{1,0:T(8,128)(2,1)S(1)}, u32[]{:S(2)}) copy-start(bf16[128,1152]{1,0:T(8,128)(2,1)S(1)} %collective-permute-done.20.refs_2_.refs_14_) | copy-start | bytes 884740
  62.8 17.0 %collective-permute-start = (bf16[128,1024]{1,0:T(8,128)(2,1)S(1)}, bf16[128,1024]{1,0:T(8,128)(2,1)S(1)}, u32[]{:S(2)}, u32[]{:S(2)}) collective-permute-start(bf16[128,1024]{1,0:T(8,128)(2,1)S(1)} %copy-done.18), channel_id=1, source_target_pairs={{0,2},{1,3},{2,0},{3,1},{4,6},{5,7},{6,4},{7,5},{8,10},{9,11},{10,... | collective-permute-start | bytes 786440 | tf_op jit(solution)/shard_map/ppermute | solution.py:331
  67.9 23.2 %copy-start.30 = (bf16[128,1024]{1,0:T(8,128)(2,1)}, bf16[128,1024]{1,0:T(8,128)(2,1)S(1)}, u32[]{:S(2)}) copy-start(bf16[128,1024]{1,0:T(8,128)(2,1)S(1)} %collective-permute-done.19.refs_1_.refs_7_) | copy-start | bytes 786436
  67.9 18.3 %collective-permute-start.1 = (bf16[128,1152]{1,0:T(8,128)(2,1)S(1)}, bf16[128,1152]{1,0:T(8,128)(2,1)S(1)}, u32[]{:S(2)}, u32[]{:S(2)}) collective-permute-start(bf16[128,1152]{1,0:T(8,128)(2,1)S(1)} %get-tuple-element.28.refs_2_.refs_8_), channel_id=1, source_target_pairs={{0,2},{1,3},{2,0},{3,1},{4,6},{5,7},{6,4},{7,5},{8,10},{9,11},{10,... | collective-permute-start | bytes 884744 | tf_op jit(solution)/shard_map/ppermute | solution.py:331
  69.7 21.5 %copy-start.14 = (bf16[128,1152]{1,0:T(8,128)(2,1)}, bf16[128,1152]{1,0:T(8,128)(2,1)S(1)}, u32[]{:S(2)}) copy-start(bf16[128,1152]{1,0:T(8,128)(2,1)S(1)} %collective-permute-done.21.refs_3_.refs_15_) | copy-start | bytes 884740
  73.7 22.5 %collective-permute-start.22 = (bf16[128,1152]{1,0:T(8,128)(2,1)S(1)}, bf16[128,1152]{1,0:T(8,128)(2,1)S(1)}, u32[]{:S(2)}, u32[]{:S(2)}) collective-permute-start(bf16[128,1152]{1,0:T(8,128)(2,1)S(1)} %get-tuple-element.36), channel_id=1, source_target_pairs={{0,2},{1,3},{2,0},{3,1},{4,6},{5,7},{6,4},{7,5},{8,10},{9,11},{10,... | collective-permute-start | bytes 884744 | tf_op jit(solution)/shard_map/ppermute | solution.py:331
  74.9 21.4 %collective-permute-start.17 = (bf16[128,1152]{1,0:T(8,128)(2,1)S(1)}, bf16[128,1152]{1,0:T(8,128)(2,1)S(1)}, u32[]{:S(2)}, u32[]{:S(2)}) collective-permute-start(bf16[128,1152]{1,0:T(8,128)(2,1)S(1)} %add_convert_fusion.1), channel_id=1, source_target_pairs={{0,4},{1,5},{2,6},{3,7},{4,8},{5,9},{6,10},{7,11},{8,12},{9,13},{1... | collective-permute-start | bytes 884744 | tf_op jit(solution)/shard_map/ppermute | solution.py:328
  79.8 11.3 %copy-start.32 = (bf16[128,1024]{1,0:T(8,128)(2,1)}, bf16[128,1024]{1,0:T(8,128)(2,1)S(1)}, u32[]{:S(2)}) copy-start(bf16[128,1024]{1,0:T(8,128)(2,1)S(1)} %collective-permute-done.refs_1_) | copy-start | bytes 786436
  86.2 5.0 %copy-start.16 = (bf16[128,1152]{1,0:T(8,128)(2,1)}, bf16[128,1152]{1,0:T(8,128)(2,1)S(1)}, u32[]{:S(2)}) copy-start(bf16[128,1152]{1,0:T(8,128)(2,1)S(1)} %collective-permute-done.1.refs_3_.refs_9_) | copy-start | bytes 884740
  90.2 5.4 %copy-start = (bf16[256,2304]{1,0:T(8,128)(2,1)}, bf16[256,2304]{1,0:T(8,128)(2,1)S(1)}, u32[]{:S(2)}) copy-start(bf16[256,2304]{1,0:T(8,128)(2,1)S(1)} %get-tuple-element.39.refs_16_) | copy-start | bytes 3538948
  90.2 6.8 %collective-permute-start.5 = (bf16[128,1152]{1,0:T(8,128)(2,1)S(1)}, bf16[128,1152]{1,0:T(8,128)(2,1)S(1)}, u32[]{:S(2)}, u32[]{:S(2)}) collective-permute-start(bf16[128,1152]{1,0:T(8,128)(2,1)S(1)} %get-tuple-element.30), channel_id=1, source_target_pairs={{0,2},{1,3},{2,0},{3,1},{4,6},{5,7},{6,4},{7,5},{8,10},{9,11},{10,... | collective-permute-start | bytes 884744 | tf_op jit(solution)/shard_map/ppermute | solution.py:331
  95.6 12.0 %copy-start.35 = (s32[128,8]{1,0:T(8,128)S(1)}, s32[128,8]{1,0:T(8,128)}, u32[]{:S(2)}) copy-start(s32[128,8]{1,0:T(8,128)} %copy-done.34) | copy-start | bytes 12292
  95.6 15.7 %collective-permute-start.24 = (bf16[1024,384]{1,0:T(8,128)(2,1)}, bf16[1024,384]{1,0:T(8,128)(2,1)}, u32[]{:S(2)}, u32[]{:S(2)}) collective-permute-start(bf16[1024,384]{1,0:T(8,128)(2,1)} %get-tuple-element.43), channel_id=1, source_target_pairs={{0,1},{1,0},{2,3},{3,2},{4,5},{5,4},{6,7},{7,6},{8,9},{9,8},{10,11... | collective-permute-start | bytes 2359304 | tf_op jit(solution)/shard_map/ppermute | solution.py:334
  95.7 15.6 %collective-permute-start.25 = (bf16[1024,384]{1,0:T(8,128)(2,1)}, bf16[1024,384]{1,0:T(8,128)(2,1)}, u32[]{:S(2)}, u32[]{:S(2)}) collective-permute-start(bf16[1024,384]{1,0:T(8,128)(2,1)} %get-tuple-element.44), channel_id=1, source_target_pairs={{0,1},{1,0},{2,3},{3,2},{4,5},{5,4},{6,7},{7,6},{8,9},{9,8},{10,11... | collective-permute-start | bytes 2359304 | tf_op jit(solution)/shard_map/ppermute | solution.py:334
  96.2 15.1 %collective-permute-start.26 = (bf16[384,1024]{1,0:T(8,128)(2,1)}, bf16[384,1024]{1,0:T(8,128)(2,1)}, u32[]{:S(2)}, u32[]{:S(2)}) collective-permute-start(bf16[384,1024]{1,0:T(8,128)(2,1)} %get-tuple-element.45), channel_id=1, source_target_pairs={{0,1},{1,0},{2,3},{3,2},{4,5},{5,4},{6,7},{7,6},{8,9},{9,8},{10,11... | collective-permute-start | bytes 2359304 | tf_op jit(solution)/shard_map/ppermute | solution.py:334
  96.4 11.2 %collective-permute-start.23 = (bf16[128,1152]{1,0:T(8,128)(2,1)S(1)}, bf16[128,1152]{1,0:T(8,128)(2,1)S(1)}, u32[]{:S(2)}, u32[]{:S(2)}) collective-permute-start(bf16[128,1152]{1,0:T(8,128)(2,1)S(1)} %add_convert_fusion), channel_id=1, source_target_pairs={{0,4},{1,5},{2,6},{3,7},{4,8},{5,9},{6,10},{7,11},{8,12},{9,13},{1... | collective-permute-start | bytes 884744 | tf_op jit(solution)/shard_map/ppermute | solution.py:328
  111.3 1.3 copy-start.1
  112.6 1.0 copy-start.3
  113.5 1.0 copy-start.5
  114.5 1.0 copy-start.7
  115.4 1.0 copy-start.9
  116.4 1.0 copy-start.11
  117.4 1.0 copy-start.13
  118.3 1.0 copy-start.15
  119.3 1.0 copy-start.17
  120.3 0.9 copy-start.19
  121.2 0.9 copy-start.21
  122.2 0.9 copy-start.23
  123.1 0.9 copy-start.25
  124.1 0.9 copy-start.27
  (5 other events, 4.1 us)

commit v2 on v1

--- a/solution.py
+++ b/solution.py
@@ -19,7 +19,6 @@
 nt = (((1,), (1,)), ((), ()))
 tn = (((0,), (0,)), ((), ()))
 VMEM = pl.BlockSpec(memory_space=pltpu.VMEM)
-SMEM = pl.BlockSpec(memory_space=pltpu.SMEM)
 ANY = pl.BlockSpec(memory_space=pl.ANY)
 
 
@@ -27,37 +26,41 @@
     return pltpu.CompilerParams(vmem_limit_bytes=mib * 1024 * 1024)
 
 
+def row_iota(rows, lanes):
+    return lax.broadcasted_iota(jnp.int32, (rows, lanes), 0)
+
+
 def lane_iota(rows, lanes):
     return lax.broadcasted_iota(jnp.int32, (rows, lanes), 1)
 
 
-def plan_kernel(devices, home_cap, rep_cap, table, ids, gates, dy, dyg, kept_out):
+def plan_kernel(home_cap, rep_cap, table, ids, gates, dy, dyg, kept_out):
     tokens, width = dy.shape
     lanes = dyg.shape[1] - width
+    devices = table.shape[1]
     dyg[:, :width] = dy[...]
-    lane = lane_iota(tokens, lanes)
-    lane_row = lane_iota(8, lanes)
-
-    def count(d, total):
-        return total + jnp.where(lane_row == table[d], 1.0, 0.0)
-
-    copies = lax.fori_loop(0, devices, count, jnp.ones((8, lanes), f32))[:1]
-    named = jnp.zeros((tokens, lanes), f32)
-    weight = jnp.zeros((tokens, lanes), f32)
+    expert = row_iota(devices, tokens)
+    hosts = jnp.where(table[...] == row_iota(devices, devices), 1.0, 0.0)
+    copies = 1.0 + jnp.sum(hosts, axis=1, keepdims=True)
+    named = jnp.zeros((devices, tokens), f32)
+    weight = jnp.zeros((devices, tokens), f32)
     for k in range(TOP):
-        hit = lane == ids[:, k : k + 1]
+        hit = expert == ids[k : k + 1]
         named = jnp.where(hit, 1.0, named)
-        weight = jnp.where(hit, gates[:, k : k + 1].astype(f32), weight)
-    below = lax.broadcasted_iota(jnp.int32, (tokens, tokens), 0) > lane_iota(tokens, tokens)
+        weight = jnp.where(hit, gates[k : k + 1].astype(f32), weight)
+    earlier = row_iota(tokens, tokens) < lane_iota(tokens, tokens)
     rank = jnp.dot(
-        jnp.where(below, 1.0, 0.0).astype(bf16), named.astype(bf16), preferred_element_type=f32
+        named.astype(bf16), jnp.where(earlier, 1.0, 0.0).astype(bf16), preferred_element_type=f32
     )
     turn = rank + lax.axis_index("expert").astype(f32)
     at_home = turn == copies * jnp.floor(turn / copies + 0.5)
     cap = jnp.where(at_home, float(home_cap), float(rep_cap))
     kept = jnp.where((named > 0.0) & (rank < cap * copies), 1.0, 0.0)
-    dyg[:, width:] = (weight * kept).astype(bf16)
     kept_out[...] = kept
+    dense = (weight * kept).T
+    if lanes > devices:
+        dense = jnp.concatenate([dense, jnp.zeros((tokens, lanes - devices), f32)], axis=1)
+    dyg[:, width:] = dense.astype(bf16)
 
 
 def plan(table, ids, gates, dy, devices, lanes):
@@ -65,12 +68,12 @@
     home_cap = max(2, 5 * tokens * TOP // (4 * devices))
     rep_cap = max(2, tokens * TOP // (2 * devices))
     return pl.pallas_call(
-        functools.partial(plan_kernel, devices, home_cap, rep_cap),
+        functools.partial(plan_kernel, home_cap, rep_cap),
         out_shape=(
             jax.ShapeDtypeStruct((tokens, width + lanes), bf16),
-            jax.ShapeDtypeStruct((tokens, lanes), f32),
-        ),
-        in_specs=[SMEM, VMEM, VMEM, VMEM],
+            jax.ShapeDtypeStruct((devices, tokens), f32),
+        ),
+        in_specs=[VMEM] * 4,
         out_specs=(VMEM, VMEM),
         compiler_params=params(16),
         name="plan",
@@ -175,7 +178,7 @@
             pltpu.VMEM((2, hidden, width), bf16),
             pltpu.SemaphoreType.DMA((2 * slots + 6,)),
         ],
-        compiler_params=params(40),
+        compiler_params=params(20),
         cost_estimate=pl.CostEstimate(
             flops=flops, bytes_accessed=moved, transcendentals=2 * rows * hidden
         ),
@@ -259,7 +262,7 @@
             pltpu.VMEM((rows, 3 * hidden), bf16),
             pltpu.SemaphoreType.DMA((2 * slots + steps,)),
         ],
-        compiler_params=params(40),
+        compiler_params=params(20),
         cost_estimate=pl.CostEstimate(
             flops=6 * rows * width * hidden,
             bytes_accessed=rows * (4 * width + 6 * hidden) + 6 * width * hidden,
@@ -272,30 +275,30 @@
 def finish_kernel(parts, ids, kept, *refs):
     pieces, (tokens_out, gates_out) = refs[:parts], refs[parts:]
     tokens, width = tokens_out.shape
-    lanes = kept.shape[1]
     total = pieces[0][:, :width].astype(f32)
     gg = pieces[0][:, width:].astype(f32)
     for p in pieces[1:]:
         total = total + p[:, :width].astype(f32)
         gg = gg + p[:, width:].astype(f32)
     tokens_out[...] = total.astype(bf16)
-    gg = gg * kept[...]
-    lane = lane_iota(tokens, lanes)
-    place = lane_iota(tokens, TOP)
-    out = jnp.zeros((tokens, TOP), f32)
+    devices = kept.shape[0]
+    gg = gg.T[:devices] * kept[...]
+    expert = row_iota(devices, tokens)
+    place = row_iota(TOP, tokens)
+    out = jnp.zeros((TOP, tokens), f32)
     for k in range(TOP):
-        value = jnp.sum(jnp.where(lane == ids[:, k : k + 1], gg, 0.0), axis=1, keepdims=True)
+        value = jnp.sum(jnp.where(expert == ids[k : k + 1], gg, 0.0), axis=0, keepdims=True)
         out = jnp.where(place == k, value, out)
     gates_out[...] = out.astype(bf16)
 
 
 def finish(ids, kept, pieces, width):
-    tokens = ids.shape[0]
+    tokens = ids.shape[1]
     return pl.pallas_call(
         functools.partial(finish_kernel, len(pieces)),
         out_shape=(
             jax.ShapeDtypeStruct((tokens, width), bf16),
-            jax.ShapeDtypeStruct((tokens, TOP), bf16),
+            jax.ShapeDtypeStruct((TOP, tokens), bf16),
         ),
         in_specs=[VMEM] * (2 + len(pieces)),
         out_specs=(VMEM, VMEM),
@@ -333,22 +336,31 @@
     def send_core(v):
         return lax.ppermute(v, "expert", [(i, i ^ 1) for i in range(devices)])
 
-    dyg, kept = plan(replica_table, expert_ids, gates, grad_out, devices, lanes)
+    ids = expert_ids.T
+    dyg, kept = plan(replica_table[None], ids, gates.T, grad_out, devices, lanes)
     own = (w_gate[0], w_up[0], w_down[0])
     weights = own + tuple(send_core(w) for w in own)
 
-    xs = [[tokens_in]]
-    dygs = [[dyg]]
-    for z in range(outer):
-        if z:
-            xs.append([send_z(xs[z - 1][0])])
-            dygs.append([send_z(dygs[z - 1][0])])
-        for y in range(1, inner):
-            xs[z].append(send_y(xs[z][y - 1]))
-            if z > 0 and z == outer - 1 and y == inner - 1:
-                dygs[z].append(send_z(dygs[z - 1][y]))
+    def together(*values):
+        return lax.optimization_barrier(values)
+
+    xs, dygs = [[tokens_in]], [[dyg]]
+    for z in range(1, outer + 1):
+        for k, stream in enumerate((xs, dygs)):
+            last = stream[z - 1]
+            if z < outer:
+                ahead = send_z(last[0])
+                for y in range(1, inner):
+                    last.append(send_y(last[y - 1]))
+                if inner > 1:
+                    ahead, last[-1] = together(ahead, last[-1])
+                stream.append([ahead])
             else:
-                dygs[z].append(send_y(dygs[z][y - 1]))
+                for y in range(1, inner):
+                    if k and outer > 1 and y == inner - 1:
+                        last.append(send_z(stream[z - 2][y]))
+                    else:
+                        last.append(send_y(last[y - 1]))
 
     per = max(1, W_ROWS // (inner * tokens))
     groups = [range(z, min(outer, z + per)) for z in range(0, outer, per)]
@@ -383,20 +395,26 @@
             if z + 1 < outer:
                 sums, xs[z + 1] = lax.optimization_barrier((sums, xs[z + 1]))
 
-    if len(groups) == 1:
+    single = len(groups) == 1
+    if single:
         other = [send_core(v) for v in partial(1, groups[0], bf16)]
-        grad_w = partial(0, groups[0], bf16, other)
     else:
         other = [send_core(v.astype(bf16)) for v in sums[1]]
-        grad_w = [(v + o.astype(f32)).astype(bf16)[None] for v, o in zip(sums[0], other)]
 
     pieces = [dxs[0][0], *across[0]]
     if outer > 1:
         total = add(dxs[1][0], *across[1])
         for z in range(2, outer):
             total = add(send_z(total), dxs[z][0], *across[z])
+        total, other = together(total, other)
         pieces.append(send_z(total))
-    grad_tokens, grad_gates = finish(expert_ids, kept, pieces, width)
+    if single:
+        grad_w = partial(0, groups[0], bf16, other)
+    else:
+        grad_w = [(v + o.astype(f32)).astype(bf16)[None] for v, o in zip(sums[0], other)]
+    pieces, grad_w = together(pieces, grad_w)
+    grad_tokens, grad_gates = finish(ids, kept, pieces, width)
+    grad_gates = grad_gates.T
     return (grad_tokens, grad_gates, *grad_w)
 
 

time: 135 us -> 92.1 us (0.68)
  waiting for transfers between devices: 59.9 us -> 33.8 us
  local copies, waits for them, and re-layouts: 25.2 us -> 6.38 us
  starting transfers between devices: 18.4 us -> 25.4 us
  Pallas kernels: 29.2 us -> 25.1 us
    unnamed x87 -> x18, local copies, waits for them, and re-layouts: 25.2 us -> 6.38 us
    ppermute x11, waiting for transfers between devices: 20.3 us -> 3.39 us  [send_y(): lax.ppermute(v, 'expert', [(i, moved(i, 0, 1)) for i in range(devices)])]
    ppermute x10, waiting for transfers between devices: 39.6 us -> 27.7 us  [send_z(): lax.ppermute(v, 'expert', [(i, moved(i, 1, 0)) for i in range(devices)])]
    ppermute x10, starting transfers between devices: 5.41 us -> 10 us  [send_z(): lax.ppermute(v, 'expert', [(i, moved(i, 1, 0)) for i in range(devices)])]
    ppermute x6, waiting for transfers between devices: 0.02 us -> 2.7 us  [send_core(): return lax.ppermute(v, 'expert', [(i, i ^ 1) for i in range(devices)])]
    pallas_call x2, Pallas kernels: 10.5 us -> 7.96 us  [weights_grads(): pl.pallas_call(functools.partial(weights_kernel, j, slots, steps, len(mor...]
    ppermute x11, starting transfers between devices: 11.8 us -> 14.2 us  [send_y(): lax.ppermute(v, 'expert', [(i, moved(i, 0, 1)) for i in range(devices)])]
  transfers between devices with their start and end apart: 27 -> 27, of which waited for: 11 -> 13; matrix products, arithmetic and copies ran while one was open for 1% -> 0% of each run, Pallas kernels for 16% -> 26%
where the time goes in v2:
time: 92.1 us; the launch traced here: 91.8 us
  waiting for transfers between devices  33.8 us (37%)
  starting transfers between devices  25.4 us (28%)
  Pallas kernels  25.1 us (27%)
  local copies, waits for them, and re-layouts  6.38 us (7%)
    ppermute x10, waiting for transfers between devices, send_z(): lax.ppermute(v, 'expert', [(i, moved(i, 1, 0)) for i in range(devices)])  27.7 us
    pallas_call x4, Pallas kernels, rows_grads(): pl.pallas_call(functools.partial(rows_kernel, slots), out_shape=tuple((ja...  16 us
    ppermute x11, starting transfers between devices, send_y(): lax.ppermute(v, 'expert', [(i, moved(i, 0, 1)) for i in range(devices)])  14.2 us
    ppermute x10, starting transfers between devices, send_z(): lax.ppermute(v, 'expert', [(i, moved(i, 1, 0)) for i in range(devices)])  10 us
    pallas_call x2, Pallas kernels, weights_grads(): pl.pallas_call(functools.partial(weights_kernel, j, slots, steps, len(mor...  7.96 us
    unnamed x18, local copies, waits for them, and re-layouts  6.38 us
    ppermute x11, waiting for transfers between devices, send_y(): lax.ppermute(v, 'expert', [(i, moved(i, 0, 1)) for i in range(devices)])  3.39 us
    ppermute x6, waiting for transfers between devices, send_core(): return lax.ppermute(v, 'expert', [(i, i ^ 1) for i in range(devices)])  2.7 us
  transfers between devices with their start and end apart: 27, of which 13 were waited for; matrix products, arithmetic and copies ran while one was open for 0% of the time, Pallas kernels for 26%

profile of v2, /device:TPU:0, one launch (start us, length us, event | category | flops | bytes accessed | tf_op | source)
XLA Modules:
  0.0 91.8 jit_solution(13266240345365070477)
XLA Ops:
  0.6 3.1 %collective-permute-start = (bf16[128,1024]{1,0:T(8,128)(2,1)}, bf16[128,1024]{1,0:T(8,128)(2,1)S(1)}, u32[]{:S(2)}, u32[]{:S(2)}) collective-permute-start(bf16[128,1024]{1,0:T(8,128)(2,1)} %refs_0_.5), channel_id=1, source_target_pairs={{0,4},{1,5},{2,6},{3,7},{4,8},{5,9},{6,10},{7,11},{8,12},{9,13},{1... | collective-permute-start | bytes 786440 | tf_op jit(solution)/shard_map/ppermute | solution.py:331
  3.7 1.5 %collective-permute-start.1 = (bf16[128,1024]{1,0:T(8,128)(2,1)}, bf16[128,1024]{1,0:T(8,128)(2,1)S(1)}, u32[]{:S(2)}, u32[]{:S(2)}) collective-permute-start(bf16[128,1024]{1,0:T(8,128)(2,1)} %refs_0_.5), channel_id=1, source_target_pairs={{0,2},{1,3},{2,0},{3,1},{4,6},{5,7},{6,4},{7,5},{8,10},{9,11},{10,... | collective-permute-start | bytes 786440 | tf_op jit(solution)/shard_map/ppermute | solution.py:334
  5.2 0.9 %copy-done.1 = bf16[128,1024]{1,0:T(8,128)(2,1)S(1)} copy-done((bf16[128,1024]{1,0:T(8,128)(2,1)S(1)}, bf16[128,1024]{1,0:T(8,128)(2,1)}, u32[]{:S(2)}) %copy-start.1) | copy-done | bytes 262168
  6.2 0.7 copy-done.2
  6.9 0.7 copy-done.4
  7.5 0.7 copy-done.5
  8.2 0.2 plan.1
  8.4 1.6 %collective-permute-start.2 = (bf16[128,1152]{1,0:T(8,128)(2,1)S(1)}, bf16[128,1152]{1,0:T(8,128)(2,1)S(1)}, u32[]{:S(2)}, u32[]{:S(2)}) collective-permute-start(bf16[128,1152]{1,0:T(8,128)(2,1)S(1)} %get-tuple-element.51.refs_2_.refs_8_), channel_id=1, source_target_pairs={{0,4},{1,5},{2,6},{3,7},{4,8},{5,9},{6,10},{7,11},{8,12},{9,13},{1... | collective-permute-start | bytes 884744 | tf_op jit(solution)/shard_map/ppermute | solution.py:331
  10.1 0.5 collective-permute-start.3
  10.6 0.0 collective-permute-start.4
  10.6 1.7 %collective-permute-done.refs_0_.refs_2_ = bf16[128,1024]{1,0:T(8,128)(2,1)S(1)} collective-permute-done((bf16[128,1024]{1,0:T(8,128)(2,1)}, bf16[128,1024]{1,0:T(8,128)(2,1)S(1)}, u32[]{:S(2)}, u32[]{:S(2)}) %collective-permute-start) | collective-permute-done | bytes 262176 | tf_op jit(solution)/shard_map/ppermute | solution.py:331
  12.3 0.0 collective-permute-done.1.refs_1_
  12.3 0.5 collective-permute-start.6
  12.8 5.8 %collective-permute-done.2.refs_2_.refs_10_ = bf16[128,1152]{1,0:T(8,128)(2,1)S(1)} collective-permute-done((bf16[128,1152]{1,0:T(8,128)(2,1)S(1)}, bf16[128,1152]{1,0:T(8,128)(2,1)S(1)}, u32[]{:S(2)}, u32[]{:S(2)}) %collective-permute-start.2) | collective-permute-done | bytes 294944 | tf_op jit(solution)/shard_map/ppermute | solution.py:331
  18.6 1.5 %collective-permute-start.9 = (bf16[128,1024]{1,0:T(8,128)(2,1)S(1)}, bf16[128,1024]{1,0:T(8,128)(2,1)S(1)}, u32[]{:S(2)}, u32[]{:S(2)}) collective-permute-start(bf16[128,1024]{1,0:T(8,128)(2,1)S(1)} %collective-permute-done.refs_0_.refs_2_), channel_id=1, source_target_pairs={{0,2},{1,3},{2,0},{3,1},{4,6},{5,7},{6,4},{7,5},{8,10},{9,11},{10,... | collective-permute-start | bytes 786440 | tf_op jit(solution)/shard_map/ppermute | solution.py:334
  20.1 6.9 %collective-permute-done.8.refs_0_.refs_4_ = bf16[128,1024]{1,0:T(8,128)(2,1)S(1)} collective-permute-done((bf16[128,1024]{1,0:T(8,128)(2,1)S(1)}, bf16[128,1024]{1,0:T(8,128)(2,1)S(1)}, u32[]{:S(2)}, u32[]{:S(2)}) %collective-permute-start.8) | collective-permute-done | bytes 262176 | tf_op jit(solution)/shard_map/ppermute | solution.py:331
  27.0 0.0 collective-permute-start.10
  27.0 0.0 collective-permute-done.9.refs_1_.refs_3_
  27.0 2.1 %collective-permute-start.11 = (bf16[128,1152]{1,0:T(8,128)(2,1)S(1)}, bf16[128,1152]{1,0:T(8,128)(2,1)S(1)}, u32[]{:S(2)}, u32[]{:S(2)}) collective-permute-start(bf16[128,1152]{1,0:T(8,128)(2,1)S(1)} %collective-permute-done.2.refs_2_.refs_10_), channel_id=1, source_target_pairs={{0,2},{1,3},{2,0},{3,1},{4,6},{5,7},{6,4},{7,5},{8,10},{9,11},{10,... | collective-permute-start | bytes 884744 | tf_op jit(solution)/shard_map/ppermute | solution.py:334
  29.1 6.4 %collective-permute-done.10.refs_2_.refs_12_ = bf16[128,1152]{1,0:T(8,128)(2,1)S(1)} collective-permute-done((bf16[128,1152]{1,0:T(8,128)(2,1)S(1)}, bf16[128,1152]{1,0:T(8,128)(2,1)S(1)}, u32[]{:S(2)}, u32[]{:S(2)}) %collective-permute-start.10) | collective-permute-done | bytes 294944 | tf_op jit(solution)/shard_map/ppermute | solution.py:331
  35.5 0.0 collective-permute-done.11.refs_3_.refs_11_
  35.5 0.0 collective-permute-start.16
  35.5 2.4 %collective-permute-start.17 = (bf16[128,1152]{1,0:T(8,128)(2,1)S(1)}, bf16[128,1152]{1,0:T(8,128)(2,1)S(1)}, u32[]{:S(2)}, u32[]{:S(2)}) collective-permute-start(bf16[128,1152]{1,0:T(8,128)(2,1)S(1)} %collective-permute-done.10.refs_2_.refs_12_), channel_id=1, source_target_pairs={{0,2},{1,3},{2,0},{3,1},{4,6},{5,7},{6,4},{7,5},{8,10},{9,11},{10,... | collective-permute-start | bytes 884744 | tf_op jit(solution)/shard_map/ppermute | solution.py:334
  38.0 0.0 collective-permute-done.4.refs_7_
  38.0 0.0 collective-permute-start.14
  38.0 0.0 collective-permute-done.5.refs_8_
  38.0 0.1 collective-permute-start.15
  38.1 1.1 %copy-done.6 = bf16[1,1024,384]{2,1,0:T(8,128)(2,1)S(1)} copy-done((bf16[1,1024,384]{2,1,0:T(8,128)(2,1)S(1)}, bf16[1,1024,384]{2,1,0:T(8,128)(2,1)}, u32[]{:S(2)}) %copy-start.6) | copy-done | bytes 786456
  39.3 1.1 %copy-done.7 = bf16[1,1024,384]{2,1,0:T(8,128)(2,1)S(1)} copy-done((bf16[1,1024,384]{2,1,0:T(8,128)(2,1)S(1)}, bf16[1,1024,384]{2,1,0:T(8,128)(2,1)}, u32[]{:S(2)}) %copy-start.7) | copy-done | bytes 786456
  40.4 1.1 %copy-done.8 = bf16[1,384,1024]{2,1,0:T(8,128)(2,1)S(1)} copy-done((bf16[1,384,1024]{2,1,0:T(8,128)(2,1)S(1)}, bf16[1,384,1024]{2,1,0:T(8,128)(2,1)}, u32[]{:S(2)}) %copy-start.8) | copy-done | bytes 786456
  41.5 4.0 %rows_grads.5 = (bf16[128,1152]{1,0:T(8,128)(2,1)S(1)}, bf16[128,1152]{1,0:T(8,128)(2,1)S(1)}, bf16[256,2304]{1,0:T(8,128)(2,1)S(1)}) custom-call(bf16[128,1024]{1,0:T(8,128)(2,1)S(1)} %collective-permute-done.refs_0_.refs_2_, bf16[128,1024]{1,0:T(8,128)(2,1)S(1)} %collective-permute-done.9.refs_1_.refs_3_, ...), custom_call_target="tpu_custom_call" | custom-call | flops 2013265920 | bytes 9306112 | tf_op jit(solution)/shard_map/rows_grads/pallas_call | solution.py:168
  45.6 0.0 copy-start
  45.6 2.0 %collective-permute-start.12 = (bf16[128,1152]{1,0:T(8,128)(2,1)S(1)}, bf16[128,1152]{1,0:T(8,128)(2,1)S(1)}, u32[]{:S(2)}, u32[]{:S(2)}) collective-permute-start(bf16[128,1152]{1,0:T(8,128)(2,1)S(1)} %get-tuple-element.60), channel_id=1, source_target_pairs={{0,2},{1,3},{2,0},{3,1},{4,6},{5,7},{6,4},{7,5},{8,10},{9,11},{10,... | collective-permute-start | bytes 884744 | tf_op jit(solution)/shard_map/ppermute | solution.py:334
  47.6 0.7 collective-permute-done.14.refs_0_.refs_6_
  48.2 2.5 %collective-permute-done.15.refs_1_.refs_5_ = bf16[128,1024]{1,0:T(8,128)(2,1)S(1)} collective-permute-done((bf16[128,1024]{1,0:T(8,128)(2,1)S(1)}, bf16[128,1024]{1,0:T(8,128)(2,1)S(1)}, u32[]{:S(2)}, u32[]{:S(2)}) %collective-permute-start.15) | collective-permute-done | bytes 262176 | tf_op jit(solution)/shard_map/ppermute | solution.py:334
  50.7 1.8 %collective-permute-start.20 = (bf16[128,1024]{1,0:T(8,128)(2,1)S(1)}, bf16[128,1024]{1,0:T(8,128)(2,1)S(1)}, u32[]{:S(2)}, u32[]{:S(2)}) collective-permute-start(bf16[128,1024]{1,0:T(8,128)(2,1)S(1)} %collective-permute-done.14.refs_0_.refs_6_), channel_id=1, source_target_pairs={{0,2},{1,3},{2,0},{3,1},{4,6},{5,7},{6,4},{7,5},{8,10},{9,11},{10,... | collective-permute-start | bytes 786440 | tf_op jit(solution)/shard_map/ppermute | solution.py:334
  52.5 0.0 collective-permute-done.17.refs_3_.refs_13_
  52.5 0.0 collective-permute-start.21
  52.6 4.0 %rows_grads.6 = (bf16[128,1152]{1,0:T(8,128)(2,1)S(1)}, bf16[128,1152]{1,0:T(8,128)(2,1)S(1)}, bf16[256,2304]{1,0:T(8,128)(2,1)S(1)}) custom-call(bf16[128,1024]{1,0:T(8,128)(2,1)S(1)} %collective-permute-done.8.refs_0_.refs_4_, bf16[128,1024]{1,0:T(8,128)(2,1)S(1)} %collective-permute-done.15.refs_1_.refs_5_, ...), custom_call_target="tpu_custom_call" | custom-call | flops 2013265920 | bytes 9306112 | tf_op jit(solution)/shard_map/rows_grads/pallas_call | solution.py:168
  56.6 0.3 collective-permute-start.18
  56.8 0.2 collective-permute-done.12
  57.0 0.1 add_convert_fusion.2
  57.1 1.8 %collective-permute-start.13 = (bf16[128,1152]{1,0:T(8,128)(2,1)S(1)}, bf16[128,1152]{1,0:T(8,128)(2,1)S(1)}, u32[]{:S(2)}, u32[]{:S(2)}) collective-permute-start(bf16[128,1152]{1,0:T(8,128)(2,1)S(1)} %add_convert_fusion.2), channel_id=1, source_target_pairs={{0,4},{1,5},{2,6},{3,7},{4,8},{5,9},{6,10},{7,11},{8,12},{9,13},{1... | collective-permute-start | bytes 884744 | tf_op jit(solution)/shard_map/ppermute | solution.py:331
  58.9 4.0 %rows_grads.4 = (bf16[128,1152]{1,0:T(8,128)(2,1)S(1)}, bf16[128,1152]{1,0:T(8,128)(2,1)S(1)}, bf16[256,2304]{1,0:T(8,128)(2,1)S(1)}) custom-call(bf16[128,1024]{1,0:T(8,128)(2,1)S(1)} %copy-done, bf16[128,1024]{1,0:T(8,128)(2,1)S(1)} %collective-permute-done.1.refs_1_, bf16[128,1152]{1,0:T(8,128)(2,1)S(1)} %get-tuple-element.51.refs_2_.refs_8_, ...), custom_call_target="tpu_custom_call" | custom-call | flops 2013265920 | bytes 9306112 | tf_op jit(solution)/shard_map/rows_grads/pallas_call | solution.py:168
  62.9 4.0 %rows_grads.7 = (bf16[128,1152]{1,0:T(8,128)(2,1)S(1)}, bf16[128,1152]{1,0:T(8,128)(2,1)S(1)}, bf16[256,2304]{1,0:T(8,128)(2,1)S(1)}) custom-call(bf16[128,1024]{1,0:T(8,128)(2,1)S(1)} %collective-permute-done.14.refs_0_.refs_6_, bf16[128,1024]{1,0:T(8,128)(2,1)S(1)} %collective-permute-done.20.refs_1_.refs_7_, ...), custom_call_target="tpu_custom_call" | custom-call | flops 2013265920 | bytes 9306112 | tf_op jit(solution)/shard_map/rows_grads/pallas_call | solution.py:168
  66.9 1.6 %collective-permute-start.22 = (bf16[128,1152]{1,0:T(8,128)(2,1)S(1)}, bf16[128,1152]{1,0:T(8,128)(2,1)S(1)}, u32[]{:S(2)}, u32[]{:S(2)}) collective-permute-start(bf16[128,1152]{1,0:T(8,128)(2,1)S(1)} %get-tuple-element.70), channel_id=1, source_target_pairs={{0,2},{1,3},{2,0},{3,1},{4,6},{5,7},{6,4},{7,5},{8,10},{9,11},{10,... | collective-permute-start | bytes 884744 | tf_op jit(solution)/shard_map/ppermute | solution.py:334
  68.6 0.1 add_convert_fusion.1
  68.7 3.2 %collective-permute-start.19 = (bf16[128,1152]{1,0:T(8,128)(2,1)S(1)}, bf16[128,1152]{1,0:T(8,128)(2,1)S(1)}, u32[]{:S(2)}, u32[]{:S(2)}) collective-permute-start(bf16[128,1152]{1,0:T(8,128)(2,1)S(1)} %add_convert_fusion.1), channel_id=1, source_target_pairs={{0,4},{1,5},{2,6},{3,7},{4,8},{5,9},{6,10},{7,11},{8,12},{9,13},{1... | collective-permute-start | bytes 884744 | tf_op jit(solution)/shard_map/ppermute | solution.py:331
  71.9 3.5 %weights_grads.2 = (bf16[1024,384]{1,0:T(8,128)(2,1)S(1)}, bf16[1024,384]{1,0:T(8,128)(2,1)S(1)}, bf16[384,1024]{1,0:T(8,128)(2,1)S(1)}) custom-call(bf16[128,1024]{1,0:T(8,128)(2,1)S(1)} %copy-done, bf16[128,1024]{1,0:T(8,128)(2,1)S(1)} %collective-permute-done.1.refs_1_, bf16[128,1024]{1,0:T(8,128)(2,1)S(1)} %collective-permute-done.refs_0_.refs_2_, ...), custom_call_target="tpu_custom_call" | custom-call | flops 2415919104 | bytes 8912896 | tf_op jit(solution)/shard_map/weights_grads/pallas_call | solution.py:250
  75.5 0.1 collective-permute-start.23
  75.6 0.5 collective-permute-start.24
  76.1 0.1 collective-permute-start.25
  76.1 0.3 collective-permute-start.7
  76.4 0.9 collective-permute-done.19
  77.3 0.1 add_convert_fusion
  77.4 0.0 copy-start.3
  77.4 0.4 collective-permute-done.23.refs_20_
  77.8 1.1 %collective-permute-done.24.refs_21_ = bf16[1024,384]{1,0:T(8,128)(2,1)S(1)} collective-permute-done((bf16[1024,384]{1,0:T(8,128)(2,1)S(1)}, bf16[1024,384]{1,0:T(8,128)(2,1)S(1)}, u32[]{:S(2)}, u32[]{:S(2)}) %collective-permute-start.24) | collective-permute-done | bytes 786464 | tf_op jit(solution)/shard_map/ppermute | solution.py:337
  79.0 1.1 %collective-permute-done.25.refs_22_ = bf16[384,1024]{1,0:T(8,128)(2,1)S(1)} collective-permute-done((bf16[384,1024]{1,0:T(8,128)(2,1)S(1)}, bf16[384,1024]{1,0:T(8,128)(2,1)S(1)}, u32[]{:S(2)}, u32[]{:S(2)}) %collective-permute-start.25) | collective-permute-done | bytes 786464 | tf_op jit(solution)/shard_map/ppermute | solution.py:337
  80.1 0.3 collective-permute-start.26
  80.4 4.4 %weights_grads.3 = (bf16[1,1024,384]{2,1,0:T(8,128)(2,1)}, bf16[1,1024,384]{2,1,0:T(8,128)(2,1)}, bf16[1,384,1024]{2,1,0:T(8,128)(2,1)}) custom-call(bf16[128,1024]{1,0:T(8,128)(2,1)S(1)} %copy-done, bf16[128,1024]{1,0:T(8,128)(2,1)S(1)} %collective-permute-done.1.refs_1_, bf16[128,1024]{1,0:T(8,128)(2,1)S(1)} %collective-permute-done.refs_0_.refs_2_, ...), custom_call_target="tpu_custom_call" | custom-call | flops 2415919104 | bytes 8912896 | tf_op jit(solution)/shard_map/weights_grads/pallas_call | solution.py:250
  84.8 0.7 collective-permute-done.7.refs_1_
  85.5 5.4 %collective-permute-done.26.refs_2_ = bf16[128,1152]{1,0:T(8,128)(2,1)S(1)} collective-permute-done((bf16[128,1152]{1,0:T(8,128)(2,1)S(1)}, bf16[128,1152]{1,0:T(8,128)(2,1)S(1)}, u32[]{:S(2)}, u32[]{:S(2)}) %collective-permute-start.26) | collective-permute-done | bytes 294944 | tf_op jit(solution)/shard_map/ppermute | solution.py:331
  90.9 0.9 finish.1
  (19 shorter events, 0.0 us)
Async XLA Ops:
  0.6 11.6 %collective-permute-start = (bf16[128,1024]{1,0:T(8,128)(2,1)}, bf16[128,1024]{1,0:T(8,128)(2,1)S(1)}, u32[]{:S(2)}, u32[]{:S(2)}) collective-permute-start(bf16[128,1024]{1,0:T(8,128)(2,1)} %refs_0_.5), channel_id=1, source_target_pairs={{0,4},{1,5},{2,6},{3,7},{4,8},{5,9},{6,10},{7,11},{8,12},{9,13},{1... | collective-permute-start | bytes 786440 | tf_op jit(solution)/shard_map/ppermute | solution.py:331
  3.7 8.6 %collective-permute-start.1 = (bf16[128,1024]{1,0:T(8,128)(2,1)}, bf16[128,1024]{1,0:T(8,128)(2,1)S(1)}, u32[]{:S(2)}, u32[]{:S(2)}) collective-permute-start(bf16[128,1024]{1,0:T(8,128)(2,1)} %refs_0_.5), channel_id=1, source_target_pairs={{0,2},{1,3},{2,0},{3,1},{4,6},{5,7},{6,4},{7,5},{8,10},{9,11},{10,... | collective-permute-start | bytes 786440 | tf_op jit(solution)/shard_map/ppermute | solution.py:334
  5.2 0.9 %copy-start.1 = (bf16[128,1024]{1,0:T(8,128)(2,1)S(1)}, bf16[128,1024]{1,0:T(8,128)(2,1)}, u32[]{:S(2)}) copy-start(bf16[128,1024]{1,0:T(8,128)(2,1)} %dy.1) | copy-start | bytes 786436
  6.2 0.7 copy-start.2
  6.9 0.7 copy-start.4
  7.5 0.7 copy-start.5
  8.4 10.1 %collective-permute-start.2 = (bf16[128,1152]{1,0:T(8,128)(2,1)S(1)}, bf16[128,1152]{1,0:T(8,128)(2,1)S(1)}, u32[]{:S(2)}, u32[]{:S(2)}) collective-permute-start(bf16[128,1152]{1,0:T(8,128)(2,1)S(1)} %get-tuple-element.51.refs_2_.refs_8_), channel_id=1, source_target_pairs={{0,4},{1,5},{2,6},{3,7},{4,8},{5,9},{6,10},{7,11},{8,12},{9,13},{1... | collective-permute-start | bytes 884744 | tf_op jit(solution)/shard_map/ppermute | solution.py:331
  10.1 8.5 %collective-permute-start.3 = (bf16[128,1152]{1,0:T(8,128)(2,1)S(1)}, bf16[128,1152]{1,0:T(8,128)(2,1)S(1)}, u32[]{:S(2)}, u32[]{:S(2)}) collective-permute-start(bf16[128,1152]{1,0:T(8,128)(2,1)S(1)} %get-tuple-element.51.refs_2_.refs_8_), channel_id=1, source_target_pairs={{0,2},{1,3},{2,0},{3,1},{4,6},{5,7},{6,4},{7,5},{8,10},{9,11},{10,... | collective-permute-start | bytes 884744 | tf_op jit(solution)/shard_map/ppermute | solution.py:334
  10.6 27.4 %collective-permute-start.4 = (bf16[1024,384]{1,0:T(8,128)(2,1)}, bf16[1024,384]{1,0:T(8,128)(2,1)S(1)}, u32[]{:S(2)}, u32[]{:S(2)}) collective-permute-start(bf16[1024,384]{1,0:T(8,128)(2,1)} %bitcast.11), channel_id=1, source_target_pairs={{0,1},{1,0},{2,3},{3,2},{4,5},{5,4},{6,7},{7,6},{8,9},{9,8},{10,11... | collective-permute-start | bytes 2359304 | tf_op jit(solution)/shard_map/ppermute | solution.py:337
  12.3 25.7 %collective-permute-start.5 = (bf16[1024,384]{1,0:T(8,128)(2,1)}, bf16[1024,384]{1,0:T(8,128)(2,1)S(1)}, u32[]{:S(2)}, u32[]{:S(2)}) collective-permute-start(bf16[1024,384]{1,0:T(8,128)(2,1)} %bitcast.16), channel_id=1, source_target_pairs={{0,1},{1,0},{2,3},{3,2},{4,5},{5,4},{6,7},{7,6},{8,9},{9,8},{10,11... | collective-permute-start | bytes 2359304 | tf_op jit(solution)/shard_map/ppermute | solution.py:337
  12.3 25.9 %collective-permute-start.6 = (bf16[384,1024]{1,0:T(8,128)(2,1)}, bf16[384,1024]{1,0:T(8,128)(2,1)S(1)}, u32[]{:S(2)}, u32[]{:S(2)}) collective-permute-start(bf16[384,1024]{1,0:T(8,128)(2,1)} %bitcast.21), channel_id=1, source_target_pairs={{0,1},{1,0},{2,3},{3,2},{4,5},{5,4},{6,7},{7,6},{8,9},{9,8},{10,11... | collective-permute-start | bytes 2359304 | tf_op jit(solution)/shard_map/ppermute | solution.py:337
  18.6 8.4 %collective-permute-start.8 = (bf16[128,1024]{1,0:T(8,128)(2,1)S(1)}, bf16[128,1024]{1,0:T(8,128)(2,1)S(1)}, u32[]{:S(2)}, u32[]{:S(2)}) collective-permute-start(bf16[128,1024]{1,0:T(8,128)(2,1)S(1)} %collective-permute-done.refs_0_.refs_2_), channel_id=1, source_target_pairs={{0,4},{1,5},{2,6},{3,7},{4,8},{5,9},{6,10},{7,11},{8,12},{9,13},{1... | collective-permute-start | bytes 786440 | tf_op jit(solution)/shard_map/ppermute | solution.py:331
  18.6 8.4 %collective-permute-start.9 = (bf16[128,1024]{1,0:T(8,128)(2,1)S(1)}, bf16[128,1024]{1,0:T(8,128)(2,1)S(1)}, u32[]{:S(2)}, u32[]{:S(2)}) collective-permute-start(bf16[128,1024]{1,0:T(8,128)(2,1)S(1)} %collective-permute-done.refs_0_.refs_2_), channel_id=1, source_target_pairs={{0,2},{1,3},{2,0},{3,1},{4,6},{5,7},{6,4},{7,5},{8,10},{9,11},{10,... | collective-permute-start | bytes 786440 | tf_op jit(solution)/shard_map/ppermute | solution.py:334
  27.0 8.5 %collective-permute-start.10 = (bf16[128,1152]{1,0:T(8,128)(2,1)S(1)}, bf16[128,1152]{1,0:T(8,128)(2,1)S(1)}, u32[]{:S(2)}, u32[]{:S(2)}) collective-permute-start(bf16[128,1152]{1,0:T(8,128)(2,1)S(1)} %collective-permute-done.2.refs_2_.refs_10_), channel_id=1, source_target_pairs={{0,4},{1,5},{2,6},{3,7},{4,8},{5,9},{6,10},{7,11},{8,12},{9,13},{1... | collective-permute-start | bytes 884744 | tf_op jit(solution)/shard_map/ppermute | solution.py:331
  27.0 8.5 %collective-permute-start.11 = (bf16[128,1152]{1,0:T(8,128)(2,1)S(1)}, bf16[128,1152]{1,0:T(8,128)(2,1)S(1)}, u32[]{:S(2)}, u32[]{:S(2)}) collective-permute-start(bf16[128,1152]{1,0:T(8,128)(2,1)S(1)} %collective-permute-done.2.refs_2_.refs_10_), channel_id=1, source_target_pairs={{0,2},{1,3},{2,0},{3,1},{4,6},{5,7},{6,4},{7,5},{8,10},{9,11},{10,... | collective-permute-start | bytes 884744 | tf_op jit(solution)/shard_map/ppermute | solution.py:334
  35.5 17.0 %collective-permute-start.16 = (bf16[128,1152]{1,0:T(8,128)(2,1)S(1)}, bf16[128,1152]{1,0:T(8,128)(2,1)S(1)}, u32[]{:S(2)}, u32[]{:S(2)}) collective-permute-start(bf16[128,1152]{1,0:T(8,128)(2,1)S(1)} %collective-permute-done.10.refs_2_.refs_12_), channel_id=1, source_target_pairs={{0,4},{1,5},{2,6},{3,7},{4,8},{5,9},{6,10},{7,11},{8,12},{9,13},{1... | collective-permute-start | bytes 884744 | tf_op jit(solution)/shard_map/ppermute | solution.py:331
  35.5 17.0 %collective-permute-start.17 = (bf16[128,1152]{1,0:T(8,128)(2,1)S(1)}, bf16[128,1152]{1,0:T(8,128)(2,1)S(1)}, u32[]{:S(2)}, u32[]{:S(2)}) collective-permute-start(bf16[128,1152]{1,0:T(8,128)(2,1)S(1)} %collective-permute-done.10.refs_2_.refs_12_), channel_id=1, source_target_pairs={{0,2},{1,3},{2,0},{3,1},{4,6},{5,7},{6,4},{7,5},{8,10},{9,11},{10,... | collective-permute-start | bytes 884744 | tf_op jit(solution)/shard_map/ppermute | solution.py:334
  38.0 10.3 %collective-permute-start.14 = (bf16[128,1024]{1,0:T(8,128)(2,1)S(1)}, bf16[128,1024]{1,0:T(8,128)(2,1)S(1)}, u32[]{:S(2)}, u32[]{:S(2)}) collective-permute-start(bf16[128,1024]{1,0:T(8,128)(2,1)S(1)} %collective-permute-done.8.refs_0_.refs_4_), channel_id=1, source_target_pairs={{0,4},{1,5},{2,6},{3,7},{4,8},{5,9},{6,10},{7,11},{8,12},{9,13},{1... | collective-permute-start | bytes 786440 | tf_op jit(solution)/shard_map/ppermute | solution.py:331
  38.0 12.7 %collective-permute-start.15 = (bf16[128,1024]{1,0:T(8,128)(2,1)S(1)}, bf16[128,1024]{1,0:T(8,128)(2,1)S(1)}, u32[]{:S(2)}, u32[]{:S(2)}) collective-permute-start(bf16[128,1024]{1,0:T(8,128)(2,1)S(1)} %collective-permute-done.8.refs_0_.refs_4_), channel_id=1, source_target_pairs={{0,2},{1,3},{2,0},{3,1},{4,6},{5,7},{6,4},{7,5},{8,10},{9,11},{10,... | collective-permute-start | bytes 786440 | tf_op jit(solution)/shard_map/ppermute | solution.py:334
  38.1 1.1 %copy-start.6 = (bf16[1,1024,384]{2,1,0:T(8,128)(2,1)S(1)}, bf16[1,1024,384]{2,1,0:T(8,128)(2,1)}, u32[]{:S(2)}) copy-start(bf16[1,1024,384]{2,1,0:T(8,128)(2,1)} %param.13) | copy-start | bytes 2359300
  39.3 1.1 %copy-start.7 = (bf16[1,1024,384]{2,1,0:T(8,128)(2,1)S(1)}, bf16[1,1024,384]{2,1,0:T(8,128)(2,1)}, u32[]{:S(2)}) copy-start(bf16[1,1024,384]{2,1,0:T(8,128)(2,1)} %param.14) | copy-start | bytes 2359300
  40.4 1.1 %copy-start.8 = (bf16[1,384,1024]{2,1,0:T(8,128)(2,1)S(1)}, bf16[1,384,1024]{2,1,0:T(8,128)(2,1)}, u32[]{:S(2)}) copy-start(bf16[1,384,1024]{2,1,0:T(8,128)(2,1)} %param.15) | copy-start | bytes 2359300
  45.6 13.3 %copy-start = (bf16[128,1024]{1,0:T(8,128)(2,1)S(1)}, bf16[128,1024]{1,0:T(8,128)(2,1)}, u32[]{:S(2)}) copy-start(bf16[128,1024]{1,0:T(8,128)(2,1)} %refs_0_.5) | copy-start | bytes 786436
  45.6 11.5 %collective-permute-start.12 = (bf16[128,1152]{1,0:T(8,128)(2,1)S(1)}, bf16[128,1152]{1,0:T(8,128)(2,1)S(1)}, u32[]{:S(2)}, u32[]{:S(2)}) collective-permute-start(bf16[128,1152]{1,0:T(8,128)(2,1)S(1)} %get-tuple-element.60), channel_id=1, source_target_pairs={{0,2},{1,3},{2,0},{3,1},{4,6},{5,7},{6,4},{7,5},{8,10},{9,11},{10,... | collective-permute-start | bytes 884744 | tf_op jit(solution)/shard_map/ppermute | solution.py:334
  50.7 12.2 %collective-permute-start.20 = (bf16[128,1024]{1,0:T(8,128)(2,1)S(1)}, bf16[128,1024]{1,0:T(8,128)(2,1)S(1)}, u32[]{:S(2)}, u32[]{:S(2)}) collective-permute-start(bf16[128,1024]{1,0:T(8,128)(2,1)S(1)} %collective-permute-done.14.refs_0_.refs_6_), channel_id=1, source_target_pairs={{0,2},{1,3},{2,0},{3,1},{4,6},{5,7},{6,4},{7,5},{8,10},{9,11},{10,... | collective-permute-start | bytes 786440 | tf_op jit(solution)/shard_map/ppermute | solution.py:334
  52.5 10.4 %collective-permute-start.21 = (bf16[128,1152]{1,0:T(8,128)(2,1)S(1)}, bf16[128,1152]{1,0:T(8,128)(2,1)S(1)}, u32[]{:S(2)}, u32[]{:S(2)}) collective-permute-start(bf16[128,1152]{1,0:T(8,128)(2,1)S(1)} %collective-permute-done.17.refs_3_.refs_13_), channel_id=1, source_target_pairs={{0,4},{1,5},{2,6},{3,7},{4,8},{5,9},{6,10},{7,11},{8,12},{9,13},{1... | collective-permute-start | bytes 884744 | tf_op jit(solution)/shard_map/ppermute | solution.py:331
  56.6 12.0 %collective-permute-start.18 = (bf16[128,1152]{1,0:T(8,128)(2,1)S(1)}, bf16[128,1152]{1,0:T(8,128)(2,1)S(1)}, u32[]{:S(2)}, u32[]{:S(2)}) collective-permute-start(bf16[128,1152]{1,0:T(8,128)(2,1)S(1)} %get-tuple-element.66), channel_id=1, source_target_pairs={{0,2},{1,3},{2,0},{3,1},{4,6},{5,7},{6,4},{7,5},{8,10},{9,11},{10,... | collective-permute-start | bytes 884744 | tf_op jit(solution)/shard_map/ppermute | solution.py:334
  57.1 11.5 %collective-permute-start.13 = (bf16[128,1152]{1,0:T(8,128)(2,1)S(1)}, bf16[128,1152]{1,0:T(8,128)(2,1)S(1)}, u32[]{:S(2)}, u32[]{:S(2)}) collective-permute-start(bf16[128,1152]{1,0:T(8,128)(2,1)S(1)} %add_convert_fusion.2), channel_id=1, source_target_pairs={{0,4},{1,5},{2,6},{3,7},{4,8},{5,9},{6,10},{7,11},{8,12},{9,13},{1... | collective-permute-start | bytes 884744 | tf_op jit(solution)/shard_map/ppermute | solution.py:331
  66.9 9.2 %collective-permute-start.22 = (bf16[128,1152]{1,0:T(8,128)(2,1)S(1)}, bf16[128,1152]{1,0:T(8,128)(2,1)S(1)}, u32[]{:S(2)}, u32[]{:S(2)}) collective-permute-start(bf16[128,1152]{1,0:T(8,128)(2,1)S(1)} %get-tuple-element.70), channel_id=1, source_target_pairs={{0,2},{1,3},{2,0},{3,1},{4,6},{5,7},{6,4},{7,5},{8,10},{9,11},{10,... | collective-permute-start | bytes 884744 | tf_op jit(solution)/shard_map/ppermute | solution.py:334
  68.7 8.6 %collective-permute-start.19 = (bf16[128,1152]{1,0:T(8,128)(2,1)S(1)}, bf16[128,1152]{1,0:T(8,128)(2,1)S(1)}, u32[]{:S(2)}, u32[]{:S(2)}) collective-permute-start(bf16[128,1152]{1,0:T(8,128)(2,1)S(1)} %add_convert_fusion.1), channel_id=1, source_target_pairs={{0,4},{1,5},{2,6},{3,7},{4,8},{5,9},{6,10},{7,11},{8,12},{9,13},{1... | collective-permute-start | bytes 884744 | tf_op jit(solution)/shard_map/ppermute | solution.py:331
  75.5 2.4 %collective-permute-start.23 = (bf16[1024,384]{1,0:T(8,128)(2,1)S(1)}, bf16[1024,384]{1,0:T(8,128)(2,1)S(1)}, u32[]{:S(2)}, u32[]{:S(2)}) collective-permute-start(bf16[1024,384]{1,0:T(8,128)(2,1)S(1)} %get-tuple-element.75), channel_id=1, source_target_pairs={{0,1},{1,0},{2,3},{3,2},{4,5},{5,4},{6,7},{7,6},{8,9},{9,8},{10,11... | collective-permute-start | bytes 2359304 | tf_op jit(solution)/shard_map/ppermute | solution.py:337
  75.6 3.4 %collective-permute-start.24 = (bf16[1024,384]{1,0:T(8,128)(2,1)S(1)}, bf16[1024,384]{1,0:T(8,128)(2,1)S(1)}, u32[]{:S(2)}, u32[]{:S(2)}) collective-permute-start(bf16[1024,384]{1,0:T(8,128)(2,1)S(1)} %get-tuple-element.76), channel_id=1, source_target_pairs={{0,1},{1,0},{2,3},{3,2},{4,5},{5,4},{6,7},{7,6},{8,9},{9,8},{10,11... | collective-permute-start | bytes 2359304 | tf_op jit(solution)/shard_map/ppermute | solution.py:337
  76.1 4.0 %collective-permute-start.25 = (bf16[384,1024]{1,0:T(8,128)(2,1)S(1)}, bf16[384,1024]{1,0:T(8,128)(2,1)S(1)}, u32[]{:S(2)}, u32[]{:S(2)}) collective-permute-start(bf16[384,1024]{1,0:T(8,128)(2,1)S(1)} %get-tuple-element.77), channel_id=1, source_target_pairs={{0,1},{1,0},{2,3},{3,2},{4,5},{5,4},{6,7},{7,6},{8,9},{9,8},{10,11... | collective-permute-start | bytes 2359304 | tf_op jit(solution)/shard_map/ppermute | solution.py:337
  76.1 9.4 %collective-permute-start.7 = (bf16[128,1152]{1,0:T(8,128)(2,1)S(1)}, bf16[128,1152]{1,0:T(8,128)(2,1)S(1)}, u32[]{:S(2)}, u32[]{:S(2)}) collective-permute-start(bf16[128,1152]{1,0:T(8,128)(2,1)S(1)} %get-tuple-element.54), channel_id=1, source_target_pairs={{0,2},{1,3},{2,0},{3,1},{4,6},{5,7},{6,4},{7,5},{8,10},{9,11},{10,... | collective-permute-start | bytes 884744 | tf_op jit(solution)/shard_map/ppermute | solution.py:334
  77.4 13.6 %copy-start.3 = (s32[128,8]{0,1:T(8,128)S(1)}, s32[128,8]{0,1:T(8,128)}, u32[]{:S(2)}) copy-start(s32[128,8]{0,1:T(8,128)} %param.11) | copy-start | bytes 12292
  80.1 10.8 %collective-permute-start.26 = (bf16[128,1152]{1,0:T(8,128)(2,1)S(1)}, bf16[128,1152]{1,0:T(8,128)(2,1)S(1)}, u32[]{:S(2)}, u32[]{:S(2)}) collective-permute-start(bf16[128,1152]{1,0:T(8,128)(2,1)S(1)} %add_convert_fusion), channel_id=1, source_target_pairs={{0,4},{1,5},{2,6},{3,7},{4,8},{5,9},{6,10},{7,11},{8,12},{9,13},{1... | collective-permute-start | bytes 884744 | tf_op jit(solution)/shard_map/ppermute | solution.py:331

commit v3 on v2

--- a/solution.py
+++ b/solution.py
@@ -13,6 +13,7 @@
 LANES = 128
 ROW_BLOCK = 256
 W_ROWS = 1024
+HOLD = 10**10
 
 f32 = jnp.float32
 bf16 = jnp.bfloat16
@@ -80,6 +81,21 @@
     )(table, ids, gates, dy)
 
 
+def hold_kernel(source, out):
+    out[...] = source[...]
+
+
+def hold(value, flops):
+    return pl.pallas_call(
+        hold_kernel,
+        out_shape=jax.ShapeDtypeStruct(value.shape, value.dtype),
+        in_specs=[VMEM],
+        out_specs=VMEM,
+        cost_estimate=pl.CostEstimate(flops=flops, bytes_accessed=1000, transcendentals=0),
+        name="hold",
+    )(value)
+
+
 def rows_kernel(slots, *refs):
     x_in, dyg_in = refs[:slots], refs[slots : 2 * slots]
     weights = refs[2 * slots : 2 * slots + 6]
@@ -344,24 +360,6 @@
     def together(*values):
         return lax.optimization_barrier(values)
 
-    xs, dygs = [[tokens_in]], [[dyg]]
-    for z in range(1, outer + 1):
-        for k, stream in enumerate((xs, dygs)):
-            last = stream[z - 1]
-            if z < outer:
-                ahead = send_z(last[0])
-                for y in range(1, inner):
-                    last.append(send_y(last[y - 1]))
-                if inner > 1:
-                    ahead, last[-1] = together(ahead, last[-1])
-                stream.append([ahead])
-            else:
-                for y in range(1, inner):
-                    if k and outer > 1 and y == inner - 1:
-                        last.append(send_z(stream[z - 2][y]))
-                    else:
-                        last.append(send_y(last[y - 1]))
-
     per = max(1, W_ROWS // (inner * tokens))
     groups = [range(z, min(outer, z + per)) for z in range(0, outer, per)]
     sums = [None, None]
@@ -376,24 +374,57 @@
             more,
         )
 
+    xs, dygs = [[tokens_in]], [[dyg]]
     dxs, acts, across = [], [], []
-    for z in range(outer):
-        *dx, act = rows_grads(xs[z], dygs[z], weights)
-        dxs.append(dx)
-        acts.append(act)
+
+    def send_across(z):
         if inner > 1:
-            total = dx[1]
+            total = dxs[z][1]
             for y in range(2, inner):
-                total = add(send_y(total), dx[y])
+                total = add(send_y(total), dxs[z][y])
             across.append([send_y(total)])
         else:
             across.append([])
-        if len(groups) > 1 and z == groups[z // per][-1]:
+
+    for z in range(1, outer + 1):
+        for k, stream in enumerate((xs, dygs)):
+            last = stream[z - 1]
+            ahead = None
+            if z < outer:
+                ahead = send_z(last[0])
+            for y in range(1, inner):
+                if k and z == outer > 1 and y == inner - 1:
+                    last.append(send_z(stream[z - 2][y]))
+                else:
+                    last.append(send_y(last[y - 1]))
+            done = [last[-1]] if inner > 1 else []
+            if ahead is not None:
+                done.append(ahead)
+            if k == 0 and z == 1:
+                done, kept, weights = together(done, hold(kept, HOLD), weights)
+            elif k == 0:
+                done, dxs[z - 2], acts[z - 2] = together(done, dxs[z - 2], acts[z - 2])
+            else:
+                (done,) = together(done)
+            if ahead is not None:
+                stream.append([done.pop()])
+            if inner > 1:
+                last[-1] = done.pop()
+        if z > 2:
+            send_across(z - 2)
+        *dx, act = rows_grads(xs[z - 1], dygs[z - 1], weights)
+        dxs.append(dx)
+        acts.append(act)
+        if len(groups) > 1 and z - 1 == groups[(z - 1) // per][-1]:
             for j in range(2):
-                value = partial(j, groups[z // per], f32)
-                sums[j] = value if z < per else [t + v for t, v in zip(sums[j], value)]
-            if z + 1 < outer:
-                sums, xs[z + 1] = lax.optimization_barrier((sums, xs[z + 1]))
+                value = partial(j, groups[(z - 1) // per], f32)
+                sums[j] = value if z <= per else [t + v for t, v in zip(sums[j], value)]
+            if z < outer:
+                sums, xs[z] = together(sums, xs[z])
+    if outer > 1:
+        send_across(outer - 1)
+        dxs[0], acts[-1] = together(dxs[0], acts[-1])
+    send_across(0)
 
     single = len(groups) == 1
     if single:
@@ -401,11 +432,11 @@
     else:
         other = [send_core(v.astype(bf16)) for v in sums[1]]
 
-    pieces = [dxs[0][0], *across[0]]
+    pieces = [dxs[0][0], *across[-1]]
     if outer > 1:
-        total = add(dxs[1][0], *across[1])
+        total = add(dxs[1][0], *across[0])
         for z in range(2, outer):
-            total = add(send_z(total), dxs[z][0], *across[z])
+            total = add(send_z(total), dxs[z][0], *across[z - 1])
         total, other = together(total, other)
         pieces.append(send_z(total))
     if single:

time: 92.1 us -> 86.3 us (0.937)
  starting transfers between devices: 25.4 us -> 21.6 us
  local copies, waits for them, and re-layouts: 6.38 us -> 4.72 us
  waiting for transfers between devices: 33.8 us -> 32.4 us
  Pallas kernels: 25.1 us -> 26.2 us
    ppermute x10, waiting for transfers between devices: 27.7 us -> 19.8 us  [send_z(): lax.ppermute(v, 'expert', [(i, moved(i, 1, 0)) for i in range(devices)])]
    ppermute x11, waiting for transfers between devices: 3.39 us -> 11.1 us  [send_y(): lax.ppermute(v, 'expert', [(i, moved(i, 0, 1)) for i in range(devices)])]
    ppermute x10, starting transfers between devices: 10 us -> 7.66 us  [send_z(): lax.ppermute(v, 'expert', [(i, moved(i, 1, 0)) for i in range(devices)])]
    unnamed x18 -> x24, local copies, waits for them, and re-layouts: 6.38 us -> 4.72 us
    ppermute x11, starting transfers between devices: 14.2 us -> 12.8 us  [send_y(): lax.ppermute(v, 'expert', [(i, moved(i, 0, 1)) for i in range(devices)])]
    pallas_call x0 -> x1, Pallas kernels: none -> 1.43 us  [hold(): pl.pallas_call(hold_kernel, out_shape=jax.ShapeDtypeStruct(value.shape, v...]
    ppermute x6, waiting for transfers between devices: 2.7 us -> 1.43 us  [send_core(): return lax.ppermute(v, 'expert', [(i, i ^ 1) for i in range(devices)])]
  transfers between devices with their start and end apart: 27 -> 27, of which waited for: 13 -> 16; matrix products, arithmetic and copies ran while one was open for 0% -> 0% of each run, Pallas kernels for 26% -> 29%
where the time goes in v3:
time: 86.3 us; the launch traced here: 86 us
  waiting for transfers between devices  32.4 us (38%)
  Pallas kernels  26.2 us (30%)
  starting transfers between devices  21.6 us (25%)
  local copies, waits for them, and re-layouts  4.72 us (5%)
    ppermute x10, waiting for transfers between devices, send_z(): lax.ppermute(v, 'expert', [(i, moved(i, 1, 0)) for i in range(devices)])  19.8 us
    pallas_call x4, Pallas kernels, rows_grads(): pl.pallas_call(functools.partial(rows_kernel, slots), out_shape=tuple((ja...  15.7 us
    ppermute x11, starting transfers between devices, send_y(): lax.ppermute(v, 'expert', [(i, moved(i, 0, 1)) for i in range(devices)])  12.8 us
    ppermute x11, waiting for transfers between devices, send_y(): lax.ppermute(v, 'expert', [(i, moved(i, 0, 1)) for i in range(devices)])  11.1 us
    pallas_call x2, Pallas kernels, weights_grads(): pl.pallas_call(functools.partial(weights_kernel, j, slots, steps, len(mor...  7.95 us
    ppermute x10, starting transfers between devices, send_z(): lax.ppermute(v, 'expert', [(i, moved(i, 1, 0)) for i in range(devices)])  7.66 us
    unnamed x24, local copies, waits for them, and re-layouts  4.72 us
  transfers between devices with their start and end apart: 27, of which 16 were waited for; matrix products, arithmetic and copies ran while one was open for 0% of the time, Pallas kernels for 29%

profile of v3, /device:TPU:0, one launch (start us, length us, event | category | flops | bytes accessed | tf_op | source)
XLA Modules:
  0.0 86.0 jit_solution(8187159152151482529)
XLA Ops:
  0.6 3.0 %collective-permute-start = (bf16[128,1024]{1,0:T(8,128)(2,1)}, bf16[128,1024]{1,0:T(8,128)(2,1)S(1)}, u32[]{:S(2)}, u32[]{:S(2)}) collective-permute-start(bf16[128,1024]{1,0:T(8,128)(2,1)} %refs_0_.5), channel_id=1, source_target_pairs={{0,2},{1,3},{2,0},{3,1},{4,6},{5,7},{6,4},{7,5},{8,10},{9,11},{10,... | collective-permute-start | bytes 786440 | tf_op jit(solution)/shard_map/ppermute | solution.py:350
  3.7 1.6 %collective-permute-start.1 = (bf16[128,1024]{1,0:T(8,128)(2,1)}, bf16[128,1024]{1,0:T(8,128)(2,1)S(1)}, u32[]{:S(2)}, u32[]{:S(2)}) collective-permute-start(bf16[128,1024]{1,0:T(8,128)(2,1)} %refs_0_.5), channel_id=1, source_target_pairs={{0,4},{1,5},{2,6},{3,7},{4,8},{5,9},{6,10},{7,11},{8,12},{9,13},{1... | collective-permute-start | bytes 786440 | tf_op jit(solution)/shard_map/ppermute | solution.py:347
  5.2 0.9 %copy-done.1 = bf16[128,1024]{1,0:T(8,128)(2,1)S(1)} copy-done((bf16[128,1024]{1,0:T(8,128)(2,1)S(1)}, bf16[128,1024]{1,0:T(8,128)(2,1)}, u32[]{:S(2)}) %copy-start.1) | copy-done | bytes 262168
  6.2 0.7 copy-done.2
  6.9 0.7 copy-done.5
  7.6 0.7 copy-done.6
  8.2 0.2 plan.1
  8.5 0.0 copy-start.11
  8.5 0.6 copy-done.11
  9.1 0.5 collective-permute-start.7
  9.6 1.6 %collective-permute-start.8 = (bf16[128,1152]{1,0:T(8,128)(2,1)S(1)}, bf16[128,1152]{1,0:T(8,128)(2,1)S(1)}, u32[]{:S(2)}, u32[]{:S(2)}) collective-permute-start(bf16[128,1152]{1,0:T(8,128)(2,1)S(1)} %get-tuple-element.73.refs_2_.refs_8_), channel_id=1, source_target_pairs={{0,4},{1,5},{2,6},{3,7},{4,8},{5,9},{6,10},{7,11},{8,12},{9,13},{1... | collective-permute-start | bytes 884744 | tf_op jit(solution)/shard_map/ppermute | solution.py:347
  11.1 0.0 collective-permute-start.2
  11.2 0.5 collective-permute-start.3
  11.7 2.4 %collective-permute-done.1.refs_0_.refs_2_ = bf16[128,1024]{1,0:T(8,128)(2,1)S(1)} collective-permute-done((bf16[128,1024]{1,0:T(8,128)(2,1)}, bf16[128,1024]{1,0:T(8,128)(2,1)S(1)}, u32[]{:S(2)}, u32[]{:S(2)}) %collective-permute-start.1) | collective-permute-done | bytes 262176 | tf_op jit(solution)/shard_map/ppermute | solution.py:347
  14.1 1.4 %hold.1.kept = f32[16,128]{1,0:T(8,128)} custom-call(f32[16,128]{1,0:T(8,128)} %copy-done.11), custom_call_target="tpu_custom_call" | custom-call | flops 10000000000 | bytes 1000 | tf_op jit(solution)/shard_map/hold/pallas_call | solution.py:89
  15.5 0.0 collective-permute-done.2.refs_7_
  15.5 0.0 collective-permute-done.3.refs_8_
  15.5 1.2 %collective-permute-done.4.refs_9_ = bf16[384,1024]{1,0:T(8,128)(2,1)} collective-permute-done((bf16[384,1024]{1,0:T(8,128)(2,1)}, bf16[384,1024]{1,0:T(8,128)(2,1)}, u32[]{:S(2)}, u32[]{:S(2)}) %collective-permute-start.4) | collective-permute-done | bytes 786464 | tf_op jit(solution)/shard_map/ppermute | solution.py:353
  16.7 0.9 %collective-permute-start.5 = (bf16[128,1024]{1,0:T(8,128)(2,1)S(1)}, bf16[128,1024]{1,0:T(8,128)(2,1)S(1)}, u32[]{:S(2)}, u32[]{:S(2)}) collective-permute-start(bf16[128,1024]{1,0:T(8,128)(2,1)S(1)} %collective-permute-done.1.refs_0_.refs_2_), channel_id=1, source_target_pairs={{0,2},{1,3},{2,0},{3,1},{4,6},{5,7},{6,4},{7,5},{8,10},{9,11},{10,... | collective-permute-start | bytes 786440 | tf_op jit(solution)/shard_map/ppermute | solution.py:350
  17.5 1.6 %collective-permute-start.6 = (bf16[128,1024]{1,0:T(8,128)(2,1)S(1)}, bf16[128,1024]{1,0:T(8,128)(2,1)S(1)}, u32[]{:S(2)}, u32[]{:S(2)}) collective-permute-start(bf16[128,1024]{1,0:T(8,128)(2,1)S(1)} %collective-permute-done.1.refs_0_.refs_2_), channel_id=1, source_target_pairs={{0,4},{1,5},{2,6},{3,7},{4,8},{5,9},{6,10},{7,11},{8,12},{9,13},{1... | collective-permute-start | bytes 786440 | tf_op jit(solution)/shard_map/ppermute | solution.py:347
  19.1 0.7 collective-permute-done.8.refs_2_.refs_10_
  19.9 0.9 %collective-permute-start.11 = (bf16[128,1152]{1,0:T(8,128)(2,1)S(1)}, bf16[128,1152]{1,0:T(8,128)(2,1)S(1)}, u32[]{:S(2)}, u32[]{:S(2)}) collective-permute-start(bf16[128,1152]{1,0:T(8,128)(2,1)S(1)} %collective-permute-done.8.refs_2_.refs_10_), channel_id=1, source_target_pairs={{0,2},{1,3},{2,0},{3,1},{4,6},{5,7},{6,4},{7,5},{8,10},{9,11},{10,... | collective-permute-start | bytes 884744 | tf_op jit(solution)/shard_map/ppermute | solution.py:350
  20.8 0.0 copy-start.9
  20.8 1.1 %copy-done.9 = bf16[1,384,1024]{2,1,0:T(8,128)(2,1)S(1)} copy-done((bf16[1,384,1024]{2,1,0:T(8,128)(2,1)S(1)}, bf16[1,384,1024]{2,1,0:T(8,128)(2,1)}, u32[]{:S(2)}) %copy-start.9) | copy-done | bytes 786456
  22.0 3.9 %rows_grads.4 = (bf16[128,1152]{1,0:T(8,128)(2,1)S(1)}, bf16[128,1152]{1,0:T(8,128)(2,1)S(1)}, bf16[256,2304]{1,0:T(8,128)(2,1)S(1)}) custom-call(bf16[128,1024]{1,0:T(8,128)(2,1)S(1)} %copy-done, bf16[128,1024]{1,0:T(8,128)(2,1)S(1)} %collective-permute-done.refs_1_, bf16[128,1152]{1,0:T(8,128)(2,1)S(1)} %get-tuple-element.73.refs_2_.refs_8_, ...), custom_call_target="tpu_custom_call" | custom-call | flops 2013265920 | bytes 9306112 | tf_op jit(solution)/shard_map/rows_grads/pallas_call | solution.py:184
  25.9 0.0 collective-permute-done.5.refs_1_.refs_3_
  25.9 2.6 %collective-permute-done.6.refs_0_.refs_4_ = bf16[128,1024]{1,0:T(8,128)(2,1)S(1)} collective-permute-done((bf16[128,1024]{1,0:T(8,128)(2,1)S(1)}, bf16[128,1024]{1,0:T(8,128)(2,1)S(1)}, u32[]{:S(2)}, u32[]{:S(2)}) %collective-permute-start.6) | collective-permute-done | bytes 262176 | tf_op jit(solution)/shard_map/ppermute | solution.py:347
  28.5 1.1 %collective-permute-start.9 = (bf16[128,1024]{1,0:T(8,128)(2,1)S(1)}, bf16[128,1024]{1,0:T(8,128)(2,1)S(1)}, u32[]{:S(2)}, u32[]{:S(2)}) collective-permute-start(bf16[128,1024]{1,0:T(8,128)(2,1)S(1)} %collective-permute-done.6.refs_0_.refs_4_), channel_id=1, source_target_pairs={{0,2},{1,3},{2,0},{3,1},{4,6},{5,7},{6,4},{7,5},{8,10},{9,11},{10,... | collective-permute-start | bytes 786440 | tf_op jit(solution)/shard_map/ppermute | solution.py:350
  29.7 0.0 collective-permute-start.10
  29.7 2.5 %collective-permute-done.11.refs_3_.refs_11_ = bf16[128,1152]{1,0:T(8,128)(2,1)S(1)} collective-permute-done((bf16[128,1152]{1,0:T(8,128)(2,1)S(1)}, bf16[128,1152]{1,0:T(8,128)(2,1)S(1)}, u32[]{:S(2)}, u32[]{:S(2)}) %collective-permute-start.11) | collective-permute-done | bytes 294944 | tf_op jit(solution)/shard_map/ppermute | solution.py:350
  32.1 2.7 %collective-permute-done.12.refs_2_.refs_12_ = bf16[128,1152]{1,0:T(8,128)(2,1)S(1)} collective-permute-done((bf16[128,1152]{1,0:T(8,128)(2,1)S(1)}, bf16[128,1152]{1,0:T(8,128)(2,1)S(1)}, u32[]{:S(2)}, u32[]{:S(2)}) %collective-permute-start.12) | collective-permute-done | bytes 294944 | tf_op jit(solution)/shard_map/ppermute | solution.py:347
  34.9 1.1 %collective-permute-start.14 = (bf16[128,1152]{1,0:T(8,128)(2,1)S(1)}, bf16[128,1152]{1,0:T(8,128)(2,1)S(1)}, u32[]{:S(2)}, u32[]{:S(2)}) collective-permute-start(bf16[128,1152]{1,0:T(8,128)(2,1)S(1)} %collective-permute-done.12.refs_2_.refs_12_), channel_id=1, source_target_pairs={{0,2},{1,3},{2,0},{3,1},{4,6},{5,7},{6,4},{7,5},{8,10},{9,11},{10,... | collective-permute-start | bytes 884744 | tf_op jit(solution)/shard_map/ppermute | solution.py:350
  36.0 3.9 %rows_grads.5 = (bf16[128,1152]{1,0:T(8,128)(2,1)S(1)}, bf16[128,1152]{1,0:T(8,128)(2,1)S(1)}, bf16[256,2304]{1,0:T(8,128)(2,1)S(1)}) custom-call(bf16[128,1024]{1,0:T(8,128)(2,1)S(1)} %collective-permute-done.1.refs_0_.refs_2_, bf16[128,1024]{1,0:T(8,128)(2,1)S(1)} %collective-permute-done.5.refs_1_.refs_3_, ...), custom_call_target="tpu_custom_call" | custom-call | flops 2013265920 | bytes 9306112 | tf_op jit(solution)/shard_map/rows_grads/pallas_call | solution.py:184
  39.9 0.7 collective-permute-done.10.refs_0_.refs_6_
  40.6 1.0 %collective-permute-start.18 = (bf16[128,1152]{1,0:T(8,128)(2,1)S(1)}, bf16[128,1152]{1,0:T(8,128)(2,1)S(1)}, u32[]{:S(2)}, u32[]{:S(2)}) collective-permute-start(bf16[128,1152]{1,0:T(8,128)(2,1)S(1)} %get-tuple-element.106), channel_id=1, source_target_pairs={{0,2},{1,3},{2,0},{3,1},{4,6},{5,7},{6,4},{7,5},{8,10},{9,11},{10,... | collective-permute-start | bytes 884744 | tf_op jit(solution)/shard_map/ppermute | solution.py:350
  41.6 1.1 %collective-permute-start.13 = (bf16[128,1024]{1,0:T(8,128)(2,1)S(1)}, bf16[128,1024]{1,0:T(8,128)(2,1)S(1)}, u32[]{:S(2)}, u32[]{:S(2)}) collective-permute-start(bf16[128,1024]{1,0:T(8,128)(2,1)S(1)} %collective-permute-done.10.refs_0_.refs_6_), channel_id=1, source_target_pairs={{0,2},{1,3},{2,0},{3,1},{4,6},{5,7},{6,4},{7,5},{8,10},{9,11},{10,... | collective-permute-start | bytes 786440 | tf_op jit(solution)/shard_map/ppermute | solution.py:350
  42.7 2.1 %collective-permute-done.14.refs_3_.refs_13_ = bf16[128,1152]{1,0:T(8,128)(2,1)S(1)} collective-permute-done((bf16[128,1152]{1,0:T(8,128)(2,1)S(1)}, bf16[128,1152]{1,0:T(8,128)(2,1)S(1)}, u32[]{:S(2)}, u32[]{:S(2)}) %collective-permute-start.14) | collective-permute-done | bytes 294944 | tf_op jit(solution)/shard_map/ppermute | solution.py:350
  44.8 0.9 %collective-permute-done.15.refs_2_.refs_14_ = bf16[128,1152]{1,0:T(8,128)(2,1)S(1)} collective-permute-done((bf16[128,1152]{1,0:T(8,128)(2,1)S(1)}, bf16[128,1152]{1,0:T(8,128)(2,1)S(1)}, u32[]{:S(2)}, u32[]{:S(2)}) %collective-permute-start.15) | collective-permute-done | bytes 294944 | tf_op jit(solution)/shard_map/ppermute | solution.py:347
  45.7 3.9 %rows_grads.6 = (bf16[128,1152]{1,0:T(8,128)(2,1)S(1)}, bf16[128,1152]{1,0:T(8,128)(2,1)S(1)}, bf16[256,2304]{1,0:T(8,128)(2,1)S(1)}) custom-call(bf16[128,1024]{1,0:T(8,128)(2,1)S(1)} %collective-permute-done.6.refs_0_.refs_4_, bf16[128,1024]{1,0:T(8,128)(2,1)S(1)} %collective-permute-done.9.refs_1_.refs_5_, ...), custom_call_target="tpu_custom_call" | custom-call | flops 2013265920 | bytes 9306112 | tf_op jit(solution)/shard_map/rows_grads/pallas_call | solution.py:184
  49.6 5.6 %collective-permute-done.13.refs_1_.refs_7_ = bf16[128,1024]{1,0:T(8,128)(2,1)S(1)} collective-permute-done((bf16[128,1024]{1,0:T(8,128)(2,1)S(1)}, bf16[128,1024]{1,0:T(8,128)(2,1)S(1)}, u32[]{:S(2)}, u32[]{:S(2)}) %collective-permute-start.13) | collective-permute-done | bytes 262176 | tf_op jit(solution)/shard_map/ppermute | solution.py:350
  55.2 0.9 %collective-permute-start.20 = (bf16[128,1152]{1,0:T(8,128)(2,1)S(1)}, bf16[128,1152]{1,0:T(8,128)(2,1)S(1)}, u32[]{:S(2)}, u32[]{:S(2)}) collective-permute-start(bf16[128,1152]{1,0:T(8,128)(2,1)S(1)} %get-tuple-element.108), channel_id=1, source_target_pairs={{0,2},{1,3},{2,0},{3,1},{4,6},{5,7},{6,4},{7,5},{8,10},{9,11},{10,... | collective-permute-start | bytes 884744 | tf_op jit(solution)/shard_map/ppermute | solution.py:350
  56.1 0.1 add_convert_fusion.2
  56.2 1.8 %collective-permute-start.19 = (bf16[128,1152]{1,0:T(8,128)(2,1)S(1)}, bf16[128,1152]{1,0:T(8,128)(2,1)S(1)}, u32[]{:S(2)}, u32[]{:S(2)}) collective-permute-start(bf16[128,1152]{1,0:T(8,128)(2,1)S(1)} %add_convert_fusion.2), channel_id=1, source_target_pairs={{0,4},{1,5},{2,6},{3,7},{4,8},{5,9},{6,10},{7,11},{8,12},{9,13},{1... | collective-permute-start | bytes 884744 | tf_op jit(solution)/shard_map/ppermute | solution.py:347
  58.0 3.9 %rows_grads.7 = (bf16[128,1152]{1,0:T(8,128)(2,1)S(1)}, bf16[128,1152]{1,0:T(8,128)(2,1)S(1)}, bf16[256,2304]{1,0:T(8,128)(2,1)S(1)}) custom-call(bf16[128,1024]{1,0:T(8,128)(2,1)S(1)} %collective-permute-done.10.refs_0_.refs_6_, bf16[128,1024]{1,0:T(8,128)(2,1)S(1)} %collective-permute-done.13.refs_1_.refs_7_, ...), custom_call_target="tpu_custom_call" | custom-call | flops 2013265920 | bytes 9306112 | tf_op jit(solution)/shard_map/rows_grads/pallas_call | solution.py:184
  61.9 0.6 collective-permute-start.22
  62.5 0.2 collective-permute-done.20
  62.7 2.4 %collective-permute-done.19 = bf16[128,1152]{1,0:T(8,128)(2,1)S(1)} collective-permute-done((bf16[128,1152]{1,0:T(8,128)(2,1)S(1)}, bf16[128,1152]{1,0:T(8,128)(2,1)S(1)}, u32[]{:S(2)}, u32[]{:S(2)}) %collective-permute-start.19) | collective-permute-done | bytes 294944 | tf_op jit(solution)/shard_map/ppermute | solution.py:347
  65.1 0.1 add_convert_fusion.1
  65.3 0.8 collective-permute-start.21
  66.1 3.5 %weights_grads.2 = (bf16[1024,384]{1,0:T(8,128)(2,1)S(1)}, bf16[1024,384]{1,0:T(8,128)(2,1)S(1)}, bf16[384,1024]{1,0:T(8,128)(2,1)S(1)}) custom-call(bf16[128,1024]{1,0:T(8,128)(2,1)S(1)} %copy-done, bf16[128,1024]{1,0:T(8,128)(2,1)S(1)} %collective-permute-done.refs_1_, bf16[128,1024]{1,0:T(8,128)(2,1)S(1)} %collective-permute-done.1.refs_0_.refs_2_, ...), custom_call_target="tpu_custom_call" | custom-call | flops 2415919104 | bytes 8912896 | tf_op jit(solution)/shard_map/weights_grads/pallas_call | solution.py:266
  69.6 0.1 collective-permute-start.23
  69.7 0.5 collective-permute-start.24
  70.2 0.1 collective-permute-start.25
  70.3 1.6 %collective-permute-start.17 = (bf16[128,1152]{1,0:T(8,128)(2,1)S(1)}, bf16[128,1152]{1,0:T(8,128)(2,1)S(1)}, u32[]{:S(2)}, u32[]{:S(2)}) collective-permute-start(bf16[128,1152]{1,0:T(8,128)(2,1)S(1)} %get-tuple-element.104), channel_id=1, source_target_pairs={{0,2},{1,3},{2,0},{3,1},{4,6},{5,7},{6,4},{7,5},{8,10},{9,11},{10,... | collective-permute-start | bytes 884744 | tf_op jit(solution)/shard_map/ppermute | solution.py:350
  71.9 1.9 %collective-permute-done.21 = bf16[128,1152]{1,0:T(8,128)(2,1)S(1)} collective-permute-done((bf16[128,1152]{1,0:T(8,128)(2,1)S(1)}, bf16[128,1152]{1,0:T(8,128)(2,1)S(1)}, u32[]{:S(2)}, u32[]{:S(2)}) %collective-permute-start.21) | collective-permute-done | bytes 294944 | tf_op jit(solution)/shard_map/ppermute | solution.py:347
  73.8 0.1 add_convert_fusion
  73.9 0.0 copy-start.3
  74.0 0.0 collective-permute-done.24.refs_21_
  74.0 0.2 collective-permute-done.25.refs_22_
  74.2 0.3 collective-permute-start.26
  74.5 4.4 %weights_grads.3 = (bf16[1,1024,384]{2,1,0:T(8,128)(2,1)}, bf16[1,1024,384]{2,1,0:T(8,128)(2,1)}, bf16[1,384,1024]{2,1,0:T(8,128)(2,1)}) custom-call(bf16[128,1024]{1,0:T(8,128)(2,1)S(1)} %copy-done, bf16[128,1024]{1,0:T(8,128)(2,1)S(1)} %collective-permute-done.refs_1_, bf16[128,1024]{1,0:T(8,128)(2,1)S(1)} %collective-permute-done.1.refs_0_.refs_2_, ...), custom_call_target="tpu_custom_call" | custom-call | flops 2415919104 | bytes 8912896 | tf_op jit(solution)/shard_map/weights_grads/pallas_call | solution.py:266
  78.9 0.7 collective-permute-done.17.refs_1_
  79.6 5.4 %collective-permute-done.26.refs_2_ = bf16[128,1152]{1,0:T(8,128)(2,1)S(1)} collective-permute-done((bf16[128,1152]{1,0:T(8,128)(2,1)S(1)}, bf16[128,1152]{1,0:T(8,128)(2,1)S(1)}, u32[]{:S(2)}, u32[]{:S(2)}) %collective-permute-start.26) | collective-permute-done | bytes 294944 | tf_op jit(solution)/shard_map/ppermute | solution.py:347
  85.1 0.9 %finish.1 = (bf16[128,1024]{1,0:T(8,128)(2,1)}, bf16[8,128]{1,0:T(8,128)(2,1)}) custom-call(s32[8,128]{1,0:T(8,128)S(1)} %bitcast.8, f32[16,128]{1,0:T(8,128)S(1)} %copy-done.4, bf16[128,1152]{1,0:T(8,128)(2,1)S(1)} %get-tuple-element.125.refs_0_, bf16[128,1152]{1,0:T(8,128)(2,1)S(1)} %collective-permute-done.17.refs_1_, ...), custom_call_target="tpu_custom_call" | custom-call | tf_op jit(solution)/shard_map/finish/pallas_call | solution.py:313
  (26 shorter events, 0.1 us)
Async XLA Ops:
  0.6 10.5 %collective-permute-start = (bf16[128,1024]{1,0:T(8,128)(2,1)}, bf16[128,1024]{1,0:T(8,128)(2,1)S(1)}, u32[]{:S(2)}, u32[]{:S(2)}) collective-permute-start(bf16[128,1024]{1,0:T(8,128)(2,1)} %refs_0_.5), channel_id=1, source_target_pairs={{0,2},{1,3},{2,0},{3,1},{4,6},{5,7},{6,4},{7,5},{8,10},{9,11},{10,... | collective-permute-start | bytes 786440 | tf_op jit(solution)/shard_map/ppermute | solution.py:350
  3.7 10.4 %collective-permute-start.1 = (bf16[128,1024]{1,0:T(8,128)(2,1)}, bf16[128,1024]{1,0:T(8,128)(2,1)S(1)}, u32[]{:S(2)}, u32[]{:S(2)}) collective-permute-start(bf16[128,1024]{1,0:T(8,128)(2,1)} %refs_0_.5), channel_id=1, source_target_pairs={{0,4},{1,5},{2,6},{3,7},{4,8},{5,9},{6,10},{7,11},{8,12},{9,13},{1... | collective-permute-start | bytes 786440 | tf_op jit(solution)/shard_map/ppermute | solution.py:347
  5.2 0.9 %copy-start.1 = (bf16[128,1024]{1,0:T(8,128)(2,1)S(1)}, bf16[128,1024]{1,0:T(8,128)(2,1)}, u32[]{:S(2)}) copy-start(bf16[128,1024]{1,0:T(8,128)(2,1)} %dy.1) | copy-start | bytes 786436
  6.2 0.7 copy-start.2
  6.9 0.7 copy-start.5
  7.6 0.7 copy-start.6
  8.5 0.6 copy-start.11
  9.1 10.1 %collective-permute-start.7 = (bf16[128,1152]{1,0:T(8,128)(2,1)S(1)}, bf16[128,1152]{1,0:T(8,128)(2,1)S(1)}, u32[]{:S(2)}, u32[]{:S(2)}) collective-permute-start(bf16[128,1152]{1,0:T(8,128)(2,1)S(1)} %get-tuple-element.73.refs_2_.refs_8_), channel_id=1, source_target_pairs={{0,2},{1,3},{2,0},{3,1},{4,6},{5,7},{6,4},{7,5},{8,10},{9,11},{10,... | collective-permute-start | bytes 884744 | tf_op jit(solution)/shard_map/ppermute | solution.py:350
  9.6 10.3 %collective-permute-start.8 = (bf16[128,1152]{1,0:T(8,128)(2,1)S(1)}, bf16[128,1152]{1,0:T(8,128)(2,1)S(1)}, u32[]{:S(2)}, u32[]{:S(2)}) collective-permute-start(bf16[128,1152]{1,0:T(8,128)(2,1)S(1)} %get-tuple-element.73.refs_2_.refs_8_), channel_id=1, source_target_pairs={{0,4},{1,5},{2,6},{3,7},{4,8},{5,9},{6,10},{7,11},{8,12},{9,13},{1... | collective-permute-start | bytes 884744 | tf_op jit(solution)/shard_map/ppermute | solution.py:347
  11.1 4.3 %collective-permute-start.2 = (bf16[1024,384]{1,0:T(8,128)(2,1)}, bf16[1024,384]{1,0:T(8,128)(2,1)}, u32[]{:S(2)}, u32[]{:S(2)}) collective-permute-start(bf16[1024,384]{1,0:T(8,128)(2,1)} %bitcast.11), channel_id=1, source_target_pairs={{0,1},{1,0},{2,3},{3,2},{4,5},{5,4},{6,7},{7,6},{8,9},{9,8},{10,11... | collective-permute-start | bytes 2359304 | tf_op jit(solution)/shard_map/ppermute | solution.py:353
  11.2 4.3 %collective-permute-start.3 = (bf16[1024,384]{1,0:T(8,128)(2,1)}, bf16[1024,384]{1,0:T(8,128)(2,1)}, u32[]{:S(2)}, u32[]{:S(2)}) collective-permute-start(bf16[1024,384]{1,0:T(8,128)(2,1)} %bitcast.16), channel_id=1, source_target_pairs={{0,1},{1,0},{2,3},{3,2},{4,5},{5,4},{6,7},{7,6},{8,9},{9,8},{10,11... | collective-permute-start | bytes 2359304 | tf_op jit(solution)/shard_map/ppermute | solution.py:353
  14.0 2.6 %collective-permute-start.4 = (bf16[384,1024]{1,0:T(8,128)(2,1)}, bf16[384,1024]{1,0:T(8,128)(2,1)}, u32[]{:S(2)}, u32[]{:S(2)}) collective-permute-start(bf16[384,1024]{1,0:T(8,128)(2,1)} %bitcast.21), channel_id=1, source_target_pairs={{0,1},{1,0},{2,3},{3,2},{4,5},{5,4},{6,7},{7,6},{8,9},{9,8},{10,11... | collective-permute-start | bytes 2359304 | tf_op jit(solution)/shard_map/ppermute | solution.py:353
  14.0 6.8 %copy-start = (bf16[128,1024]{1,0:T(8,128)(2,1)S(1)}, bf16[128,1024]{1,0:T(8,128)(2,1)}, u32[]{:S(2)}) copy-start(bf16[128,1024]{1,0:T(8,128)(2,1)} %refs_0_.5) | copy-start | bytes 786436
  14.0 6.8 %copy-start.7 = (bf16[1,1024,384]{2,1,0:T(8,128)(2,1)S(1)}, bf16[1,1024,384]{2,1,0:T(8,128)(2,1)}, u32[]{:S(2)}) copy-start(bf16[1,1024,384]{2,1,0:T(8,128)(2,1)} %param.13) | copy-start | bytes 2359300
  14.0 6.8 %copy-start.8 = (bf16[1,1024,384]{2,1,0:T(8,128)(2,1)S(1)}, bf16[1,1024,384]{2,1,0:T(8,128)(2,1)}, u32[]{:S(2)}) copy-start(bf16[1,1024,384]{2,1,0:T(8,128)(2,1)} %param.14) | copy-start | bytes 2359300
  16.7 9.2 %collective-permute-start.5 = (bf16[128,1024]{1,0:T(8,128)(2,1)S(1)}, bf16[128,1024]{1,0:T(8,128)(2,1)S(1)}, u32[]{:S(2)}, u32[]{:S(2)}) collective-permute-start(bf16[128,1024]{1,0:T(8,128)(2,1)S(1)} %collective-permute-done.1.refs_0_.refs_2_), channel_id=1, source_target_pairs={{0,2},{1,3},{2,0},{3,1},{4,6},{5,7},{6,4},{7,5},{8,10},{9,11},{10,... | collective-permute-start | bytes 786440 | tf_op jit(solution)/shard_map/ppermute | solution.py:350
  17.5 11.0 %collective-permute-start.6 = (bf16[128,1024]{1,0:T(8,128)(2,1)S(1)}, bf16[128,1024]{1,0:T(8,128)(2,1)S(1)}, u32[]{:S(2)}, u32[]{:S(2)}) collective-permute-start(bf16[128,1024]{1,0:T(8,128)(2,1)S(1)} %collective-permute-done.1.refs_0_.refs_2_), channel_id=1, source_target_pairs={{0,4},{1,5},{2,6},{3,7},{4,8},{5,9},{6,10},{7,11},{8,12},{9,13},{1... | collective-permute-start | bytes 786440 | tf_op jit(solution)/shard_map/ppermute | solution.py:347
  19.9 12.3 %collective-permute-start.11 = (bf16[128,1152]{1,0:T(8,128)(2,1)S(1)}, bf16[128,1152]{1,0:T(8,128)(2,1)S(1)}, u32[]{:S(2)}, u32[]{:S(2)}) collective-permute-start(bf16[128,1152]{1,0:T(8,128)(2,1)S(1)} %collective-permute-done.8.refs_2_.refs_10_), channel_id=1, source_target_pairs={{0,2},{1,3},{2,0},{3,1},{4,6},{5,7},{6,4},{7,5},{8,10},{9,11},{10,... | collective-permute-start | bytes 884744 | tf_op jit(solution)/shard_map/ppermute | solution.py:350
  20.8 14.1 %collective-permute-start.12 = (bf16[128,1152]{1,0:T(8,128)(2,1)S(1)}, bf16[128,1152]{1,0:T(8,128)(2,1)S(1)}, u32[]{:S(2)}, u32[]{:S(2)}) collective-permute-start(bf16[128,1152]{1,0:T(8,128)(2,1)S(1)} %collective-permute-done.8.refs_2_.refs_10_), channel_id=1, source_target_pairs={{0,4},{1,5},{2,6},{3,7},{4,8},{5,9},{6,10},{7,11},{8,12},{9,13},{1... | collective-permute-start | bytes 884744 | tf_op jit(solution)/shard_map/ppermute | solution.py:347
  20.8 1.1 %copy-start.9 = (bf16[1,384,1024]{2,1,0:T(8,128)(2,1)S(1)}, bf16[1,384,1024]{2,1,0:T(8,128)(2,1)}, u32[]{:S(2)}) copy-start(bf16[1,384,1024]{2,1,0:T(8,128)(2,1)} %param.15) | copy-start | bytes 2359300
  22.0 14.0 %copy-start.10 = (bf16[1,384,1024]{2,1,0:T(8,128)(2,1)S(1)}, bf16[1,384,1024]{2,1,0:T(8,128)(2,1)}, u32[]{:S(2)}) copy-start(bf16[1,384,1024]{2,1,0:T(8,128)(2,1)} %param.15) | copy-start | bytes 2359300
  28.5 11.4 %collective-permute-start.9 = (bf16[128,1024]{1,0:T(8,128)(2,1)S(1)}, bf16[128,1024]{1,0:T(8,128)(2,1)S(1)}, u32[]{:S(2)}, u32[]{:S(2)}) collective-permute-start(bf16[128,1024]{1,0:T(8,128)(2,1)S(1)} %collective-permute-done.6.refs_0_.refs_4_), channel_id=1, source_target_pairs={{0,2},{1,3},{2,0},{3,1},{4,6},{5,7},{6,4},{7,5},{8,10},{9,11},{10,... | collective-permute-start | bytes 786440 | tf_op jit(solution)/shard_map/ppermute | solution.py:350
  29.7 11.0 %collective-permute-start.10 = (bf16[128,1024]{1,0:T(8,128)(2,1)S(1)}, bf16[128,1024]{1,0:T(8,128)(2,1)S(1)}, u32[]{:S(2)}, u32[]{:S(2)}) collective-permute-start(bf16[128,1024]{1,0:T(8,128)(2,1)S(1)} %collective-permute-done.6.refs_0_.refs_4_), channel_id=1, source_target_pairs={{0,4},{1,5},{2,6},{3,7},{4,8},{5,9},{6,10},{7,11},{8,12},{9,13},{1... | collective-permute-start | bytes 786440 | tf_op jit(solution)/shard_map/ppermute | solution.py:347
  34.9 9.9 %collective-permute-start.14 = (bf16[128,1152]{1,0:T(8,128)(2,1)S(1)}, bf16[128,1152]{1,0:T(8,128)(2,1)S(1)}, u32[]{:S(2)}, u32[]{:S(2)}) collective-permute-start(bf16[128,1152]{1,0:T(8,128)(2,1)S(1)} %collective-permute-done.12.refs_2_.refs_12_), channel_id=1, source_target_pairs={{0,2},{1,3},{2,0},{3,1},{4,6},{5,7},{6,4},{7,5},{8,10},{9,11},{10,... | collective-permute-start | bytes 884744 | tf_op jit(solution)/shard_map/ppermute | solution.py:350
  36.0 9.7 %collective-permute-start.15 = (bf16[128,1152]{1,0:T(8,128)(2,1)S(1)}, bf16[128,1152]{1,0:T(8,128)(2,1)S(1)}, u32[]{:S(2)}, u32[]{:S(2)}) collective-permute-start(bf16[128,1152]{1,0:T(8,128)(2,1)S(1)} %collective-permute-done.12.refs_2_.refs_12_), channel_id=1, source_target_pairs={{0,4},{1,5},{2,6},{3,7},{4,8},{5,9},{6,10},{7,11},{8,12},{9,13},{1... | collective-permute-start | bytes 884744 | tf_op jit(solution)/shard_map/ppermute | solution.py:347
  40.6 15.4 %collective-permute-start.18 = (bf16[128,1152]{1,0:T(8,128)(2,1)S(1)}, bf16[128,1152]{1,0:T(8,128)(2,1)S(1)}, u32[]{:S(2)}, u32[]{:S(2)}) collective-permute-start(bf16[128,1152]{1,0:T(8,128)(2,1)S(1)} %get-tuple-element.106), channel_id=1, source_target_pairs={{0,2},{1,3},{2,0},{3,1},{4,6},{5,7},{6,4},{7,5},{8,10},{9,11},{10,... | collective-permute-start | bytes 884744 | tf_op jit(solution)/shard_map/ppermute | solution.py:350
  41.6 13.6 %collective-permute-start.13 = (bf16[128,1024]{1,0:T(8,128)(2,1)S(1)}, bf16[128,1024]{1,0:T(8,128)(2,1)S(1)}, u32[]{:S(2)}, u32[]{:S(2)}) collective-permute-start(bf16[128,1024]{1,0:T(8,128)(2,1)S(1)} %collective-permute-done.10.refs_0_.refs_6_), channel_id=1, source_target_pairs={{0,2},{1,3},{2,0},{3,1},{4,6},{5,7},{6,4},{7,5},{8,10},{9,11},{10,... | collective-permute-start | bytes 786440 | tf_op jit(solution)/shard_map/ppermute | solution.py:350
  45.7 12.3 %collective-permute-start.16 = (bf16[128,1152]{1,0:T(8,128)(2,1)S(1)}, bf16[128,1152]{1,0:T(8,128)(2,1)S(1)}, u32[]{:S(2)}, u32[]{:S(2)}) collective-permute-start(bf16[128,1152]{1,0:T(8,128)(2,1)S(1)} %collective-permute-done.14.refs_3_.refs_13_), channel_id=1, source_target_pairs={{0,4},{1,5},{2,6},{3,7},{4,8},{5,9},{6,10},{7,11},{8,12},{9,13},{1... | collective-permute-start | bytes 884744 | tf_op jit(solution)/shard_map/ppermute | solution.py:347
  55.2 7.5 %collective-permute-start.20 = (bf16[128,1152]{1,0:T(8,128)(2,1)S(1)}, bf16[128,1152]{1,0:T(8,128)(2,1)S(1)}, u32[]{:S(2)}, u32[]{:S(2)}) collective-permute-start(bf16[128,1152]{1,0:T(8,128)(2,1)S(1)} %get-tuple-element.108), channel_id=1, source_target_pairs={{0,2},{1,3},{2,0},{3,1},{4,6},{5,7},{6,4},{7,5},{8,10},{9,11},{10,... | collective-permute-start | bytes 884744 | tf_op jit(solution)/shard_map/ppermute | solution.py:350
  56.2 9.0 %collective-permute-start.19 = (bf16[128,1152]{1,0:T(8,128)(2,1)S(1)}, bf16[128,1152]{1,0:T(8,128)(2,1)S(1)}, u32[]{:S(2)}, u32[]{:S(2)}) collective-permute-start(bf16[128,1152]{1,0:T(8,128)(2,1)S(1)} %add_convert_fusion.2), channel_id=1, source_target_pairs={{0,4},{1,5},{2,6},{3,7},{4,8},{5,9},{6,10},{7,11},{8,12},{9,13},{1... | collective-permute-start | bytes 884744 | tf_op jit(solution)/shard_map/ppermute | solution.py:347
  61.9 8.4 %collective-permute-start.22 = (bf16[128,1152]{1,0:T(8,128)(2,1)S(1)}, bf16[128,1152]{1,0:T(8,128)(2,1)S(1)}, u32[]{:S(2)}, u32[]{:S(2)}) collective-permute-start(bf16[128,1152]{1,0:T(8,128)(2,1)S(1)} %get-tuple-element.110), channel_id=1, source_target_pairs={{0,2},{1,3},{2,0},{3,1},{4,6},{5,7},{6,4},{7,5},{8,10},{9,11},{10,... | collective-permute-start | bytes 884744 | tf_op jit(solution)/shard_map/ppermute | solution.py:350
  65.3 8.6 %collective-permute-start.21 = (bf16[128,1152]{1,0:T(8,128)(2,1)S(1)}, bf16[128,1152]{1,0:T(8,128)(2,1)S(1)}, u32[]{:S(2)}, u32[]{:S(2)}) collective-permute-start(bf16[128,1152]{1,0:T(8,128)(2,1)S(1)} %add_convert_fusion.1), channel_id=1, source_target_pairs={{0,4},{1,5},{2,6},{3,7},{4,8},{5,9},{6,10},{7,11},{8,12},{9,13},{1... | collective-permute-start | bytes 884744 | tf_op jit(solution)/shard_map/ppermute | solution.py:347
  69.6 4.3 %collective-permute-start.23 = (bf16[1024,384]{1,0:T(8,128)(2,1)S(1)}, bf16[1024,384]{1,0:T(8,128)(2,1)S(1)}, u32[]{:S(2)}, u32[]{:S(2)}) collective-permute-start(bf16[1024,384]{1,0:T(8,128)(2,1)S(1)} %get-tuple-element.115), channel_id=1, source_target_pairs={{0,1},{1,0},{2,3},{3,2},{4,5},{5,4},{6,7},{7,6},{8,9},{9,8},{10,11... | collective-permute-start | bytes 2359304 | tf_op jit(solution)/shard_map/ppermute | solution.py:353
  69.7 4.3 %collective-permute-start.24 = (bf16[1024,384]{1,0:T(8,128)(2,1)S(1)}, bf16[1024,384]{1,0:T(8,128)(2,1)S(1)}, u32[]{:S(2)}, u32[]{:S(2)}) collective-permute-start(bf16[1024,384]{1,0:T(8,128)(2,1)S(1)} %get-tuple-element.116), channel_id=1, source_target_pairs={{0,1},{1,0},{2,3},{3,2},{4,5},{5,4},{6,7},{7,6},{8,9},{9,8},{10,11... | collective-permute-start | bytes 2359304 | tf_op jit(solution)/shard_map/ppermute | solution.py:353
  70.2 4.0 %collective-permute-start.25 = (bf16[384,1024]{1,0:T(8,128)(2,1)S(1)}, bf16[384,1024]{1,0:T(8,128)(2,1)S(1)}, u32[]{:S(2)}, u32[]{:S(2)}) collective-permute-start(bf16[384,1024]{1,0:T(8,128)(2,1)S(1)} %get-tuple-element.117), channel_id=1, source_target_pairs={{0,1},{1,0},{2,3},{3,2},{4,5},{5,4},{6,7},{7,6},{8,9},{9,8},{10,11... | collective-permute-start | bytes 2359304 | tf_op jit(solution)/shard_map/ppermute | solution.py:353
  70.3 9.4 %collective-permute-start.17 = (bf16[128,1152]{1,0:T(8,128)(2,1)S(1)}, bf16[128,1152]{1,0:T(8,128)(2,1)S(1)}, u32[]{:S(2)}, u32[]{:S(2)}) collective-permute-start(bf16[128,1152]{1,0:T(8,128)(2,1)S(1)} %get-tuple-element.104), channel_id=1, source_target_pairs={{0,2},{1,3},{2,0},{3,1},{4,6},{5,7},{6,4},{7,5},{8,10},{9,11},{10,... | collective-permute-start | bytes 884744 | tf_op jit(solution)/shard_map/ppermute | solution.py:350
  73.9 11.1 %copy-start.3 = (s32[128,8]{0,1:T(8,128)S(1)}, s32[128,8]{0,1:T(8,128)}, u32[]{:S(2)}) copy-start(s32[128,8]{0,1:T(8,128)} %param.11) | copy-start | bytes 12292
  74.0 11.1 %copy-start.4 = (f32[16,128]{1,0:T(8,128)S(1)}, f32[16,128]{1,0:T(8,128)}, u32[]{:S(2)}) copy-start(f32[16,128]{1,0:T(8,128)} %hold.1.kept) | copy-start | bytes 24580
  74.2 10.8 %collective-permute-start.26 = (bf16[128,1152]{1,0:T(8,128)(2,1)S(1)}, bf16[128,1152]{1,0:T(8,128)(2,1)S(1)}, u32[]{:S(2)}, u32[]{:S(2)}) collective-permute-start(bf16[128,1152]{1,0:T(8,128)(2,1)S(1)} %add_convert_fusion), channel_id=1, source_target_pairs={{0,4},{1,5},{2,6},{3,7},{4,8},{5,9},{6,10},{7,11},{8,12},{9,13},{1... | collective-permute-start | bytes 884744 | tf_op jit(solution)/shard_map/ppermute | solution.py:347

commit v4 on v3

--- a/solution.py
+++ b/solution.py
@@ -14,6 +14,7 @@
 ROW_BLOCK = 256
 W_ROWS = 1024
 HOLD = 10**10
+PLAN_MIB = 60
 
 f32 = jnp.float32
 bf16 = jnp.bfloat16
@@ -21,6 +22,7 @@
 tn = (((0,), (0,)), ((), ()))
 VMEM = pl.BlockSpec(memory_space=pltpu.VMEM)
 ANY = pl.BlockSpec(memory_space=pl.ANY)
+HBM = pl.BlockSpec(memory_space=pltpu.HBM)
 
 
 def params(mib):
@@ -35,37 +37,48 @@
     return lax.broadcasted_iota(jnp.int32, (rows, lanes), 1)
 
 
-def plan_kernel(home_cap, rep_cap, table, ids, gates, dy, dyg, kept_out):
-    tokens, width = dy.shape
-    lanes = dyg.shape[1] - width
+def plan_kernel(home_cap, rep_cap, table_in, ids_in, gates_in, x_in, xg, kept_out, *scratch):
+    table, ids, gates, sem = scratch
+    tokens, width = x_in.shape
+    lanes = xg.shape[1] - width
+    pairs = (
+        (table_in, table),
+        (ids_in, ids),
+        (gates_in, gates),
+        (x_in, xg.at[:, pl.ds(0, width)]),
+    )
+    copies = [pltpu.make_async_copy(src, dst, sem.at[i]) for i, (src, dst) in enumerate(pairs)]
+    for c in copies:
+        c.start()
     devices = table.shape[1]
-    dyg[:, :width] = dy[...]
+    earlier = row_iota(tokens, tokens) < lane_iota(tokens, tokens)
+    earlier = jnp.where(earlier, 1.0, 0.0).astype(bf16)
     expert = row_iota(devices, tokens)
+    for c in copies[:3]:
+        c.wait()
     hosts = jnp.where(table[...] == row_iota(devices, devices), 1.0, 0.0)
-    copies = 1.0 + jnp.sum(hosts, axis=1, keepdims=True)
+    copied = 1.0 + jnp.sum(hosts, axis=1, keepdims=True)
     named = jnp.zeros((devices, tokens), f32)
     weight = jnp.zeros((devices, tokens), f32)
     for k in range(TOP):
         hit = expert == ids[k : k + 1]
         named = jnp.where(hit, 1.0, named)
         weight = jnp.where(hit, gates[k : k + 1].astype(f32), weight)
-    earlier = row_iota(tokens, tokens) < lane_iota(tokens, tokens)
-    rank = jnp.dot(
-        named.astype(bf16), jnp.where(earlier, 1.0, 0.0).astype(bf16), preferred_element_type=f32
-    )
+    rank = jnp.dot(named.astype(bf16), earlier, preferred_element_type=f32)
     turn = rank + lax.axis_index("expert").astype(f32)
-    at_home = turn == copies * jnp.floor(turn / copies + 0.5)
+    at_home = turn == copied * jnp.floor(turn / copied + 0.5)
     cap = jnp.where(at_home, float(home_cap), float(rep_cap))
-    kept = jnp.where((named > 0.0) & (rank < cap * copies), 1.0, 0.0)
+    kept = jnp.where((named > 0.0) & (rank < cap * copied), 1.0, 0.0)
     kept_out[...] = kept
     dense = (weight * kept).T
     if lanes > devices:
         dense = jnp.concatenate([dense, jnp.zeros((tokens, lanes - devices), f32)], axis=1)
-    dyg[:, width:] = dense.astype(bf16)
-
-
-def plan(table, ids, gates, dy, devices, lanes):
-    tokens, width = dy.shape
+    xg[:, width:] = dense.astype(bf16)
+    copies[3].wait()
+
+
+def plan(table, ids, gates, x, devices, lanes):
+    tokens, width = x.shape
     home_cap = max(2, 5 * tokens * TOP // (4 * devices))
     rep_cap = max(2, tokens * TOP // (2 * devices))
     return pl.pallas_call(
@@ -74,36 +87,39 @@
             jax.ShapeDtypeStruct((tokens, width + lanes), bf16),
             jax.ShapeDtypeStruct((devices, tokens), f32),
         ),
-        in_specs=[VMEM] * 4,
+        in_specs=[HBM] * 4,
         out_specs=(VMEM, VMEM),
-        compiler_params=params(16),
+        scratch_shapes=[
+            pltpu.VMEM(table.shape, jnp.int32),
+            pltpu.VMEM(ids.shape, jnp.int32),
+            pltpu.VMEM(gates.shape, bf16),
+            pltpu.SemaphoreType.DMA((4,)),
+        ],
+        compiler_params=params(PLAN_MIB),
         name="plan",
-    )(table, ids, gates, dy)
-
-
-def hold_kernel(source, out):
-    out[...] = source[...]
+    )(table, ids, gates, x)
 
 
 def hold(value, flops):
     return pl.pallas_call(
-        hold_kernel,
+        lambda source, out: None,
         out_shape=jax.ShapeDtypeStruct(value.shape, value.dtype),
-        in_specs=[VMEM],
-        out_specs=VMEM,
+        in_specs=[ANY],
+        out_specs=ANY,
+        input_output_aliases={0: 0},
         cost_estimate=pl.CostEstimate(flops=flops, bytes_accessed=1000, transcendentals=0),
         name="hold",
     )(value)
 
 
 def rows_kernel(slots, *refs):
-    x_in, dyg_in = refs[:slots], refs[slots : 2 * slots]
+    xg_in, dy_in = refs[:slots], refs[slots : 2 * slots]
     weights = refs[2 * slots : 2 * slots + 6]
     dxg, act = refs[2 * slots + 6 : 3 * slots + 6], refs[3 * slots + 6]
-    x, dyg, w_gu, w_dn, sem = refs[3 * slots + 7 :]
-    tokens, width = x_in[0].shape
+    xg, dy, w_gu, w_dn, sem = refs[3 * slots + 7 :]
+    tokens, width = dy_in[0].shape
     hidden = weights[2].shape[0]
-    lanes = dyg.shape[1] - width
+    lanes = xg.shape[1] - width
     copies = []
 
     def fetch(src, dst):
@@ -118,9 +134,9 @@
         ]
         return up, [fetch(weights[3 * j + 2], w_dn.at[j])]
 
-    got_x = [fetch(x_in[i], x.at[pl.ds(i * tokens, tokens)]) for i in range(slots)]
+    got_x = [fetch(xg_in[i], xg.at[pl.ds(i * tokens, tokens)]) for i in range(slots)]
     own = fetch_weights(0)
-    got_dy = [fetch(dyg_in[i], dyg.at[pl.ds(i * tokens, tokens)]) for i in range(slots)]
+    got_dy = [fetch(dy_in[i], dy.at[pl.ds(i * tokens, tokens)]) for i in range(slots)]
     sibling = fetch_weights(1)
     for c in got_x + own[0]:
         c.wait()
@@ -132,12 +148,12 @@
 
     def expert(j, at, after_up):
         here = pl.ds(at, block)
-        pre = jnp.dot(x[here, :], w_gu[j], preferred_element_type=f32)
+        pre = jnp.dot(xg[here, :width], w_gu[j], preferred_element_type=f32)
         after_up()
-        back = lax.dot_general(dyg[here, :width], w_dn[j], nt, preferred_element_type=f32)
+        back = lax.dot_general(dy[here, :], w_dn[j], nt, preferred_element_type=f32)
         column = lane == (me if j == 0 else me ^ 1)
         gate = jnp.sum(
-            jnp.where(column, dyg[here, width:].astype(f32), 0.0), axis=1, keepdims=True
+            jnp.where(column, xg[here, width:].astype(f32), 0.0), axis=1, keepdims=True
         )
         a, b = pre[:, :hidden], pre[:, hidden:]
         sig = jax.nn.sigmoid(a)
@@ -173,23 +189,23 @@
             out[:, width:] = gg[part]
 
 
-def rows_grads(xs, dygs, weights):
-    slots = len(xs)
-    tokens, width = xs[0].shape
-    full = dygs[0].shape[1]
+def rows_grads(xgs, dys, weights):
+    slots = len(dys)
+    tokens, width = dys[0].shape
+    full = xgs[0].shape[1]
     hidden = weights[2].shape[0]
     rows = slots * tokens
     flops = 2 * rows * 2 * 5 * width * hidden
     moved = 4 * rows * (width + full) + 12 * width * hidden + 4 * rows * full + 12 * rows * hidden
     return pl.pallas_call(
         functools.partial(rows_kernel, slots),
-        out_shape=tuple(jax.ShapeDtypeStruct((tokens, full), bf16) for _ in xs)
+        out_shape=tuple(jax.ShapeDtypeStruct((tokens, full), bf16) for _ in dys)
         + (jax.ShapeDtypeStruct((rows, 6 * hidden), bf16),),
         in_specs=[ANY] * (2 * slots + 6),
         out_specs=(VMEM,) * (slots + 1),
         scratch_shapes=[
+            pltpu.VMEM((rows, full), bf16),
             pltpu.VMEM((rows, width), bf16),
-            pltpu.VMEM((rows, full), bf16),
             pltpu.VMEM((2, width, 2 * hidden), bf16),
             pltpu.VMEM((2, hidden, width), bf16),
             pltpu.SemaphoreType.DMA((2 * slots + 6,)),
@@ -199,16 +215,16 @@
             flops=flops, bytes_accessed=moved, transcendentals=2 * rows * hidden
         ),
         name="rows_grads",
-    )(*xs, *dygs, *weights)
+    )(*xgs, *dys, *weights)
 
 
 def weights_kernel(j, slots, steps, extra, *refs):
-    x_in, dyg_in, act_in = refs[:slots], refs[slots : 2 * slots], refs[2 * slots : 2 * slots + steps]
+    xg_in, dy_in, act_in = refs[:slots], refs[slots : 2 * slots], refs[2 * slots : 2 * slots + steps]
     refs = refs[2 * slots + steps :]
     more, refs = refs[:extra], refs[extra:]
     gate_out, up_out, down_out = refs[:3]
     x, dy, act, sem = refs[3:]
-    tokens, width = x_in[0].shape
+    tokens, width = dy_in[0].shape
     hidden = act.shape[1] // 3
     step_rows = act_in[0].shape[0]
     copies = []
@@ -223,9 +239,9 @@
             act.at[pl.ds(i * step_rows, step_rows)],
         )
     for i in range(slots):
-        fetch(x_in[i], x.at[pl.ds(i * tokens, tokens)])
+        fetch(xg_in[i].at[:, pl.ds(0, width)], x.at[pl.ds(i * tokens, tokens)])
     for i in range(slots):
-        fetch(dyg_in[i].at[:, pl.ds(0, width)], dy.at[pl.ds(i * tokens, tokens)])
+        fetch(dy_in[i], dy.at[pl.ds(i * tokens, tokens)])
     for c in copies[: steps + slots]:
         c.wait()
 
@@ -257,9 +273,9 @@
         put(down_out, here, value, 2)
 
 
-def weights_grads(j, xs, dygs, acts, dtype, more=()):
-    slots, steps = len(xs), len(acts)
-    tokens, width = xs[0].shape
+def weights_grads(j, xgs, dys, acts, dtype, more=()):
+    slots, steps = len(dys), len(acts)
+    tokens, width = dys[0].shape
     hidden = acts[0].shape[1] // 6
     rows = slots * tokens
     lead = (1,) if more else ()
@@ -285,7 +301,7 @@
             transcendentals=0,
         ),
         name="weights_grads",
-    )(*xs, *dygs, *acts, *more)
+    )(*xgs, *dys, *acts, *more)
 
 
 def finish_kernel(parts, ids, kept, *refs):
@@ -346,6 +362,9 @@
     def send_z(v):
         return lax.ppermute(v, "expert", [(i, moved(i, 1, 0)) for i in range(devices)])
 
+    def send_down(v):
+        return lax.ppermute(v, "expert", [(i, moved(i, -1, 0)) for i in range(devices)])
+
     def send_y(v):
         return lax.ppermute(v, "expert", [(i, moved(i, 0, 1)) for i in range(devices)])
 
@@ -353,7 +372,7 @@
         return lax.ppermute(v, "expert", [(i, i ^ 1) for i in range(devices)])
 
     ids = expert_ids.T
-    dyg, kept = plan(replica_table[None], ids, gates.T, grad_out, devices, lanes)
+    xg, kept = plan(replica_table[None], ids, gates.T, tokens_in, devices, lanes)
     own = (w_gate[0], w_up[0], w_down[0])
     weights = own + tuple(send_core(w) for w in own)
 
@@ -367,27 +386,26 @@
     def partial(j, group, dtype, more=()):
         return weights_grads(
             j,
-            [x for z in group for x in xs[z]],
-            [d for z in group for d in dygs[z]],
+            [x for z in group for x in xgs[z]],
+            [d for z in group for d in dys[z]],
             [acts[z] for z in group],
             dtype,
             more,
         )
 
-    xs, dygs = [[tokens_in]], [[dyg]]
+    xgs, dys = [[xg]], [[grad_out]]
     dxs, acts, across = [], [], []
 
     def send_across(z):
-        if inner > 1:
-            total = dxs[z][1]
-            for y in range(2, inner):
-                total = add(send_y(total), dxs[z][y])
-            across.append([send_y(total)])
-        else:
-            across.append([])
+        if inner == 1:
+            return []
+        total = dxs[z][1]
+        for y in range(2, inner):
+            total = add(send_y(total), dxs[z][y])
+        return [send_y(total)]
 
     for z in range(1, outer + 1):
-        for k, stream in enumerate((xs, dygs)):
+        for k, stream in enumerate((xgs, dys)):
             last = stream[z - 1]
             ahead = None
             if z < outer:
@@ -401,30 +419,27 @@
             if ahead is not None:
                 done.append(ahead)
             if k == 0 and z == 1:
-                done, kept, weights = together(done, hold(kept, HOLD), weights)
+                kept, weights = together(kept, weights)
+                done, kept = together(done, hold(kept, HOLD))
             elif k == 0:
-                done, dxs[z - 2], acts[z - 2] = together(done, dxs[z - 2], acts[z - 2])
+                done, acts[z - 2] = together(done, acts[z - 2])
             else:
                 (done,) = together(done)
             if ahead is not None:
                 stream.append([done.pop()])
             if inner > 1:
                 last[-1] = done.pop()
-        if z > 2:
-            send_across(z - 2)
-        *dx, act = rows_grads(xs[z - 1], dygs[z - 1], weights)
+        *dx, act = rows_grads(xgs[z - 1], dys[z - 1], weights)
         dxs.append(dx)
         acts.append(act)
+        if z > 2:
+            across.append(send_across(z - 1))
         if len(groups) > 1 and z - 1 == groups[(z - 1) // per][-1]:
             for j in range(2):
                 value = partial(j, groups[(z - 1) // per], f32)
                 sums[j] = value if z <= per else [t + v for t, v in zip(sums[j], value)]
             if z < outer:
-                sums, xs[z] = together(sums, xs[z])
-    if outer > 1:
-        send_across(outer - 1)
-        dxs[0], acts[-1] = together(dxs[0], acts[-1])
-    send_across(0)
+                sums, xgs[z] = together(sums, xgs[z])
 
     single = len(groups) == 1
     if single:
@@ -432,11 +447,17 @@
     else:
         other = [send_core(v.astype(bf16)) for v in sums[1]]
 
-    pieces = [dxs[0][0], *across[-1]]
+    pieces = []
     if outer > 1:
-        total = add(dxs[1][0], *across[0])
-        for z in range(2, outer):
-            total = add(send_z(total), dxs[z][0], *across[z - 1])
+        dxs[1], acts[-2] = together(dxs[1], acts[-2])
+        back = [send_down(v) for v in dxs[1]]
+        pieces.append(back[0])
+        dxs[0] = [dxs[0][0]] + [add(v, o) for v, o in zip(dxs[0][1:], back[1:])]
+    pieces += [dxs[0][0], *send_across(0)]
+    if outer > 2:
+        total = add(dxs[2][0], *across[0])
+        for z in range(3, outer):
+            total = add(send_z(total), dxs[z][0], *across[z - 2])
         total, other = together(total, other)
         pieces.append(send_z(total))
     if single:

time: 86.3 us -> 90.7 us (1.051)
  starting transfers between devices: 21.6 us -> 25 us
  local copies, waits for them, and re-layouts: 4.72 us -> 7.21 us
  waiting for transfers between devices: 32.4 us -> 30.4 us
    ppermute x0 -> x2, starting transfers between devices: none -> 3.59 us  [send_down(): lax.ppermute(v, 'expert', [(i, moved(i, -1, 0)) for i in range(devices)])]
    ppermute x11 -> x10, waiting for transfers between devices: 11.1 us -> 7.63 us  [send_y(): lax.ppermute(v, 'expert', [(i, moved(i, 0, 1)) for i in range(devices)])]
    unnamed x24 -> x34, local copies, waits for them, and re-layouts: 4.72 us -> 7.21 us
    ppermute x0 -> x2, waiting for transfers between devices: none -> 2.19 us  [send_down(): lax.ppermute(v, 'expert', [(i, moved(i, -1, 0)) for i in range(devices)])]
    pallas_call x1, Pallas kernels: 0.24 us -> 1.75 us  [plan(): pl.pallas_call(functools.partial(plan_kernel, home_cap, rep_cap), out_sha...]
    pallas_call x1, Pallas kernels: 1.43 us -> 0.01 us  [hold(): pl.pallas_call(lambda source, out: None, out_shape=jax.ShapeDtypeStruct(v...]
    ppermute x6, waiting for transfers between devices: 1.43 us -> 0.02 us  [send_core(): return lax.ppermute(v, 'expert', [(i, i ^ 1) for i in range(devices)])]
    ppermute x10 -> x9, waiting for transfers between devices: 19.8 us -> 20.6 us  [send_z(): lax.ppermute(v, 'expert', [(i, moved(i, 1, 0)) for i in range(devices)])]
  transfers between devices with their start and end apart: 27 -> 27, of which waited for: 16 -> 14; matrix products, arithmetic and copies ran while one was open for 0% -> 0% of each run, Pallas kernels for 29% -> 29%
where the time goes in v4:
time: 90.7 us; the launch traced here: 90.4 us
  waiting for transfers between devices  30.4 us (34%)
  Pallas kernels  26.7 us (29%)
  starting transfers between devices  25 us (28%)
  local copies, waits for them, and re-layouts  7.21 us (8%)
    ppermute x9, waiting for transfers between devices, send_z(): lax.ppermute(v, 'expert', [(i, moved(i, 1, 0)) for i in range(devices)])  20.6 us
    pallas_call x4, Pallas kernels, rows_grads(): pl.pallas_call(functools.partial(rows_kernel, slots), out_shape=tuple((ja...  16 us
    ppermute x10, starting transfers between devices, send_y(): lax.ppermute(v, 'expert', [(i, moved(i, 0, 1)) for i in range(devices)])  12.6 us
    pallas_call x2, Pallas kernels, weights_grads(): pl.pallas_call(functools.partial(weights_kernel, j, slots, steps, len(mor...  7.97 us
    ppermute x10, waiting for transfers between devices, send_y(): lax.ppermute(v, 'expert', [(i, moved(i, 0, 1)) for i in range(devices)])  7.63 us
    unnamed x34, local copies, waits for them, and re-layouts  7.21 us
    ppermute x9, starting transfers between devices, send_z(): lax.ppermute(v, 'expert', [(i, moved(i, 1, 0)) for i in range(devices)])  7.07 us
    ppermute x2, starting transfers between devices, send_down(): lax.ppermute(v, 'expert', [(i, moved(i, -1, 0)) for i in range(devices)])  3.59 us
  transfers between devices with their start and end apart: 27, of which 14 were waited for; matrix products, arithmetic and copies ran while one was open for 0% of the time, Pallas kernels for 29%

profile of v4, /device:TPU:0, one launch (start us, length us, event | category | flops | bytes accessed | tf_op | source)
XLA Modules:
  0.0 90.4 jit_solution(2675851365269608747)
XLA Ops:
  0.6 0.5 collective-permute-start.2
  1.1 0.1 collective-permute-start.3
  1.2 0.4 collective-permute-start.4
  1.7 1.7 %plan.1 = (bf16[128,1152]{1,0:T(8,128)(2,1)}, f32[16,128]{1,0:T(8,128)}) custom-call(s32[1,16]{1,0:T(1,128)} %bitcast.25, s32[8,128]{1,0:T(8,128)} %bitcast.7, bf16[8,128]{1,0:T(8,128)(2,1)} %bitcast.24, bf16[128,1024]{1,0:T(8,128)(2,1)} %x_in.1), custom_call_target="tpu_custom_call" | custom-call | tf_op jit(solution)/shard_map/plan/pallas_call | solution.py:84
  3.4 2.7 %collective-permute-start = (bf16[128,1152]{1,0:T(8,128)(2,1)}, bf16[128,1152]{1,0:T(8,128)(2,1)S(1)}, u32[]{:S(2)}, u32[]{:S(2)}) collective-permute-start(bf16[128,1152]{1,0:T(8,128)(2,1)} %get-tuple-element.65.refs_0_), channel_id=1, source_target_pairs={{0,2},{1,3},{2,0},{3,1},{4,6},{5,7},{6,4},{7,5},{8,10},{9,11},{10,... | collective-permute-start | bytes 884744 | tf_op jit(solution)/shard_map/ppermute | solution.py:369
  6.1 1.6 %collective-permute-start.1 = (bf16[128,1152]{1,0:T(8,128)(2,1)}, bf16[128,1152]{1,0:T(8,128)(2,1)S(1)}, u32[]{:S(2)}, u32[]{:S(2)}) collective-permute-start(bf16[128,1152]{1,0:T(8,128)(2,1)} %get-tuple-element.65.refs_0_), channel_id=1, source_target_pairs={{0,4},{1,5},{2,6},{3,7},{4,8},{5,9},{6,10},{7,11},{8,12},{9,13},{1... | collective-permute-start | bytes 884744 | tf_op jit(solution)/shard_map/ppermute | solution.py:363
  7.7 0.0 collective-permute-done.2.refs_7_
  7.7 0.9 copy-done.8
  8.5 0.5 collective-permute-start.7
  9.0 0.9 copy-done.11
  9.9 1.6 %collective-permute-start.8 = (bf16[128,1024]{1,0:T(8,128)(2,1)}, bf16[128,1024]{1,0:T(8,128)(2,1)S(1)}, u32[]{:S(2)}, u32[]{:S(2)}) collective-permute-start(bf16[128,1024]{1,0:T(8,128)(2,1)} %refs_8_.3), channel_id=1, source_target_pairs={{0,4},{1,5},{2,6},{3,7},{4,8},{5,9},{6,10},{7,11},{8,12},{9,13},{1... | collective-permute-start | bytes 786440 | tf_op jit(solution)/shard_map/ppermute | solution.py:363
  11.5 0.0 collective-permute-done.4.refs_9_
  11.5 0.9 copy-done.14
  12.4 1.7 %collective-permute-done.refs_1_ = bf16[128,1152]{1,0:T(8,128)(2,1)S(1)} collective-permute-done((bf16[128,1152]{1,0:T(8,128)(2,1)}, bf16[128,1152]{1,0:T(8,128)(2,1)S(1)}, u32[]{:S(2)}, u32[]{:S(2)}) %collective-permute-start) | collective-permute-done | bytes 294944 | tf_op jit(solution)/shard_map/ppermute | solution.py:369
  14.1 3.8 %collective-permute-done.1.refs_0_.refs_2_ = bf16[128,1152]{1,0:T(8,128)(2,1)S(1)} collective-permute-done((bf16[128,1152]{1,0:T(8,128)(2,1)}, bf16[128,1152]{1,0:T(8,128)(2,1)S(1)}, u32[]{:S(2)}, u32[]{:S(2)}) %collective-permute-start.1) | collective-permute-done | bytes 294944 | tf_op jit(solution)/shard_map/ppermute | solution.py:363
  17.9 0.3 collective-permute-start.5
  18.2 0.0 collective-permute-start.6
  18.2 1.4 %collective-permute-done.7.refs_3_.refs_9_ = bf16[128,1024]{1,0:T(8,128)(2,1)S(1)} collective-permute-done((bf16[128,1024]{1,0:T(8,128)(2,1)}, bf16[128,1024]{1,0:T(8,128)(2,1)S(1)}, u32[]{:S(2)}, u32[]{:S(2)}) %collective-permute-start.7) | collective-permute-done | bytes 262176 | tf_op jit(solution)/shard_map/ppermute | solution.py:369
  19.6 3.9 %collective-permute-done.8.refs_2_.refs_10_ = bf16[128,1024]{1,0:T(8,128)(2,1)S(1)} collective-permute-done((bf16[128,1024]{1,0:T(8,128)(2,1)}, bf16[128,1024]{1,0:T(8,128)(2,1)S(1)}, u32[]{:S(2)}, u32[]{:S(2)}) %collective-permute-start.8) | collective-permute-done | bytes 262176 | tf_op jit(solution)/shard_map/ppermute | solution.py:363
  23.5 0.3 collective-permute-start.9
  23.8 0.0 collective-permute-start.10
  23.9 0.0 copy-start.6
  23.9 1.1 %copy-done.6 = bf16[1,384,1024]{2,1,0:T(8,128)(2,1)S(1)} copy-done((bf16[1,384,1024]{2,1,0:T(8,128)(2,1)S(1)}, bf16[1,384,1024]{2,1,0:T(8,128)(2,1)}, u32[]{:S(2)}) %copy-start.6) | copy-done | bytes 786456
  25.0 1.1 %copy-done.9 = bf16[1024,384]{1,0:T(8,128)(2,1)S(1)} copy-done((bf16[1024,384]{1,0:T(8,128)(2,1)S(1)}, bf16[1024,384]{1,0:T(8,128)(2,1)}, u32[]{:S(2)}) %copy-start.9) | copy-done | bytes 786456
  26.1 1.1 %copy-done.12 = bf16[1024,384]{1,0:T(8,128)(2,1)S(1)} copy-done((bf16[1024,384]{1,0:T(8,128)(2,1)S(1)}, bf16[1024,384]{1,0:T(8,128)(2,1)}, u32[]{:S(2)}) %copy-start.12) | copy-done | bytes 786456
  27.3 1.1 %copy-done.15 = bf16[384,1024]{1,0:T(8,128)(2,1)S(1)} copy-done((bf16[384,1024]{1,0:T(8,128)(2,1)S(1)}, bf16[384,1024]{1,0:T(8,128)(2,1)}, u32[]{:S(2)}) %copy-start.15) | copy-done | bytes 786456
  28.4 4.0 %rows_grads.4 = (bf16[128,1152]{1,0:T(8,128)(2,1)S(1)}, bf16[128,1152]{1,0:T(8,128)(2,1)S(1)}, bf16[256,2304]{1,0:T(8,128)(2,1)S(1)}) custom-call(bf16[128,1152]{1,0:T(8,128)(2,1)S(1)} %copy-done, bf16[128,1152]{1,0:T(8,128)(2,1)S(1)} %collective-permute-done.refs_1_, bf16[128,1024]{1,0:T(8,128)(2,1)S(1)} %copy-done.1, ...), custom_call_target="tpu_custom_call" | custom-call | flops 2013265920 | bytes 9306112 | tf_op jit(solution)/shard_map/rows_grads/pallas_call | solution.py:200
  32.4 0.0 copy-start.16
  32.5 1.8 %collective-permute-start.11 = (bf16[128,1152]{1,0:T(8,128)(2,1)S(1)}, bf16[128,1152]{1,0:T(8,128)(2,1)S(1)}, u32[]{:S(2)}, u32[]{:S(2)}) collective-permute-start(bf16[128,1152]{1,0:T(8,128)(2,1)S(1)} %collective-permute-done.6.refs_0_.refs_4_), channel_id=1, source_target_pairs={{0,2},{1,3},{2,0},{3,1},{4,6},{5,7},{6,4},{7,5},{8,10},{9,11},{10,... | collective-permute-start | bytes 884744 | tf_op jit(solution)/shard_map/ppermute | solution.py:369
  34.3 1.4 %collective-permute-start.12 = (bf16[128,1152]{1,0:T(8,128)(2,1)S(1)}, bf16[128,1152]{1,0:T(8,128)(2,1)S(1)}, u32[]{:S(2)}, u32[]{:S(2)}) collective-permute-start(bf16[128,1152]{1,0:T(8,128)(2,1)S(1)} %collective-permute-done.6.refs_0_.refs_4_), channel_id=1, source_target_pairs={{0,4},{1,5},{2,6},{3,7},{4,8},{5,9},{6,10},{7,11},{8,12},{9,13},{1... | collective-permute-start | bytes 884744 | tf_op jit(solution)/shard_map/ppermute | solution.py:363
  35.6 0.5 collective-permute-start.14
  36.1 1.6 %collective-permute-start.15 = (bf16[128,1024]{1,0:T(8,128)(2,1)S(1)}, bf16[128,1024]{1,0:T(8,128)(2,1)S(1)}, u32[]{:S(2)}, u32[]{:S(2)}) collective-permute-start(bf16[128,1024]{1,0:T(8,128)(2,1)S(1)} %collective-permute-done.10.refs_2_.refs_12_), channel_id=1, source_target_pairs={{0,4},{1,5},{2,6},{3,7},{4,8},{5,9},{6,10},{7,11},{8,12},{9,13},{1... | collective-permute-start | bytes 786440 | tf_op jit(solution)/shard_map/ppermute | solution.py:363
  37.7 4.0 %rows_grads.5 = (bf16[128,1152]{1,0:T(8,128)(2,1)S(1)}, bf16[128,1152]{1,0:T(8,128)(2,1)S(1)}, bf16[256,2304]{1,0:T(8,128)(2,1)S(1)}) custom-call(bf16[128,1152]{1,0:T(8,128)(2,1)S(1)} %collective-permute-done.1.refs_0_.refs_2_, bf16[128,1152]{1,0:T(8,128)(2,1)S(1)} %collective-permute-done.5.refs_1_.refs_3_, ...), custom_call_target="tpu_custom_call" | custom-call | flops 2013265920 | bytes 9306112 | tf_op jit(solution)/shard_map/rows_grads/pallas_call | solution.py:200
  41.7 0.7 collective-permute-done.11.refs_1_.refs_5_
  42.5 3.5 %collective-permute-done.12.refs_0_.refs_6_ = bf16[128,1152]{1,0:T(8,128)(2,1)S(1)} collective-permute-done((bf16[128,1152]{1,0:T(8,128)(2,1)S(1)}, bf16[128,1152]{1,0:T(8,128)(2,1)S(1)}, u32[]{:S(2)}, u32[]{:S(2)}) %collective-permute-start.12) | collective-permute-done | bytes 294944 | tf_op jit(solution)/shard_map/ppermute | solution.py:363
  46.0 0.3 collective-permute-start.13
  46.3 1.8 %collective-permute-done.14.refs_3_.refs_13_ = bf16[128,1024]{1,0:T(8,128)(2,1)S(1)} collective-permute-done((bf16[128,1024]{1,0:T(8,128)(2,1)S(1)}, bf16[128,1024]{1,0:T(8,128)(2,1)S(1)}, u32[]{:S(2)}, u32[]{:S(2)}) %collective-permute-start.14) | collective-permute-done | bytes 262176 | tf_op jit(solution)/shard_map/ppermute | solution.py:369
  48.1 0.7 collective-permute-done.15.refs_2_.refs_14_
  48.8 0.9 collective-permute-start.21
  49.7 4.0 %rows_grads.6 = (bf16[128,1152]{1,0:T(8,128)(2,1)S(1)}, bf16[128,1152]{1,0:T(8,128)(2,1)S(1)}, bf16[256,2304]{1,0:T(8,128)(2,1)S(1)}) custom-call(bf16[128,1152]{1,0:T(8,128)(2,1)S(1)} %collective-permute-done.6.refs_0_.refs_4_, bf16[128,1152]{1,0:T(8,128)(2,1)S(1)} %collective-permute-done.11.refs_1_.refs_5_, ...), custom_call_target="tpu_custom_call" | custom-call | flops 2013265920 | bytes 9306112 | tf_op jit(solution)/shard_map/rows_grads/pallas_call | solution.py:200
  53.7 1.6 %collective-permute-start.19 = (bf16[128,1152]{1,0:T(8,128)(2,1)S(1)}, bf16[128,1152]{1,0:T(8,128)(2,1)S(1)}, u32[]{:S(2)}, u32[]{:S(2)}) collective-permute-start(bf16[128,1152]{1,0:T(8,128)(2,1)S(1)} %get-tuple-element.97), channel_id=1, source_target_pairs={{0,2},{1,3},{2,0},{3,1},{4,6},{5,7},{6,4},{7,5},{8,10},{9,11},{10,... | collective-permute-start | bytes 884744 | tf_op jit(solution)/shard_map/ppermute | solution.py:369
  55.3 3.3 %collective-permute-done.21.refs_3_.refs_15_ = bf16[128,1024]{1,0:T(8,128)(2,1)S(1)} collective-permute-done((bf16[128,1024]{1,0:T(8,128)(2,1)S(1)}, bf16[128,1024]{1,0:T(8,128)(2,1)S(1)}, u32[]{:S(2)}, u32[]{:S(2)}) %collective-permute-start.21) | collective-permute-done | bytes 262176 | tf_op jit(solution)/shard_map/ppermute | solution.py:363
  58.5 0.0 collective-permute-start.17
  58.5 4.0 %rows_grads.7 = (bf16[128,1152]{1,0:T(8,128)(2,1)S(1)}, bf16[128,1152]{1,0:T(8,128)(2,1)S(1)}, bf16[256,2304]{1,0:T(8,128)(2,1)S(1)}) custom-call(bf16[128,1152]{1,0:T(8,128)(2,1)S(1)} %collective-permute-done.12.refs_0_.refs_6_, bf16[128,1152]{1,0:T(8,128)(2,1)S(1)} %collective-permute-done.13.refs_1_.refs_7_, ...), custom_call_target="tpu_custom_call" | custom-call | flops 2013265920 | bytes 9306112 | tf_op jit(solution)/shard_map/rows_grads/pallas_call | solution.py:200
  62.6 4.7 %collective-permute-start.22 = (bf16[128,1152]{1,0:T(8,128)(2,1)S(1)}, bf16[128,1152]{1,0:T(8,128)(2,1)S(1)}, u32[]{:S(2)}, u32[]{:S(2)}) collective-permute-start(bf16[128,1152]{1,0:T(8,128)(2,1)S(1)} %get-tuple-element.101), channel_id=1, source_target_pairs={{0,2},{1,3},{2,0},{3,1},{4,6},{5,7},{6,4},{7,5},{8,10},{9,11},{10,... | collective-permute-start | bytes 884744 | tf_op jit(solution)/shard_map/ppermute | solution.py:369
  67.3 0.1 add_convert_fusion.1
  67.3 0.1 collective-permute-start.20
  67.4 3.6 %weights_grads.2 = (bf16[1024,384]{1,0:T(8,128)(2,1)S(1)}, bf16[1024,384]{1,0:T(8,128)(2,1)S(1)}, bf16[384,1024]{1,0:T(8,128)(2,1)S(1)}) custom-call(bf16[128,1152]{1,0:T(8,128)(2,1)S(1)} %copy-done, bf16[128,1152]{1,0:T(8,128)(2,1)S(1)} %collective-permute-done.refs_1_, bf16[128,1152]{1,0:T(8,128)(2,1)S(1)} %collective-permute-done.1.refs_0_.refs_2_, ...), custom_call_target="tpu_custom_call" | custom-call | flops 2415919104 | bytes 8912896 | tf_op jit(solution)/shard_map/weights_grads/pallas_call | solution.py:282
  71.0 0.1 collective-permute-start.23
  71.0 0.5 collective-permute-start.24
  71.5 0.1 collective-permute-start.25
  71.6 0.1 add_convert_fusion.2
  71.7 0.3 collective-permute-done.22
  72.0 3.6 %collective-permute-start.16 = (bf16[128,1152]{1,0:T(8,128)(2,1)S(1)}, bf16[128,1152]{1,0:T(8,128)(2,1)S(1)}, u32[]{:S(2)}, u32[]{:S(2)}) collective-permute-start(bf16[128,1152]{1,0:T(8,128)(2,1)S(1)} %get-tuple-element.92), channel_id=1, source_target_pairs={{0,12},{1,13},{2,14},{3,15},{4,0},{5,1},{6,2},{7,3},{8,4},{9,5},{1... | collective-permute-start | bytes 884744 | tf_op jit(solution)/shard_map/ppermute | solution.py:366
  75.5 0.6 collective-permute-done.20
  76.1 0.1 add_convert_fusion
  76.2 0.0 copy-start.2
  76.2 0.0 copy-start.3
  76.3 0.1 collective-permute-start.26
  76.3 4.4 %weights_grads.3 = (bf16[1,1024,384]{2,1,0:T(8,128)(2,1)}, bf16[1,1024,384]{2,1,0:T(8,128)(2,1)}, bf16[1,384,1024]{2,1,0:T(8,128)(2,1)}) custom-call(bf16[128,1152]{1,0:T(8,128)(2,1)S(1)} %copy-done, bf16[128,1152]{1,0:T(8,128)(2,1)S(1)} %collective-permute-done.refs_1_, bf16[128,1152]{1,0:T(8,128)(2,1)S(1)} %collective-permute-done.1.refs_0_.refs_2_, ...), custom_call_target="tpu_custom_call" | custom-call | flops 2415919104 | bytes 8912896 | tf_op jit(solution)/shard_map/weights_grads/pallas_call | solution.py:282
  80.8 2.2 %collective-permute-done.16.refs_0_ = bf16[128,1152]{1,0:T(8,128)(2,1)S(1)} collective-permute-done((bf16[128,1152]{1,0:T(8,128)(2,1)S(1)}, bf16[128,1152]{1,0:T(8,128)(2,1)S(1)}, u32[]{:S(2)}, u32[]{:S(2)}) %collective-permute-start.16) | collective-permute-done | bytes 294944 | tf_op jit(solution)/shard_map/ppermute | solution.py:366
  83.0 1.7 %collective-permute-done.18.refs_2_ = bf16[128,1152]{1,0:T(8,128)(2,1)S(1)} collective-permute-done((bf16[128,1152]{1,0:T(8,128)(2,1)S(1)}, bf16[128,1152]{1,0:T(8,128)(2,1)S(1)}, u32[]{:S(2)}, u32[]{:S(2)}) %collective-permute-start.18) | collective-permute-done | bytes 294944 | tf_op jit(solution)/shard_map/ppermute | solution.py:369
  84.6 4.8 %collective-permute-done.26.refs_3_ = bf16[128,1152]{1,0:T(8,128)(2,1)S(1)} collective-permute-done((bf16[128,1152]{1,0:T(8,128)(2,1)S(1)}, bf16[128,1152]{1,0:T(8,128)(2,1)S(1)}, u32[]{:S(2)}, u32[]{:S(2)}) %collective-permute-start.26) | collective-permute-done | bytes 294944 | tf_op jit(solution)/shard_map/ppermute | solution.py:363
  89.5 0.9 %finish.1 = (bf16[128,1024]{1,0:T(8,128)(2,1)}, bf16[8,128]{1,0:T(8,128)(2,1)}) custom-call(s32[8,128]{1,0:T(8,128)S(1)} %bitcast.8, f32[16,128]{1,0:T(8,128)S(1)} %copy-done.3, bf16[128,1152]{1,0:T(8,128)(2,1)S(1)} %collective-permute-done.16.refs_0_, bf16[128,1152]{1,0:T(8,128)(2,1)S(1)} %get-tuple-element.117.refs_1_, ...), custom_call_target="tpu_custom_call" | custom-call | tf_op jit(solution)/shard_map/finish/pallas_call | solution.py:329
  (36 shorter events, 0.1 us)
Async XLA Ops:
  0.6 7.0 %collective-permute-start.2 = (bf16[1024,384]{1,0:T(8,128)(2,1)}, bf16[1024,384]{1,0:T(8,128)(2,1)S(1)}, u32[]{:S(2)}, u32[]{:S(2)}) collective-permute-start(bf16[1024,384]{1,0:T(8,128)(2,1)} %bitcast.9), channel_id=1, source_target_pairs={{0,1},{1,0},{2,3},{3,2},{4,5},{5,4},{6,7},{7,6},{8,9},{9,8},{10,11... | collective-permute-start | bytes 2359304 | tf_op jit(solution)/shard_map/ppermute | solution.py:372
  1.1 7.9 %collective-permute-start.3 = (bf16[1024,384]{1,0:T(8,128)(2,1)}, bf16[1024,384]{1,0:T(8,128)(2,1)S(1)}, u32[]{:S(2)}, u32[]{:S(2)}) collective-permute-start(bf16[1024,384]{1,0:T(8,128)(2,1)} %bitcast.14), channel_id=1, source_target_pairs={{0,1},{1,0},{2,3},{3,2},{4,5},{5,4},{6,7},{7,6},{8,9},{9,8},{10,11... | collective-permute-start | bytes 2359304 | tf_op jit(solution)/shard_map/ppermute | solution.py:372
  1.2 10.3 %collective-permute-start.4 = (bf16[384,1024]{1,0:T(8,128)(2,1)}, bf16[384,1024]{1,0:T(8,128)(2,1)S(1)}, u32[]{:S(2)}, u32[]{:S(2)}) collective-permute-start(bf16[384,1024]{1,0:T(8,128)(2,1)} %bitcast.19), channel_id=1, source_target_pairs={{0,1},{1,0},{2,3},{3,2},{4,5},{5,4},{6,7},{7,6},{8,9},{9,8},{10,11... | collective-permute-start | bytes 2359304 | tf_op jit(solution)/shard_map/ppermute | solution.py:372
  3.4 10.7 %collective-permute-start = (bf16[128,1152]{1,0:T(8,128)(2,1)}, bf16[128,1152]{1,0:T(8,128)(2,1)S(1)}, u32[]{:S(2)}, u32[]{:S(2)}) collective-permute-start(bf16[128,1152]{1,0:T(8,128)(2,1)} %get-tuple-element.65.refs_0_), channel_id=1, source_target_pairs={{0,2},{1,3},{2,0},{3,1},{4,6},{5,7},{6,4},{7,5},{8,10},{9,11},{10,... | collective-permute-start | bytes 884744 | tf_op jit(solution)/shard_map/ppermute | solution.py:369
  6.1 11.8 %collective-permute-start.1 = (bf16[128,1152]{1,0:T(8,128)(2,1)}, bf16[128,1152]{1,0:T(8,128)(2,1)S(1)}, u32[]{:S(2)}, u32[]{:S(2)}) collective-permute-start(bf16[128,1152]{1,0:T(8,128)(2,1)} %get-tuple-element.65.refs_0_), channel_id=1, source_target_pairs={{0,4},{1,5},{2,6},{3,7},{4,8},{5,9},{6,10},{7,11},{8,12},{9,13},{1... | collective-permute-start | bytes 884744 | tf_op jit(solution)/shard_map/ppermute | solution.py:363
  7.7 0.9 copy-start.8
  8.5 11.1 %collective-permute-start.7 = (bf16[128,1024]{1,0:T(8,128)(2,1)}, bf16[128,1024]{1,0:T(8,128)(2,1)S(1)}, u32[]{:S(2)}, u32[]{:S(2)}) collective-permute-start(bf16[128,1024]{1,0:T(8,128)(2,1)} %refs_8_.3), channel_id=1, source_target_pairs={{0,2},{1,3},{2,0},{3,1},{4,6},{5,7},{6,4},{7,5},{8,10},{9,11},{10,... | collective-permute-start | bytes 786440 | tf_op jit(solution)/shard_map/ppermute | solution.py:369
  9.0 0.9 copy-start.11
  9.9 13.6 %collective-permute-start.8 = (bf16[128,1024]{1,0:T(8,128)(2,1)}, bf16[128,1024]{1,0:T(8,128)(2,1)S(1)}, u32[]{:S(2)}, u32[]{:S(2)}) collective-permute-start(bf16[128,1024]{1,0:T(8,128)(2,1)} %refs_8_.3), channel_id=1, source_target_pairs={{0,4},{1,5},{2,6},{3,7},{4,8},{5,9},{6,10},{7,11},{8,12},{9,13},{1... | collective-permute-start | bytes 786440 | tf_op jit(solution)/shard_map/ppermute | solution.py:363
  11.5 0.9 copy-start.14
  12.4 11.5 %copy-start = (bf16[128,1152]{1,0:T(8,128)(2,1)S(1)}, bf16[128,1152]{1,0:T(8,128)(2,1)}, u32[]{:S(2)}) copy-start(bf16[128,1152]{1,0:T(8,128)(2,1)} %get-tuple-element.65.refs_0_) | copy-start | bytes 884740
  12.4 11.5 %copy-start.1 = (bf16[128,1024]{1,0:T(8,128)(2,1)S(1)}, bf16[128,1024]{1,0:T(8,128)(2,1)}, u32[]{:S(2)}) copy-start(bf16[128,1024]{1,0:T(8,128)(2,1)} %refs_8_.3) | copy-start | bytes 786436
  12.4 11.5 %copy-start.4 = (bf16[1,1024,384]{2,1,0:T(8,128)(2,1)S(1)}, bf16[1,1024,384]{2,1,0:T(8,128)(2,1)}, u32[]{:S(2)}) copy-start(bf16[1,1024,384]{2,1,0:T(8,128)(2,1)} %param.13) | copy-start | bytes 2359300
  12.4 11.5 %copy-start.5 = (bf16[1,1024,384]{2,1,0:T(8,128)(2,1)S(1)}, bf16[1,1024,384]{2,1,0:T(8,128)(2,1)}, u32[]{:S(2)}) copy-start(bf16[1,1024,384]{2,1,0:T(8,128)(2,1)} %param.14) | copy-start | bytes 2359300
  17.9 14.5 %collective-permute-start.5 = (bf16[128,1152]{1,0:T(8,128)(2,1)S(1)}, bf16[128,1152]{1,0:T(8,128)(2,1)S(1)}, u32[]{:S(2)}, u32[]{:S(2)}) collective-permute-start(bf16[128,1152]{1,0:T(8,128)(2,1)S(1)} %collective-permute-done.1.refs_0_.refs_2_), channel_id=1, source_target_pairs={{0,2},{1,3},{2,0},{3,1},{4,6},{5,7},{6,4},{7,5},{8,10},{9,11},{10,... | collective-permute-start | bytes 884744 | tf_op jit(solution)/shard_map/ppermute | solution.py:369
  18.2 14.2 %collective-permute-start.6 = (bf16[128,1152]{1,0:T(8,128)(2,1)S(1)}, bf16[128,1152]{1,0:T(8,128)(2,1)S(1)}, u32[]{:S(2)}, u32[]{:S(2)}) collective-permute-start(bf16[128,1152]{1,0:T(8,128)(2,1)S(1)} %collective-permute-done.1.refs_0_.refs_2_), channel_id=1, source_target_pairs={{0,4},{1,5},{2,6},{3,7},{4,8},{5,9},{6,10},{7,11},{8,12},{9,13},{1... | collective-permute-start | bytes 884744 | tf_op jit(solution)/shard_map/ppermute | solution.py:363
  23.5 12.1 %collective-permute-start.9 = (bf16[128,1024]{1,0:T(8,128)(2,1)S(1)}, bf16[128,1024]{1,0:T(8,128)(2,1)S(1)}, u32[]{:S(2)}, u32[]{:S(2)}) collective-permute-start(bf16[128,1024]{1,0:T(8,128)(2,1)S(1)} %collective-permute-done.8.refs_2_.refs_10_), channel_id=1, source_target_pairs={{0,2},{1,3},{2,0},{3,1},{4,6},{5,7},{6,4},{7,5},{8,10},{9,11},{10,... | collective-permute-start | bytes 786440 | tf_op jit(solution)/shard_map/ppermute | solution.py:369
  23.8 11.8 %collective-permute-start.10 = (bf16[128,1024]{1,0:T(8,128)(2,1)S(1)}, bf16[128,1024]{1,0:T(8,128)(2,1)S(1)}, u32[]{:S(2)}, u32[]{:S(2)}) collective-permute-start(bf16[128,1024]{1,0:T(8,128)(2,1)S(1)} %collective-permute-done.8.refs_2_.refs_10_), channel_id=1, source_target_pairs={{0,4},{1,5},{2,6},{3,7},{4,8},{5,9},{6,10},{7,11},{8,12},{9,13},{1... | collective-permute-start | bytes 786440 | tf_op jit(solution)/shard_map/ppermute | solution.py:363
  23.9 1.1 %copy-start.6 = (bf16[1,384,1024]{2,1,0:T(8,128)(2,1)S(1)}, bf16[1,384,1024]{2,1,0:T(8,128)(2,1)}, u32[]{:S(2)}) copy-start(bf16[1,384,1024]{2,1,0:T(8,128)(2,1)} %param.15) | copy-start | bytes 2359300
  25.0 1.1 %copy-start.9 = (bf16[1024,384]{1,0:T(8,128)(2,1)S(1)}, bf16[1024,384]{1,0:T(8,128)(2,1)}, u32[]{:S(2)}) copy-start(bf16[1024,384]{1,0:T(8,128)(2,1)} %copy-done.8) | copy-start | bytes 2359300
  26.1 1.1 %copy-start.12 = (bf16[1024,384]{1,0:T(8,128)(2,1)S(1)}, bf16[1024,384]{1,0:T(8,128)(2,1)}, u32[]{:S(2)}) copy-start(bf16[1024,384]{1,0:T(8,128)(2,1)} %copy-done.11) | copy-start | bytes 2359300
  27.3 1.1 %copy-start.15 = (bf16[384,1024]{1,0:T(8,128)(2,1)S(1)}, bf16[384,1024]{1,0:T(8,128)(2,1)}, u32[]{:S(2)}) copy-start(bf16[384,1024]{1,0:T(8,128)(2,1)} %copy-done.14) | copy-start | bytes 2359300
  28.4 9.3 %copy-start.7 = (bf16[1,384,1024]{2,1,0:T(8,128)(2,1)S(1)}, bf16[1,384,1024]{2,1,0:T(8,128)(2,1)}, u32[]{:S(2)}) copy-start(bf16[1,384,1024]{2,1,0:T(8,128)(2,1)} %param.15) | copy-start | bytes 2359300
  28.4 9.3 %copy-start.10 = (bf16[1024,384]{1,0:T(8,128)(2,1)S(1)}, bf16[1024,384]{1,0:T(8,128)(2,1)}, u32[]{:S(2)}) copy-start(bf16[1024,384]{1,0:T(8,128)(2,1)} %copy-done.8) | copy-start | bytes 2359300
  28.4 9.3 %copy-start.13 = (bf16[1024,384]{1,0:T(8,128)(2,1)S(1)}, bf16[1024,384]{1,0:T(8,128)(2,1)}, u32[]{:S(2)}) copy-start(bf16[1024,384]{1,0:T(8,128)(2,1)} %copy-done.11) | copy-start | bytes 2359300
  32.4 17.2 %copy-start.16 = (bf16[384,1024]{1,0:T(8,128)(2,1)S(1)}, bf16[384,1024]{1,0:T(8,128)(2,1)}, u32[]{:S(2)}) copy-start(bf16[384,1024]{1,0:T(8,128)(2,1)} %copy-done.14) | copy-start | bytes 2359300
  32.5 10.0 %collective-permute-start.11 = (bf16[128,1152]{1,0:T(8,128)(2,1)S(1)}, bf16[128,1152]{1,0:T(8,128)(2,1)S(1)}, u32[]{:S(2)}, u32[]{:S(2)}) collective-permute-start(bf16[128,1152]{1,0:T(8,128)(2,1)S(1)} %collective-permute-done.6.refs_0_.refs_4_), channel_id=1, source_target_pairs={{0,2},{1,3},{2,0},{3,1},{4,6},{5,7},{6,4},{7,5},{8,10},{9,11},{10,... | collective-permute-start | bytes 884744 | tf_op jit(solution)/shard_map/ppermute | solution.py:369
  34.3 11.7 %collective-permute-start.12 = (bf16[128,1152]{1,0:T(8,128)(2,1)S(1)}, bf16[128,1152]{1,0:T(8,128)(2,1)S(1)}, u32[]{:S(2)}, u32[]{:S(2)}) collective-permute-start(bf16[128,1152]{1,0:T(8,128)(2,1)S(1)} %collective-permute-done.6.refs_0_.refs_4_), channel_id=1, source_target_pairs={{0,4},{1,5},{2,6},{3,7},{4,8},{5,9},{6,10},{7,11},{8,12},{9,13},{1... | collective-permute-start | bytes 884744 | tf_op jit(solution)/shard_map/ppermute | solution.py:363
  35.6 12.5 %collective-permute-start.14 = (bf16[128,1024]{1,0:T(8,128)(2,1)S(1)}, bf16[128,1024]{1,0:T(8,128)(2,1)S(1)}, u32[]{:S(2)}, u32[]{:S(2)}) collective-permute-start(bf16[128,1024]{1,0:T(8,128)(2,1)S(1)} %collective-permute-done.10.refs_2_.refs_12_), channel_id=1, source_target_pairs={{0,2},{1,3},{2,0},{3,1},{4,6},{5,7},{6,4},{7,5},{8,10},{9,11},{10,... | collective-permute-start | bytes 786440 | tf_op jit(solution)/shard_map/ppermute | solution.py:369
  36.1 12.7 %collective-permute-start.15 = (bf16[128,1024]{1,0:T(8,128)(2,1)S(1)}, bf16[128,1024]{1,0:T(8,128)(2,1)S(1)}, u32[]{:S(2)}, u32[]{:S(2)}) collective-permute-start(bf16[128,1024]{1,0:T(8,128)(2,1)S(1)} %collective-permute-done.10.refs_2_.refs_12_), channel_id=1, source_target_pairs={{0,4},{1,5},{2,6},{3,7},{4,8},{5,9},{6,10},{7,11},{8,12},{9,13},{1... | collective-permute-start | bytes 786440 | tf_op jit(solution)/shard_map/ppermute | solution.py:363
  46.0 12.5 %collective-permute-start.13 = (bf16[128,1152]{1,0:T(8,128)(2,1)S(1)}, bf16[128,1152]{1,0:T(8,128)(2,1)S(1)}, u32[]{:S(2)}, u32[]{:S(2)}) collective-permute-start(bf16[128,1152]{1,0:T(8,128)(2,1)S(1)} %collective-permute-done.12.refs_0_.refs_6_), channel_id=1, source_target_pairs={{0,2},{1,3},{2,0},{3,1},{4,6},{5,7},{6,4},{7,5},{8,10},{9,11},{10,... | collective-permute-start | bytes 884744 | tf_op jit(solution)/shard_map/ppermute | solution.py:369
  48.8 9.7 %collective-permute-start.21 = (bf16[128,1024]{1,0:T(8,128)(2,1)S(1)}, bf16[128,1024]{1,0:T(8,128)(2,1)S(1)}, u32[]{:S(2)}, u32[]{:S(2)}) collective-permute-start(bf16[128,1024]{1,0:T(8,128)(2,1)S(1)} %collective-permute-done.14.refs_3_.refs_13_), channel_id=1, source_target_pairs={{0,4},{1,5},{2,6},{3,7},{4,8},{5,9},{6,10},{7,11},{8,12},{9,13},{1... | collective-permute-start | bytes 786440 | tf_op jit(solution)/shard_map/ppermute | solution.py:363
  53.7 13.6 %collective-permute-start.19 = (bf16[128,1152]{1,0:T(8,128)(2,1)S(1)}, bf16[128,1152]{1,0:T(8,128)(2,1)S(1)}, u32[]{:S(2)}, u32[]{:S(2)}) collective-permute-start(bf16[128,1152]{1,0:T(8,128)(2,1)S(1)} %get-tuple-element.97), channel_id=1, source_target_pairs={{0,2},{1,3},{2,0},{3,1},{4,6},{5,7},{6,4},{7,5},{8,10},{9,11},{10,... | collective-permute-start | bytes 884744 | tf_op jit(solution)/shard_map/ppermute | solution.py:369
  58.5 13.0 %collective-permute-start.17 = (bf16[128,1152]{1,0:T(8,128)(2,1)S(1)}, bf16[128,1152]{1,0:T(8,128)(2,1)S(1)}, u32[]{:S(2)}, u32[]{:S(2)}) collective-permute-start(bf16[128,1152]{1,0:T(8,128)(2,1)S(1)} %get-tuple-element.95), channel_id=1, source_target_pairs={{0,12},{1,13},{2,14},{3,15},{4,0},{5,1},{6,2},{7,3},{8,4},{9,5},{1... | collective-permute-start | bytes 884744 | tf_op jit(solution)/shard_map/ppermute | solution.py:366
  62.6 9.4 %collective-permute-start.22 = (bf16[128,1152]{1,0:T(8,128)(2,1)S(1)}, bf16[128,1152]{1,0:T(8,128)(2,1)S(1)}, u32[]{:S(2)}, u32[]{:S(2)}) collective-permute-start(bf16[128,1152]{1,0:T(8,128)(2,1)S(1)} %get-tuple-element.101), channel_id=1, source_target_pairs={{0,2},{1,3},{2,0},{3,1},{4,6},{5,7},{6,4},{7,5},{8,10},{9,11},{10,... | collective-permute-start | bytes 884744 | tf_op jit(solution)/shard_map/ppermute | solution.py:369
  67.3 8.8 %collective-permute-start.20 = (bf16[128,1152]{1,0:T(8,128)(2,1)S(1)}, bf16[128,1152]{1,0:T(8,128)(2,1)S(1)}, u32[]{:S(2)}, u32[]{:S(2)}) collective-permute-start(bf16[128,1152]{1,0:T(8,128)(2,1)S(1)} %add_convert_fusion.1), channel_id=1, source_target_pairs={{0,4},{1,5},{2,6},{3,7},{4,8},{5,9},{6,10},{7,11},{8,12},{9,13},{1... | collective-permute-start | bytes 884744 | tf_op jit(solution)/shard_map/ppermute | solution.py:363
  71.0 5.3 %collective-permute-start.23 = (bf16[1024,384]{1,0:T(8,128)(2,1)S(1)}, bf16[1024,384]{1,0:T(8,128)(2,1)S(1)}, u32[]{:S(2)}, u32[]{:S(2)}) collective-permute-start(bf16[1024,384]{1,0:T(8,128)(2,1)S(1)} %get-tuple-element.105), channel_id=1, source_target_pairs={{0,1},{1,0},{2,3},{3,2},{4,5},{5,4},{6,7},{7,6},{8,9},{9,8},{10,11... | collective-permute-start | bytes 2359304 | tf_op jit(solution)/shard_map/ppermute | solution.py:372
  71.0 5.2 %collective-permute-start.24 = (bf16[1024,384]{1,0:T(8,128)(2,1)S(1)}, bf16[1024,384]{1,0:T(8,128)(2,1)S(1)}, u32[]{:S(2)}, u32[]{:S(2)}) collective-permute-start(bf16[1024,384]{1,0:T(8,128)(2,1)S(1)} %get-tuple-element.106), channel_id=1, source_target_pairs={{0,1},{1,0},{2,3},{3,2},{4,5},{5,4},{6,7},{7,6},{8,9},{9,8},{10,11... | collective-permute-start | bytes 2359304 | tf_op jit(solution)/shard_map/ppermute | solution.py:372
  71.5 4.7 %collective-permute-start.25 = (bf16[384,1024]{1,0:T(8,128)(2,1)S(1)}, bf16[384,1024]{1,0:T(8,128)(2,1)S(1)}, u32[]{:S(2)}, u32[]{:S(2)}) collective-permute-start(bf16[384,1024]{1,0:T(8,128)(2,1)S(1)} %get-tuple-element.107), channel_id=1, source_target_pairs={{0,1},{1,0},{2,3},{3,2},{4,5},{5,4},{6,7},{7,6},{8,9},{9,8},{10,11... | collective-permute-start | bytes 2359304 | tf_op jit(solution)/shard_map/ppermute | solution.py:372
  72.0 11.0 %collective-permute-start.16 = (bf16[128,1152]{1,0:T(8,128)(2,1)S(1)}, bf16[128,1152]{1,0:T(8,128)(2,1)S(1)}, u32[]{:S(2)}, u32[]{:S(2)}) collective-permute-start(bf16[128,1152]{1,0:T(8,128)(2,1)S(1)} %get-tuple-element.92), channel_id=1, source_target_pairs={{0,12},{1,13},{2,14},{3,15},{4,0},{5,1},{6,2},{7,3},{8,4},{9,5},{1... | collective-permute-start | bytes 884744 | tf_op jit(solution)/shard_map/ppermute | solution.py:366
  76.1 8.5 %collective-permute-start.18 = (bf16[128,1152]{1,0:T(8,128)(2,1)S(1)}, bf16[128,1152]{1,0:T(8,128)(2,1)S(1)}, u32[]{:S(2)}, u32[]{:S(2)}) collective-permute-start(bf16[128,1152]{1,0:T(8,128)(2,1)S(1)} %add_convert_fusion.2), channel_id=1, source_target_pairs={{0,2},{1,3},{2,0},{3,1},{4,6},{5,7},{6,4},{7,5},{8,10},{9,11},{10,... | collective-permute-start | bytes 884744 | tf_op jit(solution)/shard_map/ppermute | solution.py:369
  76.2 13.2 %copy-start.2 = (s32[128,8]{0,1:T(8,128)S(1)}, s32[128,8]{0,1:T(8,128)}, u32[]{:S(2)}) copy-start(s32[128,8]{0,1:T(8,128)} %param.11) | copy-start | bytes 12292
  76.2 13.2 %copy-start.3 = (f32[16,128]{1,0:T(8,128)S(1)}, f32[16,128]{1,0:T(8,128)}, u32[]{:S(2)}) copy-start(f32[16,128]{1,0:T(8,128)} %hold.1.kept) | copy-start | bytes 24580
  76.3 13.2 %collective-permute-start.26 = (bf16[128,1152]{1,0:T(8,128)(2,1)S(1)}, bf16[128,1152]{1,0:T(8,128)(2,1)S(1)}, u32[]{:S(2)}, u32[]{:S(2)}) collective-permute-start(bf16[128,1152]{1,0:T(8,128)(2,1)S(1)} %add_convert_fusion), channel_id=1, source_target_pairs={{0,4},{1,5},{2,6},{3,7},{4,8},{5,9},{6,10},{7,11},{8,12},{9,13},{1... | collective-permute-start | bytes 884744 | tf_op jit(solution)/shard_map/ppermute | solution.py:363

commit v5 on v4

--- a/solution.py
+++ b/solution.py
@@ -371,13 +371,14 @@
     def send_core(v):
         return lax.ppermute(v, "expert", [(i, i ^ 1) for i in range(devices)])
 
+    def together(*values):
+        return lax.optimization_barrier(values)
+
     ids = expert_ids.T
     xg, kept = plan(replica_table[None], ids, gates.T, tokens_in, devices, lanes)
     own = (w_gate[0], w_up[0], w_down[0])
+    own, kept = together(own, kept)
     weights = own + tuple(send_core(w) for w in own)
-
-    def together(*values):
-        return lax.optimization_barrier(values)
 
     per = max(1, W_ROWS // (inner * tokens))
     groups = [range(z, min(outer, z + per)) for z in range(0, outer, per)]
@@ -415,9 +416,9 @@
                     last.append(send_z(stream[z - 2][y]))
                 else:
                     last.append(send_y(last[y - 1]))
-            done = [last[-1]] if inner > 1 else []
-            if ahead is not None:
-                done.append(ahead)
+            done = [] if ahead is None else [ahead]
+            if inner > 1:
+                done.append(last[-1])
             if k == 0 and z == 1:
                 kept, weights = together(kept, weights)
                 done, kept = together(done, hold(kept, HOLD))
@@ -425,10 +426,10 @@
                 done, acts[z - 2] = together(done, acts[z - 2])
             else:
                 (done,) = together(done)
+            if inner > 1:
+                last[-1] = done.pop()
             if ahead is not None:
                 stream.append([done.pop()])
-            if inner > 1:
-                last[-1] = done.pop()
         *dx, act = rows_grads(xgs[z - 1], dys[z - 1], weights)
         dxs.append(dx)
         acts.append(act)

time: 90.7 us -> 90.4 us (level)
    ppermute x9, starting transfers between devices: 7.07 us -> 10.9 us  [send_z(): lax.ppermute(v, 'expert', [(i, moved(i, 1, 0)) for i in range(devices)])]
    ppermute x10, waiting for transfers between devices: 7.63 us -> 4.35 us  [send_y(): lax.ppermute(v, 'expert', [(i, moved(i, 0, 1)) for i in range(devices)])]
    ppermute x9, waiting for transfers between devices: 20.6 us -> 23.7 us  [send_z(): lax.ppermute(v, 'expert', [(i, moved(i, 1, 0)) for i in range(devices)])]
    ppermute x10, starting transfers between devices: 12.6 us -> 10.2 us  [send_y(): lax.ppermute(v, 'expert', [(i, moved(i, 0, 1)) for i in range(devices)])]
    ppermute x2, starting transfers between devices: 3.59 us -> 2.67 us  [send_down(): lax.ppermute(v, 'expert', [(i, moved(i, -1, 0)) for i in range(devices)])]
    unnamed x34 -> x28, local copies, waits for them, and re-layouts: 7.21 us -> 7.2 us
  transfers between devices with their start and end apart: 27 -> 27, of which waited for: 14 -> 10; matrix products, arithmetic and copies ran while one was open for 0% -> 0% of each run, Pallas kernels for 29% -> 27%
where the time goes in v5:
time: 90.4 us; the launch traced here: 90.1 us
  waiting for transfers between devices  29.7 us (33%)
  Pallas kernels  26.7 us (30%)
  starting transfers between devices  25.5 us (28%)
  local copies, waits for them, and re-layouts  7.2 us (8%)
    ppermute x9, waiting for transfers between devices, send_z(): lax.ppermute(v, 'expert', [(i, moved(i, 1, 0)) for i in range(devices)])  23.7 us
    pallas_call x4, Pallas kernels, rows_grads(): pl.pallas_call(functools.partial(rows_kernel, slots), out_shape=tuple((ja...  16 us
    ppermute x9, starting transfers between devices, send_z(): lax.ppermute(v, 'expert', [(i, moved(i, 1, 0)) for i in range(devices)])  10.9 us
    ppermute x10, starting transfers between devices, send_y(): lax.ppermute(v, 'expert', [(i, moved(i, 0, 1)) for i in range(devices)])  10.2 us
    pallas_call x2, Pallas kernels, weights_grads(): pl.pallas_call(functools.partial(weights_kernel, j, slots, steps, len(mor...  7.95 us
    unnamed x28, local copies, waits for them, and re-layouts  7.2 us
    ppermute x10, waiting for transfers between devices, send_y(): lax.ppermute(v, 'expert', [(i, moved(i, 0, 1)) for i in range(devices)])  4.35 us
    ppermute x2, starting transfers between devices, send_down(): lax.ppermute(v, 'expert', [(i, moved(i, -1, 0)) for i in range(devices)])  2.67 us
  transfers between devices with their start and end apart: 27, of which 10 were waited for; matrix products, arithmetic and copies ran while one was open for 0% of the time, Pallas kernels for 27%

profile of v5, /device:TPU:0, one launch (start us, length us, event | category | flops | bytes accessed | tf_op | source)
XLA Modules:
  0.0 90.1 jit_solution(6393866830074811959)
XLA Ops:
  0.6 1.7 %plan.1 = (bf16[128,1152]{1,0:T(8,128)(2,1)}, f32[16,128]{1,0:T(8,128)}) custom-call(s32[1,16]{1,0:T(1,128)} %bitcast.25, s32[8,128]{1,0:T(8,128)} %bitcast.7, bf16[8,128]{1,0:T(8,128)(2,1)} %bitcast.24, bf16[128,1024]{1,0:T(8,128)(2,1)} %x_in.1), custom_call_target="tpu_custom_call" | custom-call | tf_op jit(solution)/shard_map/plan/pallas_call | solution.py:84
  2.4 0.5 collective-permute-start.2
  2.9 0.1 collective-permute-start.3
  3.0 0.4 collective-permute-start.4
  3.4 2.7 %collective-permute-start = (bf16[128,1152]{1,0:T(8,128)(2,1)}, bf16[128,1152]{1,0:T(8,128)(2,1)S(1)}, u32[]{:S(2)}, u32[]{:S(2)}) collective-permute-start(bf16[128,1152]{1,0:T(8,128)(2,1)} %get-tuple-element.69.refs_0_), channel_id=1, source_target_pairs={{0,4},{1,5},{2,6},{3,7},{4,8},{5,9},{6,10},{7,11},{8,12},{9,13},{1... | collective-permute-start | bytes 884744 | tf_op jit(solution)/shard_map/ppermute | solution.py:363
  6.1 1.5 %collective-permute-start.1 = (bf16[128,1152]{1,0:T(8,128)(2,1)}, bf16[128,1152]{1,0:T(8,128)(2,1)S(1)}, u32[]{:S(2)}, u32[]{:S(2)}) collective-permute-start(bf16[128,1152]{1,0:T(8,128)(2,1)} %get-tuple-element.69.refs_0_), channel_id=1, source_target_pairs={{0,2},{1,3},{2,0},{3,1},{4,6},{5,7},{6,4},{7,5},{8,10},{9,11},{10,... | collective-permute-start | bytes 884744 | tf_op jit(solution)/shard_map/ppermute | solution.py:369
  7.6 0.0 collective-permute-done.2.refs_7_
  7.7 0.9 copy-done.8
  8.5 1.6 %collective-permute-start.7 = (bf16[128,1024]{1,0:T(8,128)(2,1)}, bf16[128,1024]{1,0:T(8,128)(2,1)S(1)}, u32[]{:S(2)}, u32[]{:S(2)}) collective-permute-start(bf16[128,1024]{1,0:T(8,128)(2,1)} %refs_8_.3), channel_id=1, source_target_pairs={{0,4},{1,5},{2,6},{3,7},{4,8},{5,9},{6,10},{7,11},{8,12},{9,13},{1... | collective-permute-start | bytes 786440 | tf_op jit(solution)/shard_map/ppermute | solution.py:363
  10.1 0.0 collective-permute-done.3.refs_8_
  10.1 0.9 copy-done.10
  11.0 0.5 collective-permute-start.8
  11.5 0.9 copy-done.12
  12.4 3.8 %collective-permute-done.refs_0_.refs_2_ = bf16[128,1152]{1,0:T(8,128)(2,1)S(1)} collective-permute-done((bf16[128,1152]{1,0:T(8,128)(2,1)}, bf16[128,1152]{1,0:T(8,128)(2,1)S(1)}, u32[]{:S(2)}, u32[]{:S(2)}) %collective-permute-start) | collective-permute-done | bytes 294944 | tf_op jit(solution)/shard_map/ppermute | solution.py:363
  16.2 1.5 %collective-permute-start.5 = (bf16[128,1152]{1,0:T(8,128)(2,1)S(1)}, bf16[128,1152]{1,0:T(8,128)(2,1)S(1)}, u32[]{:S(2)}, u32[]{:S(2)}) collective-permute-start(bf16[128,1152]{1,0:T(8,128)(2,1)S(1)} %collective-permute-done.refs_0_.refs_2_), channel_id=1, source_target_pairs={{0,4},{1,5},{2,6},{3,7},{4,8},{5,9},{6,10},{7,11},{8,12},{9,13},{1... | collective-permute-start | bytes 884744 | tf_op jit(solution)/shard_map/ppermute | solution.py:363
  17.8 1.5 %collective-permute-start.6 = (bf16[128,1152]{1,0:T(8,128)(2,1)S(1)}, bf16[128,1152]{1,0:T(8,128)(2,1)S(1)}, u32[]{:S(2)}, u32[]{:S(2)}) collective-permute-start(bf16[128,1152]{1,0:T(8,128)(2,1)S(1)} %collective-permute-done.refs_0_.refs_2_), channel_id=1, source_target_pairs={{0,2},{1,3},{2,0},{3,1},{4,6},{5,7},{6,4},{7,5},{8,10},{9,11},{10,... | collective-permute-start | bytes 884744 | tf_op jit(solution)/shard_map/ppermute | solution.py:369
  19.3 2.6 %collective-permute-done.7.refs_2_.refs_10_ = bf16[128,1024]{1,0:T(8,128)(2,1)S(1)} collective-permute-done((bf16[128,1024]{1,0:T(8,128)(2,1)}, bf16[128,1024]{1,0:T(8,128)(2,1)S(1)}, u32[]{:S(2)}, u32[]{:S(2)}) %collective-permute-start.7) | collective-permute-done | bytes 262176 | tf_op jit(solution)/shard_map/ppermute | solution.py:363
  21.8 0.0 collective-permute-done.8.refs_3_.refs_9_
  21.9 1.5 %collective-permute-start.9 = (bf16[128,1024]{1,0:T(8,128)(2,1)S(1)}, bf16[128,1024]{1,0:T(8,128)(2,1)S(1)}, u32[]{:S(2)}, u32[]{:S(2)}) collective-permute-start(bf16[128,1024]{1,0:T(8,128)(2,1)S(1)} %collective-permute-done.7.refs_2_.refs_10_), channel_id=1, source_target_pairs={{0,4},{1,5},{2,6},{3,7},{4,8},{5,9},{6,10},{7,11},{8,12},{9,13},{1... | collective-permute-start | bytes 786440 | tf_op jit(solution)/shard_map/ppermute | solution.py:363
  23.4 1.5 %collective-permute-start.10 = (bf16[128,1024]{1,0:T(8,128)(2,1)S(1)}, bf16[128,1024]{1,0:T(8,128)(2,1)S(1)}, u32[]{:S(2)}, u32[]{:S(2)}) collective-permute-start(bf16[128,1024]{1,0:T(8,128)(2,1)S(1)} %collective-permute-done.7.refs_2_.refs_10_), channel_id=1, source_target_pairs={{0,2},{1,3},{2,0},{3,1},{4,6},{5,7},{6,4},{7,5},{8,10},{9,11},{10,... | collective-permute-start | bytes 786440 | tf_op jit(solution)/shard_map/ppermute | solution.py:369
  24.9 0.0 copy-start.6
  24.9 1.1 %copy-done.6 = bf16[1,384,1024]{2,1,0:T(8,128)(2,1)S(1)} copy-done((bf16[1,384,1024]{2,1,0:T(8,128)(2,1)S(1)}, bf16[1,384,1024]{2,1,0:T(8,128)(2,1)}, u32[]{:S(2)}) %copy-start.6) | copy-done | bytes 786456
  26.1 1.1 %copy-done.9 = bf16[1024,384]{1,0:T(8,128)(2,1)S(1)} copy-done((bf16[1024,384]{1,0:T(8,128)(2,1)S(1)}, bf16[1024,384]{1,0:T(8,128)(2,1)}, u32[]{:S(2)}) %copy-start.9) | copy-done | bytes 786456
  27.2 1.1 %copy-done.11 = bf16[1024,384]{1,0:T(8,128)(2,1)S(1)} copy-done((bf16[1024,384]{1,0:T(8,128)(2,1)S(1)}, bf16[1024,384]{1,0:T(8,128)(2,1)}, u32[]{:S(2)}) %copy-start.11) | copy-done | bytes 786456
  28.3 1.1 %copy-done.13 = bf16[384,1024]{1,0:T(8,128)(2,1)S(1)} copy-done((bf16[384,1024]{1,0:T(8,128)(2,1)S(1)}, bf16[384,1024]{1,0:T(8,128)(2,1)}, u32[]{:S(2)}) %copy-start.13) | copy-done | bytes 786456
  29.5 4.0 %rows_grads.4 = (bf16[128,1152]{1,0:T(8,128)(2,1)S(1)}, bf16[128,1152]{1,0:T(8,128)(2,1)S(1)}, bf16[256,2304]{1,0:T(8,128)(2,1)S(1)}) custom-call(bf16[128,1152]{1,0:T(8,128)(2,1)S(1)} %copy-done, bf16[128,1152]{1,0:T(8,128)(2,1)S(1)} %collective-permute-done.1.refs_1_, bf16[128,1024]{1,0:T(8,128)(2,1)S(1)} %copy-done.1, ...), custom_call_target="tpu_custom_call" | custom-call | flops 2013265920 | bytes 9306112 | tf_op jit(solution)/shard_map/rows_grads/pallas_call | solution.py:200
  33.5 0.0 collective-permute-done.6.refs_1_.refs_3_
  33.5 1.6 %collective-permute-start.11 = (bf16[128,1152]{1,0:T(8,128)(2,1)S(1)}, bf16[128,1152]{1,0:T(8,128)(2,1)S(1)}, u32[]{:S(2)}, u32[]{:S(2)}) collective-permute-start(bf16[128,1152]{1,0:T(8,128)(2,1)S(1)} %collective-permute-done.5.refs_0_.refs_4_), channel_id=1, source_target_pairs={{0,4},{1,5},{2,6},{3,7},{4,8},{5,9},{6,10},{7,11},{8,12},{9,13},{1... | collective-permute-start | bytes 884744 | tf_op jit(solution)/shard_map/ppermute | solution.py:363
  35.1 0.5 collective-permute-start.12
  35.6 0.0 collective-permute-done.9.refs_2_.refs_12_
  35.6 0.1 collective-permute-start.14
  35.7 1.6 %collective-permute-start.15 = (bf16[128,1024]{1,0:T(8,128)(2,1)S(1)}, bf16[128,1024]{1,0:T(8,128)(2,1)S(1)}, u32[]{:S(2)}, u32[]{:S(2)}) collective-permute-start(bf16[128,1024]{1,0:T(8,128)(2,1)S(1)} %collective-permute-done.9.refs_2_.refs_12_), channel_id=1, source_target_pairs={{0,2},{1,3},{2,0},{3,1},{4,6},{5,7},{6,4},{7,5},{8,10},{9,11},{10,... | collective-permute-start | bytes 786440 | tf_op jit(solution)/shard_map/ppermute | solution.py:369
  37.4 4.0 %rows_grads.5 = (bf16[128,1152]{1,0:T(8,128)(2,1)S(1)}, bf16[128,1152]{1,0:T(8,128)(2,1)S(1)}, bf16[256,2304]{1,0:T(8,128)(2,1)S(1)}) custom-call(bf16[128,1152]{1,0:T(8,128)(2,1)S(1)} %collective-permute-done.refs_0_.refs_2_, bf16[128,1152]{1,0:T(8,128)(2,1)S(1)} %collective-permute-done.6.refs_1_.refs_3_, ...), custom_call_target="tpu_custom_call" | custom-call | flops 2013265920 | bytes 9306112 | tf_op jit(solution)/shard_map/rows_grads/pallas_call | solution.py:200
  41.4 3.7 %collective-permute-done.11.refs_0_.refs_6_ = bf16[128,1152]{1,0:T(8,128)(2,1)S(1)} collective-permute-done((bf16[128,1152]{1,0:T(8,128)(2,1)S(1)}, bf16[128,1152]{1,0:T(8,128)(2,1)S(1)}, u32[]{:S(2)}, u32[]{:S(2)}) %collective-permute-start.11) | collective-permute-done | bytes 294944 | tf_op jit(solution)/shard_map/ppermute | solution.py:363
  45.1 0.5 collective-permute-start.13
  45.6 2.3 %collective-permute-done.14.refs_2_.refs_14_ = bf16[128,1024]{1,0:T(8,128)(2,1)S(1)} collective-permute-done((bf16[128,1024]{1,0:T(8,128)(2,1)S(1)}, bf16[128,1024]{1,0:T(8,128)(2,1)S(1)}, u32[]{:S(2)}, u32[]{:S(2)}) %collective-permute-start.14) | collective-permute-done | bytes 262176 | tf_op jit(solution)/shard_map/ppermute | solution.py:363
  47.9 2.7 %collective-permute-done.15.refs_3_.refs_13_ = bf16[128,1024]{1,0:T(8,128)(2,1)S(1)} collective-permute-done((bf16[128,1024]{1,0:T(8,128)(2,1)S(1)}, bf16[128,1024]{1,0:T(8,128)(2,1)S(1)}, u32[]{:S(2)}, u32[]{:S(2)}) %collective-permute-start.15) | collective-permute-done | bytes 262176 | tf_op jit(solution)/shard_map/ppermute | solution.py:369
  50.5 0.4 collective-permute-start.21
  50.9 4.0 %rows_grads.6 = (bf16[128,1152]{1,0:T(8,128)(2,1)S(1)}, bf16[128,1152]{1,0:T(8,128)(2,1)S(1)}, bf16[256,2304]{1,0:T(8,128)(2,1)S(1)}) custom-call(bf16[128,1152]{1,0:T(8,128)(2,1)S(1)} %collective-permute-done.5.refs_0_.refs_4_, bf16[128,1152]{1,0:T(8,128)(2,1)S(1)} %collective-permute-done.12.refs_1_.refs_5_, ...), custom_call_target="tpu_custom_call" | custom-call | flops 2013265920 | bytes 9306112 | tf_op jit(solution)/shard_map/rows_grads/pallas_call | solution.py:200
  54.9 0.4 collective-permute-start.19
  55.4 6.1 %collective-permute-done.21.refs_3_.refs_15_ = bf16[128,1024]{1,0:T(8,128)(2,1)S(1)} collective-permute-done((bf16[128,1024]{1,0:T(8,128)(2,1)S(1)}, bf16[128,1024]{1,0:T(8,128)(2,1)S(1)}, u32[]{:S(2)}, u32[]{:S(2)}) %collective-permute-start.21) | collective-permute-done | bytes 262176 | tf_op jit(solution)/shard_map/ppermute | solution.py:363
  61.4 0.0 collective-permute-start.17
  61.4 4.0 %rows_grads.7 = (bf16[128,1152]{1,0:T(8,128)(2,1)S(1)}, bf16[128,1152]{1,0:T(8,128)(2,1)S(1)}, bf16[256,2304]{1,0:T(8,128)(2,1)S(1)}) custom-call(bf16[128,1152]{1,0:T(8,128)(2,1)S(1)} %collective-permute-done.11.refs_0_.refs_6_, bf16[128,1152]{1,0:T(8,128)(2,1)S(1)} %collective-permute-done.13.refs_1_.refs_7_, ...), custom_call_target="tpu_custom_call" | custom-call | flops 2013265920 | bytes 9306112 | tf_op jit(solution)/shard_map/rows_grads/pallas_call | solution.py:200
  65.5 1.5 %collective-permute-start.22 = (bf16[128,1152]{1,0:T(8,128)(2,1)S(1)}, bf16[128,1152]{1,0:T(8,128)(2,1)S(1)}, u32[]{:S(2)}, u32[]{:S(2)}) collective-permute-start(bf16[128,1152]{1,0:T(8,128)(2,1)S(1)} %get-tuple-element.109), channel_id=1, source_target_pairs={{0,2},{1,3},{2,0},{3,1},{4,6},{5,7},{6,4},{7,5},{8,10},{9,11},{10,... | collective-permute-start | bytes 884744 | tf_op jit(solution)/shard_map/ppermute | solution.py:369
  66.9 0.1 add_convert_fusion.1
  67.0 1.3 %collective-permute-start.20 = (bf16[128,1152]{1,0:T(8,128)(2,1)S(1)}, bf16[128,1152]{1,0:T(8,128)(2,1)S(1)}, u32[]{:S(2)}, u32[]{:S(2)}) collective-permute-start(bf16[128,1152]{1,0:T(8,128)(2,1)S(1)} %add_convert_fusion.1), channel_id=1, source_target_pairs={{0,4},{1,5},{2,6},{3,7},{4,8},{5,9},{6,10},{7,11},{8,12},{9,13},{1... | collective-permute-start | bytes 884744 | tf_op jit(solution)/shard_map/ppermute | solution.py:363
  68.3 3.5 %weights_grads.2 = (bf16[1024,384]{1,0:T(8,128)(2,1)S(1)}, bf16[1024,384]{1,0:T(8,128)(2,1)S(1)}, bf16[384,1024]{1,0:T(8,128)(2,1)S(1)}) custom-call(bf16[128,1152]{1,0:T(8,128)(2,1)S(1)} %copy-done, bf16[128,1152]{1,0:T(8,128)(2,1)S(1)} %collective-permute-done.1.refs_1_, bf16[128,1152]{1,0:T(8,128)(2,1)S(1)} %collective-permute-done.refs_0_.refs_2_, ...), custom_call_target="tpu_custom_call" | custom-call | flops 2415919104 | bytes 8912896 | tf_op jit(solution)/shard_map/weights_grads/pallas_call | solution.py:282
  71.8 0.1 collective-permute-start.23
  71.9 0.5 collective-permute-start.24
  72.4 0.1 collective-permute-start.25
  72.5 0.1 add_convert_fusion.2
  72.5 2.7 %collective-permute-start.16 = (bf16[128,1152]{1,0:T(8,128)(2,1)S(1)}, bf16[128,1152]{1,0:T(8,128)(2,1)S(1)}, u32[]{:S(2)}, u32[]{:S(2)}) collective-permute-start(bf16[128,1152]{1,0:T(8,128)(2,1)S(1)} %get-tuple-element.100), channel_id=1, source_target_pairs={{0,12},{1,13},{2,14},{3,15},{4,0},{5,1},{6,2},{7,3},{8,4},{9,5},{1... | collective-permute-start | bytes 884744 | tf_op jit(solution)/shard_map/ppermute | solution.py:366
  75.2 0.4 collective-permute-done.20
  75.6 0.6 collective-permute-start.18
  76.2 0.1 add_convert_fusion
  76.3 0.0 copy-start.2
  76.3 0.0 copy-start.3
  76.4 0.0 collective-permute-done.25.refs_22_
  76.4 0.2 collective-permute-start.26
  76.6 4.4 %weights_grads.3 = (bf16[1,1024,384]{2,1,0:T(8,128)(2,1)}, bf16[1,1024,384]{2,1,0:T(8,128)(2,1)}, bf16[1,384,1024]{2,1,0:T(8,128)(2,1)}) custom-call(bf16[128,1152]{1,0:T(8,128)(2,1)S(1)} %copy-done, bf16[128,1152]{1,0:T(8,128)(2,1)S(1)} %collective-permute-done.1.refs_1_, bf16[128,1152]{1,0:T(8,128)(2,1)S(1)} %collective-permute-done.refs_0_.refs_2_, ...), custom_call_target="tpu_custom_call" | custom-call | flops 2415919104 | bytes 8912896 | tf_op jit(solution)/shard_map/weights_grads/pallas_call | solution.py:282
  81.1 1.6 %collective-permute-done.16.refs_0_ = bf16[128,1152]{1,0:T(8,128)(2,1)S(1)} collective-permute-done((bf16[128,1152]{1,0:T(8,128)(2,1)S(1)}, bf16[128,1152]{1,0:T(8,128)(2,1)S(1)}, u32[]{:S(2)}, u32[]{:S(2)}) %collective-permute-start.16) | collective-permute-done | bytes 294944 | tf_op jit(solution)/shard_map/ppermute | solution.py:366
  82.6 1.7 %collective-permute-done.18.refs_2_ = bf16[128,1152]{1,0:T(8,128)(2,1)S(1)} collective-permute-done((bf16[128,1152]{1,0:T(8,128)(2,1)S(1)}, bf16[128,1152]{1,0:T(8,128)(2,1)S(1)}, u32[]{:S(2)}, u32[]{:S(2)}) %collective-permute-start.18) | collective-permute-done | bytes 294944 | tf_op jit(solution)/shard_map/ppermute | solution.py:369
  84.3 4.8 %collective-permute-done.26.refs_3_ = bf16[128,1152]{1,0:T(8,128)(2,1)S(1)} collective-permute-done((bf16[128,1152]{1,0:T(8,128)(2,1)S(1)}, bf16[128,1152]{1,0:T(8,128)(2,1)S(1)}, u32[]{:S(2)}, u32[]{:S(2)}) %collective-permute-start.26) | collective-permute-done | bytes 294944 | tf_op jit(solution)/shard_map/ppermute | solution.py:363
  89.1 0.9 %finish.1 = (bf16[128,1024]{1,0:T(8,128)(2,1)}, bf16[8,128]{1,0:T(8,128)(2,1)}) custom-call(s32[8,128]{1,0:T(8,128)S(1)} %bitcast.8, f32[16,128]{1,0:T(8,128)S(1)} %copy-done.3, bf16[128,1152]{1,0:T(8,128)(2,1)S(1)} %collective-permute-done.16.refs_0_, bf16[128,1152]{1,0:T(8,128)(2,1)S(1)} %get-tuple-element.125.refs_1_, ...), custom_call_target="tpu_custom_call" | custom-call | tf_op jit(solution)/shard_map/finish/pallas_call | solution.py:329
  (30 shorter events, 0.1 us)
Async XLA Ops:
  2.4 5.3 %collective-permute-start.2 = (bf16[1024,384]{1,0:T(8,128)(2,1)}, bf16[1024,384]{1,0:T(8,128)(2,1)S(1)}, u32[]{:S(2)}, u32[]{:S(2)}) collective-permute-start(bf16[1024,384]{1,0:T(8,128)(2,1)} %bitcast.9), channel_id=1, source_target_pairs={{0,1},{1,0},{2,3},{3,2},{4,5},{5,4},{6,7},{7,6},{8,9},{9,8},{10,11... | collective-permute-start | bytes 2359304 | tf_op jit(solution)/shard_map/ppermute | solution.py:372
  2.9 7.2 %collective-permute-start.3 = (bf16[1024,384]{1,0:T(8,128)(2,1)}, bf16[1024,384]{1,0:T(8,128)(2,1)S(1)}, u32[]{:S(2)}, u32[]{:S(2)}) collective-permute-start(bf16[1024,384]{1,0:T(8,128)(2,1)} %bitcast.14), channel_id=1, source_target_pairs={{0,1},{1,0},{2,3},{3,2},{4,5},{5,4},{6,7},{7,6},{8,9},{9,8},{10,11... | collective-permute-start | bytes 2359304 | tf_op jit(solution)/shard_map/ppermute | solution.py:372
  3.0 8.5 %collective-permute-start.4 = (bf16[384,1024]{1,0:T(8,128)(2,1)}, bf16[384,1024]{1,0:T(8,128)(2,1)S(1)}, u32[]{:S(2)}, u32[]{:S(2)}) collective-permute-start(bf16[384,1024]{1,0:T(8,128)(2,1)} %bitcast.19), channel_id=1, source_target_pairs={{0,1},{1,0},{2,3},{3,2},{4,5},{5,4},{6,7},{7,6},{8,9},{9,8},{10,11... | collective-permute-start | bytes 2359304 | tf_op jit(solution)/shard_map/ppermute | solution.py:372
  3.4 21.5 %copy-start = (bf16[128,1152]{1,0:T(8,128)(2,1)S(1)}, bf16[128,1152]{1,0:T(8,128)(2,1)}, u32[]{:S(2)}) copy-start(bf16[128,1152]{1,0:T(8,128)(2,1)} %get-tuple-element.69.refs_0_) | copy-start | bytes 884740
  3.4 21.5 %copy-start.1 = (bf16[128,1024]{1,0:T(8,128)(2,1)S(1)}, bf16[128,1024]{1,0:T(8,128)(2,1)}, u32[]{:S(2)}) copy-start(bf16[128,1024]{1,0:T(8,128)(2,1)} %refs_8_.3) | copy-start | bytes 786436
  3.4 21.5 %copy-start.4 = (bf16[1,1024,384]{2,1,0:T(8,128)(2,1)S(1)}, bf16[1,1024,384]{2,1,0:T(8,128)(2,1)}, u32[]{:S(2)}) copy-start(bf16[1,1024,384]{2,1,0:T(8,128)(2,1)} %param.13) | copy-start | bytes 2359300
  3.4 21.5 %copy-start.5 = (bf16[1,1024,384]{2,1,0:T(8,128)(2,1)S(1)}, bf16[1,1024,384]{2,1,0:T(8,128)(2,1)}, u32[]{:S(2)}) copy-start(bf16[1,1024,384]{2,1,0:T(8,128)(2,1)} %param.14) | copy-start | bytes 2359300
  3.4 12.8 %collective-permute-start = (bf16[128,1152]{1,0:T(8,128)(2,1)}, bf16[128,1152]{1,0:T(8,128)(2,1)S(1)}, u32[]{:S(2)}, u32[]{:S(2)}) collective-permute-start(bf16[128,1152]{1,0:T(8,128)(2,1)} %get-tuple-element.69.refs_0_), channel_id=1, source_target_pairs={{0,4},{1,5},{2,6},{3,7},{4,8},{5,9},{6,10},{7,11},{8,12},{9,13},{1... | collective-permute-start | bytes 884744 | tf_op jit(solution)/shard_map/ppermute | solution.py:363
  6.1 10.1 %collective-permute-start.1 = (bf16[128,1152]{1,0:T(8,128)(2,1)}, bf16[128,1152]{1,0:T(8,128)(2,1)S(1)}, u32[]{:S(2)}, u32[]{:S(2)}) collective-permute-start(bf16[128,1152]{1,0:T(8,128)(2,1)} %get-tuple-element.69.refs_0_), channel_id=1, source_target_pairs={{0,2},{1,3},{2,0},{3,1},{4,6},{5,7},{6,4},{7,5},{8,10},{9,11},{10,... | collective-permute-start | bytes 884744 | tf_op jit(solution)/shard_map/ppermute | solution.py:369
  7.7 0.9 copy-start.8
  8.5 13.3 %collective-permute-start.7 = (bf16[128,1024]{1,0:T(8,128)(2,1)}, bf16[128,1024]{1,0:T(8,128)(2,1)S(1)}, u32[]{:S(2)}, u32[]{:S(2)}) collective-permute-start(bf16[128,1024]{1,0:T(8,128)(2,1)} %refs_8_.3), channel_id=1, source_target_pairs={{0,4},{1,5},{2,6},{3,7},{4,8},{5,9},{6,10},{7,11},{8,12},{9,13},{1... | collective-permute-start | bytes 786440 | tf_op jit(solution)/shard_map/ppermute | solution.py:363
  10.1 0.9 copy-start.10
  11.0 10.9 %collective-permute-start.8 = (bf16[128,1024]{1,0:T(8,128)(2,1)}, bf16[128,1024]{1,0:T(8,128)(2,1)S(1)}, u32[]{:S(2)}, u32[]{:S(2)}) collective-permute-start(bf16[128,1024]{1,0:T(8,128)(2,1)} %refs_8_.3), channel_id=1, source_target_pairs={{0,2},{1,3},{2,0},{3,1},{4,6},{5,7},{6,4},{7,5},{8,10},{9,11},{10,... | collective-permute-start | bytes 786440 | tf_op jit(solution)/shard_map/ppermute | solution.py:369
  11.5 0.9 copy-start.12
  16.2 17.2 %collective-permute-start.5 = (bf16[128,1152]{1,0:T(8,128)(2,1)S(1)}, bf16[128,1152]{1,0:T(8,128)(2,1)S(1)}, u32[]{:S(2)}, u32[]{:S(2)}) collective-permute-start(bf16[128,1152]{1,0:T(8,128)(2,1)S(1)} %collective-permute-done.refs_0_.refs_2_), channel_id=1, source_target_pairs={{0,4},{1,5},{2,6},{3,7},{4,8},{5,9},{6,10},{7,11},{8,12},{9,13},{1... | collective-permute-start | bytes 884744 | tf_op jit(solution)/shard_map/ppermute | solution.py:363
  17.8 15.7 %collective-permute-start.6 = (bf16[128,1152]{1,0:T(8,128)(2,1)S(1)}, bf16[128,1152]{1,0:T(8,128)(2,1)S(1)}, u32[]{:S(2)}, u32[]{:S(2)}) collective-permute-start(bf16[128,1152]{1,0:T(8,128)(2,1)S(1)} %collective-permute-done.refs_0_.refs_2_), channel_id=1, source_target_pairs={{0,2},{1,3},{2,0},{3,1},{4,6},{5,7},{6,4},{7,5},{8,10},{9,11},{10,... | collective-permute-start | bytes 884744 | tf_op jit(solution)/shard_map/ppermute | solution.py:369
  21.9 13.8 %collective-permute-start.9 = (bf16[128,1024]{1,0:T(8,128)(2,1)S(1)}, bf16[128,1024]{1,0:T(8,128)(2,1)S(1)}, u32[]{:S(2)}, u32[]{:S(2)}) collective-permute-start(bf16[128,1024]{1,0:T(8,128)(2,1)S(1)} %collective-permute-done.7.refs_2_.refs_10_), channel_id=1, source_target_pairs={{0,4},{1,5},{2,6},{3,7},{4,8},{5,9},{6,10},{7,11},{8,12},{9,13},{1... | collective-permute-start | bytes 786440 | tf_op jit(solution)/shard_map/ppermute | solution.py:363
  23.4 12.3 %collective-permute-start.10 = (bf16[128,1024]{1,0:T(8,128)(2,1)S(1)}, bf16[128,1024]{1,0:T(8,128)(2,1)S(1)}, u32[]{:S(2)}, u32[]{:S(2)}) collective-permute-start(bf16[128,1024]{1,0:T(8,128)(2,1)S(1)} %collective-permute-done.7.refs_2_.refs_10_), channel_id=1, source_target_pairs={{0,2},{1,3},{2,0},{3,1},{4,6},{5,7},{6,4},{7,5},{8,10},{9,11},{10,... | collective-permute-start | bytes 786440 | tf_op jit(solution)/shard_map/ppermute | solution.py:369
  24.9 1.1 %copy-start.6 = (bf16[1,384,1024]{2,1,0:T(8,128)(2,1)S(1)}, bf16[1,384,1024]{2,1,0:T(8,128)(2,1)}, u32[]{:S(2)}) copy-start(bf16[1,384,1024]{2,1,0:T(8,128)(2,1)} %param.15) | copy-start | bytes 2359300
  26.1 1.1 %copy-start.9 = (bf16[1024,384]{1,0:T(8,128)(2,1)S(1)}, bf16[1024,384]{1,0:T(8,128)(2,1)}, u32[]{:S(2)}) copy-start(bf16[1024,384]{1,0:T(8,128)(2,1)} %copy-done.8) | copy-start | bytes 2359300
  27.2 1.1 %copy-start.11 = (bf16[1024,384]{1,0:T(8,128)(2,1)S(1)}, bf16[1024,384]{1,0:T(8,128)(2,1)}, u32[]{:S(2)}) copy-start(bf16[1024,384]{1,0:T(8,128)(2,1)} %copy-done.10) | copy-start | bytes 2359300
  28.3 1.1 %copy-start.13 = (bf16[384,1024]{1,0:T(8,128)(2,1)S(1)}, bf16[384,1024]{1,0:T(8,128)(2,1)}, u32[]{:S(2)}) copy-start(bf16[384,1024]{1,0:T(8,128)(2,1)} %copy-done.12) | copy-start | bytes 2359300
  29.5 7.9 %copy-start.7 = (bf16[1,384,1024]{2,1,0:T(8,128)(2,1)S(1)}, bf16[1,384,1024]{2,1,0:T(8,128)(2,1)}, u32[]{:S(2)}) copy-start(bf16[1,384,1024]{2,1,0:T(8,128)(2,1)} %param.15) | copy-start | bytes 2359300
  33.5 11.6 %collective-permute-start.11 = (bf16[128,1152]{1,0:T(8,128)(2,1)S(1)}, bf16[128,1152]{1,0:T(8,128)(2,1)S(1)}, u32[]{:S(2)}, u32[]{:S(2)}) collective-permute-start(bf16[128,1152]{1,0:T(8,128)(2,1)S(1)} %collective-permute-done.5.refs_0_.refs_4_), channel_id=1, source_target_pairs={{0,4},{1,5},{2,6},{3,7},{4,8},{5,9},{6,10},{7,11},{8,12},{9,13},{1... | collective-permute-start | bytes 884744 | tf_op jit(solution)/shard_map/ppermute | solution.py:363
  35.1 9.9 %collective-permute-start.12 = (bf16[128,1152]{1,0:T(8,128)(2,1)S(1)}, bf16[128,1152]{1,0:T(8,128)(2,1)S(1)}, u32[]{:S(2)}, u32[]{:S(2)}) collective-permute-start(bf16[128,1152]{1,0:T(8,128)(2,1)S(1)} %collective-permute-done.5.refs_0_.refs_4_), channel_id=1, source_target_pairs={{0,2},{1,3},{2,0},{3,1},{4,6},{5,7},{6,4},{7,5},{8,10},{9,11},{10,... | collective-permute-start | bytes 884744 | tf_op jit(solution)/shard_map/ppermute | solution.py:369
  35.6 12.2 %collective-permute-start.14 = (bf16[128,1024]{1,0:T(8,128)(2,1)S(1)}, bf16[128,1024]{1,0:T(8,128)(2,1)S(1)}, u32[]{:S(2)}, u32[]{:S(2)}) collective-permute-start(bf16[128,1024]{1,0:T(8,128)(2,1)S(1)} %collective-permute-done.9.refs_2_.refs_12_), channel_id=1, source_target_pairs={{0,4},{1,5},{2,6},{3,7},{4,8},{5,9},{6,10},{7,11},{8,12},{9,13},{1... | collective-permute-start | bytes 786440 | tf_op jit(solution)/shard_map/ppermute | solution.py:363
  35.7 14.8 %collective-permute-start.15 = (bf16[128,1024]{1,0:T(8,128)(2,1)S(1)}, bf16[128,1024]{1,0:T(8,128)(2,1)S(1)}, u32[]{:S(2)}, u32[]{:S(2)}) collective-permute-start(bf16[128,1024]{1,0:T(8,128)(2,1)S(1)} %collective-permute-done.9.refs_2_.refs_12_), channel_id=1, source_target_pairs={{0,2},{1,3},{2,0},{3,1},{4,6},{5,7},{6,4},{7,5},{8,10},{9,11},{10,... | collective-permute-start | bytes 786440 | tf_op jit(solution)/shard_map/ppermute | solution.py:369
  45.1 16.4 %collective-permute-start.13 = (bf16[128,1152]{1,0:T(8,128)(2,1)S(1)}, bf16[128,1152]{1,0:T(8,128)(2,1)S(1)}, u32[]{:S(2)}, u32[]{:S(2)}) collective-permute-start(bf16[128,1152]{1,0:T(8,128)(2,1)S(1)} %collective-permute-done.11.refs_0_.refs_6_), channel_id=1, source_target_pairs={{0,2},{1,3},{2,0},{3,1},{4,6},{5,7},{6,4},{7,5},{8,10},{9,11},{10,... | collective-permute-start | bytes 884744 | tf_op jit(solution)/shard_map/ppermute | solution.py:369
  50.5 10.9 %collective-permute-start.21 = (bf16[128,1024]{1,0:T(8,128)(2,1)S(1)}, bf16[128,1024]{1,0:T(8,128)(2,1)S(1)}, u32[]{:S(2)}, u32[]{:S(2)}) collective-permute-start(bf16[128,1024]{1,0:T(8,128)(2,1)S(1)} %collective-permute-done.15.refs_3_.refs_13_), channel_id=1, source_target_pairs={{0,4},{1,5},{2,6},{3,7},{4,8},{5,9},{6,10},{7,11},{8,12},{9,13},{1... | collective-permute-start | bytes 786440 | tf_op jit(solution)/shard_map/ppermute | solution.py:363
  54.9 12.0 %collective-permute-start.19 = (bf16[128,1152]{1,0:T(8,128)(2,1)S(1)}, bf16[128,1152]{1,0:T(8,128)(2,1)S(1)}, u32[]{:S(2)}, u32[]{:S(2)}) collective-permute-start(bf16[128,1152]{1,0:T(8,128)(2,1)S(1)} %get-tuple-element.105), channel_id=1, source_target_pairs={{0,2},{1,3},{2,0},{3,1},{4,6},{5,7},{6,4},{7,5},{8,10},{9,11},{10,... | collective-permute-start | bytes 884744 | tf_op jit(solution)/shard_map/ppermute | solution.py:369
  61.4 10.9 %collective-permute-start.17 = (bf16[128,1152]{1,0:T(8,128)(2,1)S(1)}, bf16[128,1152]{1,0:T(8,128)(2,1)S(1)}, u32[]{:S(2)}, u32[]{:S(2)}) collective-permute-start(bf16[128,1152]{1,0:T(8,128)(2,1)S(1)} %get-tuple-element.103), channel_id=1, source_target_pairs={{0,12},{1,13},{2,14},{3,15},{4,0},{5,1},{6,2},{7,3},{8,4},{9,5},{1... | collective-permute-start | bytes 884744 | tf_op jit(solution)/shard_map/ppermute | solution.py:366
  65.5 7.1 %collective-permute-start.22 = (bf16[128,1152]{1,0:T(8,128)(2,1)S(1)}, bf16[128,1152]{1,0:T(8,128)(2,1)S(1)}, u32[]{:S(2)}, u32[]{:S(2)}) collective-permute-start(bf16[128,1152]{1,0:T(8,128)(2,1)S(1)} %get-tuple-element.109), channel_id=1, source_target_pairs={{0,2},{1,3},{2,0},{3,1},{4,6},{5,7},{6,4},{7,5},{8,10},{9,11},{10,... | collective-permute-start | bytes 884744 | tf_op jit(solution)/shard_map/ppermute | solution.py:369
  67.0 8.6 %collective-permute-start.20 = (bf16[128,1152]{1,0:T(8,128)(2,1)S(1)}, bf16[128,1152]{1,0:T(8,128)(2,1)S(1)}, u32[]{:S(2)}, u32[]{:S(2)}) collective-permute-start(bf16[128,1152]{1,0:T(8,128)(2,1)S(1)} %add_convert_fusion.1), channel_id=1, source_target_pairs={{0,4},{1,5},{2,6},{3,7},{4,8},{5,9},{6,10},{7,11},{8,12},{9,13},{1... | collective-permute-start | bytes 884744 | tf_op jit(solution)/shard_map/ppermute | solution.py:363
  71.8 4.5 %collective-permute-start.23 = (bf16[1024,384]{1,0:T(8,128)(2,1)S(1)}, bf16[1024,384]{1,0:T(8,128)(2,1)S(1)}, u32[]{:S(2)}, u32[]{:S(2)}) collective-permute-start(bf16[1024,384]{1,0:T(8,128)(2,1)S(1)} %get-tuple-element.113), channel_id=1, source_target_pairs={{0,1},{1,0},{2,3},{3,2},{4,5},{5,4},{6,7},{7,6},{8,9},{9,8},{10,11... | collective-permute-start | bytes 2359304 | tf_op jit(solution)/shard_map/ppermute | solution.py:372
  71.9 4.5 %collective-permute-start.24 = (bf16[1024,384]{1,0:T(8,128)(2,1)S(1)}, bf16[1024,384]{1,0:T(8,128)(2,1)S(1)}, u32[]{:S(2)}, u32[]{:S(2)}) collective-permute-start(bf16[1024,384]{1,0:T(8,128)(2,1)S(1)} %get-tuple-element.114), channel_id=1, source_target_pairs={{0,1},{1,0},{2,3},{3,2},{4,5},{5,4},{6,7},{7,6},{8,9},{9,8},{10,11... | collective-permute-start | bytes 2359304 | tf_op jit(solution)/shard_map/ppermute | solution.py:372
  72.4 4.0 %collective-permute-start.25 = (bf16[384,1024]{1,0:T(8,128)(2,1)S(1)}, bf16[384,1024]{1,0:T(8,128)(2,1)S(1)}, u32[]{:S(2)}, u32[]{:S(2)}) collective-permute-start(bf16[384,1024]{1,0:T(8,128)(2,1)S(1)} %get-tuple-element.115), channel_id=1, source_target_pairs={{0,1},{1,0},{2,3},{3,2},{4,5},{5,4},{6,7},{7,6},{8,9},{9,8},{10,11... | collective-permute-start | bytes 2359304 | tf_op jit(solution)/shard_map/ppermute | solution.py:372
  72.5 10.1 %collective-permute-start.16 = (bf16[128,1152]{1,0:T(8,128)(2,1)S(1)}, bf16[128,1152]{1,0:T(8,128)(2,1)S(1)}, u32[]{:S(2)}, u32[]{:S(2)}) collective-permute-start(bf16[128,1152]{1,0:T(8,128)(2,1)S(1)} %get-tuple-element.100), channel_id=1, source_target_pairs={{0,12},{1,13},{2,14},{3,15},{4,0},{5,1},{6,2},{7,3},{8,4},{9,5},{1... | collective-permute-start | bytes 884744 | tf_op jit(solution)/shard_map/ppermute | solution.py:366
  75.6 8.7 %collective-permute-start.18 = (bf16[128,1152]{1,0:T(8,128)(2,1)S(1)}, bf16[128,1152]{1,0:T(8,128)(2,1)S(1)}, u32[]{:S(2)}, u32[]{:S(2)}) collective-permute-start(bf16[128,1152]{1,0:T(8,128)(2,1)S(1)} %add_convert_fusion.2), channel_id=1, source_target_pairs={{0,2},{1,3},{2,0},{3,1},{4,6},{5,7},{6,4},{7,5},{8,10},{9,11},{10,... | collective-permute-start | bytes 884744 | tf_op jit(solution)/shard_map/ppermute | solution.py:369
  76.3 12.8 %copy-start.2 = (s32[128,8]{0,1:T(8,128)S(1)}, s32[128,8]{0,1:T(8,128)}, u32[]{:S(2)}) copy-start(s32[128,8]{0,1:T(8,128)} %param.11) | copy-start | bytes 12292
  76.3 12.8 %copy-start.3 = (f32[16,128]{1,0:T(8,128)S(1)}, f32[16,128]{1,0:T(8,128)}, u32[]{:S(2)}) copy-start(f32[16,128]{1,0:T(8,128)} %hold.1.kept) | copy-start | bytes 24580
  76.4 12.7 %collective-permute-start.26 = (bf16[128,1152]{1,0:T(8,128)(2,1)S(1)}, bf16[128,1152]{1,0:T(8,128)(2,1)S(1)}, u32[]{:S(2)}, u32[]{:S(2)}) collective-permute-start(bf16[128,1152]{1,0:T(8,128)(2,1)S(1)} %add_convert_fusion), channel_id=1, source_target_pairs={{0,4},{1,5},{2,6},{3,7},{4,8},{5,9},{6,10},{7,11},{8,12},{9,13},{1... | collective-permute-start | bytes 884744 | tf_op jit(solution)/shard_map/ppermute | solution.py:363

commit v6 on v5

--- a/solution.py
+++ b/solution.py
@@ -107,6 +107,7 @@
         in_specs=[ANY],
         out_specs=ANY,
         input_output_aliases={0: 0},
+        compiler_params=params(1),
         cost_estimate=pl.CostEstimate(flops=flops, bytes_accessed=1000, transcendentals=0),
         name="hold",
     )(value)

time: 90.4 us -> 84.9 us (0.939)
  waiting for transfers between devices: 29.7 us -> 23.5 us
  starting transfers between devices: 25.5 us -> 31.5 us
  local copies, waits for them, and re-layouts: 7.2 us -> 1.32 us
    unnamed x28 -> x18, local copies, waits for them, and re-layouts: 7.2 us -> 1.32 us
    ppermute x9, starting transfers between devices: 10.9 us -> 15.3 us  [send_z(): lax.ppermute(v, 'expert', [(i, moved(i, 1, 0)) for i in range(devices)])]
    ppermute x10, waiting for transfers between devices: 4.35 us -> 1.74 us  [send_y(): lax.ppermute(v, 'expert', [(i, moved(i, 0, 1)) for i in range(devices)])]
    ppermute x10, starting transfers between devices: 10.2 us -> 12.4 us  [send_y(): lax.ppermute(v, 'expert', [(i, moved(i, 0, 1)) for i in range(devices)])]
    ppermute x9, waiting for transfers between devices: 23.7 us -> 21.7 us  [send_z(): lax.ppermute(v, 'expert', [(i, moved(i, 1, 0)) for i in range(devices)])]
    ppermute x2, waiting for transfers between devices: 1.56 us -> 0.01 us  [send_down(): lax.ppermute(v, 'expert', [(i, moved(i, -1, 0)) for i in range(devices)])]
  transfers between devices with their start and end apart: 27 -> 27, of which waited for: 10 -> 10; matrix products, arithmetic and copies ran while one was open for 0% -> 0% of each run, Pallas kernels for 27% -> 29%
where the time goes in v6:
time: 84.9 us; the launch traced here: 84.1 us
  starting transfers between devices  31.5 us (37%)
  Pallas kernels  26.7 us (31%)
  waiting for transfers between devices  23.5 us (28%)
  local copies, waits for them, and re-layouts  1.32 us (2%)
    ppermute x9, waiting for transfers between devices, send_z(): lax.ppermute(v, 'expert', [(i, moved(i, 1, 0)) for i in range(devices)])  21.7 us
    pallas_call x4, Pallas kernels, rows_grads(): pl.pallas_call(functools.partial(rows_kernel, slots), out_shape=tuple((ja...  16 us
    ppermute x9, starting transfers between devices, send_z(): lax.ppermute(v, 'expert', [(i, moved(i, 1, 0)) for i in range(devices)])  15.3 us
    ppermute x10, starting transfers between devices, send_y(): lax.ppermute(v, 'expert', [(i, moved(i, 0, 1)) for i in range(devices)])  12.4 us
    pallas_call x2, Pallas kernels, weights_grads(): pl.pallas_call(functools.partial(weights_kernel, j, slots, steps, len(mor...  7.96 us
    ppermute x2, starting transfers between devices, send_down(): lax.ppermute(v, 'expert', [(i, moved(i, -1, 0)) for i in range(devices)])  2.16 us
    pallas_call x1, Pallas kernels, plan(): pl.pallas_call(functools.partial(plan_kernel, home_cap, rep_cap), out_sha...  1.75 us
    ppermute x10, waiting for transfers between devices, send_y(): lax.ppermute(v, 'expert', [(i, moved(i, 0, 1)) for i in range(devices)])  1.74 us
  transfers between devices with their start and end apart: 27, of which 10 were waited for; matrix products, arithmetic and copies ran while one was open for 0% of the time, Pallas kernels for 29%

profile of v6, /device:TPU:0, one launch (start us, length us, event | category | flops | bytes accessed | tf_op | source)
XLA Modules:
  0.0 84.1 jit_solution(18035143874024242187)
XLA Ops:
  0.6 1.7 %plan.1 = (bf16[128,1152]{1,0:T(8,128)(2,1)}, f32[16,128]{1,0:T(8,128)}) custom-call(s32[1,16]{1,0:T(1,128)} %bitcast.25, s32[8,128]{1,0:T(8,128)} %bitcast.7, bf16[8,128]{1,0:T(8,128)(2,1)} %bitcast.24, bf16[128,1024]{1,0:T(8,128)(2,1)} %x_in.1), custom_call_target="tpu_custom_call" | custom-call | tf_op jit(solution)/shard_map/plan/pallas_call | solution.py:84
  2.4 0.5 collective-permute-start.2
  2.9 0.1 collective-permute-start.3
  3.0 0.4 collective-permute-start.4
  3.4 2.7 %collective-permute-start = (bf16[128,1152]{1,0:T(8,128)(2,1)}, bf16[128,1152]{1,0:T(8,128)(2,1)S(1)}, u32[]{:S(2)}, u32[]{:S(2)}) collective-permute-start(bf16[128,1152]{1,0:T(8,128)(2,1)} %get-tuple-element.69.refs_0_), channel_id=1, source_target_pairs={{0,4},{1,5},{2,6},{3,7},{4,8},{5,9},{6,10},{7,11},{8,12},{9,13},{1... | collective-permute-start | bytes 884744 | tf_op jit(solution)/shard_map/ppermute | solution.py:364
  6.1 1.5 %collective-permute-start.1 = (bf16[128,1152]{1,0:T(8,128)(2,1)}, bf16[128,1152]{1,0:T(8,128)(2,1)S(1)}, u32[]{:S(2)}, u32[]{:S(2)}) collective-permute-start(bf16[128,1152]{1,0:T(8,128)(2,1)} %get-tuple-element.69.refs_0_), channel_id=1, source_target_pairs={{0,2},{1,3},{2,0},{3,1},{4,6},{5,7},{6,4},{7,5},{8,10},{9,11},{10,... | collective-permute-start | bytes 884744 | tf_op jit(solution)/shard_map/ppermute | solution.py:370
  7.6 0.0 collective-permute-done.2.refs_7_
  7.6 1.6 %collective-permute-start.7 = (bf16[128,1024]{1,0:T(8,128)(2,1)}, bf16[128,1024]{1,0:T(8,128)(2,1)S(1)}, u32[]{:S(2)}, u32[]{:S(2)}) collective-permute-start(bf16[128,1024]{1,0:T(8,128)(2,1)} %refs_8_.3), channel_id=1, source_target_pairs={{0,4},{1,5},{2,6},{3,7},{4,8},{5,9},{6,10},{7,11},{8,12},{9,13},{1... | collective-permute-start | bytes 786440 | tf_op jit(solution)/shard_map/ppermute | solution.py:364
  9.2 0.0 collective-permute-done.3.refs_8_
  9.2 0.5 collective-permute-start.8
  9.7 0.0 collective-permute-done.4.refs_9_
  9.7 0.7 copy-done.3
  10.4 0.6 copy-done.4
  11.0 5.2 %collective-permute-done.refs_0_.refs_2_ = bf16[128,1152]{1,0:T(8,128)(2,1)S(1)} collective-permute-done((bf16[128,1152]{1,0:T(8,128)(2,1)}, bf16[128,1152]{1,0:T(8,128)(2,1)S(1)}, u32[]{:S(2)}, u32[]{:S(2)}) %collective-permute-start) | collective-permute-done | bytes 294944 | tf_op jit(solution)/shard_map/ppermute | solution.py:364
  16.2 0.0 collective-permute-done.1.refs_1_
  16.2 1.5 %collective-permute-start.5 = (bf16[128,1152]{1,0:T(8,128)(2,1)S(1)}, bf16[128,1152]{1,0:T(8,128)(2,1)S(1)}, u32[]{:S(2)}, u32[]{:S(2)}) collective-permute-start(bf16[128,1152]{1,0:T(8,128)(2,1)S(1)} %collective-permute-done.refs_0_.refs_2_), channel_id=1, source_target_pairs={{0,4},{1,5},{2,6},{3,7},{4,8},{5,9},{6,10},{7,11},{8,12},{9,13},{1... | collective-permute-start | bytes 884744 | tf_op jit(solution)/shard_map/ppermute | solution.py:364
  17.7 1.5 %collective-permute-start.6 = (bf16[128,1152]{1,0:T(8,128)(2,1)S(1)}, bf16[128,1152]{1,0:T(8,128)(2,1)S(1)}, u32[]{:S(2)}, u32[]{:S(2)}) collective-permute-start(bf16[128,1152]{1,0:T(8,128)(2,1)S(1)} %collective-permute-done.refs_0_.refs_2_), channel_id=1, source_target_pairs={{0,2},{1,3},{2,0},{3,1},{4,6},{5,7},{6,4},{7,5},{8,10},{9,11},{10,... | collective-permute-start | bytes 884744 | tf_op jit(solution)/shard_map/ppermute | solution.py:370
  19.2 2.6 %collective-permute-done.7.refs_2_.refs_10_ = bf16[128,1024]{1,0:T(8,128)(2,1)S(1)} collective-permute-done((bf16[128,1024]{1,0:T(8,128)(2,1)}, bf16[128,1024]{1,0:T(8,128)(2,1)S(1)}, u32[]{:S(2)}, u32[]{:S(2)}) %collective-permute-start.7) | collective-permute-done | bytes 262176 | tf_op jit(solution)/shard_map/ppermute | solution.py:364
  21.9 0.0 collective-permute-done.8.refs_3_.refs_9_
  21.9 1.5 %collective-permute-start.9 = (bf16[128,1024]{1,0:T(8,128)(2,1)S(1)}, bf16[128,1024]{1,0:T(8,128)(2,1)S(1)}, u32[]{:S(2)}, u32[]{:S(2)}) collective-permute-start(bf16[128,1024]{1,0:T(8,128)(2,1)S(1)} %collective-permute-done.7.refs_2_.refs_10_), channel_id=1, source_target_pairs={{0,4},{1,5},{2,6},{3,7},{4,8},{5,9},{6,10},{7,11},{8,12},{9,13},{1... | collective-permute-start | bytes 786440 | tf_op jit(solution)/shard_map/ppermute | solution.py:364
  23.3 1.5 %collective-permute-start.10 = (bf16[128,1024]{1,0:T(8,128)(2,1)S(1)}, bf16[128,1024]{1,0:T(8,128)(2,1)S(1)}, u32[]{:S(2)}, u32[]{:S(2)}) collective-permute-start(bf16[128,1024]{1,0:T(8,128)(2,1)S(1)} %collective-permute-done.7.refs_2_.refs_10_), channel_id=1, source_target_pairs={{0,2},{1,3},{2,0},{3,1},{4,6},{5,7},{6,4},{7,5},{8,10},{9,11},{10,... | collective-permute-start | bytes 786440 | tf_op jit(solution)/shard_map/ppermute | solution.py:370
  24.9 4.0 %rows_grads.4 = (bf16[128,1152]{1,0:T(8,128)(2,1)S(1)}, bf16[128,1152]{1,0:T(8,128)(2,1)S(1)}, bf16[256,2304]{1,0:T(8,128)(2,1)S(1)}) custom-call(bf16[128,1152]{1,0:T(8,128)(2,1)S(1)} %copy-done, bf16[128,1152]{1,0:T(8,128)(2,1)S(1)} %collective-permute-done.1.refs_1_, bf16[128,1024]{1,0:T(8,128)(2,1)S(1)} %copy-done.1, ...), custom_call_target="tpu_custom_call" | custom-call | flops 2013265920 | bytes 9306112 | tf_op jit(solution)/shard_map/rows_grads/pallas_call | solution.py:201
  28.9 0.0 collective-permute-done.5.refs_0_.refs_4_
  28.9 1.6 %collective-permute-start.11 = (bf16[128,1152]{1,0:T(8,128)(2,1)S(1)}, bf16[128,1152]{1,0:T(8,128)(2,1)S(1)}, u32[]{:S(2)}, u32[]{:S(2)}) collective-permute-start(bf16[128,1152]{1,0:T(8,128)(2,1)S(1)} %collective-permute-done.5.refs_0_.refs_4_), channel_id=1, source_target_pairs={{0,4},{1,5},{2,6},{3,7},{4,8},{5,9},{6,10},{7,11},{8,12},{9,13},{1... | collective-permute-start | bytes 884744 | tf_op jit(solution)/shard_map/ppermute | solution.py:364
  30.5 0.6 collective-permute-start.12
  31.2 2.6 %collective-permute-done.9.refs_2_.refs_12_ = bf16[128,1024]{1,0:T(8,128)(2,1)S(1)} collective-permute-done((bf16[128,1024]{1,0:T(8,128)(2,1)S(1)}, bf16[128,1024]{1,0:T(8,128)(2,1)S(1)}, u32[]{:S(2)}, u32[]{:S(2)}) %collective-permute-start.9) | collective-permute-done | bytes 262176 | tf_op jit(solution)/shard_map/ppermute | solution.py:364
  33.8 0.0 collective-permute-done.10.refs_3_.refs_11_
  33.8 1.5 %collective-permute-start.14 = (bf16[128,1024]{1,0:T(8,128)(2,1)S(1)}, bf16[128,1024]{1,0:T(8,128)(2,1)S(1)}, u32[]{:S(2)}, u32[]{:S(2)}) collective-permute-start(bf16[128,1024]{1,0:T(8,128)(2,1)S(1)} %collective-permute-done.9.refs_2_.refs_12_), channel_id=1, source_target_pairs={{0,4},{1,5},{2,6},{3,7},{4,8},{5,9},{6,10},{7,11},{8,12},{9,13},{1... | collective-permute-start | bytes 786440 | tf_op jit(solution)/shard_map/ppermute | solution.py:364
  35.3 1.5 %collective-permute-start.15 = (bf16[128,1024]{1,0:T(8,128)(2,1)S(1)}, bf16[128,1024]{1,0:T(8,128)(2,1)S(1)}, u32[]{:S(2)}, u32[]{:S(2)}) collective-permute-start(bf16[128,1024]{1,0:T(8,128)(2,1)S(1)} %collective-permute-done.9.refs_2_.refs_12_), channel_id=1, source_target_pairs={{0,2},{1,3},{2,0},{3,1},{4,6},{5,7},{6,4},{7,5},{8,10},{9,11},{10,... | collective-permute-start | bytes 786440 | tf_op jit(solution)/shard_map/ppermute | solution.py:370
  36.8 4.0 %rows_grads.5 = (bf16[128,1152]{1,0:T(8,128)(2,1)S(1)}, bf16[128,1152]{1,0:T(8,128)(2,1)S(1)}, bf16[256,2304]{1,0:T(8,128)(2,1)S(1)}) custom-call(bf16[128,1152]{1,0:T(8,128)(2,1)S(1)} %collective-permute-done.refs_0_.refs_2_, bf16[128,1152]{1,0:T(8,128)(2,1)S(1)} %collective-permute-done.6.refs_1_.refs_3_, ...), custom_call_target="tpu_custom_call" | custom-call | flops 2013265920 | bytes 9306112 | tf_op jit(solution)/shard_map/rows_grads/pallas_call | solution.py:201
  40.8 0.0 collective-permute-done.12.refs_1_.refs_5_
  40.8 0.9 %collective-permute-start.13 = (bf16[128,1152]{1,0:T(8,128)(2,1)S(1)}, bf16[128,1152]{1,0:T(8,128)(2,1)S(1)}, u32[]{:S(2)}, u32[]{:S(2)}) collective-permute-start(bf16[128,1152]{1,0:T(8,128)(2,1)S(1)} %collective-permute-done.11.refs_0_.refs_6_), channel_id=1, source_target_pairs={{0,2},{1,3},{2,0},{3,1},{4,6},{5,7},{6,4},{7,5},{8,10},{9,11},{10,... | collective-permute-start | bytes 884744 | tf_op jit(solution)/shard_map/ppermute | solution.py:370
  41.7 3.8 %collective-permute-done.14.refs_2_.refs_14_ = bf16[128,1024]{1,0:T(8,128)(2,1)S(1)} collective-permute-done((bf16[128,1024]{1,0:T(8,128)(2,1)S(1)}, bf16[128,1024]{1,0:T(8,128)(2,1)S(1)}, u32[]{:S(2)}, u32[]{:S(2)}) %collective-permute-start.14) | collective-permute-done | bytes 262176 | tf_op jit(solution)/shard_map/ppermute | solution.py:364
  45.5 0.6 collective-permute-done.15.refs_3_.refs_13_
  46.1 1.1 %collective-permute-start.21 = (bf16[128,1024]{1,0:T(8,128)(2,1)S(1)}, bf16[128,1024]{1,0:T(8,128)(2,1)S(1)}, u32[]{:S(2)}, u32[]{:S(2)}) collective-permute-start(bf16[128,1024]{1,0:T(8,128)(2,1)S(1)} %collective-permute-done.15.refs_3_.refs_13_), channel_id=1, source_target_pairs={{0,4},{1,5},{2,6},{3,7},{4,8},{5,9},{6,10},{7,11},{8,12},{9,13},{1... | collective-permute-start | bytes 786440 | tf_op jit(solution)/shard_map/ppermute | solution.py:364
  47.2 4.0 %rows_grads.6 = (bf16[128,1152]{1,0:T(8,128)(2,1)S(1)}, bf16[128,1152]{1,0:T(8,128)(2,1)S(1)}, bf16[256,2304]{1,0:T(8,128)(2,1)S(1)}) custom-call(bf16[128,1152]{1,0:T(8,128)(2,1)S(1)} %collective-permute-done.5.refs_0_.refs_4_, bf16[128,1152]{1,0:T(8,128)(2,1)S(1)} %collective-permute-done.12.refs_1_.refs_5_, ...), custom_call_target="tpu_custom_call" | custom-call | flops 2013265920 | bytes 9306112 | tf_op jit(solution)/shard_map/rows_grads/pallas_call | solution.py:201
  51.2 1.6 %collective-permute-start.19 = (bf16[128,1152]{1,0:T(8,128)(2,1)S(1)}, bf16[128,1152]{1,0:T(8,128)(2,1)S(1)}, u32[]{:S(2)}, u32[]{:S(2)}) collective-permute-start(bf16[128,1152]{1,0:T(8,128)(2,1)S(1)} %get-tuple-element.105), channel_id=1, source_target_pairs={{0,2},{1,3},{2,0},{3,1},{4,6},{5,7},{6,4},{7,5},{8,10},{9,11},{10,... | collective-permute-start | bytes 884744 | tf_op jit(solution)/shard_map/ppermute | solution.py:370
  52.8 1.9 %collective-permute-done.21.refs_3_.refs_15_ = bf16[128,1024]{1,0:T(8,128)(2,1)S(1)} collective-permute-done((bf16[128,1024]{1,0:T(8,128)(2,1)S(1)}, bf16[128,1024]{1,0:T(8,128)(2,1)S(1)}, u32[]{:S(2)}, u32[]{:S(2)}) %collective-permute-start.21) | collective-permute-done | bytes 262176 | tf_op jit(solution)/shard_map/ppermute | solution.py:364
  54.8 0.3 collective-permute-start.17
  55.1 4.0 %rows_grads.7 = (bf16[128,1152]{1,0:T(8,128)(2,1)S(1)}, bf16[128,1152]{1,0:T(8,128)(2,1)S(1)}, bf16[256,2304]{1,0:T(8,128)(2,1)S(1)}) custom-call(bf16[128,1152]{1,0:T(8,128)(2,1)S(1)} %collective-permute-done.11.refs_0_.refs_6_, bf16[128,1152]{1,0:T(8,128)(2,1)S(1)} %collective-permute-done.13.refs_1_.refs_7_, ...), custom_call_target="tpu_custom_call" | custom-call | flops 2013265920 | bytes 9306112 | tf_op jit(solution)/shard_map/rows_grads/pallas_call | solution.py:201
  59.1 1.9 %collective-permute-start.22 = (bf16[128,1152]{1,0:T(8,128)(2,1)S(1)}, bf16[128,1152]{1,0:T(8,128)(2,1)S(1)}, u32[]{:S(2)}, u32[]{:S(2)}) collective-permute-start(bf16[128,1152]{1,0:T(8,128)(2,1)S(1)} %get-tuple-element.109), channel_id=1, source_target_pairs={{0,2},{1,3},{2,0},{3,1},{4,6},{5,7},{6,4},{7,5},{8,10},{9,11},{10,... | collective-permute-start | bytes 884744 | tf_op jit(solution)/shard_map/ppermute | solution.py:370
  61.0 0.0 collective-permute-done.19
  61.0 0.1 add_convert_fusion.1
  61.1 2.1 %collective-permute-start.20 = (bf16[128,1152]{1,0:T(8,128)(2,1)S(1)}, bf16[128,1152]{1,0:T(8,128)(2,1)S(1)}, u32[]{:S(2)}, u32[]{:S(2)}) collective-permute-start(bf16[128,1152]{1,0:T(8,128)(2,1)S(1)} %add_convert_fusion.1), channel_id=1, source_target_pairs={{0,4},{1,5},{2,6},{3,7},{4,8},{5,9},{6,10},{7,11},{8,12},{9,13},{1... | collective-permute-start | bytes 884744 | tf_op jit(solution)/shard_map/ppermute | solution.py:364
  63.1 3.5 %weights_grads.2 = (bf16[1024,384]{1,0:T(8,128)(2,1)S(1)}, bf16[1024,384]{1,0:T(8,128)(2,1)S(1)}, bf16[384,1024]{1,0:T(8,128)(2,1)S(1)}) custom-call(bf16[128,1152]{1,0:T(8,128)(2,1)S(1)} %copy-done, bf16[128,1152]{1,0:T(8,128)(2,1)S(1)} %collective-permute-done.1.refs_1_, bf16[128,1152]{1,0:T(8,128)(2,1)S(1)} %collective-permute-done.refs_0_.refs_2_, ...), custom_call_target="tpu_custom_call" | custom-call | flops 2415919104 | bytes 8912896 | tf_op jit(solution)/shard_map/weights_grads/pallas_call | solution.py:283
  66.7 0.1 collective-permute-start.23
  66.8 0.5 collective-permute-start.24
  67.3 0.0 collective-permute-done.17
  67.3 0.1 collective-permute-start.25
  67.3 0.1 add_convert_fusion.2
  67.4 0.0 collective-permute-done.22
  67.4 1.9 %collective-permute-start.16 = (bf16[128,1152]{1,0:T(8,128)(2,1)S(1)}, bf16[128,1152]{1,0:T(8,128)(2,1)S(1)}, u32[]{:S(2)}, u32[]{:S(2)}) collective-permute-start(bf16[128,1152]{1,0:T(8,128)(2,1)S(1)} %get-tuple-element.100), channel_id=1, source_target_pairs={{0,12},{1,13},{2,14},{3,15},{4,0},{5,1},{6,2},{7,3},{8,4},{9,5},{1... | collective-permute-start | bytes 884744 | tf_op jit(solution)/shard_map/ppermute | solution.py:367
  69.3 0.9 %collective-permute-done.20 = bf16[128,1152]{1,0:T(8,128)(2,1)S(1)} collective-permute-done((bf16[128,1152]{1,0:T(8,128)(2,1)S(1)}, bf16[128,1152]{1,0:T(8,128)(2,1)S(1)}, u32[]{:S(2)}, u32[]{:S(2)}) %collective-permute-start.20) | collective-permute-done | bytes 294944 | tf_op jit(solution)/shard_map/ppermute | solution.py:364
  70.2 0.8 collective-permute-start.18
  71.0 0.1 add_convert_fusion
  71.1 0.0 copy-start.2
  71.1 0.0 copy-start.5
  71.2 0.1 collective-permute-done.25.refs_22_
  71.3 1.9 %collective-permute-start.26 = (bf16[128,1152]{1,0:T(8,128)(2,1)S(1)}, bf16[128,1152]{1,0:T(8,128)(2,1)S(1)}, u32[]{:S(2)}, u32[]{:S(2)}) collective-permute-start(bf16[128,1152]{1,0:T(8,128)(2,1)S(1)} %add_convert_fusion), channel_id=1, source_target_pairs={{0,4},{1,5},{2,6},{3,7},{4,8},{5,9},{6,10},{7,11},{8,12},{9,13},{1... | collective-permute-start | bytes 884744 | tf_op jit(solution)/shard_map/ppermute | solution.py:364
  73.2 4.4 %weights_grads.3 = (bf16[1,1024,384]{2,1,0:T(8,128)(2,1)}, bf16[1,1024,384]{2,1,0:T(8,128)(2,1)}, bf16[1,384,1024]{2,1,0:T(8,128)(2,1)}) custom-call(bf16[128,1152]{1,0:T(8,128)(2,1)S(1)} %copy-done, bf16[128,1152]{1,0:T(8,128)(2,1)S(1)} %collective-permute-done.1.refs_1_, bf16[128,1152]{1,0:T(8,128)(2,1)S(1)} %collective-permute-done.refs_0_.refs_2_, ...), custom_call_target="tpu_custom_call" | custom-call | flops 2415919104 | bytes 8912896 | tf_op jit(solution)/shard_map/weights_grads/pallas_call | solution.py:283
  77.6 0.0 collective-permute-done.16.refs_0_
  77.6 1.1 %collective-permute-done.18.refs_2_ = bf16[128,1152]{1,0:T(8,128)(2,1)S(1)} collective-permute-done((bf16[128,1152]{1,0:T(8,128)(2,1)S(1)}, bf16[128,1152]{1,0:T(8,128)(2,1)S(1)}, u32[]{:S(2)}, u32[]{:S(2)}) %collective-permute-start.18) | collective-permute-done | bytes 294944 | tf_op jit(solution)/shard_map/ppermute | solution.py:370
  78.7 4.5 %collective-permute-done.26.refs_3_ = bf16[128,1152]{1,0:T(8,128)(2,1)S(1)} collective-permute-done((bf16[128,1152]{1,0:T(8,128)(2,1)S(1)}, bf16[128,1152]{1,0:T(8,128)(2,1)S(1)}, u32[]{:S(2)}, u32[]{:S(2)}) %collective-permute-start.26) | collective-permute-done | bytes 294944 | tf_op jit(solution)/shard_map/ppermute | solution.py:364
  83.2 0.9 %finish.1 = (bf16[128,1024]{1,0:T(8,128)(2,1)}, bf16[8,128]{1,0:T(8,128)(2,1)}) custom-call(s32[8,128]{1,0:T(8,128)S(1)} %bitcast.8, f32[16,128]{1,0:T(8,128)S(1)} %copy-done.5, bf16[128,1152]{1,0:T(8,128)(2,1)S(1)} %collective-permute-done.16.refs_0_, bf16[128,1152]{1,0:T(8,128)(2,1)S(1)} %get-tuple-element.125.refs_1_, ...), custom_call_target="tpu_custom_call" | custom-call | tf_op jit(solution)/shard_map/finish/pallas_call | solution.py:330
  (20 shorter events, 0.0 us)
Async XLA Ops:
  2.4 5.2 %collective-permute-start.2 = (bf16[1024,384]{1,0:T(8,128)(2,1)}, bf16[1024,384]{1,0:T(8,128)(2,1)S(1)}, u32[]{:S(2)}, u32[]{:S(2)}) collective-permute-start(bf16[1024,384]{1,0:T(8,128)(2,1)} %bitcast.9), channel_id=1, source_target_pairs={{0,1},{1,0},{2,3},{3,2},{4,5},{5,4},{6,7},{7,6},{8,9},{9,8},{10,11... | collective-permute-start | bytes 2359304 | tf_op jit(solution)/shard_map/ppermute | solution.py:373
  2.9 6.3 %collective-permute-start.3 = (bf16[1024,384]{1,0:T(8,128)(2,1)}, bf16[1024,384]{1,0:T(8,128)(2,1)S(1)}, u32[]{:S(2)}, u32[]{:S(2)}) collective-permute-start(bf16[1024,384]{1,0:T(8,128)(2,1)} %bitcast.14), channel_id=1, source_target_pairs={{0,1},{1,0},{2,3},{3,2},{4,5},{5,4},{6,7},{7,6},{8,9},{9,8},{10,11... | collective-permute-start | bytes 2359304 | tf_op jit(solution)/shard_map/ppermute | solution.py:373
  3.0 6.7 %collective-permute-start.4 = (bf16[384,1024]{1,0:T(8,128)(2,1)}, bf16[384,1024]{1,0:T(8,128)(2,1)S(1)}, u32[]{:S(2)}, u32[]{:S(2)}) collective-permute-start(bf16[384,1024]{1,0:T(8,128)(2,1)} %bitcast.19), channel_id=1, source_target_pairs={{0,1},{1,0},{2,3},{3,2},{4,5},{5,4},{6,7},{7,6},{8,9},{9,8},{10,11... | collective-permute-start | bytes 2359304 | tf_op jit(solution)/shard_map/ppermute | solution.py:373
  3.4 21.4 %copy-start = (bf16[128,1152]{1,0:T(8,128)(2,1)S(1)}, bf16[128,1152]{1,0:T(8,128)(2,1)}, u32[]{:S(2)}) copy-start(bf16[128,1152]{1,0:T(8,128)(2,1)} %get-tuple-element.69.refs_0_) | copy-start | bytes 884740
  3.4 21.4 %copy-start.1 = (bf16[128,1024]{1,0:T(8,128)(2,1)S(1)}, bf16[128,1024]{1,0:T(8,128)(2,1)}, u32[]{:S(2)}) copy-start(bf16[128,1024]{1,0:T(8,128)(2,1)} %refs_8_.3) | copy-start | bytes 786436
  3.4 12.8 %collective-permute-start = (bf16[128,1152]{1,0:T(8,128)(2,1)}, bf16[128,1152]{1,0:T(8,128)(2,1)S(1)}, u32[]{:S(2)}, u32[]{:S(2)}) collective-permute-start(bf16[128,1152]{1,0:T(8,128)(2,1)} %get-tuple-element.69.refs_0_), channel_id=1, source_target_pairs={{0,4},{1,5},{2,6},{3,7},{4,8},{5,9},{6,10},{7,11},{8,12},{9,13},{1... | collective-permute-start | bytes 884744 | tf_op jit(solution)/shard_map/ppermute | solution.py:364
  6.1 10.2 %collective-permute-start.1 = (bf16[128,1152]{1,0:T(8,128)(2,1)}, bf16[128,1152]{1,0:T(8,128)(2,1)S(1)}, u32[]{:S(2)}, u32[]{:S(2)}) collective-permute-start(bf16[128,1152]{1,0:T(8,128)(2,1)} %get-tuple-element.69.refs_0_), channel_id=1, source_target_pairs={{0,2},{1,3},{2,0},{3,1},{4,6},{5,7},{6,4},{7,5},{8,10},{9,11},{10,... | collective-permute-start | bytes 884744 | tf_op jit(solution)/shard_map/ppermute | solution.py:370
  7.6 14.3 %collective-permute-start.7 = (bf16[128,1024]{1,0:T(8,128)(2,1)}, bf16[128,1024]{1,0:T(8,128)(2,1)S(1)}, u32[]{:S(2)}, u32[]{:S(2)}) collective-permute-start(bf16[128,1024]{1,0:T(8,128)(2,1)} %refs_8_.3), channel_id=1, source_target_pairs={{0,4},{1,5},{2,6},{3,7},{4,8},{5,9},{6,10},{7,11},{8,12},{9,13},{1... | collective-permute-start | bytes 786440 | tf_op jit(solution)/shard_map/ppermute | solution.py:364
  9.2 12.7 %collective-permute-start.8 = (bf16[128,1024]{1,0:T(8,128)(2,1)}, bf16[128,1024]{1,0:T(8,128)(2,1)S(1)}, u32[]{:S(2)}, u32[]{:S(2)}) collective-permute-start(bf16[128,1024]{1,0:T(8,128)(2,1)} %refs_8_.3), channel_id=1, source_target_pairs={{0,2},{1,3},{2,0},{3,1},{4,6},{5,7},{6,4},{7,5},{8,10},{9,11},{10,... | collective-permute-start | bytes 786440 | tf_op jit(solution)/shard_map/ppermute | solution.py:370
  9.7 0.7 copy-start.3
  10.4 14.5 %copy-start.6 = (bf16[1,1024,384]{2,1,0:T(8,128)(2,1)S(1)}, bf16[1,1024,384]{2,1,0:T(8,128)(2,1)}, u32[]{:S(2)}) copy-start(bf16[1,1024,384]{2,1,0:T(8,128)(2,1)} %param.13) | copy-start | bytes 2359300
  10.4 14.5 %copy-start.7 = (bf16[1,1024,384]{2,1,0:T(8,128)(2,1)S(1)}, bf16[1,1024,384]{2,1,0:T(8,128)(2,1)}, u32[]{:S(2)}) copy-start(bf16[1,1024,384]{2,1,0:T(8,128)(2,1)} %param.14) | copy-start | bytes 2359300
  10.4 14.5 %copy-start.8 = (bf16[1,384,1024]{2,1,0:T(8,128)(2,1)S(1)}, bf16[1,384,1024]{2,1,0:T(8,128)(2,1)}, u32[]{:S(2)}) copy-start(bf16[1,384,1024]{2,1,0:T(8,128)(2,1)} %param.15) | copy-start | bytes 2359300
  10.4 0.6 copy-start.4
  16.2 12.7 %collective-permute-start.5 = (bf16[128,1152]{1,0:T(8,128)(2,1)S(1)}, bf16[128,1152]{1,0:T(8,128)(2,1)S(1)}, u32[]{:S(2)}, u32[]{:S(2)}) collective-permute-start(bf16[128,1152]{1,0:T(8,128)(2,1)S(1)} %collective-permute-done.refs_0_.refs_2_), channel_id=1, source_target_pairs={{0,4},{1,5},{2,6},{3,7},{4,8},{5,9},{6,10},{7,11},{8,12},{9,13},{1... | collective-permute-start | bytes 884744 | tf_op jit(solution)/shard_map/ppermute | solution.py:364
  17.7 11.2 %collective-permute-start.6 = (bf16[128,1152]{1,0:T(8,128)(2,1)S(1)}, bf16[128,1152]{1,0:T(8,128)(2,1)S(1)}, u32[]{:S(2)}, u32[]{:S(2)}) collective-permute-start(bf16[128,1152]{1,0:T(8,128)(2,1)S(1)} %collective-permute-done.refs_0_.refs_2_), channel_id=1, source_target_pairs={{0,2},{1,3},{2,0},{3,1},{4,6},{5,7},{6,4},{7,5},{8,10},{9,11},{10,... | collective-permute-start | bytes 884744 | tf_op jit(solution)/shard_map/ppermute | solution.py:370
  21.9 11.9 %collective-permute-start.9 = (bf16[128,1024]{1,0:T(8,128)(2,1)S(1)}, bf16[128,1024]{1,0:T(8,128)(2,1)S(1)}, u32[]{:S(2)}, u32[]{:S(2)}) collective-permute-start(bf16[128,1024]{1,0:T(8,128)(2,1)S(1)} %collective-permute-done.7.refs_2_.refs_10_), channel_id=1, source_target_pairs={{0,4},{1,5},{2,6},{3,7},{4,8},{5,9},{6,10},{7,11},{8,12},{9,13},{1... | collective-permute-start | bytes 786440 | tf_op jit(solution)/shard_map/ppermute | solution.py:364
  23.3 10.5 %collective-permute-start.10 = (bf16[128,1024]{1,0:T(8,128)(2,1)S(1)}, bf16[128,1024]{1,0:T(8,128)(2,1)S(1)}, u32[]{:S(2)}, u32[]{:S(2)}) collective-permute-start(bf16[128,1024]{1,0:T(8,128)(2,1)S(1)} %collective-permute-done.7.refs_2_.refs_10_), channel_id=1, source_target_pairs={{0,2},{1,3},{2,0},{3,1},{4,6},{5,7},{6,4},{7,5},{8,10},{9,11},{10,... | collective-permute-start | bytes 786440 | tf_op jit(solution)/shard_map/ppermute | solution.py:370
  28.9 11.9 %collective-permute-start.11 = (bf16[128,1152]{1,0:T(8,128)(2,1)S(1)}, bf16[128,1152]{1,0:T(8,128)(2,1)S(1)}, u32[]{:S(2)}, u32[]{:S(2)}) collective-permute-start(bf16[128,1152]{1,0:T(8,128)(2,1)S(1)} %collective-permute-done.5.refs_0_.refs_4_), channel_id=1, source_target_pairs={{0,4},{1,5},{2,6},{3,7},{4,8},{5,9},{6,10},{7,11},{8,12},{9,13},{1... | collective-permute-start | bytes 884744 | tf_op jit(solution)/shard_map/ppermute | solution.py:364
  30.5 10.3 %collective-permute-start.12 = (bf16[128,1152]{1,0:T(8,128)(2,1)S(1)}, bf16[128,1152]{1,0:T(8,128)(2,1)S(1)}, u32[]{:S(2)}, u32[]{:S(2)}) collective-permute-start(bf16[128,1152]{1,0:T(8,128)(2,1)S(1)} %collective-permute-done.5.refs_0_.refs_4_), channel_id=1, source_target_pairs={{0,2},{1,3},{2,0},{3,1},{4,6},{5,7},{6,4},{7,5},{8,10},{9,11},{10,... | collective-permute-start | bytes 884744 | tf_op jit(solution)/shard_map/ppermute | solution.py:370
  33.8 11.7 %collective-permute-start.14 = (bf16[128,1024]{1,0:T(8,128)(2,1)S(1)}, bf16[128,1024]{1,0:T(8,128)(2,1)S(1)}, u32[]{:S(2)}, u32[]{:S(2)}) collective-permute-start(bf16[128,1024]{1,0:T(8,128)(2,1)S(1)} %collective-permute-done.9.refs_2_.refs_12_), channel_id=1, source_target_pairs={{0,4},{1,5},{2,6},{3,7},{4,8},{5,9},{6,10},{7,11},{8,12},{9,13},{1... | collective-permute-start | bytes 786440 | tf_op jit(solution)/shard_map/ppermute | solution.py:364
  35.3 10.8 %collective-permute-start.15 = (bf16[128,1024]{1,0:T(8,128)(2,1)S(1)}, bf16[128,1024]{1,0:T(8,128)(2,1)S(1)}, u32[]{:S(2)}, u32[]{:S(2)}) collective-permute-start(bf16[128,1024]{1,0:T(8,128)(2,1)S(1)} %collective-permute-done.9.refs_2_.refs_12_), channel_id=1, source_target_pairs={{0,2},{1,3},{2,0},{3,1},{4,6},{5,7},{6,4},{7,5},{8,10},{9,11},{10,... | collective-permute-start | bytes 786440 | tf_op jit(solution)/shard_map/ppermute | solution.py:370
  40.8 13.9 %collective-permute-start.13 = (bf16[128,1152]{1,0:T(8,128)(2,1)S(1)}, bf16[128,1152]{1,0:T(8,128)(2,1)S(1)}, u32[]{:S(2)}, u32[]{:S(2)}) collective-permute-start(bf16[128,1152]{1,0:T(8,128)(2,1)S(1)} %collective-permute-done.11.refs_0_.refs_6_), channel_id=1, source_target_pairs={{0,2},{1,3},{2,0},{3,1},{4,6},{5,7},{6,4},{7,5},{8,10},{9,11},{10,... | collective-permute-start | bytes 884744 | tf_op jit(solution)/shard_map/ppermute | solution.py:370
  46.1 8.6 %collective-permute-start.21 = (bf16[128,1024]{1,0:T(8,128)(2,1)S(1)}, bf16[128,1024]{1,0:T(8,128)(2,1)S(1)}, u32[]{:S(2)}, u32[]{:S(2)}) collective-permute-start(bf16[128,1024]{1,0:T(8,128)(2,1)S(1)} %collective-permute-done.15.refs_3_.refs_13_), channel_id=1, source_target_pairs={{0,4},{1,5},{2,6},{3,7},{4,8},{5,9},{6,10},{7,11},{8,12},{9,13},{1... | collective-permute-start | bytes 786440 | tf_op jit(solution)/shard_map/ppermute | solution.py:364
  51.2 9.8 %collective-permute-start.19 = (bf16[128,1152]{1,0:T(8,128)(2,1)S(1)}, bf16[128,1152]{1,0:T(8,128)(2,1)S(1)}, u32[]{:S(2)}, u32[]{:S(2)}) collective-permute-start(bf16[128,1152]{1,0:T(8,128)(2,1)S(1)} %get-tuple-element.105), channel_id=1, source_target_pairs={{0,2},{1,3},{2,0},{3,1},{4,6},{5,7},{6,4},{7,5},{8,10},{9,11},{10,... | collective-permute-start | bytes 884744 | tf_op jit(solution)/shard_map/ppermute | solution.py:370
  54.8 12.5 %collective-permute-start.17 = (bf16[128,1152]{1,0:T(8,128)(2,1)S(1)}, bf16[128,1152]{1,0:T(8,128)(2,1)S(1)}, u32[]{:S(2)}, u32[]{:S(2)}) collective-permute-start(bf16[128,1152]{1,0:T(8,128)(2,1)S(1)} %get-tuple-element.103), channel_id=1, source_target_pairs={{0,12},{1,13},{2,14},{3,15},{4,0},{5,1},{6,2},{7,3},{8,4},{9,5},{1... | collective-permute-start | bytes 884744 | tf_op jit(solution)/shard_map/ppermute | solution.py:367
  59.1 8.3 %collective-permute-start.22 = (bf16[128,1152]{1,0:T(8,128)(2,1)S(1)}, bf16[128,1152]{1,0:T(8,128)(2,1)S(1)}, u32[]{:S(2)}, u32[]{:S(2)}) collective-permute-start(bf16[128,1152]{1,0:T(8,128)(2,1)S(1)} %get-tuple-element.109), channel_id=1, source_target_pairs={{0,2},{1,3},{2,0},{3,1},{4,6},{5,7},{6,4},{7,5},{8,10},{9,11},{10,... | collective-permute-start | bytes 884744 | tf_op jit(solution)/shard_map/ppermute | solution.py:370
  61.1 9.1 %collective-permute-start.20 = (bf16[128,1152]{1,0:T(8,128)(2,1)S(1)}, bf16[128,1152]{1,0:T(8,128)(2,1)S(1)}, u32[]{:S(2)}, u32[]{:S(2)}) collective-permute-start(bf16[128,1152]{1,0:T(8,128)(2,1)S(1)} %add_convert_fusion.1), channel_id=1, source_target_pairs={{0,4},{1,5},{2,6},{3,7},{4,8},{5,9},{6,10},{7,11},{8,12},{9,13},{1... | collective-permute-start | bytes 884744 | tf_op jit(solution)/shard_map/ppermute | solution.py:364
  66.7 4.4 %collective-permute-start.23 = (bf16[1024,384]{1,0:T(8,128)(2,1)S(1)}, bf16[1024,384]{1,0:T(8,128)(2,1)S(1)}, u32[]{:S(2)}, u32[]{:S(2)}) collective-permute-start(bf16[1024,384]{1,0:T(8,128)(2,1)S(1)} %get-tuple-element.113), channel_id=1, source_target_pairs={{0,1},{1,0},{2,3},{3,2},{4,5},{5,4},{6,7},{7,6},{8,9},{9,8},{10,11... | collective-permute-start | bytes 2359304 | tf_op jit(solution)/shard_map/ppermute | solution.py:373
  66.8 4.4 %collective-permute-start.24 = (bf16[1024,384]{1,0:T(8,128)(2,1)S(1)}, bf16[1024,384]{1,0:T(8,128)(2,1)S(1)}, u32[]{:S(2)}, u32[]{:S(2)}) collective-permute-start(bf16[1024,384]{1,0:T(8,128)(2,1)S(1)} %get-tuple-element.114), channel_id=1, source_target_pairs={{0,1},{1,0},{2,3},{3,2},{4,5},{5,4},{6,7},{7,6},{8,9},{9,8},{10,11... | collective-permute-start | bytes 2359304 | tf_op jit(solution)/shard_map/ppermute | solution.py:373
  67.3 4.0 %collective-permute-start.25 = (bf16[384,1024]{1,0:T(8,128)(2,1)S(1)}, bf16[384,1024]{1,0:T(8,128)(2,1)S(1)}, u32[]{:S(2)}, u32[]{:S(2)}) collective-permute-start(bf16[384,1024]{1,0:T(8,128)(2,1)S(1)} %get-tuple-element.115), channel_id=1, source_target_pairs={{0,1},{1,0},{2,3},{3,2},{4,5},{5,4},{6,7},{7,6},{8,9},{9,8},{10,11... | collective-permute-start | bytes 2359304 | tf_op jit(solution)/shard_map/ppermute | solution.py:373
  67.4 10.2 %collective-permute-start.16 = (bf16[128,1152]{1,0:T(8,128)(2,1)S(1)}, bf16[128,1152]{1,0:T(8,128)(2,1)S(1)}, u32[]{:S(2)}, u32[]{:S(2)}) collective-permute-start(bf16[128,1152]{1,0:T(8,128)(2,1)S(1)} %get-tuple-element.100), channel_id=1, source_target_pairs={{0,12},{1,13},{2,14},{3,15},{4,0},{5,1},{6,2},{7,3},{8,4},{9,5},{1... | collective-permute-start | bytes 884744 | tf_op jit(solution)/shard_map/ppermute | solution.py:367
  70.2 8.5 %collective-permute-start.18 = (bf16[128,1152]{1,0:T(8,128)(2,1)S(1)}, bf16[128,1152]{1,0:T(8,128)(2,1)S(1)}, u32[]{:S(2)}, u32[]{:S(2)}) collective-permute-start(bf16[128,1152]{1,0:T(8,128)(2,1)S(1)} %add_convert_fusion.2), channel_id=1, source_target_pairs={{0,2},{1,3},{2,0},{3,1},{4,6},{5,7},{6,4},{7,5},{8,10},{9,11},{10,... | collective-permute-start | bytes 884744 | tf_op jit(solution)/shard_map/ppermute | solution.py:370
  71.1 12.1 %copy-start.2 = (s32[128,8]{0,1:T(8,128)S(1)}, s32[128,8]{0,1:T(8,128)}, u32[]{:S(2)}) copy-start(s32[128,8]{0,1:T(8,128)} %param.11) | copy-start | bytes 12292
  71.1 12.1 %copy-start.5 = (f32[16,128]{1,0:T(8,128)S(1)}, f32[16,128]{1,0:T(8,128)}, u32[]{:S(2)}) copy-start(f32[16,128]{1,0:T(8,128)} %copy-done.4) | copy-start | bytes 24580
  71.3 11.9 %collective-permute-start.26 = (bf16[128,1152]{1,0:T(8,128)(2,1)S(1)}, bf16[128,1152]{1,0:T(8,128)(2,1)S(1)}, u32[]{:S(2)}, u32[]{:S(2)}) collective-permute-start(bf16[128,1152]{1,0:T(8,128)(2,1)S(1)} %add_convert_fusion), channel_id=1, source_target_pairs={{0,4},{1,5},{2,6},{3,7},{4,8},{5,9},{6,10},{7,11},{8,12},{9,13},{1... | collective-permute-start | bytes 884744 | tf_op jit(solution)/shard_map/ppermute | solution.py:364

commit v7 on v6

--- a/solution.py
+++ b/solution.py
@@ -114,80 +114,51 @@
 
 
 def rows_kernel(slots, *refs):
-    xg_in, dy_in = refs[:slots], refs[slots : 2 * slots]
+    xg, dy = refs[:slots], refs[slots : 2 * slots]
     weights = refs[2 * slots : 2 * slots + 6]
     dxg, act = refs[2 * slots + 6 : 3 * slots + 6], refs[3 * slots + 6]
-    xg, dy, w_gu, w_dn, sem = refs[3 * slots + 7 :]
-    tokens, width = dy_in[0].shape
+    tokens, width = dy[0].shape
     hidden = weights[2].shape[0]
-    lanes = xg.shape[1] - width
-    copies = []
-
-    def fetch(src, dst):
-        copies.append(pltpu.make_async_copy(src, dst, sem.at[len(copies)]))
-        copies[-1].start()
-        return copies[-1]
-
-    def fetch_weights(j):
-        up = [
-            fetch(weights[3 * j], w_gu.at[j, :, pl.ds(0, hidden)]),
-            fetch(weights[3 * j + 1], w_gu.at[j, :, pl.ds(hidden, hidden)]),
-        ]
-        return up, [fetch(weights[3 * j + 2], w_dn.at[j])]
-
-    got_x = [fetch(xg_in[i], xg.at[pl.ds(i * tokens, tokens)]) for i in range(slots)]
-    own = fetch_weights(0)
-    got_dy = [fetch(dy_in[i], dy.at[pl.ds(i * tokens, tokens)]) for i in range(slots)]
-    sibling = fetch_weights(1)
-    for c in got_x + own[0]:
-        c.wait()
-
-    rows = slots * tokens
-    block = math.gcd(rows, max(ROW_BLOCK, tokens))
+    lanes = xg[0].shape[1] - width
+    per = max(1, ROW_BLOCK // tokens)
     me = lax.axis_index("expert")
-    lane = lane_iota(block, lanes)
-
-    def expert(j, at, after_up):
-        here = pl.ds(at, block)
-        pre = jnp.dot(xg[here, :width], w_gu[j], preferred_element_type=f32)
-        after_up()
-        back = lax.dot_general(dy[here, :], w_dn[j], nt, preferred_element_type=f32)
-        column = lane == (me if j == 0 else me ^ 1)
-        gate = jnp.sum(
-            jnp.where(column, xg[here, width:].astype(f32), 0.0), axis=1, keepdims=True
-        )
-        a, b = pre[:, :hidden], pre[:, hidden:]
-        sig = jax.nn.sigmoid(a)
-        silu = a * sig
-        h = silu * b
-        gg = jnp.sum(h.astype(bf16).astype(f32) * back, axis=1, keepdims=True)
-        scaled = gate * back
-        da = (scaled * b * sig * (1.0 + a * (1.0 - sig))).astype(bf16)
-        db = (scaled * silu).astype(bf16)
-        grads = jnp.concatenate([da, db], axis=1)
-        first = j * 3 * hidden
-        act[here, first : first + 2 * hidden] = grads
-        act[here, first + 2 * hidden : first + 3 * hidden] = (gate * h).astype(bf16)
-        dx = lax.dot_general(grads, w_gu[j], nt, preferred_element_type=f32)
-        return dx, jnp.where(column, gg, 0.0)
-
-    def wait_all(group):
-        for c in group:
-            c.wait()
-
-    for at in range(0, rows, block):
-        first = at == 0
-        dx0, gg0 = expert(0, at, lambda: wait_all(got_dy + own[1]) if first else None)
-        if first:
-            wait_all(sibling[0] + sibling[1])
-        dx1, gg1 = expert(1, at, lambda: None)
-        dx = (dx0 + dx1).astype(bf16)
-        gg = (gg0 + gg1).astype(bf16)
-        for i in range(block // tokens):
-            out = dxg[at // tokens + i]
-            part = slice(i * tokens, (i + 1) * tokens)
-            out[:, :width] = dx[part]
-            out[:, width:] = gg[part]
+
+    def stack(parts):
+        return parts[0] if len(parts) == 1 else jnp.concatenate(parts, axis=0)
+
+    for at in range(0, slots, per):
+        group = range(at, min(slots, at + per))
+        x = stack([xg[i][:, :width] for i in group])
+        up_grad = stack([dy[i][...] for i in group])
+        gates = stack([xg[i][:, width:].astype(f32) for i in group])
+        here = pl.ds(at * tokens, len(group) * tokens)
+        lane = lane_iota(len(group) * tokens, lanes)
+        dx, gg = 0.0, 0.0
+        for j in range(2):
+            w_gate, w_up, w_down = weights[3 * j : 3 * j + 3]
+            a = jnp.dot(x, w_gate[...], preferred_element_type=f32)
+            b = jnp.dot(x, w_up[...], preferred_element_type=f32)
+            back = lax.dot_general(up_grad, w_down[...], nt, preferred_element_type=f32)
+            column = lane == (me if j == 0 else me ^ 1)
+            gate = jnp.sum(jnp.where(column, gates, 0.0), axis=1, keepdims=True)
+            sig = jax.nn.sigmoid(a)
+            silu = a * sig
+            h = silu * b
+            dots = jnp.sum(h.astype(bf16).astype(f32) * back, axis=1, keepdims=True)
+            scaled = gate * back
+            da = (scaled * b * sig * (1.0 + a * (1.0 - sig))).astype(bf16)
+            db = (scaled * silu).astype(bf16)
+            first = j * 3 * hidden
+            act[here, first : first + hidden] = da
+            act[here, first + hidden : first + 2 * hidden] = db
+            act[here, first + 2 * hidden : first + 3 * hidden] = (gate * h).astype(bf16)
+            dx += lax.dot_general(da, w_gate[...], nt, preferred_element_type=f32)
+            dx += lax.dot_general(db, w_up[...], nt, preferred_element_type=f32)
+            gg += jnp.where(column, dots, 0.0)
+        for k, i in enumerate(group):
+            part = slice(k * tokens, (k + 1) * tokens)
+            dxg[i][:, :width] = dx[part].astype(bf16)
+            dxg[i][:, width:] = gg[part].astype(bf16)
 
 
 def rows_grads(xgs, dys, weights):
@@ -202,15 +173,8 @@
         functools.partial(rows_kernel, slots),
         out_shape=tuple(jax.ShapeDtypeStruct((tokens, full), bf16) for _ in dys)
         + (jax.ShapeDtypeStruct((rows, 6 * hidden), bf16),),
-        in_specs=[ANY] * (2 * slots + 6),
+        in_specs=[VMEM] * (2 * slots + 6),
         out_specs=(VMEM,) * (slots + 1),
-        scratch_shapes=[
-            pltpu.VMEM((rows, full), bf16),
-            pltpu.VMEM((rows, width), bf16),
-            pltpu.VMEM((2, width, 2 * hidden), bf16),
-            pltpu.VMEM((2, hidden, width), bf16),
-            pltpu.SemaphoreType.DMA((2 * slots + 6,)),
-        ],
         compiler_params=params(20),
         cost_estimate=pl.CostEstimate(
             flops=flops, bytes_accessed=moved, transcendentals=2 * rows * hidden
@@ -227,18 +191,20 @@
     x, dy, act, sem = refs[3:]
     tokens, width = dy_in[0].shape
     hidden = act.shape[1] // 3
-    step_rows = act_in[0].shape[0]
     copies = []
 
     def fetch(src, dst):
         copies.append(pltpu.make_async_copy(src, dst, sem.at[len(copies)]))
         copies[-1].start()
 
+    row = 0
     for i in range(steps):
+        step_rows = act_in[i].shape[0]
         fetch(
             act_in[i].at[:, pl.ds(j * 3 * hidden, 3 * hidden)],
-            act.at[pl.ds(i * step_rows, step_rows)],
+            act.at[pl.ds(row, step_rows)],
         )
+        row += step_rows
     for i in range(slots):
         fetch(xg_in[i].at[:, pl.ds(0, width)], x.at[pl.ds(i * tokens, tokens)])
     for i in range(slots):
@@ -378,7 +344,6 @@
     ids = expert_ids.T
     xg, kept = plan(replica_table[None], ids, gates.T, tokens_in, devices, lanes)
     own = (w_gate[0], w_up[0], w_down[0])
-    own, kept = together(own, kept)
     weights = own + tuple(send_core(w) for w in own)
 
     per = max(1, W_ROWS // (inner * tokens))
@@ -390,7 +355,7 @@
             j,
             [x for z in group for x in xgs[z]],
             [d for z in group for d in dys[z]],
-            [acts[z] for z in group],
+            [act for z in group for act in acts[z]],
             dtype,
             more,
         )
@@ -413,7 +378,7 @@
             if z < outer:
                 ahead = send_z(last[0])
             for y in range(1, inner):
-                if k and z == outer > 1 and y == inner - 1:
+                if k == 0 and z == outer > 1 and y == inner - 1:
                     last.append(send_z(stream[z - 2][y]))
                 else:
                     last.append(send_y(last[y - 1]))
@@ -421,7 +386,8 @@
             if inner > 1:
                 done.append(last[-1])
             if k == 0 and z == 1:
-                kept, weights = together(kept, weights)
+                done, weights = together(done, weights)
+            elif z == 1:
                 done, kept = together(done, hold(kept, HOLD))
             elif k == 0:
                 done, acts[z - 2] = together(done, acts[z - 2])
@@ -431,9 +397,14 @@
                 last[-1] = done.pop()
             if ahead is not None:
                 stream.append([done.pop()])
-        *dx, act = rows_grads(xgs[z - 1], dys[z - 1], weights)
-        dxs.append(dx)
-        acts.append(act)
+        cut = inner - 1 if z > 2 else inner
+        dxs.append([])
+        acts.append([])
+        for part in (slice(0, cut), slice(cut, inner)):
+            if xgs[z - 1][part]:
+                *dx, act = rows_grads(xgs[z - 1][part], dys[z - 1][part], weights)
+                dxs[-1] += dx
+                acts[-1].append(act)
         if z > 2:
             across.append(send_across(z - 1))
         if len(groups) > 1 and z - 1 == groups[(z - 1) // per][-1]:

time: 84.9 us -> 86.4 us (1.018)
  waiting for transfers between devices: 23.5 us -> 30.8 us
  starting transfers between devices: 31.5 us -> 26.1 us
    ppermute x9, starting transfers between devices: 15.3 us -> 8.08 us  [send_z(): lax.ppermute(v, 'expert', [(i, moved(i, 1, 0)) for i in range(devices)])]
    ppermute x9, waiting for transfers between devices: 21.7 us -> 27.4 us  [send_z(): lax.ppermute(v, 'expert', [(i, moved(i, 1, 0)) for i in range(devices)])]
    ppermute x2, starting transfers between devices: 2.16 us -> 5.29 us  [send_down(): lax.ppermute(v, 'expert', [(i, moved(i, -1, 0)) for i in range(devices)])]
    ppermute x10, waiting for transfers between devices: 1.74 us -> 2.86 us  [send_y(): lax.ppermute(v, 'expert', [(i, moved(i, 0, 1)) for i in range(devices)])]
    pallas_call x4 -> x6, Pallas kernels: 16 us -> 16.7 us  [rows_grads(): pl.pallas_call(functools.partial(rows_kernel, slots), out_shape=tuple((ja...]
  transfers between devices with their start and end apart: 27 -> 27, of which waited for: 10 -> 10; matrix products, arithmetic and copies ran while one was open for 0% -> 0% of each run, Pallas kernels for 29% -> 31%
where the time goes in v7:
time: 86.4 us; the launch traced here: 86.2 us
  waiting for transfers between devices  30.8 us (36%)
  Pallas kernels  27.4 us (32%)
  starting transfers between devices  26.1 us (30%)
    ppermute x9, waiting for transfers between devices, send_z(): lax.ppermute(v, 'expert', [(i, moved(i, 1, 0)) for i in range(devices)])  27.4 us
    pallas_call x6, Pallas kernels, rows_grads(): pl.pallas_call(functools.partial(rows_kernel, slots), out_shape=tuple((ja...  16.7 us
    ppermute x10, starting transfers between devices, send_y(): lax.ppermute(v, 'expert', [(i, moved(i, 0, 1)) for i in range(devices)])  11.6 us
    ppermute x9, starting transfers between devices, send_z(): lax.ppermute(v, 'expert', [(i, moved(i, 1, 0)) for i in range(devices)])  8.08 us
    pallas_call x2, Pallas kernels, weights_grads(): pl.pallas_call(functools.partial(weights_kernel, j, slots, steps, len(mor...  8.01 us
    ppermute x2, starting transfers between devices, send_down(): lax.ppermute(v, 'expert', [(i, moved(i, -1, 0)) for i in range(devices)])  5.29 us
    ppermute x10, waiting for transfers between devices, send_y(): lax.ppermute(v, 'expert', [(i, moved(i, 0, 1)) for i in range(devices)])  2.86 us
    pallas_call x1, Pallas kernels, plan(): pl.pallas_call(functools.partial(plan_kernel, home_cap, rep_cap), out_sha...  1.75 us
  transfers between devices with their start and end apart: 27, of which 10 were waited for; matrix products, arithmetic and copies ran while one was open for 0% of the time, Pallas kernels for 31%

profile of v7, /device:TPU:0, one launch (start us, length us, event | category | flops | bytes accessed | tf_op | source)
XLA Modules:
  0.0 86.2 jit_solution(10854424311438327463)
XLA Ops:
  0.6 3.1 %collective-permute-start = (bf16[128,1024]{1,0:T(8,128)(2,1)}, bf16[128,1024]{1,0:T(8,128)(2,1)S(1)}, u32[]{:S(2)}, u32[]{:S(2)}) collective-permute-start(bf16[128,1024]{1,0:T(8,128)(2,1)} %refs_8_.3), channel_id=1, source_target_pairs={{0,4},{1,5},{2,6},{3,7},{4,8},{5,9},{6,10},{7,11},{8,12},{9,13},{1... | collective-permute-start | bytes 786440 | tf_op jit(solution)/shard_map/ppermute | solution.py:330
  3.7 1.5 %collective-permute-start.1 = (bf16[128,1024]{1,0:T(8,128)(2,1)}, bf16[128,1024]{1,0:T(8,128)(2,1)S(1)}, u32[]{:S(2)}, u32[]{:S(2)}) collective-permute-start(bf16[128,1024]{1,0:T(8,128)(2,1)} %refs_8_.3), channel_id=1, source_target_pairs={{0,2},{1,3},{2,0},{3,1},{4,6},{5,7},{6,4},{7,5},{8,10},{9,11},{10,... | collective-permute-start | bytes 786440 | tf_op jit(solution)/shard_map/ppermute | solution.py:336
  5.2 1.7 %plan.1 = (bf16[128,1152]{1,0:T(8,128)(2,1)}, f32[16,128]{1,0:T(8,128)}) custom-call(s32[1,16]{1,0:T(1,128)} %bitcast.31, s32[8,128]{1,0:T(8,128)} %bitcast.28, bf16[8,128]{1,0:T(8,128)(2,1)} %bitcast.30, bf16[128,1024]{1,0:T(8,128)(2,1)} %x_in.1), custom_call_target="tpu_custom_call" | custom-call | tf_op jit(solution)/shard_map/plan/pallas_call | solution.py:84
  7.0 1.6 %collective-permute-start.2 = (bf16[128,1152]{1,0:T(8,128)(2,1)}, bf16[128,1152]{1,0:T(8,128)(2,1)S(1)}, u32[]{:S(2)}, u32[]{:S(2)}) collective-permute-start(bf16[128,1152]{1,0:T(8,128)(2,1)} %get-tuple-element.70.refs_0_), channel_id=1, source_target_pairs={{0,4},{1,5},{2,6},{3,7},{4,8},{5,9},{6,10},{7,11},{8,12},{9,13},{1... | collective-permute-start | bytes 884744 | tf_op jit(solution)/shard_map/ppermute | solution.py:330
  8.6 0.5 collective-permute-start.3
  9.1 0.0 collective-permute-start.4
  9.1 4.0 %collective-permute-done.refs_2_.refs_10_ = bf16[128,1024]{1,0:T(8,128)(2,1)S(1)} collective-permute-done((bf16[128,1024]{1,0:T(8,128)(2,1)}, bf16[128,1024]{1,0:T(8,128)(2,1)S(1)}, u32[]{:S(2)}, u32[]{:S(2)}) %collective-permute-start) | collective-permute-done | bytes 262176 | tf_op jit(solution)/shard_map/ppermute | solution.py:330
  13.1 0.5 collective-permute-start.6
  13.6 0.7 copy-done.6
  14.3 0.0 copy-start.4
  14.3 0.0 copy-start.7
  14.3 4.2 %collective-permute-done.2.refs_0_.refs_2_ = bf16[128,1152]{1,0:T(8,128)(2,1)S(1)} collective-permute-done((bf16[128,1152]{1,0:T(8,128)(2,1)}, bf16[128,1152]{1,0:T(8,128)(2,1)S(1)}, u32[]{:S(2)}, u32[]{:S(2)}) %collective-permute-start.2) | collective-permute-done | bytes 294944 | tf_op jit(solution)/shard_map/ppermute | solution.py:330
  18.6 0.0 collective-permute-done.3.refs_1_
  18.6 1.5 %collective-permute-start.10 = (bf16[128,1024]{1,0:T(8,128)(2,1)S(1)}, bf16[128,1024]{1,0:T(8,128)(2,1)S(1)}, u32[]{:S(2)}, u32[]{:S(2)}) collective-permute-start(bf16[128,1024]{1,0:T(8,128)(2,1)S(1)} %collective-permute-done.refs_2_.refs_10_), channel_id=1, source_target_pairs={{0,2},{1,3},{2,0},{3,1},{4,6},{5,7},{6,4},{7,5},{8,10},{9,11},{10,... | collective-permute-start | bytes 786440 | tf_op jit(solution)/shard_map/ppermute | solution.py:336
  20.1 0.0 collective-permute-done.4.refs_7_.refs_5_
  20.1 0.0 collective-permute-done.5.refs_8_.refs_6_
  20.1 0.0 collective-permute-done.6.refs_9_.refs_7_
  20.1 1.3 %collective-permute-start.7 = (bf16[128,1152]{1,0:T(8,128)(2,1)S(1)}, bf16[128,1152]{1,0:T(8,128)(2,1)S(1)}, u32[]{:S(2)}, u32[]{:S(2)}) collective-permute-start(bf16[128,1152]{1,0:T(8,128)(2,1)S(1)} %collective-permute-done.2.refs_0_.refs_2_), channel_id=1, source_target_pairs={{0,4},{1,5},{2,6},{3,7},{4,8},{5,9},{6,10},{7,11},{8,12},{9,13},{1... | collective-permute-start | bytes 884744 | tf_op jit(solution)/shard_map/ppermute | solution.py:330
  21.4 0.5 collective-permute-start.8
  22.0 7.7 %collective-permute-done.9.refs_1_.refs_12_ = bf16[128,1024]{1,0:T(8,128)(2,1)S(1)} collective-permute-done((bf16[128,1024]{1,0:T(8,128)(2,1)S(1)}, bf16[128,1024]{1,0:T(8,128)(2,1)S(1)}, u32[]{:S(2)}, u32[]{:S(2)}) %collective-permute-start.9) | collective-permute-done | bytes 262176 | tf_op jit(solution)/shard_map/ppermute | solution.py:330
  29.6 0.0 collective-permute-done.10.refs_3_.refs_11_
  29.6 0.0 collective-permute-start.14
  29.6 1.5 %collective-permute-start.15 = (bf16[128,1024]{1,0:T(8,128)(2,1)S(1)}, bf16[128,1024]{1,0:T(8,128)(2,1)S(1)}, u32[]{:S(2)}, u32[]{:S(2)}) collective-permute-start(bf16[128,1024]{1,0:T(8,128)(2,1)S(1)} %collective-permute-done.9.refs_1_.refs_12_), channel_id=1, source_target_pairs={{0,2},{1,3},{2,0},{3,1},{4,6},{5,7},{6,4},{7,5},{8,10},{9,11},{10,... | collective-permute-start | bytes 786440 | tf_op jit(solution)/shard_map/ppermute | solution.py:336
  31.2 3.2 %rows_grads.6 = (bf16[128,1152]{1,0:T(8,128)(2,1)S(1)}, bf16[128,1152]{1,0:T(8,128)(2,1)S(1)}, bf16[256,2304]{1,0:T(8,128)(2,1)S(1)}) custom-call(bf16[128,1152]{1,0:T(8,128)(2,1)S(1)} %copy-done.3, bf16[128,1152]{1,0:T(8,128)(2,1)S(1)} %collective-permute-done.3.refs_1_, bf16[128,1024]{1,0:T(8,128)(2,1)S(1)} %copy-done.4, ...), custom_call_target="tpu_custom_call" | custom-call | flops 2013265920 | bytes 9306112 | tf_op jit(solution)/shard_map/rows_grads/pallas_call | solution.py:172
  34.4 1.5 %collective-permute-done.7.refs_0_.refs_4_ = bf16[128,1152]{1,0:T(8,128)(2,1)S(1)} collective-permute-done((bf16[128,1152]{1,0:T(8,128)(2,1)S(1)}, bf16[128,1152]{1,0:T(8,128)(2,1)S(1)}, u32[]{:S(2)}, u32[]{:S(2)}) %collective-permute-start.7) | collective-permute-done | bytes 294944 | tf_op jit(solution)/shard_map/ppermute | solution.py:330
  35.9 0.0 collective-permute-done.8.refs_1_.refs_3_
  35.9 0.0 collective-permute-start.11
  35.9 1.5 %collective-permute-start.12 = (bf16[128,1152]{1,0:T(8,128)(2,1)S(1)}, bf16[128,1152]{1,0:T(8,128)(2,1)S(1)}, u32[]{:S(2)}, u32[]{:S(2)}) collective-permute-start(bf16[128,1152]{1,0:T(8,128)(2,1)S(1)} %collective-permute-done.7.refs_0_.refs_4_), channel_id=1, source_target_pairs={{0,2},{1,3},{2,0},{3,1},{4,6},{5,7},{6,4},{7,5},{8,10},{9,11},{10,... | collective-permute-start | bytes 884744 | tf_op jit(solution)/shard_map/ppermute | solution.py:336
  37.5 4.1 %collective-permute-done.14.refs_1_.refs_14_ = bf16[128,1024]{1,0:T(8,128)(2,1)S(1)} collective-permute-done((bf16[128,1024]{1,0:T(8,128)(2,1)S(1)}, bf16[128,1024]{1,0:T(8,128)(2,1)S(1)}, u32[]{:S(2)}, u32[]{:S(2)}) %collective-permute-start.14) | collective-permute-done | bytes 262176 | tf_op jit(solution)/shard_map/ppermute | solution.py:330
  41.6 0.0 collective-permute-done.15.refs_1_.refs_13_
  41.6 1.5 %collective-permute-start.21 = (bf16[128,1024]{1,0:T(8,128)(2,1)S(1)}, bf16[128,1024]{1,0:T(8,128)(2,1)S(1)}, u32[]{:S(2)}, u32[]{:S(2)}) collective-permute-start(bf16[128,1024]{1,0:T(8,128)(2,1)S(1)} %collective-permute-done.14.refs_1_.refs_14_), channel_id=1, source_target_pairs={{0,2},{1,3},{2,0},{3,1},{4,6},{5,7},{6,4},{7,5},{8,10},{9,11},{10,... | collective-permute-start | bytes 786440 | tf_op jit(solution)/shard_map/ppermute | solution.py:336
  43.1 3.2 %rows_grads.7 = (bf16[128,1152]{1,0:T(8,128)(2,1)S(1)}, bf16[128,1152]{1,0:T(8,128)(2,1)S(1)}, bf16[256,2304]{1,0:T(8,128)(2,1)S(1)}) custom-call(bf16[128,1152]{1,0:T(8,128)(2,1)S(1)} %collective-permute-done.2.refs_0_.refs_2_, bf16[128,1152]{1,0:T(8,128)(2,1)S(1)} %collective-permute-done.8.refs_1_.refs_3_, ...), custom_call_target="tpu_custom_call" | custom-call | flops 2013265920 | bytes 9306112 | tf_op jit(solution)/shard_map/rows_grads/pallas_call | solution.py:172
  46.3 0.0 collective-permute-done.11.refs_0_.refs_6_
  46.3 0.0 collective-permute-done.12.refs_0_.refs_5_
  46.3 1.2 %collective-permute-start.13 = (bf16[128,1152]{1,0:T(8,128)(2,1)S(1)}, bf16[128,1152]{1,0:T(8,128)(2,1)S(1)}, u32[]{:S(2)}, u32[]{:S(2)}) collective-permute-start(bf16[128,1152]{1,0:T(8,128)(2,1)S(1)} %collective-permute-done.12.refs_0_.refs_5_), channel_id=1, source_target_pairs={{0,4},{1,5},{2,6},{3,7},{4,8},{5,9},{6,10},{7,11},{8,12},{9,13},{1... | collective-permute-start | bytes 884744 | tf_op jit(solution)/shard_map/ppermute | solution.py:330
  47.6 2.6 %rows_grads.9 = (bf16[128,1152]{1,0:T(8,128)(2,1)S(1)}, bf16[128,2304]{1,0:T(8,128)(2,1)S(1)}) custom-call(bf16[128,1152]{1,0:T(8,128)(2,1)S(1)} %collective-permute-done.12.refs_0_.refs_5_, bf16[128,1024]{1,0:T(8,128)(2,1)S(1)} %collective-permute-done.15.refs_1_.refs_13_, bf16[1024,384]{1,0:T(8,128)(2,1)S(1)} %bitcast.10, bf16[1024,384]{1,0:T(8,128)(2,1)S(1)} %bitcast.17, ...), custom_call_target="tpu_custom_call" | custom-call | flops 1006632960 | bytes 7012352 | tf_op jit(solution)/shard_map/rows_grads/pallas_call | solution.py:172
  50.1 1.4 %collective-permute-start.19 = (bf16[128,1152]{1,0:T(8,128)(2,1)S(1)}, bf16[128,1152]{1,0:T(8,128)(2,1)S(1)}, u32[]{:S(2)}, u32[]{:S(2)}) collective-permute-start(bf16[128,1152]{1,0:T(8,128)(2,1)S(1)} %get-tuple-element.100), channel_id=1, source_target_pairs={{0,2},{1,3},{2,0},{3,1},{4,6},{5,7},{6,4},{7,5},{8,10},{9,11},{10,... | collective-permute-start | bytes 884744 | tf_op jit(solution)/shard_map/ppermute | solution.py:336
  51.5 0.0 collective-permute-done.21.refs_1_.refs_15_
  51.5 2.6 %rows_grads.8 = (bf16[128,1152]{1,0:T(8,128)(2,1)S(1)}, bf16[128,2304]{1,0:T(8,128)(2,1)S(1)}) custom-call(bf16[128,1152]{1,0:T(8,128)(2,1)S(1)} %collective-permute-done.7.refs_0_.refs_4_, bf16[128,1024]{1,0:T(8,128)(2,1)S(1)} %collective-permute-done.9.refs_1_.refs_12_, bf16[1024,384]{1,0:T(8,128)(2,1)S(1)} %bitcast.11, bf16[1024,384]{1,0:T(8,128)(2,1)S(1)} %bitcast.18, ...), custom_call_target="tpu_custom_call" | custom-call | flops 1006632960 | bytes 7012352 | tf_op jit(solution)/shard_map/rows_grads/pallas_call | solution.py:172
  54.1 2.6 %rows_grads.10 = (bf16[128,1152]{1,0:T(8,128)(2,1)S(1)}, bf16[128,2304]{1,0:T(8,128)(2,1)S(1)}) custom-call(bf16[128,1152]{1,0:T(8,128)(2,1)S(1)} %collective-permute-done.11.refs_0_.refs_6_, bf16[128,1024]{1,0:T(8,128)(2,1)S(1)} %collective-permute-done.14.refs_1_.refs_14_, bf16[1024,384]{1,0:T(8,128)(2,1)S(1)} %bitcast.12, bf16[1024,384]{1,0:T(8,128)(2,1)S(1)} %bitcast.19, ...), custom_call_target="tpu_custom_call" | custom-call | flops 1006632960 | bytes 7012352 | tf_op jit(solution)/shard_map/rows_grads/pallas_call | solution.py:172
  56.7 0.0 collective-permute-done.13.refs_0_.refs_7_
  56.7 2.6 %collective-permute-start.17 = (bf16[128,1152]{1,0:T(8,128)(2,1)S(1)}, bf16[128,1152]{1,0:T(8,128)(2,1)S(1)}, u32[]{:S(2)}, u32[]{:S(2)}) collective-permute-start(bf16[128,1152]{1,0:T(8,128)(2,1)S(1)} %get-tuple-element.98), channel_id=1, source_target_pairs={{0,12},{1,13},{2,14},{3,15},{4,0},{5,1},{6,2},{7,3},{8,4},{9,5},{1... | collective-permute-start | bytes 884744 | tf_op jit(solution)/shard_map/ppermute | solution.py:333
  59.3 2.6 %rows_grads.11 = (bf16[128,1152]{1,0:T(8,128)(2,1)S(1)}, bf16[128,2304]{1,0:T(8,128)(2,1)S(1)}) custom-call(bf16[128,1152]{1,0:T(8,128)(2,1)S(1)} %collective-permute-done.13.refs_0_.refs_7_, bf16[128,1024]{1,0:T(8,128)(2,1)S(1)} %collective-permute-done.21.refs_1_.refs_15_, bf16[1024,384]{1,0:T(8,128)(2,1)S(1)} %bitcast.13, bf16[1024,384]{1,0:T(8,128)(2,1)S(1)} %bitcast.20, ...), custom_call_target="tpu_custom_call" | custom-call | flops 1006632960 | bytes 7012352 | tf_op jit(solution)/shard_map/rows_grads/pallas_call | solution.py:172
  61.8 1.2 %collective-permute-start.22 = (bf16[128,1152]{1,0:T(8,128)(2,1)S(1)}, bf16[128,1152]{1,0:T(8,128)(2,1)S(1)}, u32[]{:S(2)}, u32[]{:S(2)}) collective-permute-start(bf16[128,1152]{1,0:T(8,128)(2,1)S(1)} %get-tuple-element.105), channel_id=1, source_target_pairs={{0,2},{1,3},{2,0},{3,1},{4,6},{5,7},{6,4},{7,5},{8,10},{9,11},{10,... | collective-permute-start | bytes 884744 | tf_op jit(solution)/shard_map/ppermute | solution.py:336
  63.0 0.1 add_convert_fusion.1
  63.1 0.1 collective-permute-start.20
  63.1 3.6 %weights_grads.2 = (bf16[1024,384]{1,0:T(8,128)(2,1)S(1)}, bf16[1024,384]{1,0:T(8,128)(2,1)S(1)}, bf16[384,1024]{1,0:T(8,128)(2,1)S(1)}) custom-call(bf16[128,1152]{1,0:T(8,128)(2,1)S(1)} %copy-done.3, bf16[128,1152]{1,0:T(8,128)(2,1)S(1)} %collective-permute-done.3.refs_1_, bf16[128,1152]{1,0:T(8,128)(2,1)S(1)} %collective-permute-done.2.refs_0_.refs_2_, ...), custom_call_target="tpu_custom_call" | custom-call | flops 2415919104 | bytes 8912896 | tf_op jit(solution)/shard_map/weights_grads/pallas_call | solution.py:249
  66.7 0.1 collective-permute-start.23
  66.8 0.5 collective-permute-start.24
  67.3 0.1 collective-permute-start.25
  67.4 0.1 add_convert_fusion.2
  67.5 1.2 %collective-permute-done.22 = bf16[128,1152]{1,0:T(8,128)(2,1)S(1)} collective-permute-done((bf16[128,1152]{1,0:T(8,128)(2,1)S(1)}, bf16[128,1152]{1,0:T(8,128)(2,1)S(1)}, u32[]{:S(2)}, u32[]{:S(2)}) %collective-permute-start.22) | collective-permute-done | bytes 294944 | tf_op jit(solution)/shard_map/ppermute | solution.py:336
  68.6 2.7 %collective-permute-start.16 = (bf16[128,1152]{1,0:T(8,128)(2,1)S(1)}, bf16[128,1152]{1,0:T(8,128)(2,1)S(1)}, u32[]{:S(2)}, u32[]{:S(2)}) collective-permute-start(bf16[128,1152]{1,0:T(8,128)(2,1)S(1)} %get-tuple-element.95), channel_id=1, source_target_pairs={{0,12},{1,13},{2,14},{3,15},{4,0},{5,1},{6,2},{7,3},{8,4},{9,5},{1... | collective-permute-start | bytes 884744 | tf_op jit(solution)/shard_map/ppermute | solution.py:333
  71.3 1.1 %collective-permute-done.20 = bf16[128,1152]{1,0:T(8,128)(2,1)S(1)} collective-permute-done((bf16[128,1152]{1,0:T(8,128)(2,1)S(1)}, bf16[128,1152]{1,0:T(8,128)(2,1)S(1)}, u32[]{:S(2)}, u32[]{:S(2)}) %collective-permute-start.20) | collective-permute-done | bytes 294944 | tf_op jit(solution)/shard_map/ppermute | solution.py:330
  72.4 0.5 collective-permute-start.18
  72.9 0.1 add_convert_fusion
  73.0 0.0 copy-start.5
  73.0 0.0 copy-start.8
  73.1 0.7 collective-permute-start.26
  73.8 4.4 %weights_grads.3 = (bf16[1,1024,384]{2,1,0:T(8,128)(2,1)}, bf16[1,1024,384]{2,1,0:T(8,128)(2,1)}, bf16[1,384,1024]{2,1,0:T(8,128)(2,1)}) custom-call(bf16[128,1152]{1,0:T(8,128)(2,1)S(1)} %copy-done.3, bf16[128,1152]{1,0:T(8,128)(2,1)S(1)} %collective-permute-done.3.refs_1_, bf16[128,1152]{1,0:T(8,128)(2,1)S(1)} %collective-permute-done.2.refs_0_.refs_2_, ...), custom_call_target="tpu_custom_call" | custom-call | flops 2415919104 | bytes 8912896 | tf_op jit(solution)/shard_map/weights_grads/pallas_call | solution.py:249
  78.2 0.5 collective-permute-done.16.refs_0_
  78.7 1.7 %collective-permute-done.18.refs_2_ = bf16[128,1152]{1,0:T(8,128)(2,1)S(1)} collective-permute-done((bf16[128,1152]{1,0:T(8,128)(2,1)S(1)}, bf16[128,1152]{1,0:T(8,128)(2,1)S(1)}, u32[]{:S(2)}, u32[]{:S(2)}) %collective-permute-start.18) | collective-permute-done | bytes 294944 | tf_op jit(solution)/shard_map/ppermute | solution.py:336
  80.4 4.8 %collective-permute-done.26.refs_3_ = bf16[128,1152]{1,0:T(8,128)(2,1)S(1)} collective-permute-done((bf16[128,1152]{1,0:T(8,128)(2,1)S(1)}, bf16[128,1152]{1,0:T(8,128)(2,1)S(1)}, u32[]{:S(2)}, u32[]{:S(2)}) %collective-permute-start.26) | collective-permute-done | bytes 294944 | tf_op jit(solution)/shard_map/ppermute | solution.py:330
  85.2 0.9 %finish.1 = (bf16[128,1024]{1,0:T(8,128)(2,1)}, bf16[8,128]{1,0:T(8,128)(2,1)}) custom-call(s32[8,128]{1,0:T(8,128)S(1)} %bitcast.29, f32[16,128]{1,0:T(8,128)S(1)} %copy-done.8, bf16[128,1152]{1,0:T(8,128)(2,1)S(1)} %collective-permute-done.16.refs_0_, bf16[128,1152]{1,0:T(8,128)(2,1)S(1)} %get-tuple-element.123.refs_1_, ...), custom_call_target="tpu_custom_call" | custom-call | tf_op jit(solution)/shard_map/finish/pallas_call | solution.py:296
  (22 shorter events, 0.0 us)
Async XLA Ops:
  0.6 12.4 %collective-permute-start = (bf16[128,1024]{1,0:T(8,128)(2,1)}, bf16[128,1024]{1,0:T(8,128)(2,1)S(1)}, u32[]{:S(2)}, u32[]{:S(2)}) collective-permute-start(bf16[128,1024]{1,0:T(8,128)(2,1)} %refs_8_.3), channel_id=1, source_target_pairs={{0,4},{1,5},{2,6},{3,7},{4,8},{5,9},{6,10},{7,11},{8,12},{9,13},{1... | collective-permute-start | bytes 786440 | tf_op jit(solution)/shard_map/ppermute | solution.py:330
  3.7 9.4 %collective-permute-start.1 = (bf16[128,1024]{1,0:T(8,128)(2,1)}, bf16[128,1024]{1,0:T(8,128)(2,1)S(1)}, u32[]{:S(2)}, u32[]{:S(2)}) collective-permute-start(bf16[128,1024]{1,0:T(8,128)(2,1)} %refs_8_.3), channel_id=1, source_target_pairs={{0,2},{1,3},{2,0},{3,1},{4,6},{5,7},{6,4},{7,5},{8,10},{9,11},{10,... | collective-permute-start | bytes 786440 | tf_op jit(solution)/shard_map/ppermute | solution.py:336
  7.0 11.6 %collective-permute-start.2 = (bf16[128,1152]{1,0:T(8,128)(2,1)}, bf16[128,1152]{1,0:T(8,128)(2,1)S(1)}, u32[]{:S(2)}, u32[]{:S(2)}) collective-permute-start(bf16[128,1152]{1,0:T(8,128)(2,1)} %get-tuple-element.70.refs_0_), channel_id=1, source_target_pairs={{0,4},{1,5},{2,6},{3,7},{4,8},{5,9},{6,10},{7,11},{8,12},{9,13},{1... | collective-permute-start | bytes 884744 | tf_op jit(solution)/shard_map/ppermute | solution.py:330
  8.6 10.0 %collective-permute-start.3 = (bf16[128,1152]{1,0:T(8,128)(2,1)}, bf16[128,1152]{1,0:T(8,128)(2,1)S(1)}, u32[]{:S(2)}, u32[]{:S(2)}) collective-permute-start(bf16[128,1152]{1,0:T(8,128)(2,1)} %get-tuple-element.70.refs_0_), channel_id=1, source_target_pairs={{0,2},{1,3},{2,0},{3,1},{4,6},{5,7},{6,4},{7,5},{8,10},{9,11},{10,... | collective-permute-start | bytes 884744 | tf_op jit(solution)/shard_map/ppermute | solution.py:336
  9.1 11.0 %collective-permute-start.4 = (bf16[1024,384]{1,0:T(8,128)(2,1)}, bf16[1024,384]{1,0:T(8,128)(2,1)S(1)}, u32[]{:S(2)}, u32[]{:S(2)}) collective-permute-start(bf16[1024,384]{1,0:T(8,128)(2,1)} %bitcast.7), channel_id=1, source_target_pairs={{0,1},{1,0},{2,3},{3,2},{4,5},{5,4},{6,7},{7,6},{8,9},{9,8},{10,11... | collective-permute-start | bytes 2359304 | tf_op jit(solution)/shard_map/ppermute | solution.py:339
  13.1 7.0 %collective-permute-start.5 = (bf16[1024,384]{1,0:T(8,128)(2,1)}, bf16[1024,384]{1,0:T(8,128)(2,1)S(1)}, u32[]{:S(2)}, u32[]{:S(2)}) collective-permute-start(bf16[1024,384]{1,0:T(8,128)(2,1)} %bitcast.14), channel_id=1, source_target_pairs={{0,1},{1,0},{2,3},{3,2},{4,5},{5,4},{6,7},{7,6},{8,9},{9,8},{10,11... | collective-permute-start | bytes 2359304 | tf_op jit(solution)/shard_map/ppermute | solution.py:339
  13.1 7.0 %collective-permute-start.6 = (bf16[384,1024]{1,0:T(8,128)(2,1)}, bf16[384,1024]{1,0:T(8,128)(2,1)S(1)}, u32[]{:S(2)}, u32[]{:S(2)}) collective-permute-start(bf16[384,1024]{1,0:T(8,128)(2,1)} %bitcast.21), channel_id=1, source_target_pairs={{0,1},{1,0},{2,3},{3,2},{4,5},{5,4},{6,7},{7,6},{8,9},{9,8},{10,11... | collective-permute-start | bytes 2359304 | tf_op jit(solution)/shard_map/ppermute | solution.py:339
  13.6 0.7 copy-start.6
  14.3 16.9 %copy-start = (bf16[1,1024,384]{2,1,0:T(8,128)(2,1)S(1)}, bf16[1,1024,384]{2,1,0:T(8,128)(2,1)}, u32[]{:S(2)}) copy-start(bf16[1,1024,384]{2,1,0:T(8,128)(2,1)} %param.13) | copy-start | bytes 2359300
  14.3 16.9 %copy-start.1 = (bf16[1,1024,384]{2,1,0:T(8,128)(2,1)S(1)}, bf16[1,1024,384]{2,1,0:T(8,128)(2,1)}, u32[]{:S(2)}) copy-start(bf16[1,1024,384]{2,1,0:T(8,128)(2,1)} %param.14) | copy-start | bytes 2359300
  14.3 16.9 %copy-start.2 = (bf16[1,384,1024]{2,1,0:T(8,128)(2,1)S(1)}, bf16[1,384,1024]{2,1,0:T(8,128)(2,1)}, u32[]{:S(2)}) copy-start(bf16[1,384,1024]{2,1,0:T(8,128)(2,1)} %param.15) | copy-start | bytes 2359300
  14.3 16.9 %copy-start.3 = (bf16[128,1152]{1,0:T(8,128)(2,1)S(1)}, bf16[128,1152]{1,0:T(8,128)(2,1)}, u32[]{:S(2)}) copy-start(bf16[128,1152]{1,0:T(8,128)(2,1)} %get-tuple-element.70.refs_0_) | copy-start | bytes 884740
  14.3 16.9 %copy-start.4 = (bf16[128,1024]{1,0:T(8,128)(2,1)S(1)}, bf16[128,1024]{1,0:T(8,128)(2,1)}, u32[]{:S(2)}) copy-start(bf16[128,1024]{1,0:T(8,128)(2,1)} %refs_8_.3) | copy-start | bytes 786436
  14.3 20.1 %copy-start.7 = (f32[16,128]{1,0:T(8,128)}, f32[16,128]{1,0:T(8,128)S(1)}, u32[]{:S(2)}) copy-start(f32[16,128]{1,0:T(8,128)S(1)} %hold.1.kept) | copy-start | bytes 24580
  18.6 11.0 %collective-permute-start.9 = (bf16[128,1024]{1,0:T(8,128)(2,1)S(1)}, bf16[128,1024]{1,0:T(8,128)(2,1)S(1)}, u32[]{:S(2)}, u32[]{:S(2)}) collective-permute-start(bf16[128,1024]{1,0:T(8,128)(2,1)S(1)} %collective-permute-done.refs_2_.refs_10_), channel_id=1, source_target_pairs={{0,4},{1,5},{2,6},{3,7},{4,8},{5,9},{6,10},{7,11},{8,12},{9,13},{1... | collective-permute-start | bytes 786440 | tf_op jit(solution)/shard_map/ppermute | solution.py:330
  18.6 11.0 %collective-permute-start.10 = (bf16[128,1024]{1,0:T(8,128)(2,1)S(1)}, bf16[128,1024]{1,0:T(8,128)(2,1)S(1)}, u32[]{:S(2)}, u32[]{:S(2)}) collective-permute-start(bf16[128,1024]{1,0:T(8,128)(2,1)S(1)} %collective-permute-done.refs_2_.refs_10_), channel_id=1, source_target_pairs={{0,2},{1,3},{2,0},{3,1},{4,6},{5,7},{6,4},{7,5},{8,10},{9,11},{10,... | collective-permute-start | bytes 786440 | tf_op jit(solution)/shard_map/ppermute | solution.py:336
  20.1 15.8 %collective-permute-start.7 = (bf16[128,1152]{1,0:T(8,128)(2,1)S(1)}, bf16[128,1152]{1,0:T(8,128)(2,1)S(1)}, u32[]{:S(2)}, u32[]{:S(2)}) collective-permute-start(bf16[128,1152]{1,0:T(8,128)(2,1)S(1)} %collective-permute-done.2.refs_0_.refs_2_), channel_id=1, source_target_pairs={{0,4},{1,5},{2,6},{3,7},{4,8},{5,9},{6,10},{7,11},{8,12},{9,13},{1... | collective-permute-start | bytes 884744 | tf_op jit(solution)/shard_map/ppermute | solution.py:330
  21.4 14.5 %collective-permute-start.8 = (bf16[128,1152]{1,0:T(8,128)(2,1)S(1)}, bf16[128,1152]{1,0:T(8,128)(2,1)S(1)}, u32[]{:S(2)}, u32[]{:S(2)}) collective-permute-start(bf16[128,1152]{1,0:T(8,128)(2,1)S(1)} %collective-permute-done.2.refs_0_.refs_2_), channel_id=1, source_target_pairs={{0,2},{1,3},{2,0},{3,1},{4,6},{5,7},{6,4},{7,5},{8,10},{9,11},{10,... | collective-permute-start | bytes 884744 | tf_op jit(solution)/shard_map/ppermute | solution.py:336
  29.6 11.9 %collective-permute-start.14 = (bf16[128,1024]{1,0:T(8,128)(2,1)S(1)}, bf16[128,1024]{1,0:T(8,128)(2,1)S(1)}, u32[]{:S(2)}, u32[]{:S(2)}) collective-permute-start(bf16[128,1024]{1,0:T(8,128)(2,1)S(1)} %collective-permute-done.9.refs_1_.refs_12_), channel_id=1, source_target_pairs={{0,4},{1,5},{2,6},{3,7},{4,8},{5,9},{6,10},{7,11},{8,12},{9,13},{1... | collective-permute-start | bytes 786440 | tf_op jit(solution)/shard_map/ppermute | solution.py:330
  29.6 11.9 %collective-permute-start.15 = (bf16[128,1024]{1,0:T(8,128)(2,1)S(1)}, bf16[128,1024]{1,0:T(8,128)(2,1)S(1)}, u32[]{:S(2)}, u32[]{:S(2)}) collective-permute-start(bf16[128,1024]{1,0:T(8,128)(2,1)S(1)} %collective-permute-done.9.refs_1_.refs_12_), channel_id=1, source_target_pairs={{0,2},{1,3},{2,0},{3,1},{4,6},{5,7},{6,4},{7,5},{8,10},{9,11},{10,... | collective-permute-start | bytes 786440 | tf_op jit(solution)/shard_map/ppermute | solution.py:336
  35.9 10.4 %collective-permute-start.11 = (bf16[128,1152]{1,0:T(8,128)(2,1)S(1)}, bf16[128,1152]{1,0:T(8,128)(2,1)S(1)}, u32[]{:S(2)}, u32[]{:S(2)}) collective-permute-start(bf16[128,1152]{1,0:T(8,128)(2,1)S(1)} %collective-permute-done.7.refs_0_.refs_4_), channel_id=1, source_target_pairs={{0,4},{1,5},{2,6},{3,7},{4,8},{5,9},{6,10},{7,11},{8,12},{9,13},{1... | collective-permute-start | bytes 884744 | tf_op jit(solution)/shard_map/ppermute | solution.py:330
  35.9 10.4 %collective-permute-start.12 = (bf16[128,1152]{1,0:T(8,128)(2,1)S(1)}, bf16[128,1152]{1,0:T(8,128)(2,1)S(1)}, u32[]{:S(2)}, u32[]{:S(2)}) collective-permute-start(bf16[128,1152]{1,0:T(8,128)(2,1)S(1)} %collective-permute-done.7.refs_0_.refs_4_), channel_id=1, source_target_pairs={{0,2},{1,3},{2,0},{3,1},{4,6},{5,7},{6,4},{7,5},{8,10},{9,11},{10,... | collective-permute-start | bytes 884744 | tf_op jit(solution)/shard_map/ppermute | solution.py:336
  41.6 10.0 %collective-permute-start.21 = (bf16[128,1024]{1,0:T(8,128)(2,1)S(1)}, bf16[128,1024]{1,0:T(8,128)(2,1)S(1)}, u32[]{:S(2)}, u32[]{:S(2)}) collective-permute-start(bf16[128,1024]{1,0:T(8,128)(2,1)S(1)} %collective-permute-done.14.refs_1_.refs_14_), channel_id=1, source_target_pairs={{0,2},{1,3},{2,0},{3,1},{4,6},{5,7},{6,4},{7,5},{8,10},{9,11},{10,... | collective-permute-start | bytes 786440 | tf_op jit(solution)/shard_map/ppermute | solution.py:336
  46.3 10.3 %collective-permute-start.13 = (bf16[128,1152]{1,0:T(8,128)(2,1)S(1)}, bf16[128,1152]{1,0:T(8,128)(2,1)S(1)}, u32[]{:S(2)}, u32[]{:S(2)}) collective-permute-start(bf16[128,1152]{1,0:T(8,128)(2,1)S(1)} %collective-permute-done.12.refs_0_.refs_5_), channel_id=1, source_target_pairs={{0,4},{1,5},{2,6},{3,7},{4,8},{5,9},{6,10},{7,11},{8,12},{9,13},{1... | collective-permute-start | bytes 884744 | tf_op jit(solution)/shard_map/ppermute | solution.py:330
  50.1 12.9 %collective-permute-start.19 = (bf16[128,1152]{1,0:T(8,128)(2,1)S(1)}, bf16[128,1152]{1,0:T(8,128)(2,1)S(1)}, u32[]{:S(2)}, u32[]{:S(2)}) collective-permute-start(bf16[128,1152]{1,0:T(8,128)(2,1)S(1)} %get-tuple-element.100), channel_id=1, source_target_pairs={{0,2},{1,3},{2,0},{3,1},{4,6},{5,7},{6,4},{7,5},{8,10},{9,11},{10,... | collective-permute-start | bytes 884744 | tf_op jit(solution)/shard_map/ppermute | solution.py:336
  56.7 10.6 %collective-permute-start.17 = (bf16[128,1152]{1,0:T(8,128)(2,1)S(1)}, bf16[128,1152]{1,0:T(8,128)(2,1)S(1)}, u32[]{:S(2)}, u32[]{:S(2)}) collective-permute-start(bf16[128,1152]{1,0:T(8,128)(2,1)S(1)} %get-tuple-element.98), channel_id=1, source_target_pairs={{0,12},{1,13},{2,14},{3,15},{4,0},{5,1},{6,2},{7,3},{8,4},{9,5},{1... | collective-permute-start | bytes 884744 | tf_op jit(solution)/shard_map/ppermute | solution.py:333
  61.8 6.8 %collective-permute-start.22 = (bf16[128,1152]{1,0:T(8,128)(2,1)S(1)}, bf16[128,1152]{1,0:T(8,128)(2,1)S(1)}, u32[]{:S(2)}, u32[]{:S(2)}) collective-permute-start(bf16[128,1152]{1,0:T(8,128)(2,1)S(1)} %get-tuple-element.105), channel_id=1, source_target_pairs={{0,2},{1,3},{2,0},{3,1},{4,6},{5,7},{6,4},{7,5},{8,10},{9,11},{10,... | collective-permute-start | bytes 884744 | tf_op jit(solution)/shard_map/ppermute | solution.py:336
  63.1 9.4 %collective-permute-start.20 = (bf16[128,1152]{1,0:T(8,128)(2,1)S(1)}, bf16[128,1152]{1,0:T(8,128)(2,1)S(1)}, u32[]{:S(2)}, u32[]{:S(2)}) collective-permute-start(bf16[128,1152]{1,0:T(8,128)(2,1)S(1)} %add_convert_fusion.1), channel_id=1, source_target_pairs={{0,4},{1,5},{2,6},{3,7},{4,8},{5,9},{6,10},{7,11},{8,12},{9,13},{1... | collective-permute-start | bytes 884744 | tf_op jit(solution)/shard_map/ppermute | solution.py:330
  66.7 6.3 %collective-permute-start.23 = (bf16[1024,384]{1,0:T(8,128)(2,1)S(1)}, bf16[1024,384]{1,0:T(8,128)(2,1)S(1)}, u32[]{:S(2)}, u32[]{:S(2)}) collective-permute-start(bf16[1024,384]{1,0:T(8,128)(2,1)S(1)} %get-tuple-element.110), channel_id=1, source_target_pairs={{0,1},{1,0},{2,3},{3,2},{4,5},{5,4},{6,7},{7,6},{8,9},{9,8},{10,11... | collective-permute-start | bytes 2359304 | tf_op jit(solution)/shard_map/ppermute | solution.py:339
  66.8 6.3 %collective-permute-start.24 = (bf16[1024,384]{1,0:T(8,128)(2,1)S(1)}, bf16[1024,384]{1,0:T(8,128)(2,1)S(1)}, u32[]{:S(2)}, u32[]{:S(2)}) collective-permute-start(bf16[1024,384]{1,0:T(8,128)(2,1)S(1)} %get-tuple-element.111), channel_id=1, source_target_pairs={{0,1},{1,0},{2,3},{3,2},{4,5},{5,4},{6,7},{7,6},{8,9},{9,8},{10,11... | collective-permute-start | bytes 2359304 | tf_op jit(solution)/shard_map/ppermute | solution.py:339
  67.3 5.8 %collective-permute-start.25 = (bf16[384,1024]{1,0:T(8,128)(2,1)S(1)}, bf16[384,1024]{1,0:T(8,128)(2,1)S(1)}, u32[]{:S(2)}, u32[]{:S(2)}) collective-permute-start(bf16[384,1024]{1,0:T(8,128)(2,1)S(1)} %get-tuple-element.112), channel_id=1, source_target_pairs={{0,1},{1,0},{2,3},{3,2},{4,5},{5,4},{6,7},{7,6},{8,9},{9,8},{10,11... | collective-permute-start | bytes 2359304 | tf_op jit(solution)/shard_map/ppermute | solution.py:339
  68.6 10.1 %collective-permute-start.16 = (bf16[128,1152]{1,0:T(8,128)(2,1)S(1)}, bf16[128,1152]{1,0:T(8,128)(2,1)S(1)}, u32[]{:S(2)}, u32[]{:S(2)}) collective-permute-start(bf16[128,1152]{1,0:T(8,128)(2,1)S(1)} %get-tuple-element.95), channel_id=1, source_target_pairs={{0,12},{1,13},{2,14},{3,15},{4,0},{5,1},{6,2},{7,3},{8,4},{9,5},{1... | collective-permute-start | bytes 884744 | tf_op jit(solution)/shard_map/ppermute | solution.py:333
  72.4 7.9 %collective-permute-start.18 = (bf16[128,1152]{1,0:T(8,128)(2,1)S(1)}, bf16[128,1152]{1,0:T(8,128)(2,1)S(1)}, u32[]{:S(2)}, u32[]{:S(2)}) collective-permute-start(bf16[128,1152]{1,0:T(8,128)(2,1)S(1)} %add_convert_fusion.2), channel_id=1, source_target_pairs={{0,2},{1,3},{2,0},{3,1},{4,6},{5,7},{6,4},{7,5},{8,10},{9,11},{10,... | collective-permute-start | bytes 884744 | tf_op jit(solution)/shard_map/ppermute | solution.py:336
  73.0 12.2 %copy-start.5 = (s32[128,8]{0,1:T(8,128)S(1)}, s32[128,8]{0,1:T(8,128)}, u32[]{:S(2)}) copy-start(s32[128,8]{0,1:T(8,128)} %param.11) | copy-start | bytes 12292
  73.0 12.2 %copy-start.8 = (f32[16,128]{1,0:T(8,128)S(1)}, f32[16,128]{1,0:T(8,128)}, u32[]{:S(2)}) copy-start(f32[16,128]{1,0:T(8,128)} %copy-done.7) | copy-start | bytes 24580
  73.1 12.2 %collective-permute-start.26 = (bf16[128,1152]{1,0:T(8,128)(2,1)S(1)}, bf16[128,1152]{1,0:T(8,128)(2,1)S(1)}, u32[]{:S(2)}, u32[]{:S(2)}) collective-permute-start(bf16[128,1152]{1,0:T(8,128)(2,1)S(1)} %add_convert_fusion), channel_id=1, source_target_pairs={{0,4},{1,5},{2,6},{3,7},{4,8},{5,9},{6,10},{7,11},{8,12},{9,13},{1... | collective-permute-start | bytes 884744 | tf_op jit(solution)/shard_map/ppermute | solution.py:330

commit v8 on v7

--- a/solution.py
+++ b/solution.py
@@ -191,20 +191,18 @@
     x, dy, act, sem = refs[3:]
     tokens, width = dy_in[0].shape
     hidden = act.shape[1] // 3
+    step_rows = act_in[0].shape[0]
     copies = []
 
     def fetch(src, dst):
         copies.append(pltpu.make_async_copy(src, dst, sem.at[len(copies)]))
         copies[-1].start()
 
-    row = 0
     for i in range(steps):
-        step_rows = act_in[i].shape[0]
         fetch(
             act_in[i].at[:, pl.ds(j * 3 * hidden, 3 * hidden)],
-            act.at[pl.ds(row, step_rows)],
+            act.at[pl.ds(i * step_rows, step_rows)],
         )
-        row += step_rows
     for i in range(slots):
         fetch(xg_in[i].at[:, pl.ds(0, width)], x.at[pl.ds(i * tokens, tokens)])
     for i in range(slots):
@@ -344,6 +342,7 @@
     ids = expert_ids.T
     xg, kept = plan(replica_table[None], ids, gates.T, tokens_in, devices, lanes)
     own = (w_gate[0], w_up[0], w_down[0])
+    own, kept = together(own, kept)
     weights = own + tuple(send_core(w) for w in own)
 
     per = max(1, W_ROWS // (inner * tokens))
@@ -355,7 +354,7 @@
             j,
             [x for z in group for x in xgs[z]],
             [d for z in group for d in dys[z]],
-            [act for z in group for act in acts[z]],
+            [acts[z] for z in group],
             dtype,
             more,
         )
@@ -378,7 +377,7 @@
             if z < outer:
                 ahead = send_z(last[0])
             for y in range(1, inner):
-                if k == 0 and z == outer > 1 and y == inner - 1:
+                if k and z == outer > 1 and y == inner - 1:
                     last.append(send_z(stream[z - 2][y]))
                 else:
                     last.append(send_y(last[y - 1]))
@@ -386,8 +385,7 @@
             if inner > 1:
                 done.append(last[-1])
             if k == 0 and z == 1:
-                done, weights = together(done, weights)
-            elif z == 1:
+                kept, weights = together(kept, weights)
                 done, kept = together(done, hold(kept, HOLD))
             elif k == 0:
                 done, acts[z - 2] = together(done, acts[z - 2])
@@ -397,14 +395,11 @@
                 last[-1] = done.pop()
             if ahead is not None:
                 stream.append([done.pop()])
-        cut = inner - 1 if z > 2 else inner
-        dxs.append([])
-        acts.append([])
-        for part in (slice(0, cut), slice(cut, inner)):
-            if xgs[z - 1][part]:
-                *dx, act = rows_grads(xgs[z - 1][part], dys[z - 1][part], weights)
-                dxs[-1] += dx
-                acts[-1].append(act)
+        if z == outer > 2:
+            first, xgs[z - 1] = together(send_z(dxs[1][0]), xgs[z - 1])
+        *dx, act = rows_grads(xgs[z - 1], dys[z - 1], weights)
+        dxs.append(dx)
+        acts.append(act)
         if z > 2:
             across.append(send_across(z - 1))
         if len(groups) > 1 and z - 1 == groups[(z - 1) // per][-1]:
@@ -422,13 +417,14 @@
 
     pieces = []
     if outer > 1:
+        if outer == 2:
+            pieces.append(send_z(dxs[1][0]))
         dxs[1], acts[-2] = together(dxs[1], acts[-2])
-        back = [send_down(v) for v in dxs[1]]
-        pieces.append(back[0])
-        dxs[0] = [dxs[0][0]] + [add(v, o) for v, o in zip(dxs[0][1:], back[1:])]
+        down = [send_down(v) for v in dxs[1][1:]]
+        dxs[0] = [dxs[0][0]] + [add(v, o) for v, o in zip(dxs[0][1:], down)]
     pieces += [dxs[0][0], *send_across(0)]
     if outer > 2:
-        total = add(dxs[2][0], *across[0])
+        total = add(dxs[2][0], first, *across[0])
         for z in range(3, outer):
             total = add(send_z(total), dxs[z][0], *across[z - 2])
         total, other = together(total, other)

time: 86.4 us -> 84.5 us (0.978)
  starting transfers between devices: 26.1 us -> 31.4 us
  Pallas kernels: 27.4 us -> 23.4 us
  waiting for transfers between devices: 30.8 us -> 27 us
    ppermute x9 -> x10, starting transfers between devices: 8.08 us -> 13.8 us  [send_z(): lax.ppermute(v, 'expert', [(i, moved(i, 1, 0)) for i in range(devices)])]
    pallas_call x6 -> x4, Pallas kernels: 16.7 us -> 12.9 us  [rows_grads(): pl.pallas_call(functools.partial(rows_kernel, slots), out_shape=tuple((ja...]
    ppermute x2 -> x1, starting transfers between devices: 5.29 us -> 1.69 us  [send_down(): lax.ppermute(v, 'expert', [(i, moved(i, -1, 0)) for i in range(devices)])]
    ppermute x10, starting transfers between devices: 11.6 us -> 14.3 us  [send_y(): lax.ppermute(v, 'expert', [(i, moved(i, 0, 1)) for i in range(devices)])]
    ppermute x9 -> x10, waiting for transfers between devices: 27.4 us -> 25 us  [send_z(): lax.ppermute(v, 'expert', [(i, moved(i, 1, 0)) for i in range(devices)])]
  transfers between devices with their start and end apart: 27 -> 27, of which waited for: 10 -> 10; matrix products, arithmetic and copies ran while one was open for 0% -> 0% of each run, Pallas kernels for 31% -> 25%
where the time goes in v8:
time: 84.5 us; the launch traced here: 84.3 us
  starting transfers between devices  31.4 us (37%)
  waiting for transfers between devices  27 us (32%)
  Pallas kernels  23.4 us (28%)
  local copies, waits for them, and re-layouts  1.32 us (2%)
    ppermute x10, waiting for transfers between devices, send_z(): lax.ppermute(v, 'expert', [(i, moved(i, 1, 0)) for i in range(devices)])  25 us
    ppermute x10, starting transfers between devices, send_y(): lax.ppermute(v, 'expert', [(i, moved(i, 0, 1)) for i in range(devices)])  14.3 us
    ppermute x10, starting transfers between devices, send_z(): lax.ppermute(v, 'expert', [(i, moved(i, 1, 0)) for i in range(devices)])  13.8 us
    pallas_call x4, Pallas kernels, rows_grads(): pl.pallas_call(functools.partial(rows_kernel, slots), out_shape=tuple((ja...  12.9 us
    pallas_call x2, Pallas kernels, weights_grads(): pl.pallas_call(functools.partial(weights_kernel, j, slots, steps, len(mor...  7.94 us
    ppermute x10, waiting for transfers between devices, send_y(): lax.ppermute(v, 'expert', [(i, moved(i, 0, 1)) for i in range(devices)])  2.05 us
    pallas_call x1, Pallas kernels, plan(): pl.pallas_call(functools.partial(plan_kernel, home_cap, rep_cap), out_sha...  1.75 us
    ppermute x1, starting transfers between devices, send_down(): lax.ppermute(v, 'expert', [(i, moved(i, -1, 0)) for i in range(devices)])  1.69 us
  transfers between devices with their start and end apart: 27, of which 10 were waited for; matrix products, arithmetic and copies ran while one was open for 0% of the time, Pallas kernels for 25%

profile of v8, /device:TPU:0, one launch (start us, length us, event | category | flops | bytes accessed | tf_op | source)
XLA Modules:
  0.0 84.3 jit_solution(1546060591210526554)
XLA Ops:
  0.6 1.7 %plan.1 = (bf16[128,1152]{1,0:T(8,128)(2,1)}, f32[16,128]{1,0:T(8,128)}) custom-call(s32[1,16]{1,0:T(1,128)} %bitcast.25, s32[8,128]{1,0:T(8,128)} %bitcast.7, bf16[8,128]{1,0:T(8,128)(2,1)} %bitcast.24, bf16[128,1024]{1,0:T(8,128)(2,1)} %x_in.1), custom_call_target="tpu_custom_call" | custom-call | tf_op jit(solution)/shard_map/plan/pallas_call | solution.py:84
  2.4 0.5 collective-permute-start.2
  2.9 0.1 collective-permute-start.3
  3.0 0.4 collective-permute-start.4
  3.4 2.7 %collective-permute-start = (bf16[128,1152]{1,0:T(8,128)(2,1)}, bf16[128,1152]{1,0:T(8,128)(2,1)S(1)}, u32[]{:S(2)}, u32[]{:S(2)}) collective-permute-start(bf16[128,1152]{1,0:T(8,128)(2,1)} %get-tuple-element.70.refs_0_), channel_id=1, source_target_pairs={{0,4},{1,5},{2,6},{3,7},{4,8},{5,9},{6,10},{7,11},{8,12},{9,13},{1... | collective-permute-start | bytes 884744 | tf_op jit(solution)/shard_map/ppermute | solution.py:328
  6.1 1.5 %collective-permute-start.1 = (bf16[128,1152]{1,0:T(8,128)(2,1)}, bf16[128,1152]{1,0:T(8,128)(2,1)S(1)}, u32[]{:S(2)}, u32[]{:S(2)}) collective-permute-start(bf16[128,1152]{1,0:T(8,128)(2,1)} %get-tuple-element.70.refs_0_), channel_id=1, source_target_pairs={{0,2},{1,3},{2,0},{3,1},{4,6},{5,7},{6,4},{7,5},{8,10},{9,11},{10,... | collective-permute-start | bytes 884744 | tf_op jit(solution)/shard_map/ppermute | solution.py:334
  7.6 0.0 collective-permute-done.2.refs_7_
  7.6 1.6 %collective-permute-start.5 = (bf16[128,1024]{1,0:T(8,128)(2,1)}, bf16[128,1024]{1,0:T(8,128)(2,1)S(1)}, u32[]{:S(2)}, u32[]{:S(2)}) collective-permute-start(bf16[128,1024]{1,0:T(8,128)(2,1)} %refs_8_.3), channel_id=1, source_target_pairs={{0,4},{1,5},{2,6},{3,7},{4,8},{5,9},{6,10},{7,11},{8,12},{9,13},{1... | collective-permute-start | bytes 786440 | tf_op jit(solution)/shard_map/ppermute | solution.py:328
  9.2 0.0 collective-permute-done.3.refs_8_
  9.2 0.5 collective-permute-start.6
  9.7 0.0 collective-permute-done.4.refs_9_
  9.7 0.7 copy-done.3
  10.4 0.6 copy-done.4
  11.0 5.2 %collective-permute-done.refs_0_.refs_2_ = bf16[128,1152]{1,0:T(8,128)(2,1)S(1)} collective-permute-done((bf16[128,1152]{1,0:T(8,128)(2,1)}, bf16[128,1152]{1,0:T(8,128)(2,1)S(1)}, u32[]{:S(2)}, u32[]{:S(2)}) %collective-permute-start) | collective-permute-done | bytes 294944 | tf_op jit(solution)/shard_map/ppermute | solution.py:328
  16.2 0.0 collective-permute-done.1.refs_1_
  16.2 1.5 %collective-permute-start.7 = (bf16[128,1152]{1,0:T(8,128)(2,1)S(1)}, bf16[128,1152]{1,0:T(8,128)(2,1)S(1)}, u32[]{:S(2)}, u32[]{:S(2)}) collective-permute-start(bf16[128,1152]{1,0:T(8,128)(2,1)S(1)} %collective-permute-done.refs_0_.refs_2_), channel_id=1, source_target_pairs={{0,4},{1,5},{2,6},{3,7},{4,8},{5,9},{6,10},{7,11},{8,12},{9,13},{1... | collective-permute-start | bytes 884744 | tf_op jit(solution)/shard_map/ppermute | solution.py:328
  17.7 1.5 %collective-permute-start.8 = (bf16[128,1152]{1,0:T(8,128)(2,1)S(1)}, bf16[128,1152]{1,0:T(8,128)(2,1)S(1)}, u32[]{:S(2)}, u32[]{:S(2)}) collective-permute-start(bf16[128,1152]{1,0:T(8,128)(2,1)S(1)} %collective-permute-done.refs_0_.refs_2_), channel_id=1, source_target_pairs={{0,2},{1,3},{2,0},{3,1},{4,6},{5,7},{6,4},{7,5},{8,10},{9,11},{10,... | collective-permute-start | bytes 884744 | tf_op jit(solution)/shard_map/ppermute | solution.py:334
  19.2 2.6 %collective-permute-done.5.refs_2_.refs_10_ = bf16[128,1024]{1,0:T(8,128)(2,1)S(1)} collective-permute-done((bf16[128,1024]{1,0:T(8,128)(2,1)}, bf16[128,1024]{1,0:T(8,128)(2,1)S(1)}, u32[]{:S(2)}, u32[]{:S(2)}) %collective-permute-start.5) | collective-permute-done | bytes 262176 | tf_op jit(solution)/shard_map/ppermute | solution.py:328
  21.9 0.0 collective-permute-done.6.refs_3_.refs_9_
  21.9 1.5 %collective-permute-start.9 = (bf16[128,1024]{1,0:T(8,128)(2,1)S(1)}, bf16[128,1024]{1,0:T(8,128)(2,1)S(1)}, u32[]{:S(2)}, u32[]{:S(2)}) collective-permute-start(bf16[128,1024]{1,0:T(8,128)(2,1)S(1)} %collective-permute-done.5.refs_2_.refs_10_), channel_id=1, source_target_pairs={{0,4},{1,5},{2,6},{3,7},{4,8},{5,9},{6,10},{7,11},{8,12},{9,13},{1... | collective-permute-start | bytes 786440 | tf_op jit(solution)/shard_map/ppermute | solution.py:328
  23.3 1.5 %collective-permute-start.10 = (bf16[128,1024]{1,0:T(8,128)(2,1)S(1)}, bf16[128,1024]{1,0:T(8,128)(2,1)S(1)}, u32[]{:S(2)}, u32[]{:S(2)}) collective-permute-start(bf16[128,1024]{1,0:T(8,128)(2,1)S(1)} %collective-permute-done.5.refs_2_.refs_10_), channel_id=1, source_target_pairs={{0,2},{1,3},{2,0},{3,1},{4,6},{5,7},{6,4},{7,5},{8,10},{9,11},{10,... | collective-permute-start | bytes 786440 | tf_op jit(solution)/shard_map/ppermute | solution.py:334
  24.9 3.2 %rows_grads.4 = (bf16[128,1152]{1,0:T(8,128)(2,1)S(1)}, bf16[128,1152]{1,0:T(8,128)(2,1)S(1)}, bf16[256,2304]{1,0:T(8,128)(2,1)S(1)}) custom-call(bf16[128,1152]{1,0:T(8,128)(2,1)S(1)} %copy-done, bf16[128,1152]{1,0:T(8,128)(2,1)S(1)} %collective-permute-done.1.refs_1_, bf16[128,1024]{1,0:T(8,128)(2,1)S(1)} %copy-done.1, ...), custom_call_target="tpu_custom_call" | custom-call | flops 2013265920 | bytes 9306112 | tf_op jit(solution)/shard_map/rows_grads/pallas_call | solution.py:172
  28.1 0.1 collective-permute-done.7.refs_0_.refs_4_
  28.2 0.0 collective-permute-done.8.refs_1_.refs_3_
  28.2 1.6 %collective-permute-start.11 = (bf16[128,1152]{1,0:T(8,128)(2,1)S(1)}, bf16[128,1152]{1,0:T(8,128)(2,1)S(1)}, u32[]{:S(2)}, u32[]{:S(2)}) collective-permute-start(bf16[128,1152]{1,0:T(8,128)(2,1)S(1)} %collective-permute-done.7.refs_0_.refs_4_), channel_id=1, source_target_pairs={{0,4},{1,5},{2,6},{3,7},{4,8},{5,9},{6,10},{7,11},{8,12},{9,13},{1... | collective-permute-start | bytes 884744 | tf_op jit(solution)/shard_map/ppermute | solution.py:328
  29.8 1.4 %collective-permute-start.12 = (bf16[128,1152]{1,0:T(8,128)(2,1)S(1)}, bf16[128,1152]{1,0:T(8,128)(2,1)S(1)}, u32[]{:S(2)}, u32[]{:S(2)}) collective-permute-start(bf16[128,1152]{1,0:T(8,128)(2,1)S(1)} %collective-permute-done.7.refs_0_.refs_4_), channel_id=1, source_target_pairs={{0,2},{1,3},{2,0},{3,1},{4,6},{5,7},{6,4},{7,5},{8,10},{9,11},{10,... | collective-permute-start | bytes 884744 | tf_op jit(solution)/shard_map/ppermute | solution.py:334
  31.2 2.6 %collective-permute-done.9.refs_2_.refs_12_ = bf16[128,1024]{1,0:T(8,128)(2,1)S(1)} collective-permute-done((bf16[128,1024]{1,0:T(8,128)(2,1)S(1)}, bf16[128,1024]{1,0:T(8,128)(2,1)S(1)}, u32[]{:S(2)}, u32[]{:S(2)}) %collective-permute-start.9) | collective-permute-done | bytes 262176 | tf_op jit(solution)/shard_map/ppermute | solution.py:328
  33.8 1.5 %collective-permute-start.14 = (bf16[128,1024]{1,0:T(8,128)(2,1)S(1)}, bf16[128,1024]{1,0:T(8,128)(2,1)S(1)}, u32[]{:S(2)}, u32[]{:S(2)}) collective-permute-start(bf16[128,1024]{1,0:T(8,128)(2,1)S(1)} %collective-permute-done.9.refs_2_.refs_12_), channel_id=1, source_target_pairs={{0,4},{1,5},{2,6},{3,7},{4,8},{5,9},{6,10},{7,11},{8,12},{9,13},{1... | collective-permute-start | bytes 786440 | tf_op jit(solution)/shard_map/ppermute | solution.py:328
  35.3 1.5 %collective-permute-start.15 = (bf16[128,1024]{1,0:T(8,128)(2,1)S(1)}, bf16[128,1024]{1,0:T(8,128)(2,1)S(1)}, u32[]{:S(2)}, u32[]{:S(2)}) collective-permute-start(bf16[128,1024]{1,0:T(8,128)(2,1)S(1)} %collective-permute-done.9.refs_2_.refs_12_), channel_id=1, source_target_pairs={{0,2},{1,3},{2,0},{3,1},{4,6},{5,7},{6,4},{7,5},{8,10},{9,11},{10,... | collective-permute-start | bytes 786440 | tf_op jit(solution)/shard_map/ppermute | solution.py:334
  36.8 3.2 %rows_grads.5 = (bf16[128,1152]{1,0:T(8,128)(2,1)S(1)}, bf16[128,1152]{1,0:T(8,128)(2,1)S(1)}, bf16[256,2304]{1,0:T(8,128)(2,1)S(1)}) custom-call(bf16[128,1152]{1,0:T(8,128)(2,1)S(1)} %collective-permute-done.refs_0_.refs_2_, bf16[128,1152]{1,0:T(8,128)(2,1)S(1)} %collective-permute-done.8.refs_1_.refs_3_, ...), custom_call_target="tpu_custom_call" | custom-call | flops 2013265920 | bytes 9306112 | tf_op jit(solution)/shard_map/rows_grads/pallas_call | solution.py:172
  40.0 0.1 collective-permute-done.11.refs_0_.refs_6_
  40.1 1.6 %collective-permute-start.13 = (bf16[128,1152]{1,0:T(8,128)(2,1)S(1)}, bf16[128,1152]{1,0:T(8,128)(2,1)S(1)}, u32[]{:S(2)}, u32[]{:S(2)}) collective-permute-start(bf16[128,1152]{1,0:T(8,128)(2,1)S(1)} %collective-permute-done.11.refs_0_.refs_6_), channel_id=1, source_target_pairs={{0,2},{1,3},{2,0},{3,1},{4,6},{5,7},{6,4},{7,5},{8,10},{9,11},{10,... | collective-permute-start | bytes 884744 | tf_op jit(solution)/shard_map/ppermute | solution.py:334
  41.7 1.4 %collective-permute-start.18 = (bf16[128,1152]{1,0:T(8,128)(2,1)S(1)}, bf16[128,1152]{1,0:T(8,128)(2,1)S(1)}, u32[]{:S(2)}, u32[]{:S(2)}) collective-permute-start(bf16[128,1152]{1,0:T(8,128)(2,1)S(1)} %get-tuple-element.93), channel_id=1, source_target_pairs={{0,4},{1,5},{2,6},{3,7},{4,8},{5,9},{6,10},{7,11},{8,12},{9,13},{1... | collective-permute-start | bytes 884744 | tf_op jit(solution)/shard_map/ppermute | solution.py:328
  43.1 2.5 %collective-permute-done.14.refs_2_.refs_14_ = bf16[128,1024]{1,0:T(8,128)(2,1)S(1)} collective-permute-done((bf16[128,1024]{1,0:T(8,128)(2,1)S(1)}, bf16[128,1024]{1,0:T(8,128)(2,1)S(1)}, u32[]{:S(2)}, u32[]{:S(2)}) %collective-permute-start.14) | collective-permute-done | bytes 262176 | tf_op jit(solution)/shard_map/ppermute | solution.py:328
  45.6 0.0 collective-permute-done.15.refs_3_.refs_13_
  45.6 1.6 %collective-permute-start.21 = (bf16[128,1024]{1,0:T(8,128)(2,1)S(1)}, bf16[128,1024]{1,0:T(8,128)(2,1)S(1)}, u32[]{:S(2)}, u32[]{:S(2)}) collective-permute-start(bf16[128,1024]{1,0:T(8,128)(2,1)S(1)} %collective-permute-done.15.refs_3_.refs_13_), channel_id=1, source_target_pairs={{0,4},{1,5},{2,6},{3,7},{4,8},{5,9},{6,10},{7,11},{8,12},{9,13},{1... | collective-permute-start | bytes 786440 | tf_op jit(solution)/shard_map/ppermute | solution.py:328
  47.2 3.2 %rows_grads.6 = (bf16[128,1152]{1,0:T(8,128)(2,1)S(1)}, bf16[128,1152]{1,0:T(8,128)(2,1)S(1)}, bf16[256,2304]{1,0:T(8,128)(2,1)S(1)}) custom-call(bf16[128,1152]{1,0:T(8,128)(2,1)S(1)} %collective-permute-done.7.refs_0_.refs_4_, bf16[128,1152]{1,0:T(8,128)(2,1)S(1)} %collective-permute-done.12.refs_1_.refs_5_, ...), custom_call_target="tpu_custom_call" | custom-call | flops 2013265920 | bytes 9306112 | tf_op jit(solution)/shard_map/rows_grads/pallas_call | solution.py:172
  50.4 1.6 %collective-permute-start.19 = (bf16[128,1152]{1,0:T(8,128)(2,1)S(1)}, bf16[128,1152]{1,0:T(8,128)(2,1)S(1)}, u32[]{:S(2)}, u32[]{:S(2)}) collective-permute-start(bf16[128,1152]{1,0:T(8,128)(2,1)S(1)} %get-tuple-element.107), channel_id=1, source_target_pairs={{0,2},{1,3},{2,0},{3,1},{4,6},{5,7},{6,4},{7,5},{8,10},{9,11},{10,... | collective-permute-start | bytes 884744 | tf_op jit(solution)/shard_map/ppermute | solution.py:334
  52.0 5.4 %collective-permute-done.21.refs_3_.refs_15_ = bf16[128,1024]{1,0:T(8,128)(2,1)S(1)} collective-permute-done((bf16[128,1024]{1,0:T(8,128)(2,1)S(1)}, bf16[128,1024]{1,0:T(8,128)(2,1)S(1)}, u32[]{:S(2)}, u32[]{:S(2)}) %collective-permute-start.21) | collective-permute-done | bytes 262176 | tf_op jit(solution)/shard_map/ppermute | solution.py:328
  57.4 0.0 collective-permute-done.13.refs_1_.refs_7_
  57.4 1.7 %collective-permute-start.16 = (bf16[128,1152]{1,0:T(8,128)(2,1)S(1)}, bf16[128,1152]{1,0:T(8,128)(2,1)S(1)}, u32[]{:S(2)}, u32[]{:S(2)}) collective-permute-start(bf16[128,1152]{1,0:T(8,128)(2,1)S(1)} %get-tuple-element.103), channel_id=1, source_target_pairs={{0,12},{1,13},{2,14},{3,15},{4,0},{5,1},{6,2},{7,3},{8,4},{9,5},{1... | collective-permute-start | bytes 884744 | tf_op jit(solution)/shard_map/ppermute | solution.py:331
  59.1 0.0 collective-permute-done.18
  59.1 3.2 %rows_grads.7 = (bf16[128,1152]{1,0:T(8,128)(2,1)S(1)}, bf16[128,1152]{1,0:T(8,128)(2,1)S(1)}, bf16[256,2304]{1,0:T(8,128)(2,1)S(1)}) custom-call(bf16[128,1152]{1,0:T(8,128)(2,1)S(1)} %collective-permute-done.11.refs_0_.refs_6_, bf16[128,1152]{1,0:T(8,128)(2,1)S(1)} %collective-permute-done.13.refs_1_.refs_7_, ...), custom_call_target="tpu_custom_call" | custom-call | flops 2013265920 | bytes 9306112 | tf_op jit(solution)/shard_map/rows_grads/pallas_call | solution.py:172
  62.3 1.6 %collective-permute-start.22 = (bf16[128,1152]{1,0:T(8,128)(2,1)S(1)}, bf16[128,1152]{1,0:T(8,128)(2,1)S(1)}, u32[]{:S(2)}, u32[]{:S(2)}) collective-permute-start(bf16[128,1152]{1,0:T(8,128)(2,1)S(1)} %get-tuple-element.112), channel_id=1, source_target_pairs={{0,2},{1,3},{2,0},{3,1},{4,6},{5,7},{6,4},{7,5},{8,10},{9,11},{10,... | collective-permute-start | bytes 884744 | tf_op jit(solution)/shard_map/ppermute | solution.py:334
  63.9 0.0 collective-permute-done.19
  63.9 0.1 add_convert_fusion.1
  64.0 0.4 collective-permute-start.20
  64.4 3.5 %weights_grads.2 = (bf16[1024,384]{1,0:T(8,128)(2,1)S(1)}, bf16[1024,384]{1,0:T(8,128)(2,1)S(1)}, bf16[384,1024]{1,0:T(8,128)(2,1)S(1)}) custom-call(bf16[128,1152]{1,0:T(8,128)(2,1)S(1)} %copy-done, bf16[128,1152]{1,0:T(8,128)(2,1)S(1)} %collective-permute-done.1.refs_1_, bf16[128,1152]{1,0:T(8,128)(2,1)S(1)} %collective-permute-done.refs_0_.refs_2_, ...), custom_call_target="tpu_custom_call" | custom-call | flops 2415919104 | bytes 8912896 | tf_op jit(solution)/shard_map/weights_grads/pallas_call | solution.py:247
  68.0 0.1 collective-permute-start.23
  68.0 0.5 collective-permute-start.24
  68.5 0.1 collective-permute-start.25
  68.6 0.1 add_convert_fusion.2
  68.7 2.0 %collective-permute-done.22 = bf16[128,1152]{1,0:T(8,128)(2,1)S(1)} collective-permute-done((bf16[128,1152]{1,0:T(8,128)(2,1)S(1)}, bf16[128,1152]{1,0:T(8,128)(2,1)S(1)}, u32[]{:S(2)}, u32[]{:S(2)}) %collective-permute-start.22) | collective-permute-done | bytes 294944 | tf_op jit(solution)/shard_map/ppermute | solution.py:334
  70.7 1.5 %collective-permute-start.17 = (bf16[128,1152]{1,0:T(8,128)(2,1)S(1)}, bf16[128,1152]{1,0:T(8,128)(2,1)S(1)}, u32[]{:S(2)}, u32[]{:S(2)}) collective-permute-start(bf16[128,1152]{1,0:T(8,128)(2,1)S(1)} %add_convert_fusion.2), channel_id=1, source_target_pairs={{0,2},{1,3},{2,0},{3,1},{4,6},{5,7},{6,4},{7,5},{8,10},{9,11},{10,... | collective-permute-start | bytes 884744 | tf_op jit(solution)/shard_map/ppermute | solution.py:334
  72.2 1.7 %collective-permute-done.20 = bf16[128,1152]{1,0:T(8,128)(2,1)S(1)} collective-permute-done((bf16[128,1152]{1,0:T(8,128)(2,1)S(1)}, bf16[128,1152]{1,0:T(8,128)(2,1)S(1)}, u32[]{:S(2)}, u32[]{:S(2)}) %collective-permute-start.20) | collective-permute-done | bytes 294944 | tf_op jit(solution)/shard_map/ppermute | solution.py:328
  73.9 0.1 add_convert_fusion
  74.0 0.0 copy-start.2
  74.0 0.0 copy-start.5
  74.0 0.0 collective-permute-done.23.refs_20_
  74.1 0.2 collective-permute-start.26
  74.2 4.4 %weights_grads.3 = (bf16[1,1024,384]{2,1,0:T(8,128)(2,1)}, bf16[1,1024,384]{2,1,0:T(8,128)(2,1)}, bf16[1,384,1024]{2,1,0:T(8,128)(2,1)}) custom-call(bf16[128,1152]{1,0:T(8,128)(2,1)S(1)} %copy-done, bf16[128,1152]{1,0:T(8,128)(2,1)S(1)} %collective-permute-done.1.refs_1_, bf16[128,1152]{1,0:T(8,128)(2,1)S(1)} %collective-permute-done.refs_0_.refs_2_, ...), custom_call_target="tpu_custom_call" | custom-call | flops 2415919104 | bytes 8912896 | tf_op jit(solution)/shard_map/weights_grads/pallas_call | solution.py:247
  78.6 0.0 collective-permute-done.17.refs_1_
  78.7 4.8 %collective-permute-done.26.refs_2_ = bf16[128,1152]{1,0:T(8,128)(2,1)S(1)} collective-permute-done((bf16[128,1152]{1,0:T(8,128)(2,1)S(1)}, bf16[128,1152]{1,0:T(8,128)(2,1)S(1)}, u32[]{:S(2)}, u32[]{:S(2)}) %collective-permute-start.26) | collective-permute-done | bytes 294944 | tf_op jit(solution)/shard_map/ppermute | solution.py:328
  83.4 0.9 %finish.1 = (bf16[128,1024]{1,0:T(8,128)(2,1)}, bf16[8,128]{1,0:T(8,128)(2,1)}) custom-call(s32[8,128]{1,0:T(8,128)S(1)} %bitcast.8, f32[16,128]{1,0:T(8,128)S(1)} %copy-done.5, bf16[128,1152]{1,0:T(8,128)(2,1)S(1)} %get-tuple-element.127.refs_0_, bf16[128,1152]{1,0:T(8,128)(2,1)S(1)} %collective-permute-done.17.refs_1_, ...), custom_call_target="tpu_custom_call" | custom-call | tf_op jit(solution)/shard_map/finish/pallas_call | solution.py:294
  (20 shorter events, 0.0 us)
Async XLA Ops:
  2.4 5.2 %collective-permute-start.2 = (bf16[1024,384]{1,0:T(8,128)(2,1)}, bf16[1024,384]{1,0:T(8,128)(2,1)S(1)}, u32[]{:S(2)}, u32[]{:S(2)}) collective-permute-start(bf16[1024,384]{1,0:T(8,128)(2,1)} %bitcast.9), channel_id=1, source_target_pairs={{0,1},{1,0},{2,3},{3,2},{4,5},{5,4},{6,7},{7,6},{8,9},{9,8},{10,11... | collective-permute-start | bytes 2359304 | tf_op jit(solution)/shard_map/ppermute | solution.py:337
  2.9 6.3 %collective-permute-start.3 = (bf16[1024,384]{1,0:T(8,128)(2,1)}, bf16[1024,384]{1,0:T(8,128)(2,1)S(1)}, u32[]{:S(2)}, u32[]{:S(2)}) collective-permute-start(bf16[1024,384]{1,0:T(8,128)(2,1)} %bitcast.14), channel_id=1, source_target_pairs={{0,1},{1,0},{2,3},{3,2},{4,5},{5,4},{6,7},{7,6},{8,9},{9,8},{10,11... | collective-permute-start | bytes 2359304 | tf_op jit(solution)/shard_map/ppermute | solution.py:337
  3.0 6.7 %collective-permute-start.4 = (bf16[384,1024]{1,0:T(8,128)(2,1)}, bf16[384,1024]{1,0:T(8,128)(2,1)S(1)}, u32[]{:S(2)}, u32[]{:S(2)}) collective-permute-start(bf16[384,1024]{1,0:T(8,128)(2,1)} %bitcast.19), channel_id=1, source_target_pairs={{0,1},{1,0},{2,3},{3,2},{4,5},{5,4},{6,7},{7,6},{8,9},{9,8},{10,11... | collective-permute-start | bytes 2359304 | tf_op jit(solution)/shard_map/ppermute | solution.py:337
  3.4 21.4 %copy-start = (bf16[128,1152]{1,0:T(8,128)(2,1)S(1)}, bf16[128,1152]{1,0:T(8,128)(2,1)}, u32[]{:S(2)}) copy-start(bf16[128,1152]{1,0:T(8,128)(2,1)} %get-tuple-element.70.refs_0_) | copy-start | bytes 884740
  3.4 21.4 %copy-start.1 = (bf16[128,1024]{1,0:T(8,128)(2,1)S(1)}, bf16[128,1024]{1,0:T(8,128)(2,1)}, u32[]{:S(2)}) copy-start(bf16[128,1024]{1,0:T(8,128)(2,1)} %refs_8_.3) | copy-start | bytes 786436
  3.4 12.8 %collective-permute-start = (bf16[128,1152]{1,0:T(8,128)(2,1)}, bf16[128,1152]{1,0:T(8,128)(2,1)S(1)}, u32[]{:S(2)}, u32[]{:S(2)}) collective-permute-start(bf16[128,1152]{1,0:T(8,128)(2,1)} %get-tuple-element.70.refs_0_), channel_id=1, source_target_pairs={{0,4},{1,5},{2,6},{3,7},{4,8},{5,9},{6,10},{7,11},{8,12},{9,13},{1... | collective-permute-start | bytes 884744 | tf_op jit(solution)/shard_map/ppermute | solution.py:328
  6.1 10.2 %collective-permute-start.1 = (bf16[128,1152]{1,0:T(8,128)(2,1)}, bf16[128,1152]{1,0:T(8,128)(2,1)S(1)}, u32[]{:S(2)}, u32[]{:S(2)}) collective-permute-start(bf16[128,1152]{1,0:T(8,128)(2,1)} %get-tuple-element.70.refs_0_), channel_id=1, source_target_pairs={{0,2},{1,3},{2,0},{3,1},{4,6},{5,7},{6,4},{7,5},{8,10},{9,11},{10,... | collective-permute-start | bytes 884744 | tf_op jit(solution)/shard_map/ppermute | solution.py:334
  7.6 14.3 %collective-permute-start.5 = (bf16[128,1024]{1,0:T(8,128)(2,1)}, bf16[128,1024]{1,0:T(8,128)(2,1)S(1)}, u32[]{:S(2)}, u32[]{:S(2)}) collective-permute-start(bf16[128,1024]{1,0:T(8,128)(2,1)} %refs_8_.3), channel_id=1, source_target_pairs={{0,4},{1,5},{2,6},{3,7},{4,8},{5,9},{6,10},{7,11},{8,12},{9,13},{1... | collective-permute-start | bytes 786440 | tf_op jit(solution)/shard_map/ppermute | solution.py:328
  9.2 12.7 %collective-permute-start.6 = (bf16[128,1024]{1,0:T(8,128)(2,1)}, bf16[128,1024]{1,0:T(8,128)(2,1)S(1)}, u32[]{:S(2)}, u32[]{:S(2)}) collective-permute-start(bf16[128,1024]{1,0:T(8,128)(2,1)} %refs_8_.3), channel_id=1, source_target_pairs={{0,2},{1,3},{2,0},{3,1},{4,6},{5,7},{6,4},{7,5},{8,10},{9,11},{10,... | collective-permute-start | bytes 786440 | tf_op jit(solution)/shard_map/ppermute | solution.py:334
  9.7 0.7 copy-start.3
  10.4 14.5 %copy-start.6 = (bf16[1,1024,384]{2,1,0:T(8,128)(2,1)S(1)}, bf16[1,1024,384]{2,1,0:T(8,128)(2,1)}, u32[]{:S(2)}) copy-start(bf16[1,1024,384]{2,1,0:T(8,128)(2,1)} %param.13) | copy-start | bytes 2359300
  10.4 14.5 %copy-start.7 = (bf16[1,1024,384]{2,1,0:T(8,128)(2,1)S(1)}, bf16[1,1024,384]{2,1,0:T(8,128)(2,1)}, u32[]{:S(2)}) copy-start(bf16[1,1024,384]{2,1,0:T(8,128)(2,1)} %param.14) | copy-start | bytes 2359300
  10.4 14.5 %copy-start.8 = (bf16[1,384,1024]{2,1,0:T(8,128)(2,1)S(1)}, bf16[1,384,1024]{2,1,0:T(8,128)(2,1)}, u32[]{:S(2)}) copy-start(bf16[1,384,1024]{2,1,0:T(8,128)(2,1)} %param.15) | copy-start | bytes 2359300
  10.4 0.6 copy-start.4
  16.2 11.9 %collective-permute-start.7 = (bf16[128,1152]{1,0:T(8,128)(2,1)S(1)}, bf16[128,1152]{1,0:T(8,128)(2,1)S(1)}, u32[]{:S(2)}, u32[]{:S(2)}) collective-permute-start(bf16[128,1152]{1,0:T(8,128)(2,1)S(1)} %collective-permute-done.refs_0_.refs_2_), channel_id=1, source_target_pairs={{0,4},{1,5},{2,6},{3,7},{4,8},{5,9},{6,10},{7,11},{8,12},{9,13},{1... | collective-permute-start | bytes 884744 | tf_op jit(solution)/shard_map/ppermute | solution.py:328
  17.7 10.5 %collective-permute-start.8 = (bf16[128,1152]{1,0:T(8,128)(2,1)S(1)}, bf16[128,1152]{1,0:T(8,128)(2,1)S(1)}, u32[]{:S(2)}, u32[]{:S(2)}) collective-permute-start(bf16[128,1152]{1,0:T(8,128)(2,1)S(1)} %collective-permute-done.refs_0_.refs_2_), channel_id=1, source_target_pairs={{0,2},{1,3},{2,0},{3,1},{4,6},{5,7},{6,4},{7,5},{8,10},{9,11},{10,... | collective-permute-start | bytes 884744 | tf_op jit(solution)/shard_map/ppermute | solution.py:334
  21.9 11.9 %collective-permute-start.9 = (bf16[128,1024]{1,0:T(8,128)(2,1)S(1)}, bf16[128,1024]{1,0:T(8,128)(2,1)S(1)}, u32[]{:S(2)}, u32[]{:S(2)}) collective-permute-start(bf16[128,1024]{1,0:T(8,128)(2,1)S(1)} %collective-permute-done.5.refs_2_.refs_10_), channel_id=1, source_target_pairs={{0,4},{1,5},{2,6},{3,7},{4,8},{5,9},{6,10},{7,11},{8,12},{9,13},{1... | collective-permute-start | bytes 786440 | tf_op jit(solution)/shard_map/ppermute | solution.py:328
  23.3 10.5 %collective-permute-start.10 = (bf16[128,1024]{1,0:T(8,128)(2,1)S(1)}, bf16[128,1024]{1,0:T(8,128)(2,1)S(1)}, u32[]{:S(2)}, u32[]{:S(2)}) collective-permute-start(bf16[128,1024]{1,0:T(8,128)(2,1)S(1)} %collective-permute-done.5.refs_2_.refs_10_), channel_id=1, source_target_pairs={{0,2},{1,3},{2,0},{3,1},{4,6},{5,7},{6,4},{7,5},{8,10},{9,11},{10,... | collective-permute-start | bytes 786440 | tf_op jit(solution)/shard_map/ppermute | solution.py:334
  28.2 11.9 %collective-permute-start.11 = (bf16[128,1152]{1,0:T(8,128)(2,1)S(1)}, bf16[128,1152]{1,0:T(8,128)(2,1)S(1)}, u32[]{:S(2)}, u32[]{:S(2)}) collective-permute-start(bf16[128,1152]{1,0:T(8,128)(2,1)S(1)} %collective-permute-done.7.refs_0_.refs_4_), channel_id=1, source_target_pairs={{0,4},{1,5},{2,6},{3,7},{4,8},{5,9},{6,10},{7,11},{8,12},{9,13},{1... | collective-permute-start | bytes 884744 | tf_op jit(solution)/shard_map/ppermute | solution.py:328
  29.8 10.4 %collective-permute-start.12 = (bf16[128,1152]{1,0:T(8,128)(2,1)S(1)}, bf16[128,1152]{1,0:T(8,128)(2,1)S(1)}, u32[]{:S(2)}, u32[]{:S(2)}) collective-permute-start(bf16[128,1152]{1,0:T(8,128)(2,1)S(1)} %collective-permute-done.7.refs_0_.refs_4_), channel_id=1, source_target_pairs={{0,2},{1,3},{2,0},{3,1},{4,6},{5,7},{6,4},{7,5},{8,10},{9,11},{10,... | collective-permute-start | bytes 884744 | tf_op jit(solution)/shard_map/ppermute | solution.py:334
  33.8 11.8 %collective-permute-start.14 = (bf16[128,1024]{1,0:T(8,128)(2,1)S(1)}, bf16[128,1024]{1,0:T(8,128)(2,1)S(1)}, u32[]{:S(2)}, u32[]{:S(2)}) collective-permute-start(bf16[128,1024]{1,0:T(8,128)(2,1)S(1)} %collective-permute-done.9.refs_2_.refs_12_), channel_id=1, source_target_pairs={{0,4},{1,5},{2,6},{3,7},{4,8},{5,9},{6,10},{7,11},{8,12},{9,13},{1... | collective-permute-start | bytes 786440 | tf_op jit(solution)/shard_map/ppermute | solution.py:328
  35.3 10.4 %collective-permute-start.15 = (bf16[128,1024]{1,0:T(8,128)(2,1)S(1)}, bf16[128,1024]{1,0:T(8,128)(2,1)S(1)}, u32[]{:S(2)}, u32[]{:S(2)}) collective-permute-start(bf16[128,1024]{1,0:T(8,128)(2,1)S(1)} %collective-permute-done.9.refs_2_.refs_12_), channel_id=1, source_target_pairs={{0,2},{1,3},{2,0},{3,1},{4,6},{5,7},{6,4},{7,5},{8,10},{9,11},{10,... | collective-permute-start | bytes 786440 | tf_op jit(solution)/shard_map/ppermute | solution.py:334
  40.1 17.3 %collective-permute-start.13 = (bf16[128,1152]{1,0:T(8,128)(2,1)S(1)}, bf16[128,1152]{1,0:T(8,128)(2,1)S(1)}, u32[]{:S(2)}, u32[]{:S(2)}) collective-permute-start(bf16[128,1152]{1,0:T(8,128)(2,1)S(1)} %collective-permute-done.11.refs_0_.refs_6_), channel_id=1, source_target_pairs={{0,2},{1,3},{2,0},{3,1},{4,6},{5,7},{6,4},{7,5},{8,10},{9,11},{10,... | collective-permute-start | bytes 884744 | tf_op jit(solution)/shard_map/ppermute | solution.py:334
  41.7 17.4 %collective-permute-start.18 = (bf16[128,1152]{1,0:T(8,128)(2,1)S(1)}, bf16[128,1152]{1,0:T(8,128)(2,1)S(1)}, u32[]{:S(2)}, u32[]{:S(2)}) collective-permute-start(bf16[128,1152]{1,0:T(8,128)(2,1)S(1)} %get-tuple-element.93), channel_id=1, source_target_pairs={{0,4},{1,5},{2,6},{3,7},{4,8},{5,9},{6,10},{7,11},{8,12},{9,13},{1... | collective-permute-start | bytes 884744 | tf_op jit(solution)/shard_map/ppermute | solution.py:328
  45.6 11.8 %collective-permute-start.21 = (bf16[128,1024]{1,0:T(8,128)(2,1)S(1)}, bf16[128,1024]{1,0:T(8,128)(2,1)S(1)}, u32[]{:S(2)}, u32[]{:S(2)}) collective-permute-start(bf16[128,1024]{1,0:T(8,128)(2,1)S(1)} %collective-permute-done.15.refs_3_.refs_13_), channel_id=1, source_target_pairs={{0,4},{1,5},{2,6},{3,7},{4,8},{5,9},{6,10},{7,11},{8,12},{9,13},{1... | collective-permute-start | bytes 786440 | tf_op jit(solution)/shard_map/ppermute | solution.py:328
  50.4 13.5 %collective-permute-start.19 = (bf16[128,1152]{1,0:T(8,128)(2,1)S(1)}, bf16[128,1152]{1,0:T(8,128)(2,1)S(1)}, u32[]{:S(2)}, u32[]{:S(2)}) collective-permute-start(bf16[128,1152]{1,0:T(8,128)(2,1)S(1)} %get-tuple-element.107), channel_id=1, source_target_pairs={{0,2},{1,3},{2,0},{3,1},{4,6},{5,7},{6,4},{7,5},{8,10},{9,11},{10,... | collective-permute-start | bytes 884744 | tf_op jit(solution)/shard_map/ppermute | solution.py:334
  57.4 11.1 %collective-permute-start.16 = (bf16[128,1152]{1,0:T(8,128)(2,1)S(1)}, bf16[128,1152]{1,0:T(8,128)(2,1)S(1)}, u32[]{:S(2)}, u32[]{:S(2)}) collective-permute-start(bf16[128,1152]{1,0:T(8,128)(2,1)S(1)} %get-tuple-element.103), channel_id=1, source_target_pairs={{0,12},{1,13},{2,14},{3,15},{4,0},{5,1},{6,2},{7,3},{8,4},{9,5},{1... | collective-permute-start | bytes 884744 | tf_op jit(solution)/shard_map/ppermute | solution.py:331
  62.3 8.4 %collective-permute-start.22 = (bf16[128,1152]{1,0:T(8,128)(2,1)S(1)}, bf16[128,1152]{1,0:T(8,128)(2,1)S(1)}, u32[]{:S(2)}, u32[]{:S(2)}) collective-permute-start(bf16[128,1152]{1,0:T(8,128)(2,1)S(1)} %get-tuple-element.112), channel_id=1, source_target_pairs={{0,2},{1,3},{2,0},{3,1},{4,6},{5,7},{6,4},{7,5},{8,10},{9,11},{10,... | collective-permute-start | bytes 884744 | tf_op jit(solution)/shard_map/ppermute | solution.py:334
  64.0 9.9 %collective-permute-start.20 = (bf16[128,1152]{1,0:T(8,128)(2,1)S(1)}, bf16[128,1152]{1,0:T(8,128)(2,1)S(1)}, u32[]{:S(2)}, u32[]{:S(2)}) collective-permute-start(bf16[128,1152]{1,0:T(8,128)(2,1)S(1)} %add_convert_fusion.1), channel_id=1, source_target_pairs={{0,4},{1,5},{2,6},{3,7},{4,8},{5,9},{6,10},{7,11},{8,12},{9,13},{1... | collective-permute-start | bytes 884744 | tf_op jit(solution)/shard_map/ppermute | solution.py:328
  68.0 6.1 %collective-permute-start.23 = (bf16[1024,384]{1,0:T(8,128)(2,1)S(1)}, bf16[1024,384]{1,0:T(8,128)(2,1)S(1)}, u32[]{:S(2)}, u32[]{:S(2)}) collective-permute-start(bf16[1024,384]{1,0:T(8,128)(2,1)S(1)} %get-tuple-element.116), channel_id=1, source_target_pairs={{0,1},{1,0},{2,3},{3,2},{4,5},{5,4},{6,7},{7,6},{8,9},{9,8},{10,11... | collective-permute-start | bytes 2359304 | tf_op jit(solution)/shard_map/ppermute | solution.py:337
  68.0 6.0 %collective-permute-start.24 = (bf16[1024,384]{1,0:T(8,128)(2,1)S(1)}, bf16[1024,384]{1,0:T(8,128)(2,1)S(1)}, u32[]{:S(2)}, u32[]{:S(2)}) collective-permute-start(bf16[1024,384]{1,0:T(8,128)(2,1)S(1)} %get-tuple-element.117), channel_id=1, source_target_pairs={{0,1},{1,0},{2,3},{3,2},{4,5},{5,4},{6,7},{7,6},{8,9},{9,8},{10,11... | collective-permute-start | bytes 2359304 | tf_op jit(solution)/shard_map/ppermute | solution.py:337
  68.5 5.5 %collective-permute-start.25 = (bf16[384,1024]{1,0:T(8,128)(2,1)S(1)}, bf16[384,1024]{1,0:T(8,128)(2,1)S(1)}, u32[]{:S(2)}, u32[]{:S(2)}) collective-permute-start(bf16[384,1024]{1,0:T(8,128)(2,1)S(1)} %get-tuple-element.118), channel_id=1, source_target_pairs={{0,1},{1,0},{2,3},{3,2},{4,5},{5,4},{6,7},{7,6},{8,9},{9,8},{10,11... | collective-permute-start | bytes 2359304 | tf_op jit(solution)/shard_map/ppermute | solution.py:337
  70.7 8.0 %collective-permute-start.17 = (bf16[128,1152]{1,0:T(8,128)(2,1)S(1)}, bf16[128,1152]{1,0:T(8,128)(2,1)S(1)}, u32[]{:S(2)}, u32[]{:S(2)}) collective-permute-start(bf16[128,1152]{1,0:T(8,128)(2,1)S(1)} %add_convert_fusion.2), channel_id=1, source_target_pairs={{0,2},{1,3},{2,0},{3,1},{4,6},{5,7},{6,4},{7,5},{8,10},{9,11},{10,... | collective-permute-start | bytes 884744 | tf_op jit(solution)/shard_map/ppermute | solution.py:334
  74.0 9.4 %copy-start.2 = (s32[128,8]{0,1:T(8,128)S(1)}, s32[128,8]{0,1:T(8,128)}, u32[]{:S(2)}) copy-start(s32[128,8]{0,1:T(8,128)} %param.11) | copy-start | bytes 12292
  74.0 9.4 %copy-start.5 = (f32[16,128]{1,0:T(8,128)S(1)}, f32[16,128]{1,0:T(8,128)}, u32[]{:S(2)}) copy-start(f32[16,128]{1,0:T(8,128)} %copy-done.4) | copy-start | bytes 24580
  74.1 9.3 %collective-permute-start.26 = (bf16[128,1152]{1,0:T(8,128)(2,1)S(1)}, bf16[128,1152]{1,0:T(8,128)(2,1)S(1)}, u32[]{:S(2)}, u32[]{:S(2)}) collective-permute-start(bf16[128,1152]{1,0:T(8,128)(2,1)S(1)} %add_convert_fusion), channel_id=1, source_target_pairs={{0,4},{1,5},{2,6},{3,7},{4,8},{5,9},{6,10},{7,11},{8,12},{9,13},{1... | collective-permute-start | bytes 884744 | tf_op jit(solution)/shard_map/ppermute | solution.py:328

commit v9 on v8

--- a/solution.py
+++ b/solution.py
@@ -40,12 +40,12 @@
 def plan_kernel(home_cap, rep_cap, table_in, ids_in, gates_in, x_in, xg, kept_out, *scratch):
     table, ids, gates, sem = scratch
     tokens, width = x_in.shape
-    lanes = xg.shape[1] - width
+    extra = xg.shape[0] - tokens
     pairs = (
         (table_in, table),
         (ids_in, ids),
         (gates_in, gates),
-        (x_in, xg.at[:, pl.ds(0, width)]),
+        (x_in, xg.at[pl.ds(0, tokens)]),
     )
     copies = [pltpu.make_async_copy(src, dst, sem.at[i]) for i, (src, dst) in enumerate(pairs)]
     for c in copies:
@@ -70,21 +70,23 @@
     cap = jnp.where(at_home, float(home_cap), float(rep_cap))
     kept = jnp.where((named > 0.0) & (rank < cap * copied), 1.0, 0.0)
     kept_out[...] = kept
-    dense = (weight * kept).T
-    if lanes > devices:
-        dense = jnp.concatenate([dense, jnp.zeros((tokens, lanes - devices), f32)], axis=1)
-    xg[:, width:] = dense.astype(bf16)
+    dense = weight * kept
+    for k in range(width // tokens):
+        part = jnp.zeros((extra, tokens), f32)
+        if k * extra < devices:
+            part = dense[k * extra : (k + 1) * extra]
+        xg[tokens:, k * tokens : (k + 1) * tokens] = part.astype(bf16)
     copies[3].wait()
 
 
-def plan(table, ids, gates, x, devices, lanes):
+def plan(table, ids, gates, x, devices, extra):
     tokens, width = x.shape
     home_cap = max(2, 5 * tokens * TOP // (4 * devices))
     rep_cap = max(2, tokens * TOP // (2 * devices))
     return pl.pallas_call(
         functools.partial(plan_kernel, home_cap, rep_cap),
         out_shape=(
-            jax.ShapeDtypeStruct((tokens, width + lanes), bf16),
+            jax.ShapeDtypeStruct((tokens + extra, width), bf16),
             jax.ShapeDtypeStruct((devices, tokens), f32),
         ),
         in_specs=[HBM] * 4,
@@ -119,28 +121,38 @@
     dxg, act = refs[2 * slots + 6 : 3 * slots + 6], refs[3 * slots + 6]
     tokens, width = dy[0].shape
     hidden = weights[2].shape[0]
-    lanes = xg[0].shape[1] - width
+    extra = xg[0].shape[0] - tokens
     per = max(1, ROW_BLOCK // tokens)
     me = lax.axis_index("expert")
 
     def stack(parts):
         return parts[0] if len(parts) == 1 else jnp.concatenate(parts, axis=0)
 
+    def unpack(ref):
+        total = jnp.zeros((extra, tokens), f32)
+        for c in range(width // tokens):
+            part = ref[tokens:, c * tokens : (c + 1) * tokens].astype(f32)
+            total = jnp.where(me // extra == c, part, total)
+        return total.T
+
     for at in range(0, slots, per):
         group = range(at, min(slots, at + per))
-        x = stack([xg[i][:, :width] for i in group])
+        x = stack([xg[i][:tokens] for i in group])
         up_grad = stack([dy[i][...] for i in group])
-        gates = stack([xg[i][:, width:].astype(f32) for i in group])
-        here = pl.ds(at * tokens, len(group) * tokens)
-        lane = lane_iota(len(group) * tokens, lanes)
+        rows = len(group) * tokens
+        here = pl.ds(at * tokens, rows)
+        gates = stack([unpack(xg[i]) for i in group])
+        lane = lane_iota(rows, LANES)
         dx, gg = 0.0, 0.0
         for j in range(2):
             w_gate, w_up, w_down = weights[3 * j : 3 * j + 3]
             a = jnp.dot(x, w_gate[...], preferred_element_type=f32)
             b = jnp.dot(x, w_up[...], preferred_element_type=f32)
             back = lax.dot_general(up_grad, w_down[...], nt, preferred_element_type=f32)
-            column = lane == (me if j == 0 else me ^ 1)
-            gate = jnp.sum(jnp.where(column, gates, 0.0), axis=1, keepdims=True)
+            column = (me if j == 0 else me ^ 1) % extra
+            gate = jnp.sum(
+                jnp.where(lane_iota(rows, extra) == column, gates, 0.0), axis=1, keepdims=True
+            )
             sig = jax.nn.sigmoid(a)
             silu = a * sig
             h = silu * b
@@ -154,24 +166,28 @@
             act[here, first + 2 * hidden : first + 3 * hidden] = (gate * h).astype(bf16)
             dx += lax.dot_general(da, w_gate[...], nt, preferred_element_type=f32)
             dx += lax.dot_general(db, w_up[...], nt, preferred_element_type=f32)
-            gg += jnp.where(column, dots, 0.0)
+            gg += jnp.where(lane == column, dots, 0.0)
         for k, i in enumerate(group):
             part = slice(k * tokens, (k + 1) * tokens)
-            dxg[i][:, :width] = dx[part].astype(bf16)
-            dxg[i][:, width:] = gg[part].astype(bf16)
+            dxg[i][:tokens] = dx[part].astype(bf16)
+            packed = gg[part].T[:extra]
+            for c in range(width // tokens):
+                dxg[i][tokens:, c * tokens : (c + 1) * tokens] = jnp.where(
+                    me // extra == c, packed, 0.0
+                ).astype(bf16)
 
 
 def rows_grads(xgs, dys, weights):
     slots = len(dys)
     tokens, width = dys[0].shape
-    full = xgs[0].shape[1]
+    full = xgs[0].shape[0]
     hidden = weights[2].shape[0]
     rows = slots * tokens
     flops = 2 * rows * 2 * 5 * width * hidden
-    moved = 4 * rows * (width + full) + 12 * width * hidden + 4 * rows * full + 12 * rows * hidden
+    moved = 12 * rows * width + 12 * width * hidden + 12 * rows * hidden
     return pl.pallas_call(
         functools.partial(rows_kernel, slots),
-        out_shape=tuple(jax.ShapeDtypeStruct((tokens, full), bf16) for _ in dys)
+        out_shape=tuple(jax.ShapeDtypeStruct((full, width), bf16) for _ in dys)
         + (jax.ShapeDtypeStruct((rows, 6 * hidden), bf16),),
         in_specs=[VMEM] * (2 * slots + 6),
         out_specs=(VMEM,) * (slots + 1),
@@ -204,7 +220,7 @@
             act.at[pl.ds(i * step_rows, step_rows)],
         )
     for i in range(slots):
-        fetch(xg_in[i].at[:, pl.ds(0, width)], x.at[pl.ds(i * tokens, tokens)])
+        fetch(xg_in[i].at[pl.ds(0, tokens)], x.at[pl.ds(i * tokens, tokens)])
     for i in range(slots):
         fetch(dy_in[i], dy.at[pl.ds(i * tokens, tokens)])
     for c in copies[: steps + slots]:
@@ -261,8 +277,8 @@
         ],
         compiler_params=params(20),
         cost_estimate=pl.CostEstimate(
-            flops=6 * rows * width * hidden,
-            bytes_accessed=rows * (4 * width + 6 * hidden) + 6 * width * hidden,
+            flops=1000,
+            bytes_accessed=1000,
             transcendentals=0,
         ),
         name="weights_grads",
@@ -272,14 +288,14 @@
 def finish_kernel(parts, ids, kept, *refs):
     pieces, (tokens_out, gates_out) = refs[:parts], refs[parts:]
     tokens, width = tokens_out.shape
-    total = pieces[0][:, :width].astype(f32)
-    gg = pieces[0][:, width:].astype(f32)
+    total = pieces[0][...].astype(f32)
     for p in pieces[1:]:
-        total = total + p[:, :width].astype(f32)
-        gg = gg + p[:, width:].astype(f32)
-    tokens_out[...] = total.astype(bf16)
+        total = total + p[...].astype(f32)
+    tokens_out[...] = total[:tokens].astype(bf16)
     devices = kept.shape[0]
-    gg = gg.T[:devices] * kept[...]
+    extra = pieces[0].shape[0] - tokens
+    gg = [total[tokens:, k * tokens : (k + 1) * tokens] for k in range(devices // extra)]
+    gg = jnp.concatenate(gg, axis=0) * kept[...]
     expert = row_iota(devices, tokens)
     place = row_iota(TOP, tokens)
     out = jnp.zeros((TOP, tokens), f32)
@@ -314,7 +330,7 @@
 def on_device(tokens_in, grad_out, gates, expert_ids, replica_table, w_gate, w_up, w_down):
     devices = lax.axis_size("expert")
     tokens, width = tokens_in.shape
-    lanes = -(-devices // LANES) * LANES
+    extra = 8 * -(-devices * tokens // (8 * width))
     chips = devices // CORES
     inner = 2 ** (int(math.log2(chips)) // 2)
     outer = chips // inner
@@ -340,9 +356,8 @@
         return lax.optimization_barrier(values)
 
     ids = expert_ids.T
-    xg, kept = plan(replica_table[None], ids, gates.T, tokens_in, devices, lanes)
+    xg, kept = plan(replica_table[None], ids, gates.T, tokens_in, devices, extra)
     own = (w_gate[0], w_up[0], w_down[0])
-    own, kept = together(own, kept)
     weights = own + tuple(send_core(w) for w in own)
 
     per = max(1, W_ROWS // (inner * tokens))
@@ -381,9 +396,9 @@
                     last.append(send_z(stream[z - 2][y]))
                 else:
                     last.append(send_y(last[y - 1]))
-            done = [] if ahead is None else [ahead]
-            if inner > 1:
-                done.append(last[-1])
+            done = [last[-1]] if inner > 1 else []
+            if ahead is not None:
+                done.append(ahead)
             if k == 0 and z == 1:
                 kept, weights = together(kept, weights)
                 done, kept = together(done, hold(kept, HOLD))
@@ -391,10 +406,10 @@
                 done, acts[z - 2] = together(done, acts[z - 2])
             else:
                 (done,) = together(done)
+            if ahead is not None:
+                stream.append([done.pop()])
             if inner > 1:
                 last[-1] = done.pop()
-            if ahead is not None:
-                stream.append([done.pop()])
         if z == outer > 2:
             first, xgs[z - 1] = together(send_z(dxs[1][0]), xgs[z - 1])
         *dx, act = rows_grads(xgs[z - 1], dys[z - 1], weights)
@@ -427,7 +442,7 @@
         total = add(dxs[2][0], first, *across[0])
         for z in range(3, outer):
             total = add(send_z(total), dxs[z][0], *across[z - 2])
-        total, other = together(total, other)
+        _, other = together(total, other)
         pieces.append(send_z(total))
     if single:
         grad_w = partial(0, groups[0], bf16, other)

time: 84.5 us -> 84.8 us (level)
  waiting for transfers between devices: 27 us -> 29.7 us
  starting transfers between devices: 31.4 us -> 29 us
    ppermute x10, waiting for transfers between devices: 25 us -> 27.1 us  [send_z(): lax.ppermute(v, 'expert', [(i, moved(i, 1, 0)) for i in range(devices)])]
    ppermute x1, starting transfers between devices: 1.69 us -> 0.01 us  [send_down(): lax.ppermute(v, 'expert', [(i, moved(i, -1, 0)) for i in range(devices)])]
    ppermute x10, starting transfers between devices: 13.8 us -> 12.4 us  [send_z(): lax.ppermute(v, 'expert', [(i, moved(i, 1, 0)) for i in range(devices)])]
  transfers between devices with their start and end apart: 27 -> 27, of which waited for: 10 -> 9; matrix products, arithmetic and copies ran while one was open for 0% -> 0% of each run, Pallas kernels for 25% -> 27%
where the time goes in v9:
time: 84.8 us; the launch traced here: 84.6 us
  waiting for transfers between devices  29.7 us (35%)
  starting transfers between devices  29 us (34%)
  Pallas kernels  23.3 us (27%)
  local copies, waits for them, and re-layouts  1.32 us (2%)
    ppermute x10, waiting for transfers between devices, send_z(): lax.ppermute(v, 'expert', [(i, moved(i, 1, 0)) for i in range(devices)])  27.1 us
    ppermute x10, starting transfers between devices, send_y(): lax.ppermute(v, 'expert', [(i, moved(i, 0, 1)) for i in range(devices)])  15 us
    pallas_call x4, Pallas kernels, rows_grads(): pl.pallas_call(functools.partial(rows_kernel, slots), out_shape=tuple((ja...  12.9 us
    ppermute x10, starting transfers between devices, send_z(): lax.ppermute(v, 'expert', [(i, moved(i, 1, 0)) for i in range(devices)])  12.4 us
    pallas_call x2, Pallas kernels, weights_grads(): pl.pallas_call(functools.partial(weights_kernel, j, slots, steps, len(mor...  7.94 us
    ppermute x10, waiting for transfers between devices, send_y(): lax.ppermute(v, 'expert', [(i, moved(i, 0, 1)) for i in range(devices)])  2.41 us
    pallas_call x1, Pallas kernels, plan(): pl.pallas_call(functools.partial(plan_kernel, home_cap, rep_cap), out_sha...  1.74 us
  transfers between devices with their start and end apart: 27, of which 9 were waited for; matrix products, arithmetic and copies ran while one was open for 0% of the time, Pallas kernels for 27%

profile of v9, /device:TPU:0, one launch (start us, length us, event | category | flops | bytes accessed | tf_op | source)
XLA Modules:
  0.0 84.6 jit_solution(1617792336121152183)
XLA Ops:
  0.6 0.5 collective-permute-start.2
  1.1 0.1 collective-permute-start.3
  1.2 0.4 collective-permute-start.4
  1.7 2.7 %collective-permute-start.6 = (bf16[128,1024]{1,0:T(8,128)(2,1)}, bf16[128,1024]{1,0:T(8,128)(2,1)S(1)}, u32[]{:S(2)}, u32[]{:S(2)}) collective-permute-start(bf16[128,1024]{1,0:T(8,128)(2,1)} %refs_8_.3), channel_id=1, source_target_pairs={{0,4},{1,5},{2,6},{3,7},{4,8},{5,9},{6,10},{7,11},{8,12},{9,13},{1... | collective-permute-start | bytes 786440 | tf_op jit(solution)/shard_map/ppermute | solution.py:344
  4.3 1.5 %collective-permute-start.5 = (bf16[128,1024]{1,0:T(8,128)(2,1)}, bf16[128,1024]{1,0:T(8,128)(2,1)S(1)}, u32[]{:S(2)}, u32[]{:S(2)}) collective-permute-start(bf16[128,1024]{1,0:T(8,128)(2,1)} %refs_8_.3), channel_id=1, source_target_pairs={{0,2},{1,3},{2,0},{3,1},{4,6},{5,7},{6,4},{7,5},{8,10},{9,11},{10,... | collective-permute-start | bytes 786440 | tf_op jit(solution)/shard_map/ppermute | solution.py:350
  5.8 1.7 %plan.1 = (bf16[136,1024]{1,0:T(8,128)(2,1)}, f32[16,128]{1,0:T(8,128)}) custom-call(s32[1,16]{1,0:T(1,128)} %bitcast.25, s32[8,128]{1,0:T(8,128)} %bitcast.7, bf16[8,128]{1,0:T(8,128)(2,1)} %bitcast.24, bf16[128,1024]{1,0:T(8,128)(2,1)} %x_in.1), custom_call_target="tpu_custom_call" | custom-call | tf_op jit(solution)/shard_map/plan/pallas_call | solution.py:86
  7.6 0.0 collective-permute-done.2.refs_7_
  7.6 1.6 %collective-permute-start.1 = (bf16[136,1024]{1,0:T(8,128)(2,1)}, bf16[136,1024]{1,0:T(8,128)(2,1)S(1)}, u32[]{:S(2)}, u32[]{:S(2)}) collective-permute-start(bf16[136,1024]{1,0:T(8,128)(2,1)} %get-tuple-element.65.refs_0_), channel_id=1, source_target_pairs={{0,4},{1,5},{2,6},{3,7},{4,8},{5,9},{6,10},{7,11},{8,12},{9,13},{1... | collective-permute-start | bytes 835592 | tf_op jit(solution)/shard_map/ppermute | solution.py:344
  9.2 0.0 collective-permute-done.3.refs_8_
  9.2 0.5 collective-permute-start
  9.7 0.0 collective-permute-done.4.refs_9_
  9.7 0.7 copy-done.3
  10.4 0.0 copy-start.8
  10.5 0.0 copy-start.4
  10.5 0.6 copy-done.4
  11.1 8.3 %collective-permute-done.1.refs_0_.refs_2_ = bf16[136,1024]{1,0:T(8,128)(2,1)S(1)} collective-permute-done((bf16[136,1024]{1,0:T(8,128)(2,1)}, bf16[136,1024]{1,0:T(8,128)(2,1)S(1)}, u32[]{:S(2)}, u32[]{:S(2)}) %collective-permute-start.1) | collective-permute-done | bytes 278560 | tf_op jit(solution)/shard_map/ppermute | solution.py:344
  19.4 0.0 collective-permute-done.refs_1_
  19.4 1.0 %collective-permute-start.8 = (bf16[136,1024]{1,0:T(8,128)(2,1)S(1)}, bf16[136,1024]{1,0:T(8,128)(2,1)S(1)}, u32[]{:S(2)}, u32[]{:S(2)}) collective-permute-start(bf16[136,1024]{1,0:T(8,128)(2,1)S(1)} %collective-permute-done.1.refs_0_.refs_2_), channel_id=1, source_target_pairs={{0,4},{1,5},{2,6},{3,7},{4,8},{5,9},{6,10},{7,11},{8,12},{9,13},{1... | collective-permute-start | bytes 835592 | tf_op jit(solution)/shard_map/ppermute | solution.py:344
  20.4 1.5 %collective-permute-start.7 = (bf16[136,1024]{1,0:T(8,128)(2,1)S(1)}, bf16[136,1024]{1,0:T(8,128)(2,1)S(1)}, u32[]{:S(2)}, u32[]{:S(2)}) collective-permute-start(bf16[136,1024]{1,0:T(8,128)(2,1)S(1)} %collective-permute-done.1.refs_0_.refs_2_), channel_id=1, source_target_pairs={{0,2},{1,3},{2,0},{3,1},{4,6},{5,7},{6,4},{7,5},{8,10},{9,11},{10,... | collective-permute-start | bytes 835592 | tf_op jit(solution)/shard_map/ppermute | solution.py:350
  22.0 1.6 %collective-permute-start.10 = (bf16[128,1024]{1,0:T(8,128)(2,1)S(1)}, bf16[128,1024]{1,0:T(8,128)(2,1)S(1)}, u32[]{:S(2)}, u32[]{:S(2)}) collective-permute-start(bf16[128,1024]{1,0:T(8,128)(2,1)S(1)} %collective-permute-done.6.refs_2_.refs_10_), channel_id=1, source_target_pairs={{0,4},{1,5},{2,6},{3,7},{4,8},{5,9},{6,10},{7,11},{8,12},{9,13},{1... | collective-permute-start | bytes 786440 | tf_op jit(solution)/shard_map/ppermute | solution.py:344
  23.5 0.5 collective-permute-start.9
  24.1 3.2 %rows_grads.4 = (bf16[136,1024]{1,0:T(8,128)(2,1)S(1)}, bf16[136,1024]{1,0:T(8,128)(2,1)S(1)}, bf16[256,2304]{1,0:T(8,128)(2,1)S(1)}) custom-call(bf16[136,1024]{1,0:T(8,128)(2,1)S(1)} %copy-done, bf16[136,1024]{1,0:T(8,128)(2,1)S(1)} %collective-permute-done.refs_1_, bf16[128,1024]{1,0:T(8,128)(2,1)S(1)} %copy-done.1, ...), custom_call_target="tpu_custom_call" | custom-call | flops 2013265920 | bytes 9043968 | tf_op jit(solution)/shard_map/rows_grads/pallas_call | solution.py:188
  27.3 3.5 %collective-permute-done.8.refs_0_.refs_4_ = bf16[136,1024]{1,0:T(8,128)(2,1)S(1)} collective-permute-done((bf16[136,1024]{1,0:T(8,128)(2,1)S(1)}, bf16[136,1024]{1,0:T(8,128)(2,1)S(1)}, u32[]{:S(2)}, u32[]{:S(2)}) %collective-permute-start.8) | collective-permute-done | bytes 278560 | tf_op jit(solution)/shard_map/ppermute | solution.py:344
  30.8 0.0 collective-permute-done.7.refs_1_.refs_3_
  30.8 0.8 %collective-permute-start.12 = (bf16[136,1024]{1,0:T(8,128)(2,1)S(1)}, bf16[136,1024]{1,0:T(8,128)(2,1)S(1)}, u32[]{:S(2)}, u32[]{:S(2)}) collective-permute-start(bf16[136,1024]{1,0:T(8,128)(2,1)S(1)} %collective-permute-done.8.refs_0_.refs_4_), channel_id=1, source_target_pairs={{0,4},{1,5},{2,6},{3,7},{4,8},{5,9},{6,10},{7,11},{8,12},{9,13},{1... | collective-permute-start | bytes 835592 | tf_op jit(solution)/shard_map/ppermute | solution.py:344
  31.6 1.5 %collective-permute-start.11 = (bf16[136,1024]{1,0:T(8,128)(2,1)S(1)}, bf16[136,1024]{1,0:T(8,128)(2,1)S(1)}, u32[]{:S(2)}, u32[]{:S(2)}) collective-permute-start(bf16[136,1024]{1,0:T(8,128)(2,1)S(1)} %collective-permute-done.8.refs_0_.refs_4_), channel_id=1, source_target_pairs={{0,2},{1,3},{2,0},{3,1},{4,6},{5,7},{6,4},{7,5},{8,10},{9,11},{10,... | collective-permute-start | bytes 835592 | tf_op jit(solution)/shard_map/ppermute | solution.py:350
  33.1 3.2 %collective-permute-done.10.refs_2_.refs_12_ = bf16[128,1024]{1,0:T(8,128)(2,1)S(1)} collective-permute-done((bf16[128,1024]{1,0:T(8,128)(2,1)S(1)}, bf16[128,1024]{1,0:T(8,128)(2,1)S(1)}, u32[]{:S(2)}, u32[]{:S(2)}) %collective-permute-start.10) | collective-permute-done | bytes 262176 | tf_op jit(solution)/shard_map/ppermute | solution.py:344
  36.4 0.0 collective-permute-done.9.refs_3_.refs_11_
  36.4 0.8 %collective-permute-start.15 = (bf16[128,1024]{1,0:T(8,128)(2,1)S(1)}, bf16[128,1024]{1,0:T(8,128)(2,1)S(1)}, u32[]{:S(2)}, u32[]{:S(2)}) collective-permute-start(bf16[128,1024]{1,0:T(8,128)(2,1)S(1)} %collective-permute-done.10.refs_2_.refs_12_), channel_id=1, source_target_pairs={{0,4},{1,5},{2,6},{3,7},{4,8},{5,9},{6,10},{7,11},{8,12},{9,13},{1... | collective-permute-start | bytes 786440 | tf_op jit(solution)/shard_map/ppermute | solution.py:344
  37.2 1.5 %collective-permute-start.14 = (bf16[128,1024]{1,0:T(8,128)(2,1)S(1)}, bf16[128,1024]{1,0:T(8,128)(2,1)S(1)}, u32[]{:S(2)}, u32[]{:S(2)}) collective-permute-start(bf16[128,1024]{1,0:T(8,128)(2,1)S(1)} %collective-permute-done.10.refs_2_.refs_12_), channel_id=1, source_target_pairs={{0,2},{1,3},{2,0},{3,1},{4,6},{5,7},{6,4},{7,5},{8,10},{9,11},{10,... | collective-permute-start | bytes 786440 | tf_op jit(solution)/shard_map/ppermute | solution.py:350
  38.8 3.2 %rows_grads.5 = (bf16[136,1024]{1,0:T(8,128)(2,1)S(1)}, bf16[136,1024]{1,0:T(8,128)(2,1)S(1)}, bf16[256,2304]{1,0:T(8,128)(2,1)S(1)}) custom-call(bf16[136,1024]{1,0:T(8,128)(2,1)S(1)} %collective-permute-done.1.refs_0_.refs_2_, bf16[136,1024]{1,0:T(8,128)(2,1)S(1)} %collective-permute-done.7.refs_1_.refs_3_, ...), custom_call_target="tpu_custom_call" | custom-call | flops 2013265920 | bytes 9043968 | tf_op jit(solution)/shard_map/rows_grads/pallas_call | solution.py:188
  42.0 0.4 collective-permute-done.12.refs_0_.refs_6_
  42.3 0.0 collective-permute-done.11.refs_1_.refs_5_
  42.4 1.5 %collective-permute-start.13 = (bf16[136,1024]{1,0:T(8,128)(2,1)S(1)}, bf16[136,1024]{1,0:T(8,128)(2,1)S(1)}, u32[]{:S(2)}, u32[]{:S(2)}) collective-permute-start(bf16[136,1024]{1,0:T(8,128)(2,1)S(1)} %collective-permute-done.12.refs_0_.refs_6_), channel_id=1, source_target_pairs={{0,2},{1,3},{2,0},{3,1},{4,6},{5,7},{6,4},{7,5},{8,10},{9,11},{10,... | collective-permute-start | bytes 835592 | tf_op jit(solution)/shard_map/ppermute | solution.py:350
  43.9 0.8 collective-permute-start.18
  44.7 3.2 %collective-permute-done.15.refs_2_.refs_14_ = bf16[128,1024]{1,0:T(8,128)(2,1)S(1)} collective-permute-done((bf16[128,1024]{1,0:T(8,128)(2,1)S(1)}, bf16[128,1024]{1,0:T(8,128)(2,1)S(1)}, u32[]{:S(2)}, u32[]{:S(2)}) %collective-permute-start.15) | collective-permute-done | bytes 262176 | tf_op jit(solution)/shard_map/ppermute | solution.py:344
  48.0 0.8 %collective-permute-start.21 = (bf16[128,1024]{1,0:T(8,128)(2,1)S(1)}, bf16[128,1024]{1,0:T(8,128)(2,1)S(1)}, u32[]{:S(2)}, u32[]{:S(2)}) collective-permute-start(bf16[128,1024]{1,0:T(8,128)(2,1)S(1)} %collective-permute-done.14.refs_3_.refs_13_), channel_id=1, source_target_pairs={{0,4},{1,5},{2,6},{3,7},{4,8},{5,9},{6,10},{7,11},{8,12},{9,13},{1... | collective-permute-start | bytes 786440 | tf_op jit(solution)/shard_map/ppermute | solution.py:344
  48.8 3.2 %rows_grads.6 = (bf16[136,1024]{1,0:T(8,128)(2,1)S(1)}, bf16[136,1024]{1,0:T(8,128)(2,1)S(1)}, bf16[256,2304]{1,0:T(8,128)(2,1)S(1)}) custom-call(bf16[136,1024]{1,0:T(8,128)(2,1)S(1)} %collective-permute-done.8.refs_0_.refs_4_, bf16[136,1024]{1,0:T(8,128)(2,1)S(1)} %collective-permute-done.11.refs_1_.refs_5_, ...), custom_call_target="tpu_custom_call" | custom-call | flops 2013265920 | bytes 9043968 | tf_op jit(solution)/shard_map/rows_grads/pallas_call | solution.py:188
  52.0 1.6 %collective-permute-start.19 = (bf16[136,1024]{1,0:T(8,128)(2,1)S(1)}, bf16[136,1024]{1,0:T(8,128)(2,1)S(1)}, u32[]{:S(2)}, u32[]{:S(2)}) collective-permute-start(bf16[136,1024]{1,0:T(8,128)(2,1)S(1)} %get-tuple-element.98), channel_id=1, source_target_pairs={{0,2},{1,3},{2,0},{3,1},{4,6},{5,7},{6,4},{7,5},{8,10},{9,11},{10,... | collective-permute-start | bytes 835592 | tf_op jit(solution)/shard_map/ppermute | solution.py:350
  53.6 4.9 %collective-permute-done.21.refs_3_.refs_15_ = bf16[128,1024]{1,0:T(8,128)(2,1)S(1)} collective-permute-done((bf16[128,1024]{1,0:T(8,128)(2,1)S(1)}, bf16[128,1024]{1,0:T(8,128)(2,1)S(1)}, u32[]{:S(2)}, u32[]{:S(2)}) %collective-permute-start.21) | collective-permute-done | bytes 262176 | tf_op jit(solution)/shard_map/ppermute | solution.py:344
  58.5 0.0 collective-permute-done.13.refs_1_.refs_7_
  58.5 0.0 collective-permute-done.18
  58.5 0.0 collective-permute-start.16
  58.5 3.2 %rows_grads.7 = (bf16[136,1024]{1,0:T(8,128)(2,1)S(1)}, bf16[136,1024]{1,0:T(8,128)(2,1)S(1)}, bf16[256,2304]{1,0:T(8,128)(2,1)S(1)}) custom-call(bf16[136,1024]{1,0:T(8,128)(2,1)S(1)} %collective-permute-done.12.refs_0_.refs_6_, bf16[136,1024]{1,0:T(8,128)(2,1)S(1)} %collective-permute-done.13.refs_1_.refs_7_, ...), custom_call_target="tpu_custom_call" | custom-call | flops 2013265920 | bytes 9043968 | tf_op jit(solution)/shard_map/rows_grads/pallas_call | solution.py:188
  61.8 1.4 %collective-permute-start.22 = (bf16[136,1024]{1,0:T(8,128)(2,1)S(1)}, bf16[136,1024]{1,0:T(8,128)(2,1)S(1)}, u32[]{:S(2)}, u32[]{:S(2)}) collective-permute-start(bf16[136,1024]{1,0:T(8,128)(2,1)S(1)} %get-tuple-element.103), channel_id=1, source_target_pairs={{0,2},{1,3},{2,0},{3,1},{4,6},{5,7},{6,4},{7,5},{8,10},{9,11},{10,... | collective-permute-start | bytes 835592 | tf_op jit(solution)/shard_map/ppermute | solution.py:350
  63.2 0.1 add_convert_fusion.1
  63.3 2.1 %collective-permute-start.20 = (bf16[136,1024]{1,0:T(8,128)(2,1)S(1)}, bf16[136,1024]{1,0:T(8,128)(2,1)S(1)}, u32[]{:S(2)}, u32[]{:S(2)}) collective-permute-start(bf16[136,1024]{1,0:T(8,128)(2,1)S(1)} %add_convert_fusion.1), channel_id=1, source_target_pairs={{0,4},{1,5},{2,6},{3,7},{4,8},{5,9},{6,10},{7,11},{8,12},{9,13},{1... | collective-permute-start | bytes 835592 | tf_op jit(solution)/shard_map/ppermute | solution.py:344
  65.4 3.5 %weights_grads.2 = (bf16[1024,384]{1,0:T(8,128)(2,1)S(1)}, bf16[1024,384]{1,0:T(8,128)(2,1)S(1)}, bf16[384,1024]{1,0:T(8,128)(2,1)S(1)}) custom-call(bf16[136,1024]{1,0:T(8,128)(2,1)S(1)} %copy-done, bf16[136,1024]{1,0:T(8,128)(2,1)S(1)} %collective-permute-done.refs_1_, bf16[136,1024]{1,0:T(8,128)(2,1)S(1)} %collective-permute-done.1.refs_0_.refs_2_, ...), custom_call_target="tpu_custom_call" | custom-call | flops 1000 | bytes 1000 | tf_op jit(solution)/shard_map/weights_grads/pallas_call | solution.py:263
  68.9 0.1 collective-permute-start.24
  69.0 0.5 collective-permute-start.25
  69.5 0.0 collective-permute-done.16
  69.5 0.1 collective-permute-start.26
  69.6 0.1 add_convert_fusion.2
  69.7 3.3 %collective-permute-start.17 = (bf16[136,1024]{1,0:T(8,128)(2,1)S(1)}, bf16[136,1024]{1,0:T(8,128)(2,1)S(1)}, u32[]{:S(2)}, u32[]{:S(2)}) collective-permute-start(bf16[136,1024]{1,0:T(8,128)(2,1)S(1)} %add_convert_fusion.2), channel_id=1, source_target_pairs={{0,2},{1,3},{2,0},{3,1},{4,6},{5,7},{6,4},{7,5},{8,10},{9,11},{10,... | collective-permute-start | bytes 835592 | tf_op jit(solution)/shard_map/ppermute | solution.py:350
  73.0 0.0 collective-permute-done.20
  73.0 0.1 add_convert_fusion
  73.2 0.0 copy-start.2
  73.2 0.0 copy-start.5
  73.2 0.1 collective-permute-start.23
  73.3 0.3 collective-permute-done.26.refs_22_
  73.5 4.4 %weights_grads.3 = (bf16[1,1024,384]{2,1,0:T(8,128)(2,1)}, bf16[1,1024,384]{2,1,0:T(8,128)(2,1)}, bf16[1,384,1024]{2,1,0:T(8,128)(2,1)}) custom-call(bf16[136,1024]{1,0:T(8,128)(2,1)S(1)} %copy-done, bf16[136,1024]{1,0:T(8,128)(2,1)S(1)} %collective-permute-done.refs_1_, bf16[136,1024]{1,0:T(8,128)(2,1)S(1)} %collective-permute-done.1.refs_0_.refs_2_, ...), custom_call_target="tpu_custom_call" | custom-call | flops 1000 | bytes 1000 | tf_op jit(solution)/shard_map/weights_grads/pallas_call | solution.py:263
  78.0 2.4 %collective-permute-done.17.refs_1_ = bf16[136,1024]{1,0:T(8,128)(2,1)S(1)} collective-permute-done((bf16[136,1024]{1,0:T(8,128)(2,1)S(1)}, bf16[136,1024]{1,0:T(8,128)(2,1)S(1)}, u32[]{:S(2)}, u32[]{:S(2)}) %collective-permute-start.17) | collective-permute-done | bytes 278560 | tf_op jit(solution)/shard_map/ppermute | solution.py:350
  80.3 3.5 %collective-permute-done.23.refs_2_ = bf16[136,1024]{1,0:T(8,128)(2,1)S(1)} collective-permute-done((bf16[136,1024]{1,0:T(8,128)(2,1)S(1)}, bf16[136,1024]{1,0:T(8,128)(2,1)S(1)}, u32[]{:S(2)}, u32[]{:S(2)}) %collective-permute-start.23) | collective-permute-done | bytes 278560 | tf_op jit(solution)/shard_map/ppermute | solution.py:344
  83.8 0.8 finish.1
  (20 shorter events, 0.0 us)
Async XLA Ops:
  0.6 7.0 %collective-permute-start.2 = (bf16[1024,384]{1,0:T(8,128)(2,1)}, bf16[1024,384]{1,0:T(8,128)(2,1)S(1)}, u32[]{:S(2)}, u32[]{:S(2)}) collective-permute-start(bf16[1024,384]{1,0:T(8,128)(2,1)} %bitcast.9), channel_id=1, source_target_pairs={{0,1},{1,0},{2,3},{3,2},{4,5},{5,4},{6,7},{7,6},{8,9},{9,8},{10,11... | collective-permute-start | bytes 2359304 | tf_op jit(solution)/shard_map/ppermute | solution.py:353
  1.1 8.1 %collective-permute-start.3 = (bf16[1024,384]{1,0:T(8,128)(2,1)}, bf16[1024,384]{1,0:T(8,128)(2,1)S(1)}, u32[]{:S(2)}, u32[]{:S(2)}) collective-permute-start(bf16[1024,384]{1,0:T(8,128)(2,1)} %bitcast.14), channel_id=1, source_target_pairs={{0,1},{1,0},{2,3},{3,2},{4,5},{5,4},{6,7},{7,6},{8,9},{9,8},{10,11... | collective-permute-start | bytes 2359304 | tf_op jit(solution)/shard_map/ppermute | solution.py:353
  1.2 8.5 %collective-permute-start.4 = (bf16[384,1024]{1,0:T(8,128)(2,1)}, bf16[384,1024]{1,0:T(8,128)(2,1)S(1)}, u32[]{:S(2)}, u32[]{:S(2)}) collective-permute-start(bf16[384,1024]{1,0:T(8,128)(2,1)} %bitcast.19), channel_id=1, source_target_pairs={{0,1},{1,0},{2,3},{3,2},{4,5},{5,4},{6,7},{7,6},{8,9},{9,8},{10,11... | collective-permute-start | bytes 2359304 | tf_op jit(solution)/shard_map/ppermute | solution.py:353
  1.7 20.3 %collective-permute-start.6 = (bf16[128,1024]{1,0:T(8,128)(2,1)}, bf16[128,1024]{1,0:T(8,128)(2,1)S(1)}, u32[]{:S(2)}, u32[]{:S(2)}) collective-permute-start(bf16[128,1024]{1,0:T(8,128)(2,1)} %refs_8_.3), channel_id=1, source_target_pairs={{0,4},{1,5},{2,6},{3,7},{4,8},{5,9},{6,10},{7,11},{8,12},{9,13},{1... | collective-permute-start | bytes 786440 | tf_op jit(solution)/shard_map/ppermute | solution.py:344
  4.3 17.7 %collective-permute-start.5 = (bf16[128,1024]{1,0:T(8,128)(2,1)}, bf16[128,1024]{1,0:T(8,128)(2,1)S(1)}, u32[]{:S(2)}, u32[]{:S(2)}) collective-permute-start(bf16[128,1024]{1,0:T(8,128)(2,1)} %refs_8_.3), channel_id=1, source_target_pairs={{0,2},{1,3},{2,0},{3,1},{4,6},{5,7},{6,4},{7,5},{8,10},{9,11},{10,... | collective-permute-start | bytes 786440 | tf_op jit(solution)/shard_map/ppermute | solution.py:350
  7.6 11.8 %collective-permute-start.1 = (bf16[136,1024]{1,0:T(8,128)(2,1)}, bf16[136,1024]{1,0:T(8,128)(2,1)S(1)}, u32[]{:S(2)}, u32[]{:S(2)}) collective-permute-start(bf16[136,1024]{1,0:T(8,128)(2,1)} %get-tuple-element.65.refs_0_), channel_id=1, source_target_pairs={{0,4},{1,5},{2,6},{3,7},{4,8},{5,9},{6,10},{7,11},{8,12},{9,13},{1... | collective-permute-start | bytes 835592 | tf_op jit(solution)/shard_map/ppermute | solution.py:344
  9.2 10.2 %collective-permute-start = (bf16[136,1024]{1,0:T(8,128)(2,1)}, bf16[136,1024]{1,0:T(8,128)(2,1)S(1)}, u32[]{:S(2)}, u32[]{:S(2)}) collective-permute-start(bf16[136,1024]{1,0:T(8,128)(2,1)} %get-tuple-element.65.refs_0_), channel_id=1, source_target_pairs={{0,2},{1,3},{2,0},{3,1},{4,6},{5,7},{6,4},{7,5},{8,10},{9,11},{10,... | collective-permute-start | bytes 835592 | tf_op jit(solution)/shard_map/ppermute | solution.py:350
  9.7 0.7 copy-start.3
  10.4 13.6 %copy-start = (bf16[136,1024]{1,0:T(8,128)(2,1)S(1)}, bf16[136,1024]{1,0:T(8,128)(2,1)}, u32[]{:S(2)}) copy-start(bf16[136,1024]{1,0:T(8,128)(2,1)} %get-tuple-element.65.refs_0_) | copy-start | bytes 835588
  10.4 13.6 %copy-start.1 = (bf16[128,1024]{1,0:T(8,128)(2,1)S(1)}, bf16[128,1024]{1,0:T(8,128)(2,1)}, u32[]{:S(2)}) copy-start(bf16[128,1024]{1,0:T(8,128)(2,1)} %refs_8_.3) | copy-start | bytes 786436
  10.4 13.6 %copy-start.6 = (bf16[1,1024,384]{2,1,0:T(8,128)(2,1)S(1)}, bf16[1,1024,384]{2,1,0:T(8,128)(2,1)}, u32[]{:S(2)}) copy-start(bf16[1,1024,384]{2,1,0:T(8,128)(2,1)} %param.13) | copy-start | bytes 2359300
  10.4 13.6 %copy-start.7 = (bf16[1,1024,384]{2,1,0:T(8,128)(2,1)S(1)}, bf16[1,1024,384]{2,1,0:T(8,128)(2,1)}, u32[]{:S(2)}) copy-start(bf16[1,1024,384]{2,1,0:T(8,128)(2,1)} %param.14) | copy-start | bytes 2359300
  10.4 13.6 %copy-start.8 = (bf16[1,384,1024]{2,1,0:T(8,128)(2,1)S(1)}, bf16[1,384,1024]{2,1,0:T(8,128)(2,1)}, u32[]{:S(2)}) copy-start(bf16[1,384,1024]{2,1,0:T(8,128)(2,1)} %param.15) | copy-start | bytes 2359300
  10.5 0.6 copy-start.4
  19.4 11.3 %collective-permute-start.8 = (bf16[136,1024]{1,0:T(8,128)(2,1)S(1)}, bf16[136,1024]{1,0:T(8,128)(2,1)S(1)}, u32[]{:S(2)}, u32[]{:S(2)}) collective-permute-start(bf16[136,1024]{1,0:T(8,128)(2,1)S(1)} %collective-permute-done.1.refs_0_.refs_2_), channel_id=1, source_target_pairs={{0,4},{1,5},{2,6},{3,7},{4,8},{5,9},{6,10},{7,11},{8,12},{9,13},{1... | collective-permute-start | bytes 835592 | tf_op jit(solution)/shard_map/ppermute | solution.py:344
  20.4 10.3 %collective-permute-start.7 = (bf16[136,1024]{1,0:T(8,128)(2,1)S(1)}, bf16[136,1024]{1,0:T(8,128)(2,1)S(1)}, u32[]{:S(2)}, u32[]{:S(2)}) collective-permute-start(bf16[136,1024]{1,0:T(8,128)(2,1)S(1)} %collective-permute-done.1.refs_0_.refs_2_), channel_id=1, source_target_pairs={{0,2},{1,3},{2,0},{3,1},{4,6},{5,7},{6,4},{7,5},{8,10},{9,11},{10,... | collective-permute-start | bytes 835592 | tf_op jit(solution)/shard_map/ppermute | solution.py:350
  22.0 14.4 %collective-permute-start.10 = (bf16[128,1024]{1,0:T(8,128)(2,1)S(1)}, bf16[128,1024]{1,0:T(8,128)(2,1)S(1)}, u32[]{:S(2)}, u32[]{:S(2)}) collective-permute-start(bf16[128,1024]{1,0:T(8,128)(2,1)S(1)} %collective-permute-done.6.refs_2_.refs_10_), channel_id=1, source_target_pairs={{0,4},{1,5},{2,6},{3,7},{4,8},{5,9},{6,10},{7,11},{8,12},{9,13},{1... | collective-permute-start | bytes 786440 | tf_op jit(solution)/shard_map/ppermute | solution.py:344
  23.5 12.8 %collective-permute-start.9 = (bf16[128,1024]{1,0:T(8,128)(2,1)S(1)}, bf16[128,1024]{1,0:T(8,128)(2,1)S(1)}, u32[]{:S(2)}, u32[]{:S(2)}) collective-permute-start(bf16[128,1024]{1,0:T(8,128)(2,1)S(1)} %collective-permute-done.6.refs_2_.refs_10_), channel_id=1, source_target_pairs={{0,2},{1,3},{2,0},{3,1},{4,6},{5,7},{6,4},{7,5},{8,10},{9,11},{10,... | collective-permute-start | bytes 786440 | tf_op jit(solution)/shard_map/ppermute | solution.py:350
  30.8 11.6 %collective-permute-start.12 = (bf16[136,1024]{1,0:T(8,128)(2,1)S(1)}, bf16[136,1024]{1,0:T(8,128)(2,1)S(1)}, u32[]{:S(2)}, u32[]{:S(2)}) collective-permute-start(bf16[136,1024]{1,0:T(8,128)(2,1)S(1)} %collective-permute-done.8.refs_0_.refs_4_), channel_id=1, source_target_pairs={{0,4},{1,5},{2,6},{3,7},{4,8},{5,9},{6,10},{7,11},{8,12},{9,13},{1... | collective-permute-start | bytes 835592 | tf_op jit(solution)/shard_map/ppermute | solution.py:344
  31.6 10.7 %collective-permute-start.11 = (bf16[136,1024]{1,0:T(8,128)(2,1)S(1)}, bf16[136,1024]{1,0:T(8,128)(2,1)S(1)}, u32[]{:S(2)}, u32[]{:S(2)}) collective-permute-start(bf16[136,1024]{1,0:T(8,128)(2,1)S(1)} %collective-permute-done.8.refs_0_.refs_4_), channel_id=1, source_target_pairs={{0,2},{1,3},{2,0},{3,1},{4,6},{5,7},{6,4},{7,5},{8,10},{9,11},{10,... | collective-permute-start | bytes 835592 | tf_op jit(solution)/shard_map/ppermute | solution.py:350
  36.4 11.6 %collective-permute-start.15 = (bf16[128,1024]{1,0:T(8,128)(2,1)S(1)}, bf16[128,1024]{1,0:T(8,128)(2,1)S(1)}, u32[]{:S(2)}, u32[]{:S(2)}) collective-permute-start(bf16[128,1024]{1,0:T(8,128)(2,1)S(1)} %collective-permute-done.10.refs_2_.refs_12_), channel_id=1, source_target_pairs={{0,4},{1,5},{2,6},{3,7},{4,8},{5,9},{6,10},{7,11},{8,12},{9,13},{1... | collective-permute-start | bytes 786440 | tf_op jit(solution)/shard_map/ppermute | solution.py:344
  37.2 10.7 %collective-permute-start.14 = (bf16[128,1024]{1,0:T(8,128)(2,1)S(1)}, bf16[128,1024]{1,0:T(8,128)(2,1)S(1)}, u32[]{:S(2)}, u32[]{:S(2)}) collective-permute-start(bf16[128,1024]{1,0:T(8,128)(2,1)S(1)} %collective-permute-done.10.refs_2_.refs_12_), channel_id=1, source_target_pairs={{0,2},{1,3},{2,0},{3,1},{4,6},{5,7},{6,4},{7,5},{8,10},{9,11},{10,... | collective-permute-start | bytes 786440 | tf_op jit(solution)/shard_map/ppermute | solution.py:350
  42.4 16.2 %collective-permute-start.13 = (bf16[136,1024]{1,0:T(8,128)(2,1)S(1)}, bf16[136,1024]{1,0:T(8,128)(2,1)S(1)}, u32[]{:S(2)}, u32[]{:S(2)}) collective-permute-start(bf16[136,1024]{1,0:T(8,128)(2,1)S(1)} %collective-permute-done.12.refs_0_.refs_6_), channel_id=1, source_target_pairs={{0,2},{1,3},{2,0},{3,1},{4,6},{5,7},{6,4},{7,5},{8,10},{9,11},{10,... | collective-permute-start | bytes 835592 | tf_op jit(solution)/shard_map/ppermute | solution.py:350
  43.9 14.6 %collective-permute-start.18 = (bf16[136,1024]{1,0:T(8,128)(2,1)S(1)}, bf16[136,1024]{1,0:T(8,128)(2,1)S(1)}, u32[]{:S(2)}, u32[]{:S(2)}) collective-permute-start(bf16[136,1024]{1,0:T(8,128)(2,1)S(1)} %get-tuple-element.84), channel_id=1, source_target_pairs={{0,4},{1,5},{2,6},{3,7},{4,8},{5,9},{6,10},{7,11},{8,12},{9,13},{1... | collective-permute-start | bytes 835592 | tf_op jit(solution)/shard_map/ppermute | solution.py:344
  48.0 10.6 %collective-permute-start.21 = (bf16[128,1024]{1,0:T(8,128)(2,1)S(1)}, bf16[128,1024]{1,0:T(8,128)(2,1)S(1)}, u32[]{:S(2)}, u32[]{:S(2)}) collective-permute-start(bf16[128,1024]{1,0:T(8,128)(2,1)S(1)} %collective-permute-done.14.refs_3_.refs_13_), channel_id=1, source_target_pairs={{0,4},{1,5},{2,6},{3,7},{4,8},{5,9},{6,10},{7,11},{8,12},{9,13},{1... | collective-permute-start | bytes 786440 | tf_op jit(solution)/shard_map/ppermute | solution.py:344
  52.0 11.1 %collective-permute-start.19 = (bf16[136,1024]{1,0:T(8,128)(2,1)S(1)}, bf16[136,1024]{1,0:T(8,128)(2,1)S(1)}, u32[]{:S(2)}, u32[]{:S(2)}) collective-permute-start(bf16[136,1024]{1,0:T(8,128)(2,1)S(1)} %get-tuple-element.98), channel_id=1, source_target_pairs={{0,2},{1,3},{2,0},{3,1},{4,6},{5,7},{6,4},{7,5},{8,10},{9,11},{10,... | collective-permute-start | bytes 835592 | tf_op jit(solution)/shard_map/ppermute | solution.py:350
  58.5 11.0 %collective-permute-start.16 = (bf16[136,1024]{1,0:T(8,128)(2,1)S(1)}, bf16[136,1024]{1,0:T(8,128)(2,1)S(1)}, u32[]{:S(2)}, u32[]{:S(2)}) collective-permute-start(bf16[136,1024]{1,0:T(8,128)(2,1)S(1)} %get-tuple-element.94), channel_id=1, source_target_pairs={{0,12},{1,13},{2,14},{3,15},{4,0},{5,1},{6,2},{7,3},{8,4},{9,5},{1... | collective-permute-start | bytes 835592 | tf_op jit(solution)/shard_map/ppermute | solution.py:347
  61.8 7.9 %collective-permute-start.22 = (bf16[136,1024]{1,0:T(8,128)(2,1)S(1)}, bf16[136,1024]{1,0:T(8,128)(2,1)S(1)}, u32[]{:S(2)}, u32[]{:S(2)}) collective-permute-start(bf16[136,1024]{1,0:T(8,128)(2,1)S(1)} %get-tuple-element.103), channel_id=1, source_target_pairs={{0,2},{1,3},{2,0},{3,1},{4,6},{5,7},{6,4},{7,5},{8,10},{9,11},{10,... | collective-permute-start | bytes 835592 | tf_op jit(solution)/shard_map/ppermute | solution.py:350
  63.3 9.7 %collective-permute-start.20 = (bf16[136,1024]{1,0:T(8,128)(2,1)S(1)}, bf16[136,1024]{1,0:T(8,128)(2,1)S(1)}, u32[]{:S(2)}, u32[]{:S(2)}) collective-permute-start(bf16[136,1024]{1,0:T(8,128)(2,1)S(1)} %add_convert_fusion.1), channel_id=1, source_target_pairs={{0,4},{1,5},{2,6},{3,7},{4,8},{5,9},{6,10},{7,11},{8,12},{9,13},{1... | collective-permute-start | bytes 835592 | tf_op jit(solution)/shard_map/ppermute | solution.py:344
  68.9 4.3 %collective-permute-start.24 = (bf16[1024,384]{1,0:T(8,128)(2,1)S(1)}, bf16[1024,384]{1,0:T(8,128)(2,1)S(1)}, u32[]{:S(2)}, u32[]{:S(2)}) collective-permute-start(bf16[1024,384]{1,0:T(8,128)(2,1)S(1)} %get-tuple-element.108), channel_id=1, source_target_pairs={{0,1},{1,0},{2,3},{3,2},{4,5},{5,4},{6,7},{7,6},{8,9},{9,8},{10,11... | collective-permute-start | bytes 2359304 | tf_op jit(solution)/shard_map/ppermute | solution.py:353
  69.0 4.2 %collective-permute-start.25 = (bf16[1024,384]{1,0:T(8,128)(2,1)S(1)}, bf16[1024,384]{1,0:T(8,128)(2,1)S(1)}, u32[]{:S(2)}, u32[]{:S(2)}) collective-permute-start(bf16[1024,384]{1,0:T(8,128)(2,1)S(1)} %get-tuple-element.109), channel_id=1, source_target_pairs={{0,1},{1,0},{2,3},{3,2},{4,5},{5,4},{6,7},{7,6},{8,9},{9,8},{10,11... | collective-permute-start | bytes 2359304 | tf_op jit(solution)/shard_map/ppermute | solution.py:353
  69.5 4.0 %collective-permute-start.26 = (bf16[384,1024]{1,0:T(8,128)(2,1)S(1)}, bf16[384,1024]{1,0:T(8,128)(2,1)S(1)}, u32[]{:S(2)}, u32[]{:S(2)}) collective-permute-start(bf16[384,1024]{1,0:T(8,128)(2,1)S(1)} %get-tuple-element.110), channel_id=1, source_target_pairs={{0,1},{1,0},{2,3},{3,2},{4,5},{5,4},{6,7},{7,6},{8,9},{9,8},{10,11... | collective-permute-start | bytes 2359304 | tf_op jit(solution)/shard_map/ppermute | solution.py:353
  69.7 10.7 %collective-permute-start.17 = (bf16[136,1024]{1,0:T(8,128)(2,1)S(1)}, bf16[136,1024]{1,0:T(8,128)(2,1)S(1)}, u32[]{:S(2)}, u32[]{:S(2)}) collective-permute-start(bf16[136,1024]{1,0:T(8,128)(2,1)S(1)} %add_convert_fusion.2), channel_id=1, source_target_pairs={{0,2},{1,3},{2,0},{3,1},{4,6},{5,7},{6,4},{7,5},{8,10},{9,11},{10,... | collective-permute-start | bytes 835592 | tf_op jit(solution)/shard_map/ppermute | solution.py:350
  73.2 10.7 %copy-start.2 = (s32[128,8]{0,1:T(8,128)S(1)}, s32[128,8]{0,1:T(8,128)}, u32[]{:S(2)}) copy-start(s32[128,8]{0,1:T(8,128)} %param.11) | copy-start | bytes 12292
  73.2 10.7 %copy-start.5 = (f32[16,128]{1,0:T(8,128)S(1)}, f32[16,128]{1,0:T(8,128)}, u32[]{:S(2)}) copy-start(f32[16,128]{1,0:T(8,128)} %copy-done.4) | copy-start | bytes 24580
  73.2 10.6 %collective-permute-start.23 = (bf16[136,1024]{1,0:T(8,128)(2,1)S(1)}, bf16[136,1024]{1,0:T(8,128)(2,1)S(1)}, u32[]{:S(2)}, u32[]{:S(2)}) collective-permute-start(bf16[136,1024]{1,0:T(8,128)(2,1)S(1)} %add_convert_fusion), channel_id=1, source_target_pairs={{0,4},{1,5},{2,6},{3,7},{4,8},{5,9},{6,10},{7,11},{8,12},{9,13},{1... | collective-permute-start | bytes 835592 | tf_op jit(solution)/shard_map/ppermute | solution.py:344

commit v10 on v9

--- a/solution.py
+++ b/solution.py
@@ -183,7 +183,7 @@
     full = xgs[0].shape[0]
     hidden = weights[2].shape[0]
     rows = slots * tokens
-    flops = 2 * rows * 2 * 5 * width * hidden
+    flops = 1 * rows * 2 * 5 * width * hidden
     moved = 12 * rows * width + 12 * width * hidden + 12 * rows * hidden
     return pl.pallas_call(
         functools.partial(rows_kernel, slots),
@@ -400,8 +400,11 @@
             if ahead is not None:
                 done.append(ahead)
             if k == 0 and z == 1:
-                kept, weights = together(kept, weights)
-                done, kept = together(done, hold(kept, HOLD))
+                done, kept, held = together(done, hold(kept, HOLD), weights[3:5])
+                weights = own + held + weights[5:]
+            elif z == 1:
+                done, held = together(done, weights[5:])
+                weights = weights[:5] + held
             elif k == 0:
                 done, acts[z - 2] = together(done, acts[z - 2])
             else:

time: 84.8 us -> 84.5 us (level)
  starting transfers between devices: 29 us -> 28 us
    ppermute x10, starting transfers between devices: 12.4 us -> 9.87 us  [send_z(): lax.ppermute(v, 'expert', [(i, moved(i, 1, 0)) for i in range(devices)])]
    ppermute x10, starting transfers between devices: 15 us -> 16.8 us  [send_y(): lax.ppermute(v, 'expert', [(i, moved(i, 0, 1)) for i in range(devices)])]
  transfers between devices with their start and end apart: 27 -> 27, of which waited for: 9 -> 11; matrix products, arithmetic and copies ran while one was open for 0% -> 0% of each run, Pallas kernels for 27% -> 25%
where the time goes in v10:
time: 84.5 us; the launch traced here: 84.3 us
  waiting for transfers between devices  30.4 us (36%)
  starting transfers between devices  28 us (33%)
  Pallas kernels  23.4 us (28%)
  local copies, waits for them, and re-layouts  1.32 us (2%)
    ppermute x10, waiting for transfers between devices, send_z(): lax.ppermute(v, 'expert', [(i, moved(i, 1, 0)) for i in range(devices)])  27 us
    ppermute x10, starting transfers between devices, send_y(): lax.ppermute(v, 'expert', [(i, moved(i, 0, 1)) for i in range(devices)])  16.8 us
    pallas_call x4, Pallas kernels, rows_grads(): pl.pallas_call(functools.partial(rows_kernel, slots), out_shape=tuple((ja...  12.9 us
    ppermute x10, starting transfers between devices, send_z(): lax.ppermute(v, 'expert', [(i, moved(i, 1, 0)) for i in range(devices)])  9.87 us
    pallas_call x2, Pallas kernels, weights_grads(): pl.pallas_call(functools.partial(weights_kernel, j, slots, steps, len(mor...  7.96 us
    ppermute x10, waiting for transfers between devices, send_y(): lax.ppermute(v, 'expert', [(i, moved(i, 0, 1)) for i in range(devices)])  2.72 us
    pallas_call x1, Pallas kernels, plan(): pl.pallas_call(functools.partial(plan_kernel, home_cap, rep_cap), out_sha...  1.74 us
  transfers between devices with their start and end apart: 27, of which 11 were waited for; matrix products, arithmetic and copies ran while one was open for 0% of the time, Pallas kernels for 25%

profile of v10, /device:TPU:0, one launch (start us, length us, event | category | flops | bytes accessed | tf_op | source)
XLA Modules:
  0.0 84.3 jit_solution(13440714742770041831)
XLA Ops:
  0.6 1.7 %plan.1 = (bf16[136,1024]{1,0:T(8,128)(2,1)}, f32[16,128]{1,0:T(8,128)}) custom-call(s32[1,16]{1,0:T(1,128)} %bitcast.25, s32[8,128]{1,0:T(8,128)} %bitcast.22, bf16[8,128]{1,0:T(8,128)(2,1)} %bitcast.24, bf16[128,1024]{1,0:T(8,128)(2,1)} %x_in.1), custom_call_target="tpu_custom_call" | custom-call | tf_op jit(solution)/shard_map/plan/pallas_call | solution.py:86
  2.4 3.1 %collective-permute-start.1 = (bf16[136,1024]{1,0:T(8,128)(2,1)}, bf16[136,1024]{1,0:T(8,128)(2,1)S(1)}, u32[]{:S(2)}, u32[]{:S(2)}) collective-permute-start(bf16[136,1024]{1,0:T(8,128)(2,1)} %get-tuple-element.61.refs_0_), channel_id=1, source_target_pairs={{0,4},{1,5},{2,6},{3,7},{4,8},{5,9},{6,10},{7,11},{8,12},{9,13},{1... | collective-permute-start | bytes 835592 | tf_op jit(solution)/shard_map/ppermute | solution.py:344
  5.5 1.5 %collective-permute-start = (bf16[136,1024]{1,0:T(8,128)(2,1)}, bf16[136,1024]{1,0:T(8,128)(2,1)S(1)}, u32[]{:S(2)}, u32[]{:S(2)}) collective-permute-start(bf16[136,1024]{1,0:T(8,128)(2,1)} %get-tuple-element.61.refs_0_), channel_id=1, source_target_pairs={{0,2},{1,3},{2,0},{3,1},{4,6},{5,7},{6,4},{7,5},{8,10},{9,11},{10,... | collective-permute-start | bytes 835592 | tf_op jit(solution)/shard_map/ppermute | solution.py:350
  7.0 1.6 %collective-permute-start.5 = (bf16[128,1024]{1,0:T(8,128)(2,1)}, bf16[128,1024]{1,0:T(8,128)(2,1)S(1)}, u32[]{:S(2)}, u32[]{:S(2)}) collective-permute-start(bf16[128,1024]{1,0:T(8,128)(2,1)} %refs_8_.3), channel_id=1, source_target_pairs={{0,4},{1,5},{2,6},{3,7},{4,8},{5,9},{6,10},{7,11},{8,12},{9,13},{1... | collective-permute-start | bytes 786440 | tf_op jit(solution)/shard_map/ppermute | solution.py:344
  8.6 0.5 collective-permute-start.4
  9.1 0.0 collective-permute-start.2
  9.1 6.1 %collective-permute-done.1.refs_0_.refs_2_ = bf16[136,1024]{1,0:T(8,128)(2,1)S(1)} collective-permute-done((bf16[136,1024]{1,0:T(8,128)(2,1)}, bf16[136,1024]{1,0:T(8,128)(2,1)S(1)}, u32[]{:S(2)}, u32[]{:S(2)}) %collective-permute-start.1) | collective-permute-done | bytes 278560 | tf_op jit(solution)/shard_map/ppermute | solution.py:344
  15.2 0.0 collective-permute-start.3
  15.2 0.1 collective-permute-done.refs_1_
  15.3 0.4 collective-permute-start.6
  15.7 0.7 copy-done.6
  16.4 0.0 copy-start.7
  16.4 0.6 copy-done.7
  17.0 0.0 collective-permute-done.2.refs_7_
  17.0 0.6 collective-permute-done.3.refs_8_
  17.7 0.5 collective-permute-start.8
  18.2 1.5 %collective-permute-start.7 = (bf16[136,1024]{1,0:T(8,128)(2,1)S(1)}, bf16[136,1024]{1,0:T(8,128)(2,1)S(1)}, u32[]{:S(2)}, u32[]{:S(2)}) collective-permute-start(bf16[136,1024]{1,0:T(8,128)(2,1)S(1)} %collective-permute-done.1.refs_0_.refs_2_), channel_id=1, source_target_pairs={{0,2},{1,3},{2,0},{3,1},{4,6},{5,7},{6,4},{7,5},{8,10},{9,11},{10,... | collective-permute-start | bytes 835592 | tf_op jit(solution)/shard_map/ppermute | solution.py:350
  19.7 0.3 collective-permute-done.5.refs_2_.refs_10_
  20.0 0.0 collective-permute-done.4.refs_3_.refs_9_
  20.0 0.0 collective-permute-done.6.refs_9_
  20.0 1.4 %collective-permute-start.10 = (bf16[128,1024]{1,0:T(8,128)(2,1)S(1)}, bf16[128,1024]{1,0:T(8,128)(2,1)S(1)}, u32[]{:S(2)}, u32[]{:S(2)}) collective-permute-start(bf16[128,1024]{1,0:T(8,128)(2,1)S(1)} %collective-permute-done.5.refs_2_.refs_10_), channel_id=1, source_target_pairs={{0,4},{1,5},{2,6},{3,7},{4,8},{5,9},{6,10},{7,11},{8,12},{9,13},{1... | collective-permute-start | bytes 786440 | tf_op jit(solution)/shard_map/ppermute | solution.py:344
  21.3 1.2 %collective-permute-start.9 = (bf16[128,1024]{1,0:T(8,128)(2,1)S(1)}, bf16[128,1024]{1,0:T(8,128)(2,1)S(1)}, u32[]{:S(2)}, u32[]{:S(2)}) collective-permute-start(bf16[128,1024]{1,0:T(8,128)(2,1)S(1)} %collective-permute-done.5.refs_2_.refs_10_), channel_id=1, source_target_pairs={{0,2},{1,3},{2,0},{3,1},{4,6},{5,7},{6,4},{7,5},{8,10},{9,11},{10,... | collective-permute-start | bytes 786440 | tf_op jit(solution)/shard_map/ppermute | solution.py:350
  22.5 3.2 %rows_grads.4 = (bf16[136,1024]{1,0:T(8,128)(2,1)S(1)}, bf16[136,1024]{1,0:T(8,128)(2,1)S(1)}, bf16[256,2304]{1,0:T(8,128)(2,1)S(1)}) custom-call(bf16[136,1024]{1,0:T(8,128)(2,1)S(1)} %copy-done.3, bf16[136,1024]{1,0:T(8,128)(2,1)S(1)} %collective-permute-done.refs_1_, bf16[128,1024]{1,0:T(8,128)(2,1)S(1)} %copy-done.4, ...), custom_call_target="tpu_custom_call" | custom-call | flops 1006632960 | bytes 9043968 | tf_op jit(solution)/shard_map/rows_grads/pallas_call | solution.py:188
  25.7 3.2 %collective-permute-done.8.refs_0_.refs_4_ = bf16[136,1024]{1,0:T(8,128)(2,1)S(1)} collective-permute-done((bf16[136,1024]{1,0:T(8,128)(2,1)S(1)}, bf16[136,1024]{1,0:T(8,128)(2,1)S(1)}, u32[]{:S(2)}, u32[]{:S(2)}) %collective-permute-start.8) | collective-permute-done | bytes 278560 | tf_op jit(solution)/shard_map/ppermute | solution.py:344
  29.0 0.0 collective-permute-done.7.refs_1_.refs_3_
  29.0 0.3 collective-permute-start.12
  29.2 1.5 %collective-permute-start.11 = (bf16[136,1024]{1,0:T(8,128)(2,1)S(1)}, bf16[136,1024]{1,0:T(8,128)(2,1)S(1)}, u32[]{:S(2)}, u32[]{:S(2)}) collective-permute-start(bf16[136,1024]{1,0:T(8,128)(2,1)S(1)} %collective-permute-done.8.refs_0_.refs_4_), channel_id=1, source_target_pairs={{0,2},{1,3},{2,0},{3,1},{4,6},{5,7},{6,4},{7,5},{8,10},{9,11},{10,... | collective-permute-start | bytes 835592 | tf_op jit(solution)/shard_map/ppermute | solution.py:350
  30.8 3.8 %collective-permute-done.10.refs_2_.refs_12_ = bf16[128,1024]{1,0:T(8,128)(2,1)S(1)} collective-permute-done((bf16[128,1024]{1,0:T(8,128)(2,1)S(1)}, bf16[128,1024]{1,0:T(8,128)(2,1)S(1)}, u32[]{:S(2)}, u32[]{:S(2)}) %collective-permute-start.10) | collective-permute-done | bytes 262176 | tf_op jit(solution)/shard_map/ppermute | solution.py:344
  34.6 0.0 collective-permute-done.9.refs_3_.refs_11_
  34.6 0.3 collective-permute-start.15
  34.9 1.5 %collective-permute-start.14 = (bf16[128,1024]{1,0:T(8,128)(2,1)S(1)}, bf16[128,1024]{1,0:T(8,128)(2,1)S(1)}, u32[]{:S(2)}, u32[]{:S(2)}) collective-permute-start(bf16[128,1024]{1,0:T(8,128)(2,1)S(1)} %collective-permute-done.10.refs_2_.refs_12_), channel_id=1, source_target_pairs={{0,2},{1,3},{2,0},{3,1},{4,6},{5,7},{6,4},{7,5},{8,10},{9,11},{10,... | collective-permute-start | bytes 786440 | tf_op jit(solution)/shard_map/ppermute | solution.py:350
  36.4 3.2 %rows_grads.5 = (bf16[136,1024]{1,0:T(8,128)(2,1)S(1)}, bf16[136,1024]{1,0:T(8,128)(2,1)S(1)}, bf16[256,2304]{1,0:T(8,128)(2,1)S(1)}) custom-call(bf16[136,1024]{1,0:T(8,128)(2,1)S(1)} %collective-permute-done.1.refs_0_.refs_2_, bf16[136,1024]{1,0:T(8,128)(2,1)S(1)} %collective-permute-done.7.refs_1_.refs_3_, ...), custom_call_target="tpu_custom_call" | custom-call | flops 1006632960 | bytes 9043968 | tf_op jit(solution)/shard_map/rows_grads/pallas_call | solution.py:188
  39.6 1.0 %collective-permute-done.12.refs_0_.refs_6_ = bf16[136,1024]{1,0:T(8,128)(2,1)S(1)} collective-permute-done((bf16[136,1024]{1,0:T(8,128)(2,1)S(1)}, bf16[136,1024]{1,0:T(8,128)(2,1)S(1)}, u32[]{:S(2)}, u32[]{:S(2)}) %collective-permute-start.12) | collective-permute-done | bytes 278560 | tf_op jit(solution)/shard_map/ppermute | solution.py:344
  40.6 1.8 %collective-permute-start.13 = (bf16[136,1024]{1,0:T(8,128)(2,1)S(1)}, bf16[136,1024]{1,0:T(8,128)(2,1)S(1)}, u32[]{:S(2)}, u32[]{:S(2)}) collective-permute-start(bf16[136,1024]{1,0:T(8,128)(2,1)S(1)} %collective-permute-done.12.refs_0_.refs_6_), channel_id=1, source_target_pairs={{0,2},{1,3},{2,0},{3,1},{4,6},{5,7},{6,4},{7,5},{8,10},{9,11},{10,... | collective-permute-start | bytes 835592 | tf_op jit(solution)/shard_map/ppermute | solution.py:350
  42.3 0.0 collective-permute-start.18
  42.3 3.4 %collective-permute-done.15.refs_2_.refs_14_ = bf16[128,1024]{1,0:T(8,128)(2,1)S(1)} collective-permute-done((bf16[128,1024]{1,0:T(8,128)(2,1)S(1)}, bf16[128,1024]{1,0:T(8,128)(2,1)S(1)}, u32[]{:S(2)}, u32[]{:S(2)}) %collective-permute-start.15) | collective-permute-done | bytes 262176 | tf_op jit(solution)/shard_map/ppermute | solution.py:344
  45.7 0.7 collective-permute-start.21
  46.4 3.2 %rows_grads.6 = (bf16[136,1024]{1,0:T(8,128)(2,1)S(1)}, bf16[136,1024]{1,0:T(8,128)(2,1)S(1)}, bf16[256,2304]{1,0:T(8,128)(2,1)S(1)}) custom-call(bf16[136,1024]{1,0:T(8,128)(2,1)S(1)} %collective-permute-done.8.refs_0_.refs_4_, bf16[136,1024]{1,0:T(8,128)(2,1)S(1)} %collective-permute-done.11.refs_1_.refs_5_, ...), custom_call_target="tpu_custom_call" | custom-call | flops 1006632960 | bytes 9043968 | tf_op jit(solution)/shard_map/rows_grads/pallas_call | solution.py:188
  49.7 1.6 %collective-permute-start.19 = (bf16[136,1024]{1,0:T(8,128)(2,1)S(1)}, bf16[136,1024]{1,0:T(8,128)(2,1)S(1)}, u32[]{:S(2)}, u32[]{:S(2)}) collective-permute-start(bf16[136,1024]{1,0:T(8,128)(2,1)S(1)} %get-tuple-element.90), channel_id=1, source_target_pairs={{0,2},{1,3},{2,0},{3,1},{4,6},{5,7},{6,4},{7,5},{8,10},{9,11},{10,... | collective-permute-start | bytes 835592 | tf_op jit(solution)/shard_map/ppermute | solution.py:350
  51.2 5.7 %collective-permute-done.21.refs_3_.refs_15_ = bf16[128,1024]{1,0:T(8,128)(2,1)S(1)} collective-permute-done((bf16[128,1024]{1,0:T(8,128)(2,1)S(1)}, bf16[128,1024]{1,0:T(8,128)(2,1)S(1)}, u32[]{:S(2)}, u32[]{:S(2)}) %collective-permute-start.21) | collective-permute-done | bytes 262176 | tf_op jit(solution)/shard_map/ppermute | solution.py:344
  57.0 0.0 collective-permute-done.13.refs_1_.refs_7_
  57.0 0.0 collective-permute-done.18
  57.0 0.3 collective-permute-start.16
  57.2 3.2 %rows_grads.7 = (bf16[136,1024]{1,0:T(8,128)(2,1)S(1)}, bf16[136,1024]{1,0:T(8,128)(2,1)S(1)}, bf16[256,2304]{1,0:T(8,128)(2,1)S(1)}) custom-call(bf16[136,1024]{1,0:T(8,128)(2,1)S(1)} %collective-permute-done.12.refs_0_.refs_6_, bf16[136,1024]{1,0:T(8,128)(2,1)S(1)} %collective-permute-done.13.refs_1_.refs_7_, ...), custom_call_target="tpu_custom_call" | custom-call | flops 1006632960 | bytes 9043968 | tf_op jit(solution)/shard_map/rows_grads/pallas_call | solution.py:188
  60.5 1.6 %collective-permute-start.22 = (bf16[136,1024]{1,0:T(8,128)(2,1)S(1)}, bf16[136,1024]{1,0:T(8,128)(2,1)S(1)}, u32[]{:S(2)}, u32[]{:S(2)}) collective-permute-start(bf16[136,1024]{1,0:T(8,128)(2,1)S(1)} %get-tuple-element.95), channel_id=1, source_target_pairs={{0,2},{1,3},{2,0},{3,1},{4,6},{5,7},{6,4},{7,5},{8,10},{9,11},{10,... | collective-permute-start | bytes 835592 | tf_op jit(solution)/shard_map/ppermute | solution.py:350
  62.0 0.0 collective-permute-done.19
  62.0 0.1 add_convert_fusion.1
  62.2 2.1 %collective-permute-start.20 = (bf16[136,1024]{1,0:T(8,128)(2,1)S(1)}, bf16[136,1024]{1,0:T(8,128)(2,1)S(1)}, u32[]{:S(2)}, u32[]{:S(2)}) collective-permute-start(bf16[136,1024]{1,0:T(8,128)(2,1)S(1)} %add_convert_fusion.1), channel_id=1, source_target_pairs={{0,4},{1,5},{2,6},{3,7},{4,8},{5,9},{6,10},{7,11},{8,12},{9,13},{1... | collective-permute-start | bytes 835592 | tf_op jit(solution)/shard_map/ppermute | solution.py:344
  64.3 3.5 %weights_grads.2 = (bf16[1024,384]{1,0:T(8,128)(2,1)S(1)}, bf16[1024,384]{1,0:T(8,128)(2,1)S(1)}, bf16[384,1024]{1,0:T(8,128)(2,1)S(1)}) custom-call(bf16[136,1024]{1,0:T(8,128)(2,1)S(1)} %copy-done.3, bf16[136,1024]{1,0:T(8,128)(2,1)S(1)} %collective-permute-done.refs_1_, bf16[136,1024]{1,0:T(8,128)(2,1)S(1)} %collective-permute-done.1.refs_0_.refs_2_, ...), custom_call_target="tpu_custom_call" | custom-call | flops 1000 | bytes 1000 | tf_op jit(solution)/shard_map/weights_grads/pallas_call | solution.py:263
  67.8 0.1 collective-permute-start.24
  67.9 0.5 collective-permute-start.25
  68.4 0.1 collective-permute-start.26
  68.4 0.1 add_convert_fusion.2
  68.5 4.1 %collective-permute-start.17 = (bf16[136,1024]{1,0:T(8,128)(2,1)S(1)}, bf16[136,1024]{1,0:T(8,128)(2,1)S(1)}, u32[]{:S(2)}, u32[]{:S(2)}) collective-permute-start(bf16[136,1024]{1,0:T(8,128)(2,1)S(1)} %add_convert_fusion.2), channel_id=1, source_target_pairs={{0,2},{1,3},{2,0},{3,1},{4,6},{5,7},{6,4},{7,5},{8,10},{9,11},{10,... | collective-permute-start | bytes 835592 | tf_op jit(solution)/shard_map/ppermute | solution.py:350
  72.7 0.1 add_convert_fusion
  72.8 0.0 copy-start.5
  72.8 0.0 copy-start.8
  72.8 0.1 collective-permute-start.23
  72.9 0.0 collective-permute-done.24.refs_20_
  72.9 0.0 collective-permute-done.25.refs_21_
  72.9 4.4 %weights_grads.3 = (bf16[1,1024,384]{2,1,0:T(8,128)(2,1)}, bf16[1,1024,384]{2,1,0:T(8,128)(2,1)}, bf16[1,384,1024]{2,1,0:T(8,128)(2,1)}) custom-call(bf16[136,1024]{1,0:T(8,128)(2,1)S(1)} %copy-done.3, bf16[136,1024]{1,0:T(8,128)(2,1)S(1)} %collective-permute-done.refs_1_, bf16[136,1024]{1,0:T(8,128)(2,1)S(1)} %collective-permute-done.1.refs_0_.refs_2_, ...), custom_call_target="tpu_custom_call" | custom-call | flops 1000 | bytes 1000 | tf_op jit(solution)/shard_map/weights_grads/pallas_call | solution.py:263
  77.4 2.6 %collective-permute-done.17.refs_1_ = bf16[136,1024]{1,0:T(8,128)(2,1)S(1)} collective-permute-done((bf16[136,1024]{1,0:T(8,128)(2,1)S(1)}, bf16[136,1024]{1,0:T(8,128)(2,1)S(1)}, u32[]{:S(2)}, u32[]{:S(2)}) %collective-permute-start.17) | collective-permute-done | bytes 278560 | tf_op jit(solution)/shard_map/ppermute | solution.py:350
  80.0 3.5 %collective-permute-done.23.refs_2_ = bf16[136,1024]{1,0:T(8,128)(2,1)S(1)} collective-permute-done((bf16[136,1024]{1,0:T(8,128)(2,1)S(1)}, bf16[136,1024]{1,0:T(8,128)(2,1)S(1)}, u32[]{:S(2)}, u32[]{:S(2)}) %collective-permute-start.23) | collective-permute-done | bytes 278560 | tf_op jit(solution)/shard_map/ppermute | solution.py:344
  83.5 0.8 finish.1
  (20 shorter events, 0.0 us)
Async XLA Ops:
  2.4 12.8 %collective-permute-start.1 = (bf16[136,1024]{1,0:T(8,128)(2,1)}, bf16[136,1024]{1,0:T(8,128)(2,1)S(1)}, u32[]{:S(2)}, u32[]{:S(2)}) collective-permute-start(bf16[136,1024]{1,0:T(8,128)(2,1)} %get-tuple-element.61.refs_0_), channel_id=1, source_target_pairs={{0,4},{1,5},{2,6},{3,7},{4,8},{5,9},{6,10},{7,11},{8,12},{9,13},{1... | collective-permute-start | bytes 835592 | tf_op jit(solution)/shard_map/ppermute | solution.py:344
  5.5 9.8 %collective-permute-start = (bf16[136,1024]{1,0:T(8,128)(2,1)}, bf16[136,1024]{1,0:T(8,128)(2,1)S(1)}, u32[]{:S(2)}, u32[]{:S(2)}) collective-permute-start(bf16[136,1024]{1,0:T(8,128)(2,1)} %get-tuple-element.61.refs_0_), channel_id=1, source_target_pairs={{0,2},{1,3},{2,0},{3,1},{4,6},{5,7},{6,4},{7,5},{8,10},{9,11},{10,... | collective-permute-start | bytes 835592 | tf_op jit(solution)/shard_map/ppermute | solution.py:350
  7.0 13.0 %collective-permute-start.5 = (bf16[128,1024]{1,0:T(8,128)(2,1)}, bf16[128,1024]{1,0:T(8,128)(2,1)S(1)}, u32[]{:S(2)}, u32[]{:S(2)}) collective-permute-start(bf16[128,1024]{1,0:T(8,128)(2,1)} %refs_8_.3), channel_id=1, source_target_pairs={{0,4},{1,5},{2,6},{3,7},{4,8},{5,9},{6,10},{7,11},{8,12},{9,13},{1... | collective-permute-start | bytes 786440 | tf_op jit(solution)/shard_map/ppermute | solution.py:344
  8.6 11.4 %collective-permute-start.4 = (bf16[128,1024]{1,0:T(8,128)(2,1)}, bf16[128,1024]{1,0:T(8,128)(2,1)S(1)}, u32[]{:S(2)}, u32[]{:S(2)}) collective-permute-start(bf16[128,1024]{1,0:T(8,128)(2,1)} %refs_8_.3), channel_id=1, source_target_pairs={{0,2},{1,3},{2,0},{3,1},{4,6},{5,7},{6,4},{7,5},{8,10},{9,11},{10,... | collective-permute-start | bytes 786440 | tf_op jit(solution)/shard_map/ppermute | solution.py:350
  9.1 8.0 %collective-permute-start.2 = (bf16[1024,384]{1,0:T(8,128)(2,1)}, bf16[1024,384]{1,0:T(8,128)(2,1)S(1)}, u32[]{:S(2)}, u32[]{:S(2)}) collective-permute-start(bf16[1024,384]{1,0:T(8,128)(2,1)} %bitcast.7), channel_id=1, source_target_pairs={{0,1},{1,0},{2,3},{3,2},{4,5},{5,4},{6,7},{7,6},{8,9},{9,8},{10,11... | collective-permute-start | bytes 2359304 | tf_op jit(solution)/shard_map/ppermute | solution.py:353
  15.2 2.5 %collective-permute-start.3 = (bf16[1024,384]{1,0:T(8,128)(2,1)}, bf16[1024,384]{1,0:T(8,128)(2,1)S(1)}, u32[]{:S(2)}, u32[]{:S(2)}) collective-permute-start(bf16[1024,384]{1,0:T(8,128)(2,1)} %bitcast.12), channel_id=1, source_target_pairs={{0,1},{1,0},{2,3},{3,2},{4,5},{5,4},{6,7},{7,6},{8,9},{9,8},{10,11... | collective-permute-start | bytes 2359304 | tf_op jit(solution)/shard_map/ppermute | solution.py:353
  15.3 4.7 %collective-permute-start.6 = (bf16[384,1024]{1,0:T(8,128)(2,1)}, bf16[384,1024]{1,0:T(8,128)(2,1)S(1)}, u32[]{:S(2)}, u32[]{:S(2)}) collective-permute-start(bf16[384,1024]{1,0:T(8,128)(2,1)} %bitcast.17), channel_id=1, source_target_pairs={{0,1},{1,0},{2,3},{3,2},{4,5},{5,4},{6,7},{7,6},{8,9},{9,8},{10,11... | collective-permute-start | bytes 2359304 | tf_op jit(solution)/shard_map/ppermute | solution.py:353
  15.7 0.7 copy-start.6
  16.4 6.1 %copy-start = (bf16[1,1024,384]{2,1,0:T(8,128)(2,1)S(1)}, bf16[1,1024,384]{2,1,0:T(8,128)(2,1)}, u32[]{:S(2)}) copy-start(bf16[1,1024,384]{2,1,0:T(8,128)(2,1)} %param.13) | copy-start | bytes 2359300
  16.4 6.1 %copy-start.1 = (bf16[1,1024,384]{2,1,0:T(8,128)(2,1)S(1)}, bf16[1,1024,384]{2,1,0:T(8,128)(2,1)}, u32[]{:S(2)}) copy-start(bf16[1,1024,384]{2,1,0:T(8,128)(2,1)} %param.14) | copy-start | bytes 2359300
  16.4 6.1 %copy-start.2 = (bf16[1,384,1024]{2,1,0:T(8,128)(2,1)S(1)}, bf16[1,384,1024]{2,1,0:T(8,128)(2,1)}, u32[]{:S(2)}) copy-start(bf16[1,384,1024]{2,1,0:T(8,128)(2,1)} %param.15) | copy-start | bytes 2359300
  16.4 6.1 %copy-start.3 = (bf16[136,1024]{1,0:T(8,128)(2,1)S(1)}, bf16[136,1024]{1,0:T(8,128)(2,1)}, u32[]{:S(2)}) copy-start(bf16[136,1024]{1,0:T(8,128)(2,1)} %get-tuple-element.61.refs_0_) | copy-start | bytes 835588
  16.4 6.1 %copy-start.4 = (bf16[128,1024]{1,0:T(8,128)(2,1)S(1)}, bf16[128,1024]{1,0:T(8,128)(2,1)}, u32[]{:S(2)}) copy-start(bf16[128,1024]{1,0:T(8,128)(2,1)} %refs_8_.3) | copy-start | bytes 786436
  16.4 0.6 copy-start.7
  17.7 11.3 %collective-permute-start.8 = (bf16[136,1024]{1,0:T(8,128)(2,1)S(1)}, bf16[136,1024]{1,0:T(8,128)(2,1)S(1)}, u32[]{:S(2)}, u32[]{:S(2)}) collective-permute-start(bf16[136,1024]{1,0:T(8,128)(2,1)S(1)} %collective-permute-done.1.refs_0_.refs_2_), channel_id=1, source_target_pairs={{0,4},{1,5},{2,6},{3,7},{4,8},{5,9},{6,10},{7,11},{8,12},{9,13},{1... | collective-permute-start | bytes 835592 | tf_op jit(solution)/shard_map/ppermute | solution.py:344
  18.2 10.8 %collective-permute-start.7 = (bf16[136,1024]{1,0:T(8,128)(2,1)S(1)}, bf16[136,1024]{1,0:T(8,128)(2,1)S(1)}, u32[]{:S(2)}, u32[]{:S(2)}) collective-permute-start(bf16[136,1024]{1,0:T(8,128)(2,1)S(1)} %collective-permute-done.1.refs_0_.refs_2_), channel_id=1, source_target_pairs={{0,2},{1,3},{2,0},{3,1},{4,6},{5,7},{6,4},{7,5},{8,10},{9,11},{10,... | collective-permute-start | bytes 835592 | tf_op jit(solution)/shard_map/ppermute | solution.py:350
  20.0 14.6 %collective-permute-start.10 = (bf16[128,1024]{1,0:T(8,128)(2,1)S(1)}, bf16[128,1024]{1,0:T(8,128)(2,1)S(1)}, u32[]{:S(2)}, u32[]{:S(2)}) collective-permute-start(bf16[128,1024]{1,0:T(8,128)(2,1)S(1)} %collective-permute-done.5.refs_2_.refs_10_), channel_id=1, source_target_pairs={{0,4},{1,5},{2,6},{3,7},{4,8},{5,9},{6,10},{7,11},{8,12},{9,13},{1... | collective-permute-start | bytes 786440 | tf_op jit(solution)/shard_map/ppermute | solution.py:344
  21.3 13.3 %collective-permute-start.9 = (bf16[128,1024]{1,0:T(8,128)(2,1)S(1)}, bf16[128,1024]{1,0:T(8,128)(2,1)S(1)}, u32[]{:S(2)}, u32[]{:S(2)}) collective-permute-start(bf16[128,1024]{1,0:T(8,128)(2,1)S(1)} %collective-permute-done.5.refs_2_.refs_10_), channel_id=1, source_target_pairs={{0,2},{1,3},{2,0},{3,1},{4,6},{5,7},{6,4},{7,5},{8,10},{9,11},{10,... | collective-permute-start | bytes 786440 | tf_op jit(solution)/shard_map/ppermute | solution.py:350
  29.0 11.6 %collective-permute-start.12 = (bf16[136,1024]{1,0:T(8,128)(2,1)S(1)}, bf16[136,1024]{1,0:T(8,128)(2,1)S(1)}, u32[]{:S(2)}, u32[]{:S(2)}) collective-permute-start(bf16[136,1024]{1,0:T(8,128)(2,1)S(1)} %collective-permute-done.8.refs_0_.refs_4_), channel_id=1, source_target_pairs={{0,4},{1,5},{2,6},{3,7},{4,8},{5,9},{6,10},{7,11},{8,12},{9,13},{1... | collective-permute-start | bytes 835592 | tf_op jit(solution)/shard_map/ppermute | solution.py:344
  29.2 11.3 %collective-permute-start.11 = (bf16[136,1024]{1,0:T(8,128)(2,1)S(1)}, bf16[136,1024]{1,0:T(8,128)(2,1)S(1)}, u32[]{:S(2)}, u32[]{:S(2)}) collective-permute-start(bf16[136,1024]{1,0:T(8,128)(2,1)S(1)} %collective-permute-done.8.refs_0_.refs_4_), channel_id=1, source_target_pairs={{0,2},{1,3},{2,0},{3,1},{4,6},{5,7},{6,4},{7,5},{8,10},{9,11},{10,... | collective-permute-start | bytes 835592 | tf_op jit(solution)/shard_map/ppermute | solution.py:350
  34.6 11.1 %collective-permute-start.15 = (bf16[128,1024]{1,0:T(8,128)(2,1)S(1)}, bf16[128,1024]{1,0:T(8,128)(2,1)S(1)}, u32[]{:S(2)}, u32[]{:S(2)}) collective-permute-start(bf16[128,1024]{1,0:T(8,128)(2,1)S(1)} %collective-permute-done.10.refs_2_.refs_12_), channel_id=1, source_target_pairs={{0,4},{1,5},{2,6},{3,7},{4,8},{5,9},{6,10},{7,11},{8,12},{9,13},{1... | collective-permute-start | bytes 786440 | tf_op jit(solution)/shard_map/ppermute | solution.py:344
  34.9 10.9 %collective-permute-start.14 = (bf16[128,1024]{1,0:T(8,128)(2,1)S(1)}, bf16[128,1024]{1,0:T(8,128)(2,1)S(1)}, u32[]{:S(2)}, u32[]{:S(2)}) collective-permute-start(bf16[128,1024]{1,0:T(8,128)(2,1)S(1)} %collective-permute-done.10.refs_2_.refs_12_), channel_id=1, source_target_pairs={{0,2},{1,3},{2,0},{3,1},{4,6},{5,7},{6,4},{7,5},{8,10},{9,11},{10,... | collective-permute-start | bytes 786440 | tf_op jit(solution)/shard_map/ppermute | solution.py:350
  40.6 16.4 %collective-permute-start.13 = (bf16[136,1024]{1,0:T(8,128)(2,1)S(1)}, bf16[136,1024]{1,0:T(8,128)(2,1)S(1)}, u32[]{:S(2)}, u32[]{:S(2)}) collective-permute-start(bf16[136,1024]{1,0:T(8,128)(2,1)S(1)} %collective-permute-done.12.refs_0_.refs_6_), channel_id=1, source_target_pairs={{0,2},{1,3},{2,0},{3,1},{4,6},{5,7},{6,4},{7,5},{8,10},{9,11},{10,... | collective-permute-start | bytes 835592 | tf_op jit(solution)/shard_map/ppermute | solution.py:350
  42.3 14.6 %collective-permute-start.18 = (bf16[136,1024]{1,0:T(8,128)(2,1)S(1)}, bf16[136,1024]{1,0:T(8,128)(2,1)S(1)}, u32[]{:S(2)}, u32[]{:S(2)}) collective-permute-start(bf16[136,1024]{1,0:T(8,128)(2,1)S(1)} %get-tuple-element.76), channel_id=1, source_target_pairs={{0,4},{1,5},{2,6},{3,7},{4,8},{5,9},{6,10},{7,11},{8,12},{9,13},{1... | collective-permute-start | bytes 835592 | tf_op jit(solution)/shard_map/ppermute | solution.py:344
  45.7 11.2 %collective-permute-start.21 = (bf16[128,1024]{1,0:T(8,128)(2,1)S(1)}, bf16[128,1024]{1,0:T(8,128)(2,1)S(1)}, u32[]{:S(2)}, u32[]{:S(2)}) collective-permute-start(bf16[128,1024]{1,0:T(8,128)(2,1)S(1)} %collective-permute-done.14.refs_3_.refs_13_), channel_id=1, source_target_pairs={{0,4},{1,5},{2,6},{3,7},{4,8},{5,9},{6,10},{7,11},{8,12},{9,13},{1... | collective-permute-start | bytes 786440 | tf_op jit(solution)/shard_map/ppermute | solution.py:344
  49.7 12.4 %collective-permute-start.19 = (bf16[136,1024]{1,0:T(8,128)(2,1)S(1)}, bf16[136,1024]{1,0:T(8,128)(2,1)S(1)}, u32[]{:S(2)}, u32[]{:S(2)}) collective-permute-start(bf16[136,1024]{1,0:T(8,128)(2,1)S(1)} %get-tuple-element.90), channel_id=1, source_target_pairs={{0,2},{1,3},{2,0},{3,1},{4,6},{5,7},{6,4},{7,5},{8,10},{9,11},{10,... | collective-permute-start | bytes 835592 | tf_op jit(solution)/shard_map/ppermute | solution.py:350
  57.0 11.4 %collective-permute-start.16 = (bf16[136,1024]{1,0:T(8,128)(2,1)S(1)}, bf16[136,1024]{1,0:T(8,128)(2,1)S(1)}, u32[]{:S(2)}, u32[]{:S(2)}) collective-permute-start(bf16[136,1024]{1,0:T(8,128)(2,1)S(1)} %get-tuple-element.86), channel_id=1, source_target_pairs={{0,12},{1,13},{2,14},{3,15},{4,0},{5,1},{6,2},{7,3},{8,4},{9,5},{1... | collective-permute-start | bytes 835592 | tf_op jit(solution)/shard_map/ppermute | solution.py:347
  60.5 8.1 %collective-permute-start.22 = (bf16[136,1024]{1,0:T(8,128)(2,1)S(1)}, bf16[136,1024]{1,0:T(8,128)(2,1)S(1)}, u32[]{:S(2)}, u32[]{:S(2)}) collective-permute-start(bf16[136,1024]{1,0:T(8,128)(2,1)S(1)} %get-tuple-element.95), channel_id=1, source_target_pairs={{0,2},{1,3},{2,0},{3,1},{4,6},{5,7},{6,4},{7,5},{8,10},{9,11},{10,... | collective-permute-start | bytes 835592 | tf_op jit(solution)/shard_map/ppermute | solution.py:350
  62.2 10.5 %collective-permute-start.20 = (bf16[136,1024]{1,0:T(8,128)(2,1)S(1)}, bf16[136,1024]{1,0:T(8,128)(2,1)S(1)}, u32[]{:S(2)}, u32[]{:S(2)}) collective-permute-start(bf16[136,1024]{1,0:T(8,128)(2,1)S(1)} %add_convert_fusion.1), channel_id=1, source_target_pairs={{0,4},{1,5},{2,6},{3,7},{4,8},{5,9},{6,10},{7,11},{8,12},{9,13},{1... | collective-permute-start | bytes 835592 | tf_op jit(solution)/shard_map/ppermute | solution.py:344
  67.8 5.1 %collective-permute-start.24 = (bf16[1024,384]{1,0:T(8,128)(2,1)S(1)}, bf16[1024,384]{1,0:T(8,128)(2,1)S(1)}, u32[]{:S(2)}, u32[]{:S(2)}) collective-permute-start(bf16[1024,384]{1,0:T(8,128)(2,1)S(1)} %get-tuple-element.100), channel_id=1, source_target_pairs={{0,1},{1,0},{2,3},{3,2},{4,5},{5,4},{6,7},{7,6},{8,9},{9,8},{10,11... | collective-permute-start | bytes 2359304 | tf_op jit(solution)/shard_map/ppermute | solution.py:353
  67.9 5.0 %collective-permute-start.25 = (bf16[1024,384]{1,0:T(8,128)(2,1)S(1)}, bf16[1024,384]{1,0:T(8,128)(2,1)S(1)}, u32[]{:S(2)}, u32[]{:S(2)}) collective-permute-start(bf16[1024,384]{1,0:T(8,128)(2,1)S(1)} %get-tuple-element.101), channel_id=1, source_target_pairs={{0,1},{1,0},{2,3},{3,2},{4,5},{5,4},{6,7},{7,6},{8,9},{9,8},{10,11... | collective-permute-start | bytes 2359304 | tf_op jit(solution)/shard_map/ppermute | solution.py:353
  68.4 4.6 %collective-permute-start.26 = (bf16[384,1024]{1,0:T(8,128)(2,1)S(1)}, bf16[384,1024]{1,0:T(8,128)(2,1)S(1)}, u32[]{:S(2)}, u32[]{:S(2)}) collective-permute-start(bf16[384,1024]{1,0:T(8,128)(2,1)S(1)} %get-tuple-element.102), channel_id=1, source_target_pairs={{0,1},{1,0},{2,3},{3,2},{4,5},{5,4},{6,7},{7,6},{8,9},{9,8},{10,11... | collective-permute-start | bytes 2359304 | tf_op jit(solution)/shard_map/ppermute | solution.py:353
  68.5 11.5 %collective-permute-start.17 = (bf16[136,1024]{1,0:T(8,128)(2,1)S(1)}, bf16[136,1024]{1,0:T(8,128)(2,1)S(1)}, u32[]{:S(2)}, u32[]{:S(2)}) collective-permute-start(bf16[136,1024]{1,0:T(8,128)(2,1)S(1)} %add_convert_fusion.2), channel_id=1, source_target_pairs={{0,2},{1,3},{2,0},{3,1},{4,6},{5,7},{6,4},{7,5},{8,10},{9,11},{10,... | collective-permute-start | bytes 835592 | tf_op jit(solution)/shard_map/ppermute | solution.py:350
  72.8 10.7 %copy-start.5 = (s32[128,8]{0,1:T(8,128)S(1)}, s32[128,8]{0,1:T(8,128)}, u32[]{:S(2)}) copy-start(s32[128,8]{0,1:T(8,128)} %param.11) | copy-start | bytes 12292
  72.8 10.7 %copy-start.8 = (f32[16,128]{1,0:T(8,128)S(1)}, f32[16,128]{1,0:T(8,128)}, u32[]{:S(2)}) copy-start(f32[16,128]{1,0:T(8,128)} %copy-done.7) | copy-start | bytes 24580
  72.8 10.6 %collective-permute-start.23 = (bf16[136,1024]{1,0:T(8,128)(2,1)S(1)}, bf16[136,1024]{1,0:T(8,128)(2,1)S(1)}, u32[]{:S(2)}, u32[]{:S(2)}) collective-permute-start(bf16[136,1024]{1,0:T(8,128)(2,1)S(1)} %add_convert_fusion), channel_id=1, source_target_pairs={{0,4},{1,5},{2,6},{3,7},{4,8},{5,9},{6,10},{7,11},{8,12},{9,13},{1... | collective-permute-start | bytes 835592 | tf_op jit(solution)/shard_map/ppermute | solution.py:344

commit v11 on v10

--- a/solution.py
+++ b/solution.py
@@ -102,17 +102,19 @@
     )(table, ids, gates, x)
 
 
-def hold(value, flops):
+def hold_kernel(out):
+    out[...] = jnp.zeros_like(out)
+
+
+def hold(flops):
     return pl.pallas_call(
-        lambda source, out: None,
-        out_shape=jax.ShapeDtypeStruct(value.shape, value.dtype),
-        in_specs=[ANY],
-        out_specs=ANY,
-        input_output_aliases={0: 0},
+        hold_kernel,
+        out_shape=jax.ShapeDtypeStruct((8, LANES), f32),
+        out_specs=VMEM,
         compiler_params=params(1),
         cost_estimate=pl.CostEstimate(flops=flops, bytes_accessed=1000, transcendentals=0),
         name="hold",
-    )(value)
+    )()
 
 
 def rows_kernel(slots, *refs):
@@ -286,7 +288,7 @@
 
 
 def finish_kernel(parts, ids, kept, *refs):
-    pieces, (tokens_out, gates_out) = refs[:parts], refs[parts:]
+    pieces, (_, tokens_out, gates_out) = refs[:parts], refs[parts:]
     tokens, width = tokens_out.shape
     total = pieces[0][...].astype(f32)
     for p in pieces[1:]:
@@ -305,7 +307,7 @@
     gates_out[...] = out.astype(bf16)
 
 
-def finish(ids, kept, pieces, width):
+def finish(ids, kept, pieces, mark, width):
     tokens = ids.shape[1]
     return pl.pallas_call(
         functools.partial(finish_kernel, len(pieces)),
@@ -313,11 +315,11 @@
             jax.ShapeDtypeStruct((tokens, width), bf16),
             jax.ShapeDtypeStruct((TOP, tokens), bf16),
         ),
-        in_specs=[VMEM] * (2 + len(pieces)),
+        in_specs=[VMEM] * (2 + len(pieces)) + [ANY],
         out_specs=(VMEM, VMEM),
         compiler_params=params(16),
         name="finish",
-    )(ids, kept, *pieces)
+    )(ids, kept, *pieces, mark)
 
 
 def add(*terms):
@@ -374,7 +376,7 @@
             more,
         )
 
-    xgs, dys = [[xg]], [[grad_out]]
+    xgs, dys, mark = [[xg]], [[grad_out]], kept
     dxs, acts, across = [], [], []
 
     def send_across(z):
@@ -400,7 +402,7 @@
             if ahead is not None:
                 done.append(ahead)
             if k == 0 and z == 1:
-                done, kept, held = together(done, hold(kept, HOLD), weights[3:5])
+                done, mark, held = together(done, hold(HOLD), weights[3:5])
                 weights = own + held + weights[5:]
             elif z == 1:
                 done, held = together(done, weights[5:])
@@ -452,7 +454,7 @@
     else:
         grad_w = [(v + o.astype(f32)).astype(bf16)[None] for v, o in zip(sums[0], other)]
     pieces, grad_w = together(pieces, grad_w)
-    grad_tokens, grad_gates = finish(ids, kept, pieces, width)
+    grad_tokens, grad_gates = finish(ids, kept, pieces, mark, width)
     grad_gates = grad_gates.T
     return (grad_tokens, grad_gates, *grad_w)
 

time: 84.5 us -> 84.4 us (level)
  waiting for transfers between devices: 30.4 us -> 32.4 us
  local copies, waits for them, and re-layouts: 1.32 us -> 0.03 us
    ppermute x10, starting transfers between devices: 9.87 us -> 8.12 us  [send_z(): lax.ppermute(v, 'expert', [(i, moved(i, 1, 0)) for i in range(devices)])]
    unnamed x18 -> x14, local copies, waits for them, and re-layouts: 1.32 us -> 0.03 us
    ppermute x10, starting transfers between devices: 16.8 us -> 18.1 us  [send_y(): lax.ppermute(v, 'expert', [(i, moved(i, 0, 1)) for i in range(devices)])]
    ppermute x6, waiting for transfers between devices: 0.66 us -> 1.89 us  [send_core(): return lax.ppermute(v, 'expert', [(i, i ^ 1) for i in range(devices)])]
where the time goes in v11:
time: 84.4 us; the launch traced here: 84.3 us
  waiting for transfers between devices  32.4 us (38%)
  starting transfers between devices  27.3 us (32%)
  Pallas kernels  23.4 us (28%)
    ppermute x10, waiting for transfers between devices, send_z(): lax.ppermute(v, 'expert', [(i, moved(i, 1, 0)) for i in range(devices)])  27.8 us
    ppermute x10, starting transfers between devices, send_y(): lax.ppermute(v, 'expert', [(i, moved(i, 0, 1)) for i in range(devices)])  18.1 us
    pallas_call x4, Pallas kernels, rows_grads(): pl.pallas_call(functools.partial(rows_kernel, slots), out_shape=tuple((ja...  12.9 us
    ppermute x10, starting transfers between devices, send_z(): lax.ppermute(v, 'expert', [(i, moved(i, 1, 0)) for i in range(devices)])  8.12 us
    pallas_call x2, Pallas kernels, weights_grads(): pl.pallas_call(functools.partial(weights_kernel, j, slots, steps, len(mor...  7.96 us
    ppermute x10, waiting for transfers between devices, send_y(): lax.ppermute(v, 'expert', [(i, moved(i, 0, 1)) for i in range(devices)])  2.71 us
    ppermute x6, waiting for transfers between devices, send_core(): return lax.ppermute(v, 'expert', [(i, i ^ 1) for i in range(devices)])  1.89 us
    pallas_call x1, Pallas kernels, plan(): pl.pallas_call(functools.partial(plan_kernel, home_cap, rep_cap), out_sha...  1.74 us
  transfers between devices with their start and end apart: 27, of which 11 were waited for; matrix products, arithmetic and copies ran while one was open for 0% of the time, Pallas kernels for 25%

profile of v11, /device:TPU:0, one launch (start us, length us, event | category | flops | bytes accessed | tf_op | source)
XLA Modules:
  0.0 84.3 jit_solution(18081769318822943639)
XLA Ops:
  0.6 1.7 %plan.1 = (bf16[136,1024]{1,0:T(8,128)(2,1)}, f32[16,128]{1,0:T(8,128)}) custom-call(s32[1,16]{1,0:T(1,128)} %bitcast.25, s32[8,128]{1,0:T(8,128)} %bitcast.22, bf16[8,128]{1,0:T(8,128)(2,1)} %bitcast.24, bf16[128,1024]{1,0:T(8,128)(2,1)} %x_in.1), custom_call_target="tpu_custom_call" | custom-call | tf_op jit(solution)/shard_map/plan/pallas_call | solution.py:86
  2.4 3.1 %collective-permute-start.1 = (bf16[136,1024]{1,0:T(8,128)(2,1)}, bf16[136,1024]{1,0:T(8,128)(2,1)S(1)}, u32[]{:S(2)}, u32[]{:S(2)}) collective-permute-start(bf16[136,1024]{1,0:T(8,128)(2,1)} %get-tuple-element.62.refs_0_), channel_id=1, source_target_pairs={{0,4},{1,5},{2,6},{3,7},{4,8},{5,9},{6,10},{7,11},{8,12},{9,13},{1... | collective-permute-start | bytes 835592 | tf_op jit(solution)/shard_map/ppermute | solution.py:346
  5.5 1.5 %collective-permute-start = (bf16[136,1024]{1,0:T(8,128)(2,1)}, bf16[136,1024]{1,0:T(8,128)(2,1)S(1)}, u32[]{:S(2)}, u32[]{:S(2)}) collective-permute-start(bf16[136,1024]{1,0:T(8,128)(2,1)} %get-tuple-element.62.refs_0_), channel_id=1, source_target_pairs={{0,2},{1,3},{2,0},{3,1},{4,6},{5,7},{6,4},{7,5},{8,10},{9,11},{10,... | collective-permute-start | bytes 835592 | tf_op jit(solution)/shard_map/ppermute | solution.py:352
  7.0 1.6 %collective-permute-start.5 = (bf16[128,1024]{1,0:T(8,128)(2,1)}, bf16[128,1024]{1,0:T(8,128)(2,1)S(1)}, u32[]{:S(2)}, u32[]{:S(2)}) collective-permute-start(bf16[128,1024]{1,0:T(8,128)(2,1)} %refs_8_.3), channel_id=1, source_target_pairs={{0,4},{1,5},{2,6},{3,7},{4,8},{5,9},{6,10},{7,11},{8,12},{9,13},{1... | collective-permute-start | bytes 786440 | tf_op jit(solution)/shard_map/ppermute | solution.py:346
  8.6 0.5 collective-permute-start.4
  9.1 0.0 collective-permute-start.2
  9.1 6.1 %collective-permute-done.1.refs_0_.refs_2_ = bf16[136,1024]{1,0:T(8,128)(2,1)S(1)} collective-permute-done((bf16[136,1024]{1,0:T(8,128)(2,1)}, bf16[136,1024]{1,0:T(8,128)(2,1)S(1)}, u32[]{:S(2)}, u32[]{:S(2)}) %collective-permute-start.1) | collective-permute-done | bytes 278560 | tf_op jit(solution)/shard_map/ppermute | solution.py:346
  15.2 0.0 collective-permute-start.3
  15.2 0.1 collective-permute-done.refs_1_
  15.3 0.5 collective-permute-start.6
  15.8 0.0 collective-permute-done.2.refs_7_
  15.8 1.9 %collective-permute-done.3.refs_8_ = bf16[1024,384]{1,0:T(8,128)(2,1)S(1)} collective-permute-done((bf16[1024,384]{1,0:T(8,128)(2,1)}, bf16[1024,384]{1,0:T(8,128)(2,1)S(1)}, u32[]{:S(2)}, u32[]{:S(2)}) %collective-permute-start.3) | collective-permute-done | bytes 786464 | tf_op jit(solution)/shard_map/ppermute | solution.py:355
  17.7 0.0 collective-permute-start.8
  17.7 1.7 %collective-permute-start.7 = (bf16[136,1024]{1,0:T(8,128)(2,1)S(1)}, bf16[136,1024]{1,0:T(8,128)(2,1)S(1)}, u32[]{:S(2)}, u32[]{:S(2)}) collective-permute-start(bf16[136,1024]{1,0:T(8,128)(2,1)S(1)} %collective-permute-done.1.refs_0_.refs_2_), channel_id=1, source_target_pairs={{0,2},{1,3},{2,0},{3,1},{4,6},{5,7},{6,4},{7,5},{8,10},{9,11},{10,... | collective-permute-start | bytes 835592 | tf_op jit(solution)/shard_map/ppermute | solution.py:352
  19.4 0.5 collective-permute-done.5.refs_2_.refs_10_
  20.0 0.0 collective-permute-done.4.refs_3_.refs_9_
  20.0 0.0 collective-permute-done.6.refs_9_
  20.0 1.0 %collective-permute-start.10 = (bf16[128,1024]{1,0:T(8,128)(2,1)S(1)}, bf16[128,1024]{1,0:T(8,128)(2,1)S(1)}, u32[]{:S(2)}, u32[]{:S(2)}) collective-permute-start(bf16[128,1024]{1,0:T(8,128)(2,1)S(1)} %collective-permute-done.5.refs_2_.refs_10_), channel_id=1, source_target_pairs={{0,4},{1,5},{2,6},{3,7},{4,8},{5,9},{6,10},{7,11},{8,12},{9,13},{1... | collective-permute-start | bytes 786440 | tf_op jit(solution)/shard_map/ppermute | solution.py:346
  21.0 1.5 %collective-permute-start.9 = (bf16[128,1024]{1,0:T(8,128)(2,1)S(1)}, bf16[128,1024]{1,0:T(8,128)(2,1)S(1)}, u32[]{:S(2)}, u32[]{:S(2)}) collective-permute-start(bf16[128,1024]{1,0:T(8,128)(2,1)S(1)} %collective-permute-done.5.refs_2_.refs_10_), channel_id=1, source_target_pairs={{0,2},{1,3},{2,0},{3,1},{4,6},{5,7},{6,4},{7,5},{8,10},{9,11},{10,... | collective-permute-start | bytes 786440 | tf_op jit(solution)/shard_map/ppermute | solution.py:352
  22.5 3.2 %rows_grads.4 = (bf16[136,1024]{1,0:T(8,128)(2,1)S(1)}, bf16[136,1024]{1,0:T(8,128)(2,1)S(1)}, bf16[256,2304]{1,0:T(8,128)(2,1)S(1)}) custom-call(bf16[136,1024]{1,0:T(8,128)(2,1)S(1)} %copy-done.3, bf16[136,1024]{1,0:T(8,128)(2,1)S(1)} %collective-permute-done.refs_1_, bf16[128,1024]{1,0:T(8,128)(2,1)S(1)} %copy-done.4, ...), custom_call_target="tpu_custom_call" | custom-call | flops 1006632960 | bytes 9043968 | tf_op jit(solution)/shard_map/rows_grads/pallas_call | solution.py:190
  25.7 3.2 %collective-permute-done.8.refs_0_.refs_4_ = bf16[136,1024]{1,0:T(8,128)(2,1)S(1)} collective-permute-done((bf16[136,1024]{1,0:T(8,128)(2,1)S(1)}, bf16[136,1024]{1,0:T(8,128)(2,1)S(1)}, u32[]{:S(2)}, u32[]{:S(2)}) %collective-permute-start.8) | collective-permute-done | bytes 278560 | tf_op jit(solution)/shard_map/ppermute | solution.py:346
  29.0 0.0 collective-permute-done.7.refs_1_.refs_3_
  29.0 0.0 collective-permute-start.12
  29.0 1.8 %collective-permute-start.11 = (bf16[136,1024]{1,0:T(8,128)(2,1)S(1)}, bf16[136,1024]{1,0:T(8,128)(2,1)S(1)}, u32[]{:S(2)}, u32[]{:S(2)}) collective-permute-start(bf16[136,1024]{1,0:T(8,128)(2,1)S(1)} %collective-permute-done.8.refs_0_.refs_4_), channel_id=1, source_target_pairs={{0,2},{1,3},{2,0},{3,1},{4,6},{5,7},{6,4},{7,5},{8,10},{9,11},{10,... | collective-permute-start | bytes 835592 | tf_op jit(solution)/shard_map/ppermute | solution.py:352
  30.7 3.8 %collective-permute-done.10.refs_2_.refs_12_ = bf16[128,1024]{1,0:T(8,128)(2,1)S(1)} collective-permute-done((bf16[128,1024]{1,0:T(8,128)(2,1)S(1)}, bf16[128,1024]{1,0:T(8,128)(2,1)S(1)}, u32[]{:S(2)}, u32[]{:S(2)}) %collective-permute-start.10) | collective-permute-done | bytes 262176 | tf_op jit(solution)/shard_map/ppermute | solution.py:346
  34.6 0.0 collective-permute-done.9.refs_3_.refs_11_
  34.6 0.0 collective-permute-start.15
  34.6 1.8 %collective-permute-start.14 = (bf16[128,1024]{1,0:T(8,128)(2,1)S(1)}, bf16[128,1024]{1,0:T(8,128)(2,1)S(1)}, u32[]{:S(2)}, u32[]{:S(2)}) collective-permute-start(bf16[128,1024]{1,0:T(8,128)(2,1)S(1)} %collective-permute-done.10.refs_2_.refs_12_), channel_id=1, source_target_pairs={{0,2},{1,3},{2,0},{3,1},{4,6},{5,7},{6,4},{7,5},{8,10},{9,11},{10,... | collective-permute-start | bytes 786440 | tf_op jit(solution)/shard_map/ppermute | solution.py:352
  36.4 3.2 %rows_grads.5 = (bf16[136,1024]{1,0:T(8,128)(2,1)S(1)}, bf16[136,1024]{1,0:T(8,128)(2,1)S(1)}, bf16[256,2304]{1,0:T(8,128)(2,1)S(1)}) custom-call(bf16[136,1024]{1,0:T(8,128)(2,1)S(1)} %collective-permute-done.1.refs_0_.refs_2_, bf16[136,1024]{1,0:T(8,128)(2,1)S(1)} %collective-permute-done.7.refs_1_.refs_3_, ...), custom_call_target="tpu_custom_call" | custom-call | flops 1006632960 | bytes 9043968 | tf_op jit(solution)/shard_map/rows_grads/pallas_call | solution.py:190
  39.6 1.0 %collective-permute-done.12.refs_0_.refs_6_ = bf16[136,1024]{1,0:T(8,128)(2,1)S(1)} collective-permute-done((bf16[136,1024]{1,0:T(8,128)(2,1)S(1)}, bf16[136,1024]{1,0:T(8,128)(2,1)S(1)}, u32[]{:S(2)}, u32[]{:S(2)}) %collective-permute-start.12) | collective-permute-done | bytes 278560 | tf_op jit(solution)/shard_map/ppermute | solution.py:346
  40.6 0.0 collective-permute-done.11.refs_1_.refs_5_
  40.6 1.8 %collective-permute-start.13 = (bf16[136,1024]{1,0:T(8,128)(2,1)S(1)}, bf16[136,1024]{1,0:T(8,128)(2,1)S(1)}, u32[]{:S(2)}, u32[]{:S(2)}) collective-permute-start(bf16[136,1024]{1,0:T(8,128)(2,1)S(1)} %collective-permute-done.12.refs_0_.refs_6_), channel_id=1, source_target_pairs={{0,2},{1,3},{2,0},{3,1},{4,6},{5,7},{6,4},{7,5},{8,10},{9,11},{10,... | collective-permute-start | bytes 835592 | tf_op jit(solution)/shard_map/ppermute | solution.py:352
  42.3 0.0 collective-permute-start.18
  42.3 3.4 %collective-permute-done.15.refs_2_.refs_14_ = bf16[128,1024]{1,0:T(8,128)(2,1)S(1)} collective-permute-done((bf16[128,1024]{1,0:T(8,128)(2,1)S(1)}, bf16[128,1024]{1,0:T(8,128)(2,1)S(1)}, u32[]{:S(2)}, u32[]{:S(2)}) %collective-permute-start.15) | collective-permute-done | bytes 262176 | tf_op jit(solution)/shard_map/ppermute | solution.py:346
  45.7 0.0 collective-permute-done.14.refs_3_.refs_13_
  45.7 0.3 collective-permute-start.21
  46.0 3.2 %rows_grads.6 = (bf16[136,1024]{1,0:T(8,128)(2,1)S(1)}, bf16[136,1024]{1,0:T(8,128)(2,1)S(1)}, bf16[256,2304]{1,0:T(8,128)(2,1)S(1)}) custom-call(bf16[136,1024]{1,0:T(8,128)(2,1)S(1)} %collective-permute-done.8.refs_0_.refs_4_, bf16[136,1024]{1,0:T(8,128)(2,1)S(1)} %collective-permute-done.11.refs_1_.refs_5_, ...), custom_call_target="tpu_custom_call" | custom-call | flops 1006632960 | bytes 9043968 | tf_op jit(solution)/shard_map/rows_grads/pallas_call | solution.py:190
  49.2 2.0 %collective-permute-start.19 = (bf16[136,1024]{1,0:T(8,128)(2,1)S(1)}, bf16[136,1024]{1,0:T(8,128)(2,1)S(1)}, u32[]{:S(2)}, u32[]{:S(2)}) collective-permute-start(bf16[136,1024]{1,0:T(8,128)(2,1)S(1)} %get-tuple-element.89), channel_id=1, source_target_pairs={{0,2},{1,3},{2,0},{3,1},{4,6},{5,7},{6,4},{7,5},{8,10},{9,11},{10,... | collective-permute-start | bytes 835592 | tf_op jit(solution)/shard_map/ppermute | solution.py:352
  51.2 6.2 %collective-permute-done.21.refs_3_.refs_15_ = bf16[128,1024]{1,0:T(8,128)(2,1)S(1)} collective-permute-done((bf16[128,1024]{1,0:T(8,128)(2,1)S(1)}, bf16[128,1024]{1,0:T(8,128)(2,1)S(1)}, u32[]{:S(2)}, u32[]{:S(2)}) %collective-permute-start.21) | collective-permute-done | bytes 262176 | tf_op jit(solution)/shard_map/ppermute | solution.py:346
  57.4 0.0 collective-permute-done.13.refs_1_.refs_7_
  57.5 0.0 collective-permute-done.18
  57.5 0.0 collective-permute-start.16
  57.5 3.2 %rows_grads.7 = (bf16[136,1024]{1,0:T(8,128)(2,1)S(1)}, bf16[136,1024]{1,0:T(8,128)(2,1)S(1)}, bf16[256,2304]{1,0:T(8,128)(2,1)S(1)}) custom-call(bf16[136,1024]{1,0:T(8,128)(2,1)S(1)} %collective-permute-done.12.refs_0_.refs_6_, bf16[136,1024]{1,0:T(8,128)(2,1)S(1)} %collective-permute-done.13.refs_1_.refs_7_, ...), custom_call_target="tpu_custom_call" | custom-call | flops 1006632960 | bytes 9043968 | tf_op jit(solution)/shard_map/rows_grads/pallas_call | solution.py:190
  60.7 1.6 %collective-permute-start.22 = (bf16[136,1024]{1,0:T(8,128)(2,1)S(1)}, bf16[136,1024]{1,0:T(8,128)(2,1)S(1)}, u32[]{:S(2)}, u32[]{:S(2)}) collective-permute-start(bf16[136,1024]{1,0:T(8,128)(2,1)S(1)} %get-tuple-element.94), channel_id=1, source_target_pairs={{0,2},{1,3},{2,0},{3,1},{4,6},{5,7},{6,4},{7,5},{8,10},{9,11},{10,... | collective-permute-start | bytes 835592 | tf_op jit(solution)/shard_map/ppermute | solution.py:352
  62.3 0.0 collective-permute-done.19
  62.3 0.1 add_convert_fusion.1
  62.5 2.1 %collective-permute-start.20 = (bf16[136,1024]{1,0:T(8,128)(2,1)S(1)}, bf16[136,1024]{1,0:T(8,128)(2,1)S(1)}, u32[]{:S(2)}, u32[]{:S(2)}) collective-permute-start(bf16[136,1024]{1,0:T(8,128)(2,1)S(1)} %add_convert_fusion.1), channel_id=1, source_target_pairs={{0,4},{1,5},{2,6},{3,7},{4,8},{5,9},{6,10},{7,11},{8,12},{9,13},{1... | collective-permute-start | bytes 835592 | tf_op jit(solution)/shard_map/ppermute | solution.py:346
  64.5 3.5 %weights_grads.2 = (bf16[1024,384]{1,0:T(8,128)(2,1)S(1)}, bf16[1024,384]{1,0:T(8,128)(2,1)S(1)}, bf16[384,1024]{1,0:T(8,128)(2,1)S(1)}) custom-call(bf16[136,1024]{1,0:T(8,128)(2,1)S(1)} %copy-done.3, bf16[136,1024]{1,0:T(8,128)(2,1)S(1)} %collective-permute-done.refs_1_, bf16[136,1024]{1,0:T(8,128)(2,1)S(1)} %collective-permute-done.1.refs_0_.refs_2_, ...), custom_call_target="tpu_custom_call" | custom-call | flops 1000 | bytes 1000 | tf_op jit(solution)/shard_map/weights_grads/pallas_call | solution.py:265
  68.1 0.1 collective-permute-start.24
  68.2 0.5 collective-permute-start.25
  68.7 0.1 collective-permute-start.26
  68.7 0.1 add_convert_fusion.2
  68.8 0.0 collective-permute-done.22
  68.8 3.8 %collective-permute-start.17 = (bf16[136,1024]{1,0:T(8,128)(2,1)S(1)}, bf16[136,1024]{1,0:T(8,128)(2,1)S(1)}, u32[]{:S(2)}, u32[]{:S(2)}) collective-permute-start(bf16[136,1024]{1,0:T(8,128)(2,1)S(1)} %add_convert_fusion.2), channel_id=1, source_target_pairs={{0,2},{1,3},{2,0},{3,1},{4,6},{5,7},{6,4},{7,5},{8,10},{9,11},{10,... | collective-permute-start | bytes 835592 | tf_op jit(solution)/shard_map/ppermute | solution.py:352
  72.7 0.1 add_convert_fusion
  72.8 0.0 copy-start.5
  72.8 0.0 copy-start.6
  72.8 0.1 collective-permute-start.23
  72.9 0.0 collective-permute-done.24.refs_20_
  72.9 0.0 collective-permute-done.25.refs_21_
  72.9 4.4 %weights_grads.3 = (bf16[1,1024,384]{2,1,0:T(8,128)(2,1)}, bf16[1,1024,384]{2,1,0:T(8,128)(2,1)}, bf16[1,384,1024]{2,1,0:T(8,128)(2,1)}) custom-call(bf16[136,1024]{1,0:T(8,128)(2,1)S(1)} %copy-done.3, bf16[136,1024]{1,0:T(8,128)(2,1)S(1)} %collective-permute-done.refs_1_, bf16[136,1024]{1,0:T(8,128)(2,1)S(1)} %collective-permute-done.1.refs_0_.refs_2_, ...), custom_call_target="tpu_custom_call" | custom-call | flops 1000 | bytes 1000 | tf_op jit(solution)/shard_map/weights_grads/pallas_call | solution.py:265
  77.4 2.6 %collective-permute-done.17.refs_1_ = bf16[136,1024]{1,0:T(8,128)(2,1)S(1)} collective-permute-done((bf16[136,1024]{1,0:T(8,128)(2,1)S(1)}, bf16[136,1024]{1,0:T(8,128)(2,1)S(1)}, u32[]{:S(2)}, u32[]{:S(2)}) %collective-permute-start.17) | collective-permute-done | bytes 278560 | tf_op jit(solution)/shard_map/ppermute | solution.py:352
  80.0 3.5 %collective-permute-done.23.refs_2_ = bf16[136,1024]{1,0:T(8,128)(2,1)S(1)} collective-permute-done((bf16[136,1024]{1,0:T(8,128)(2,1)S(1)}, bf16[136,1024]{1,0:T(8,128)(2,1)S(1)}, u32[]{:S(2)}, u32[]{:S(2)}) %collective-permute-start.23) | collective-permute-done | bytes 278560 | tf_op jit(solution)/shard_map/ppermute | solution.py:346
  83.5 0.8 finish.1
  (16 shorter events, 0.0 us)
Async XLA Ops:
  2.4 12.8 %collective-permute-start.1 = (bf16[136,1024]{1,0:T(8,128)(2,1)}, bf16[136,1024]{1,0:T(8,128)(2,1)S(1)}, u32[]{:S(2)}, u32[]{:S(2)}) collective-permute-start(bf16[136,1024]{1,0:T(8,128)(2,1)} %get-tuple-element.62.refs_0_), channel_id=1, source_target_pairs={{0,4},{1,5},{2,6},{3,7},{4,8},{5,9},{6,10},{7,11},{8,12},{9,13},{1... | collective-permute-start | bytes 835592 | tf_op jit(solution)/shard_map/ppermute | solution.py:346
  5.5 9.8 %collective-permute-start = (bf16[136,1024]{1,0:T(8,128)(2,1)}, bf16[136,1024]{1,0:T(8,128)(2,1)S(1)}, u32[]{:S(2)}, u32[]{:S(2)}) collective-permute-start(bf16[136,1024]{1,0:T(8,128)(2,1)} %get-tuple-element.62.refs_0_), channel_id=1, source_target_pairs={{0,2},{1,3},{2,0},{3,1},{4,6},{5,7},{6,4},{7,5},{8,10},{9,11},{10,... | collective-permute-start | bytes 835592 | tf_op jit(solution)/shard_map/ppermute | solution.py:352
  7.0 13.0 %collective-permute-start.5 = (bf16[128,1024]{1,0:T(8,128)(2,1)}, bf16[128,1024]{1,0:T(8,128)(2,1)S(1)}, u32[]{:S(2)}, u32[]{:S(2)}) collective-permute-start(bf16[128,1024]{1,0:T(8,128)(2,1)} %refs_8_.3), channel_id=1, source_target_pairs={{0,4},{1,5},{2,6},{3,7},{4,8},{5,9},{6,10},{7,11},{8,12},{9,13},{1... | collective-permute-start | bytes 786440 | tf_op jit(solution)/shard_map/ppermute | solution.py:346
  8.6 11.4 %collective-permute-start.4 = (bf16[128,1024]{1,0:T(8,128)(2,1)}, bf16[128,1024]{1,0:T(8,128)(2,1)S(1)}, u32[]{:S(2)}, u32[]{:S(2)}) collective-permute-start(bf16[128,1024]{1,0:T(8,128)(2,1)} %refs_8_.3), channel_id=1, source_target_pairs={{0,2},{1,3},{2,0},{3,1},{4,6},{5,7},{6,4},{7,5},{8,10},{9,11},{10,... | collective-permute-start | bytes 786440 | tf_op jit(solution)/shard_map/ppermute | solution.py:352
  9.1 6.7 %collective-permute-start.2 = (bf16[1024,384]{1,0:T(8,128)(2,1)}, bf16[1024,384]{1,0:T(8,128)(2,1)S(1)}, u32[]{:S(2)}, u32[]{:S(2)}) collective-permute-start(bf16[1024,384]{1,0:T(8,128)(2,1)} %bitcast.7), channel_id=1, source_target_pairs={{0,1},{1,0},{2,3},{3,2},{4,5},{5,4},{6,7},{7,6},{8,9},{9,8},{10,11... | collective-permute-start | bytes 2359304 | tf_op jit(solution)/shard_map/ppermute | solution.py:355
  15.2 2.5 %collective-permute-start.3 = (bf16[1024,384]{1,0:T(8,128)(2,1)}, bf16[1024,384]{1,0:T(8,128)(2,1)S(1)}, u32[]{:S(2)}, u32[]{:S(2)}) collective-permute-start(bf16[1024,384]{1,0:T(8,128)(2,1)} %bitcast.12), channel_id=1, source_target_pairs={{0,1},{1,0},{2,3},{3,2},{4,5},{5,4},{6,7},{7,6},{8,9},{9,8},{10,11... | collective-permute-start | bytes 2359304 | tf_op jit(solution)/shard_map/ppermute | solution.py:355
  15.3 7.3 %copy-start = (bf16[1,1024,384]{2,1,0:T(8,128)(2,1)S(1)}, bf16[1,1024,384]{2,1,0:T(8,128)(2,1)}, u32[]{:S(2)}) copy-start(bf16[1,1024,384]{2,1,0:T(8,128)(2,1)} %param.13) | copy-start | bytes 2359300
  15.3 7.3 %copy-start.1 = (bf16[1,1024,384]{2,1,0:T(8,128)(2,1)S(1)}, bf16[1,1024,384]{2,1,0:T(8,128)(2,1)}, u32[]{:S(2)}) copy-start(bf16[1,1024,384]{2,1,0:T(8,128)(2,1)} %param.14) | copy-start | bytes 2359300
  15.3 7.3 %copy-start.2 = (bf16[1,384,1024]{2,1,0:T(8,128)(2,1)S(1)}, bf16[1,384,1024]{2,1,0:T(8,128)(2,1)}, u32[]{:S(2)}) copy-start(bf16[1,384,1024]{2,1,0:T(8,128)(2,1)} %param.15) | copy-start | bytes 2359300
  15.3 7.3 %copy-start.3 = (bf16[136,1024]{1,0:T(8,128)(2,1)S(1)}, bf16[136,1024]{1,0:T(8,128)(2,1)}, u32[]{:S(2)}) copy-start(bf16[136,1024]{1,0:T(8,128)(2,1)} %get-tuple-element.62.refs_0_) | copy-start | bytes 835588
  15.3 7.3 %copy-start.4 = (bf16[128,1024]{1,0:T(8,128)(2,1)S(1)}, bf16[128,1024]{1,0:T(8,128)(2,1)}, u32[]{:S(2)}) copy-start(bf16[128,1024]{1,0:T(8,128)(2,1)} %refs_8_.3) | copy-start | bytes 786436
  15.3 4.7 %collective-permute-start.6 = (bf16[384,1024]{1,0:T(8,128)(2,1)}, bf16[384,1024]{1,0:T(8,128)(2,1)S(1)}, u32[]{:S(2)}, u32[]{:S(2)}) collective-permute-start(bf16[384,1024]{1,0:T(8,128)(2,1)} %bitcast.17), channel_id=1, source_target_pairs={{0,1},{1,0},{2,3},{3,2},{4,5},{5,4},{6,7},{7,6},{8,9},{9,8},{10,11... | collective-permute-start | bytes 2359304 | tf_op jit(solution)/shard_map/ppermute | solution.py:355
  17.7 11.3 %collective-permute-start.8 = (bf16[136,1024]{1,0:T(8,128)(2,1)S(1)}, bf16[136,1024]{1,0:T(8,128)(2,1)S(1)}, u32[]{:S(2)}, u32[]{:S(2)}) collective-permute-start(bf16[136,1024]{1,0:T(8,128)(2,1)S(1)} %collective-permute-done.1.refs_0_.refs_2_), channel_id=1, source_target_pairs={{0,4},{1,5},{2,6},{3,7},{4,8},{5,9},{6,10},{7,11},{8,12},{9,13},{1... | collective-permute-start | bytes 835592 | tf_op jit(solution)/shard_map/ppermute | solution.py:346
  17.7 11.3 %collective-permute-start.7 = (bf16[136,1024]{1,0:T(8,128)(2,1)S(1)}, bf16[136,1024]{1,0:T(8,128)(2,1)S(1)}, u32[]{:S(2)}, u32[]{:S(2)}) collective-permute-start(bf16[136,1024]{1,0:T(8,128)(2,1)S(1)} %collective-permute-done.1.refs_0_.refs_2_), channel_id=1, source_target_pairs={{0,2},{1,3},{2,0},{3,1},{4,6},{5,7},{6,4},{7,5},{8,10},{9,11},{10,... | collective-permute-start | bytes 835592 | tf_op jit(solution)/shard_map/ppermute | solution.py:352
  20.0 14.6 %collective-permute-start.10 = (bf16[128,1024]{1,0:T(8,128)(2,1)S(1)}, bf16[128,1024]{1,0:T(8,128)(2,1)S(1)}, u32[]{:S(2)}, u32[]{:S(2)}) collective-permute-start(bf16[128,1024]{1,0:T(8,128)(2,1)S(1)} %collective-permute-done.5.refs_2_.refs_10_), channel_id=1, source_target_pairs={{0,4},{1,5},{2,6},{3,7},{4,8},{5,9},{6,10},{7,11},{8,12},{9,13},{1... | collective-permute-start | bytes 786440 | tf_op jit(solution)/shard_map/ppermute | solution.py:346
  21.0 13.6 %collective-permute-start.9 = (bf16[128,1024]{1,0:T(8,128)(2,1)S(1)}, bf16[128,1024]{1,0:T(8,128)(2,1)S(1)}, u32[]{:S(2)}, u32[]{:S(2)}) collective-permute-start(bf16[128,1024]{1,0:T(8,128)(2,1)S(1)} %collective-permute-done.5.refs_2_.refs_10_), channel_id=1, source_target_pairs={{0,2},{1,3},{2,0},{3,1},{4,6},{5,7},{6,4},{7,5},{8,10},{9,11},{10,... | collective-permute-start | bytes 786440 | tf_op jit(solution)/shard_map/ppermute | solution.py:352
  29.0 11.6 %collective-permute-start.12 = (bf16[136,1024]{1,0:T(8,128)(2,1)S(1)}, bf16[136,1024]{1,0:T(8,128)(2,1)S(1)}, u32[]{:S(2)}, u32[]{:S(2)}) collective-permute-start(bf16[136,1024]{1,0:T(8,128)(2,1)S(1)} %collective-permute-done.8.refs_0_.refs_4_), channel_id=1, source_target_pairs={{0,4},{1,5},{2,6},{3,7},{4,8},{5,9},{6,10},{7,11},{8,12},{9,13},{1... | collective-permute-start | bytes 835592 | tf_op jit(solution)/shard_map/ppermute | solution.py:346
  29.0 11.6 %collective-permute-start.11 = (bf16[136,1024]{1,0:T(8,128)(2,1)S(1)}, bf16[136,1024]{1,0:T(8,128)(2,1)S(1)}, u32[]{:S(2)}, u32[]{:S(2)}) collective-permute-start(bf16[136,1024]{1,0:T(8,128)(2,1)S(1)} %collective-permute-done.8.refs_0_.refs_4_), channel_id=1, source_target_pairs={{0,2},{1,3},{2,0},{3,1},{4,6},{5,7},{6,4},{7,5},{8,10},{9,11},{10,... | collective-permute-start | bytes 835592 | tf_op jit(solution)/shard_map/ppermute | solution.py:352
  34.6 11.1 %collective-permute-start.15 = (bf16[128,1024]{1,0:T(8,128)(2,1)S(1)}, bf16[128,1024]{1,0:T(8,128)(2,1)S(1)}, u32[]{:S(2)}, u32[]{:S(2)}) collective-permute-start(bf16[128,1024]{1,0:T(8,128)(2,1)S(1)} %collective-permute-done.10.refs_2_.refs_12_), channel_id=1, source_target_pairs={{0,4},{1,5},{2,6},{3,7},{4,8},{5,9},{6,10},{7,11},{8,12},{9,13},{1... | collective-permute-start | bytes 786440 | tf_op jit(solution)/shard_map/ppermute | solution.py:346
  34.6 11.1 %collective-permute-start.14 = (bf16[128,1024]{1,0:T(8,128)(2,1)S(1)}, bf16[128,1024]{1,0:T(8,128)(2,1)S(1)}, u32[]{:S(2)}, u32[]{:S(2)}) collective-permute-start(bf16[128,1024]{1,0:T(8,128)(2,1)S(1)} %collective-permute-done.10.refs_2_.refs_12_), channel_id=1, source_target_pairs={{0,2},{1,3},{2,0},{3,1},{4,6},{5,7},{6,4},{7,5},{8,10},{9,11},{10,... | collective-permute-start | bytes 786440 | tf_op jit(solution)/shard_map/ppermute | solution.py:352
  40.6 16.9 %collective-permute-start.13 = (bf16[136,1024]{1,0:T(8,128)(2,1)S(1)}, bf16[136,1024]{1,0:T(8,128)(2,1)S(1)}, u32[]{:S(2)}, u32[]{:S(2)}) collective-permute-start(bf16[136,1024]{1,0:T(8,128)(2,1)S(1)} %collective-permute-done.12.refs_0_.refs_6_), channel_id=1, source_target_pairs={{0,2},{1,3},{2,0},{3,1},{4,6},{5,7},{6,4},{7,5},{8,10},{9,11},{10,... | collective-permute-start | bytes 835592 | tf_op jit(solution)/shard_map/ppermute | solution.py:352
  42.3 15.1 %collective-permute-start.18 = (bf16[136,1024]{1,0:T(8,128)(2,1)S(1)}, bf16[136,1024]{1,0:T(8,128)(2,1)S(1)}, u32[]{:S(2)}, u32[]{:S(2)}) collective-permute-start(bf16[136,1024]{1,0:T(8,128)(2,1)S(1)} %get-tuple-element.75), channel_id=1, source_target_pairs={{0,4},{1,5},{2,6},{3,7},{4,8},{5,9},{6,10},{7,11},{8,12},{9,13},{1... | collective-permute-start | bytes 835592 | tf_op jit(solution)/shard_map/ppermute | solution.py:346
  45.7 11.7 %collective-permute-start.21 = (bf16[128,1024]{1,0:T(8,128)(2,1)S(1)}, bf16[128,1024]{1,0:T(8,128)(2,1)S(1)}, u32[]{:S(2)}, u32[]{:S(2)}) collective-permute-start(bf16[128,1024]{1,0:T(8,128)(2,1)S(1)} %collective-permute-done.14.refs_3_.refs_13_), channel_id=1, source_target_pairs={{0,4},{1,5},{2,6},{3,7},{4,8},{5,9},{6,10},{7,11},{8,12},{9,13},{1... | collective-permute-start | bytes 786440 | tf_op jit(solution)/shard_map/ppermute | solution.py:346
  49.2 13.1 %collective-permute-start.19 = (bf16[136,1024]{1,0:T(8,128)(2,1)S(1)}, bf16[136,1024]{1,0:T(8,128)(2,1)S(1)}, u32[]{:S(2)}, u32[]{:S(2)}) collective-permute-start(bf16[136,1024]{1,0:T(8,128)(2,1)S(1)} %get-tuple-element.89), channel_id=1, source_target_pairs={{0,2},{1,3},{2,0},{3,1},{4,6},{5,7},{6,4},{7,5},{8,10},{9,11},{10,... | collective-permute-start | bytes 835592 | tf_op jit(solution)/shard_map/ppermute | solution.py:352
  57.5 11.2 %collective-permute-start.16 = (bf16[136,1024]{1,0:T(8,128)(2,1)S(1)}, bf16[136,1024]{1,0:T(8,128)(2,1)S(1)}, u32[]{:S(2)}, u32[]{:S(2)}) collective-permute-start(bf16[136,1024]{1,0:T(8,128)(2,1)S(1)} %get-tuple-element.85), channel_id=1, source_target_pairs={{0,12},{1,13},{2,14},{3,15},{4,0},{5,1},{6,2},{7,3},{8,4},{9,5},{1... | collective-permute-start | bytes 835592 | tf_op jit(solution)/shard_map/ppermute | solution.py:349
  60.7 8.1 %collective-permute-start.22 = (bf16[136,1024]{1,0:T(8,128)(2,1)S(1)}, bf16[136,1024]{1,0:T(8,128)(2,1)S(1)}, u32[]{:S(2)}, u32[]{:S(2)}) collective-permute-start(bf16[136,1024]{1,0:T(8,128)(2,1)S(1)} %get-tuple-element.94), channel_id=1, source_target_pairs={{0,2},{1,3},{2,0},{3,1},{4,6},{5,7},{6,4},{7,5},{8,10},{9,11},{10,... | collective-permute-start | bytes 835592 | tf_op jit(solution)/shard_map/ppermute | solution.py:352
  62.5 10.2 %collective-permute-start.20 = (bf16[136,1024]{1,0:T(8,128)(2,1)S(1)}, bf16[136,1024]{1,0:T(8,128)(2,1)S(1)}, u32[]{:S(2)}, u32[]{:S(2)}) collective-permute-start(bf16[136,1024]{1,0:T(8,128)(2,1)S(1)} %add_convert_fusion.1), channel_id=1, source_target_pairs={{0,4},{1,5},{2,6},{3,7},{4,8},{5,9},{6,10},{7,11},{8,12},{9,13},{1... | collective-permute-start | bytes 835592 | tf_op jit(solution)/shard_map/ppermute | solution.py:346
  68.1 4.8 %collective-permute-start.24 = (bf16[1024,384]{1,0:T(8,128)(2,1)S(1)}, bf16[1024,384]{1,0:T(8,128)(2,1)S(1)}, u32[]{:S(2)}, u32[]{:S(2)}) collective-permute-start(bf16[1024,384]{1,0:T(8,128)(2,1)S(1)} %get-tuple-element.99), channel_id=1, source_target_pairs={{0,1},{1,0},{2,3},{3,2},{4,5},{5,4},{6,7},{7,6},{8,9},{9,8},{10,11... | collective-permute-start | bytes 2359304 | tf_op jit(solution)/shard_map/ppermute | solution.py:355
  68.2 4.8 %collective-permute-start.25 = (bf16[1024,384]{1,0:T(8,128)(2,1)S(1)}, bf16[1024,384]{1,0:T(8,128)(2,1)S(1)}, u32[]{:S(2)}, u32[]{:S(2)}) collective-permute-start(bf16[1024,384]{1,0:T(8,128)(2,1)S(1)} %get-tuple-element.100), channel_id=1, source_target_pairs={{0,1},{1,0},{2,3},{3,2},{4,5},{5,4},{6,7},{7,6},{8,9},{9,8},{10,11... | collective-permute-start | bytes 2359304 | tf_op jit(solution)/shard_map/ppermute | solution.py:355
  68.7 4.3 %collective-permute-start.26 = (bf16[384,1024]{1,0:T(8,128)(2,1)S(1)}, bf16[384,1024]{1,0:T(8,128)(2,1)S(1)}, u32[]{:S(2)}, u32[]{:S(2)}) collective-permute-start(bf16[384,1024]{1,0:T(8,128)(2,1)S(1)} %get-tuple-element.101), channel_id=1, source_target_pairs={{0,1},{1,0},{2,3},{3,2},{4,5},{5,4},{6,7},{7,6},{8,9},{9,8},{10,11... | collective-permute-start | bytes 2359304 | tf_op jit(solution)/shard_map/ppermute | solution.py:355
  68.8 11.2 %collective-permute-start.17 = (bf16[136,1024]{1,0:T(8,128)(2,1)S(1)}, bf16[136,1024]{1,0:T(8,128)(2,1)S(1)}, u32[]{:S(2)}, u32[]{:S(2)}) collective-permute-start(bf16[136,1024]{1,0:T(8,128)(2,1)S(1)} %add_convert_fusion.2), channel_id=1, source_target_pairs={{0,2},{1,3},{2,0},{3,1},{4,6},{5,7},{6,4},{7,5},{8,10},{9,11},{10,... | collective-permute-start | bytes 835592 | tf_op jit(solution)/shard_map/ppermute | solution.py:352
  72.8 10.7 %copy-start.5 = (s32[128,8]{0,1:T(8,128)S(1)}, s32[128,8]{0,1:T(8,128)}, u32[]{:S(2)}) copy-start(s32[128,8]{0,1:T(8,128)} %param.11) | copy-start | bytes 12292
  72.8 10.7 %copy-start.6 = (f32[16,128]{1,0:T(8,128)S(1)}, f32[16,128]{1,0:T(8,128)}, u32[]{:S(2)}) copy-start(f32[16,128]{1,0:T(8,128)} %get-tuple-element.61.kept) | copy-start | bytes 24580
  72.8 10.6 %collective-permute-start.23 = (bf16[136,1024]{1,0:T(8,128)(2,1)S(1)}, bf16[136,1024]{1,0:T(8,128)(2,1)S(1)}, u32[]{:S(2)}, u32[]{:S(2)}) collective-permute-start(bf16[136,1024]{1,0:T(8,128)(2,1)S(1)} %add_convert_fusion), channel_id=1, source_target_pairs={{0,4},{1,5},{2,6},{3,7},{4,8},{5,9},{6,10},{7,11},{8,12},{9,13},{1... | collective-permute-start | bytes 835592 | tf_op jit(solution)/shard_map/ppermute | solution.py:346

commit v12 on v11

--- a/solution.py
+++ b/solution.py
@@ -429,6 +429,8 @@
             if z < outer:
                 sums, xgs[z] = together(sums, xgs[z])
 
+    if outer > 1:
+        down = [send_down(v) for v in dxs[1][1:]]
     single = len(groups) == 1
     if single:
         other = [send_core(v) for v in partial(1, groups[0], bf16)]
@@ -439,8 +441,6 @@
     if outer > 1:
         if outer == 2:
             pieces.append(send_z(dxs[1][0]))
-        dxs[1], acts[-2] = together(dxs[1], acts[-2])
-        down = [send_down(v) for v in dxs[1][1:]]
         dxs[0] = [dxs[0][0]] + [add(v, o) for v, o in zip(dxs[0][1:], down)]
     pieces += [dxs[0][0], *send_across(0)]
     if outer > 2:

time: 84.4 us -> 81.1 us (0.961)
  starting transfers between devices: 27.3 us -> 25 us
  waiting for transfers between devices: 32.4 us -> 31.4 us
    ppermute x10, starting transfers between devices: 18.1 us -> 13.9 us  [send_y(): lax.ppermute(v, 'expert', [(i, moved(i, 0, 1)) for i in range(devices)])]
    ppermute x1, starting transfers between devices: 0.01 us -> 3.82 us  [send_down(): lax.ppermute(v, 'expert', [(i, moved(i, -1, 0)) for i in range(devices)])]
    ppermute x10, starting transfers between devices: 8.12 us -> 6.11 us  [send_z(): lax.ppermute(v, 'expert', [(i, moved(i, 1, 0)) for i in range(devices)])]
  transfers between devices with their start and end apart: 27 -> 27, of which waited for: 11 -> 13; matrix products, arithmetic and copies ran while one was open for 0% -> 0% of each run, Pallas kernels for 25% -> 26%
where the time goes in v12:
time: 81.1 us; the launch traced here: 81 us
  waiting for transfers between devices  31.4 us (39%)
  starting transfers between devices  25 us (31%)
  Pallas kernels  23.4 us (29%)
  between operations  0.82 us (1%)
    ppermute x10, waiting for transfers between devices, send_z(): lax.ppermute(v, 'expert', [(i, moved(i, 1, 0)) for i in range(devices)])  27.6 us
    ppermute x10, starting transfers between devices, send_y(): lax.ppermute(v, 'expert', [(i, moved(i, 0, 1)) for i in range(devices)])  13.9 us
    pallas_call x4, Pallas kernels, rows_grads(): pl.pallas_call(functools.partial(rows_kernel, slots), out_shape=tuple((ja...  12.8 us
    pallas_call x2, Pallas kernels, weights_grads(): pl.pallas_call(functools.partial(weights_kernel, j, slots, steps, len(mor...  7.99 us
    ppermute x10, starting transfers between devices, send_z(): lax.ppermute(v, 'expert', [(i, moved(i, 1, 0)) for i in range(devices)])  6.11 us
    ppermute x1, starting transfers between devices, send_down(): lax.ppermute(v, 'expert', [(i, moved(i, -1, 0)) for i in range(devices)])  3.82 us
    ppermute x10, waiting for transfers between devices, send_y(): lax.ppermute(v, 'expert', [(i, moved(i, 0, 1)) for i in range(devices)])  1.92 us
    ppermute x6, waiting for transfers between devices, send_core(): return lax.ppermute(v, 'expert', [(i, i ^ 1) for i in range(devices)])  1.89 us
  transfers between devices with their start and end apart: 27, of which 13 were waited for; matrix products, arithmetic and copies ran while one was open for 0% of the time, Pallas kernels for 26%

profile of v12, /device:TPU:0, one launch (start us, length us, event | category | flops | bytes accessed | tf_op | source)
XLA Modules:
  0.0 81.0 jit_solution(5446323400630186070)
XLA Ops:
  0.6 1.7 %plan.1 = (bf16[136,1024]{1,0:T(8,128)(2,1)}, f32[16,128]{1,0:T(8,128)}) custom-call(s32[1,16]{1,0:T(1,128)} %bitcast.25, s32[8,128]{1,0:T(8,128)} %bitcast.22, bf16[8,128]{1,0:T(8,128)(2,1)} %bitcast.24, bf16[128,1024]{1,0:T(8,128)(2,1)} %x_in.1), custom_call_target="tpu_custom_call" | custom-call | tf_op jit(solution)/shard_map/plan/pallas_call | solution.py:86
  2.4 3.1 %collective-permute-start.1 = (bf16[136,1024]{1,0:T(8,128)(2,1)}, bf16[136,1024]{1,0:T(8,128)(2,1)S(1)}, u32[]{:S(2)}, u32[]{:S(2)}) collective-permute-start(bf16[136,1024]{1,0:T(8,128)(2,1)} %get-tuple-element.60.refs_0_), channel_id=1, source_target_pairs={{0,4},{1,5},{2,6},{3,7},{4,8},{5,9},{6,10},{7,11},{8,12},{9,13},{1... | collective-permute-start | bytes 835592 | tf_op jit(solution)/shard_map/ppermute | solution.py:346
  5.5 1.5 %collective-permute-start = (bf16[136,1024]{1,0:T(8,128)(2,1)}, bf16[136,1024]{1,0:T(8,128)(2,1)S(1)}, u32[]{:S(2)}, u32[]{:S(2)}) collective-permute-start(bf16[136,1024]{1,0:T(8,128)(2,1)} %get-tuple-element.60.refs_0_), channel_id=1, source_target_pairs={{0,2},{1,3},{2,0},{3,1},{4,6},{5,7},{6,4},{7,5},{8,10},{9,11},{10,... | collective-permute-start | bytes 835592 | tf_op jit(solution)/shard_map/ppermute | solution.py:352
  7.0 1.6 %collective-permute-start.5 = (bf16[128,1024]{1,0:T(8,128)(2,1)}, bf16[128,1024]{1,0:T(8,128)(2,1)S(1)}, u32[]{:S(2)}, u32[]{:S(2)}) collective-permute-start(bf16[128,1024]{1,0:T(8,128)(2,1)} %refs_8_.3), channel_id=1, source_target_pairs={{0,4},{1,5},{2,6},{3,7},{4,8},{5,9},{6,10},{7,11},{8,12},{9,13},{1... | collective-permute-start | bytes 786440 | tf_op jit(solution)/shard_map/ppermute | solution.py:346
  8.6 0.5 collective-permute-start.4
  9.1 0.0 collective-permute-start.2
  9.1 6.1 %collective-permute-done.1.refs_0_.refs_2_ = bf16[136,1024]{1,0:T(8,128)(2,1)S(1)} collective-permute-done((bf16[136,1024]{1,0:T(8,128)(2,1)}, bf16[136,1024]{1,0:T(8,128)(2,1)S(1)}, u32[]{:S(2)}, u32[]{:S(2)}) %collective-permute-start.1) | collective-permute-done | bytes 278560 | tf_op jit(solution)/shard_map/ppermute | solution.py:346
  15.2 0.0 collective-permute-start.3
  15.2 0.1 collective-permute-done.refs_1_
  15.3 0.5 collective-permute-start.6
  15.8 0.0 collective-permute-done.2.refs_7_
  15.8 1.9 %collective-permute-done.3.refs_8_ = bf16[1024,384]{1,0:T(8,128)(2,1)S(1)} collective-permute-done((bf16[1024,384]{1,0:T(8,128)(2,1)}, bf16[1024,384]{1,0:T(8,128)(2,1)S(1)}, u32[]{:S(2)}, u32[]{:S(2)}) %collective-permute-start.3) | collective-permute-done | bytes 786464 | tf_op jit(solution)/shard_map/ppermute | solution.py:355
  17.7 0.0 collective-permute-start.8
  17.7 1.7 %collective-permute-start.7 = (bf16[136,1024]{1,0:T(8,128)(2,1)S(1)}, bf16[136,1024]{1,0:T(8,128)(2,1)S(1)}, u32[]{:S(2)}, u32[]{:S(2)}) collective-permute-start(bf16[136,1024]{1,0:T(8,128)(2,1)S(1)} %collective-permute-done.1.refs_0_.refs_2_), channel_id=1, source_target_pairs={{0,2},{1,3},{2,0},{3,1},{4,6},{5,7},{6,4},{7,5},{8,10},{9,11},{10,... | collective-permute-start | bytes 835592 | tf_op jit(solution)/shard_map/ppermute | solution.py:352
  19.4 0.5 collective-permute-done.5.refs_2_.refs_10_
  20.0 0.0 collective-permute-done.4.refs_3_.refs_9_
  20.0 0.0 collective-permute-done.6.refs_9_
  20.0 1.0 %collective-permute-start.10 = (bf16[128,1024]{1,0:T(8,128)(2,1)S(1)}, bf16[128,1024]{1,0:T(8,128)(2,1)S(1)}, u32[]{:S(2)}, u32[]{:S(2)}) collective-permute-start(bf16[128,1024]{1,0:T(8,128)(2,1)S(1)} %collective-permute-done.5.refs_2_.refs_10_), channel_id=1, source_target_pairs={{0,4},{1,5},{2,6},{3,7},{4,8},{5,9},{6,10},{7,11},{8,12},{9,13},{1... | collective-permute-start | bytes 786440 | tf_op jit(solution)/shard_map/ppermute | solution.py:346
  21.0 1.5 %collective-permute-start.9 = (bf16[128,1024]{1,0:T(8,128)(2,1)S(1)}, bf16[128,1024]{1,0:T(8,128)(2,1)S(1)}, u32[]{:S(2)}, u32[]{:S(2)}) collective-permute-start(bf16[128,1024]{1,0:T(8,128)(2,1)S(1)} %collective-permute-done.5.refs_2_.refs_10_), channel_id=1, source_target_pairs={{0,2},{1,3},{2,0},{3,1},{4,6},{5,7},{6,4},{7,5},{8,10},{9,11},{10,... | collective-permute-start | bytes 786440 | tf_op jit(solution)/shard_map/ppermute | solution.py:352
  22.5 3.2 %rows_grads.4 = (bf16[136,1024]{1,0:T(8,128)(2,1)S(1)}, bf16[136,1024]{1,0:T(8,128)(2,1)S(1)}, bf16[256,2304]{1,0:T(8,128)(2,1)S(1)}) custom-call(bf16[136,1024]{1,0:T(8,128)(2,1)S(1)} %copy-done.3, bf16[136,1024]{1,0:T(8,128)(2,1)S(1)} %collective-permute-done.refs_1_, bf16[128,1024]{1,0:T(8,128)(2,1)S(1)} %copy-done.4, ...), custom_call_target="tpu_custom_call" | custom-call | flops 1006632960 | bytes 9043968 | tf_op jit(solution)/shard_map/rows_grads/pallas_call | solution.py:190
  25.7 3.2 %collective-permute-done.8.refs_0_.refs_4_ = bf16[136,1024]{1,0:T(8,128)(2,1)S(1)} collective-permute-done((bf16[136,1024]{1,0:T(8,128)(2,1)S(1)}, bf16[136,1024]{1,0:T(8,128)(2,1)S(1)}, u32[]{:S(2)}, u32[]{:S(2)}) %collective-permute-start.8) | collective-permute-done | bytes 278560 | tf_op jit(solution)/shard_map/ppermute | solution.py:346
  29.0 0.0 collective-permute-done.7.refs_1_.refs_3_
  29.0 0.0 collective-permute-start.14
  29.0 1.8 %collective-permute-start.13 = (bf16[136,1024]{1,0:T(8,128)(2,1)S(1)}, bf16[136,1024]{1,0:T(8,128)(2,1)S(1)}, u32[]{:S(2)}, u32[]{:S(2)}) collective-permute-start(bf16[136,1024]{1,0:T(8,128)(2,1)S(1)} %collective-permute-done.8.refs_0_.refs_4_), channel_id=1, source_target_pairs={{0,2},{1,3},{2,0},{3,1},{4,6},{5,7},{6,4},{7,5},{8,10},{9,11},{10,... | collective-permute-start | bytes 835592 | tf_op jit(solution)/shard_map/ppermute | solution.py:352
  30.7 3.8 %collective-permute-done.10.refs_2_.refs_12_ = bf16[128,1024]{1,0:T(8,128)(2,1)S(1)} collective-permute-done((bf16[128,1024]{1,0:T(8,128)(2,1)S(1)}, bf16[128,1024]{1,0:T(8,128)(2,1)S(1)}, u32[]{:S(2)}, u32[]{:S(2)}) %collective-permute-start.10) | collective-permute-done | bytes 262176 | tf_op jit(solution)/shard_map/ppermute | solution.py:346
  34.6 0.0 collective-permute-done.9.refs_3_.refs_11_
  34.6 0.0 collective-permute-start.16
  34.6 1.8 %collective-permute-start.15 = (bf16[128,1024]{1,0:T(8,128)(2,1)S(1)}, bf16[128,1024]{1,0:T(8,128)(2,1)S(1)}, u32[]{:S(2)}, u32[]{:S(2)}) collective-permute-start(bf16[128,1024]{1,0:T(8,128)(2,1)S(1)} %collective-permute-done.10.refs_2_.refs_12_), channel_id=1, source_target_pairs={{0,2},{1,3},{2,0},{3,1},{4,6},{5,7},{6,4},{7,5},{8,10},{9,11},{10,... | collective-permute-start | bytes 786440 | tf_op jit(solution)/shard_map/ppermute | solution.py:352
  36.4 3.2 %rows_grads.5 = (bf16[136,1024]{1,0:T(8,128)(2,1)S(1)}, bf16[136,1024]{1,0:T(8,128)(2,1)S(1)}, bf16[256,2304]{1,0:T(8,128)(2,1)S(1)}) custom-call(bf16[136,1024]{1,0:T(8,128)(2,1)S(1)} %collective-permute-done.1.refs_0_.refs_2_, bf16[136,1024]{1,0:T(8,128)(2,1)S(1)} %collective-permute-done.7.refs_1_.refs_3_, ...), custom_call_target="tpu_custom_call" | custom-call | flops 1006632960 | bytes 9043968 | tf_op jit(solution)/shard_map/rows_grads/pallas_call | solution.py:190
  39.6 1.0 %collective-permute-done.14.refs_0_.refs_6_ = bf16[136,1024]{1,0:T(8,128)(2,1)S(1)} collective-permute-done((bf16[136,1024]{1,0:T(8,128)(2,1)S(1)}, bf16[136,1024]{1,0:T(8,128)(2,1)S(1)}, u32[]{:S(2)}, u32[]{:S(2)}) %collective-permute-start.14) | collective-permute-done | bytes 278560 | tf_op jit(solution)/shard_map/ppermute | solution.py:346
  40.6 0.0 collective-permute-done.13.refs_1_.refs_5_
  40.6 1.8 %collective-permute-start.18 = (bf16[136,1024]{1,0:T(8,128)(2,1)S(1)}, bf16[136,1024]{1,0:T(8,128)(2,1)S(1)}, u32[]{:S(2)}, u32[]{:S(2)}) collective-permute-start(bf16[136,1024]{1,0:T(8,128)(2,1)S(1)} %collective-permute-done.14.refs_0_.refs_6_), channel_id=1, source_target_pairs={{0,2},{1,3},{2,0},{3,1},{4,6},{5,7},{6,4},{7,5},{8,10},{9,11},{10,... | collective-permute-start | bytes 835592 | tf_op jit(solution)/shard_map/ppermute | solution.py:352
  42.3 0.0 collective-permute-start.17
  42.3 3.4 %collective-permute-done.16.refs_2_.refs_14_ = bf16[128,1024]{1,0:T(8,128)(2,1)S(1)} collective-permute-done((bf16[128,1024]{1,0:T(8,128)(2,1)S(1)}, bf16[128,1024]{1,0:T(8,128)(2,1)S(1)}, u32[]{:S(2)}, u32[]{:S(2)}) %collective-permute-start.16) | collective-permute-done | bytes 262176 | tf_op jit(solution)/shard_map/ppermute | solution.py:346
  45.7 0.3 collective-permute-start.21
  46.0 3.2 %rows_grads.6 = (bf16[136,1024]{1,0:T(8,128)(2,1)S(1)}, bf16[136,1024]{1,0:T(8,128)(2,1)S(1)}, bf16[256,2304]{1,0:T(8,128)(2,1)S(1)}) custom-call(bf16[136,1024]{1,0:T(8,128)(2,1)S(1)} %collective-permute-done.8.refs_0_.refs_4_, bf16[136,1024]{1,0:T(8,128)(2,1)S(1)} %collective-permute-done.13.refs_1_.refs_5_, ...), custom_call_target="tpu_custom_call" | custom-call | flops 1006632960 | bytes 9043968 | tf_op jit(solution)/shard_map/rows_grads/pallas_call | solution.py:190
  49.2 2.0 %collective-permute-start.19 = (bf16[136,1024]{1,0:T(8,128)(2,1)S(1)}, bf16[136,1024]{1,0:T(8,128)(2,1)S(1)}, u32[]{:S(2)}, u32[]{:S(2)}) collective-permute-start(bf16[136,1024]{1,0:T(8,128)(2,1)S(1)} %get-tuple-element.85), channel_id=1, source_target_pairs={{0,2},{1,3},{2,0},{3,1},{4,6},{5,7},{6,4},{7,5},{8,10},{9,11},{10,... | collective-permute-start | bytes 835592 | tf_op jit(solution)/shard_map/ppermute | solution.py:352
  51.2 3.8 %collective-permute-start.11 = (bf16[136,1024]{1,0:T(8,128)(2,1)S(1)}, bf16[136,1024]{1,0:T(8,128)(2,1)S(1)}, u32[]{:S(2)}, u32[]{:S(2)}) collective-permute-start(bf16[136,1024]{1,0:T(8,128)(2,1)S(1)} %get-tuple-element.73), channel_id=1, source_target_pairs={{0,12},{1,13},{2,14},{3,15},{4,0},{5,1},{6,2},{7,3},{8,4},{9,5},{1... | collective-permute-start | bytes 835592 | tf_op jit(solution)/shard_map/ppermute | solution.py:349
  55.1 4.2 %collective-permute-done.21.refs_3_.refs_15_ = bf16[128,1024]{1,0:T(8,128)(2,1)S(1)} collective-permute-done((bf16[128,1024]{1,0:T(8,128)(2,1)S(1)}, bf16[128,1024]{1,0:T(8,128)(2,1)S(1)}, u32[]{:S(2)}, u32[]{:S(2)}) %collective-permute-start.21) | collective-permute-done | bytes 262176 | tf_op jit(solution)/shard_map/ppermute | solution.py:346
  59.2 0.0 collective-permute-done.18.refs_1_.refs_7_
  59.2 0.0 collective-permute-done.17
  59.2 3.2 %rows_grads.7 = (bf16[136,1024]{1,0:T(8,128)(2,1)S(1)}, bf16[136,1024]{1,0:T(8,128)(2,1)S(1)}, bf16[256,2304]{1,0:T(8,128)(2,1)S(1)}) custom-call(bf16[136,1024]{1,0:T(8,128)(2,1)S(1)} %collective-permute-done.14.refs_0_.refs_6_, bf16[136,1024]{1,0:T(8,128)(2,1)S(1)} %collective-permute-done.18.refs_1_.refs_7_, ...), custom_call_target="tpu_custom_call" | custom-call | flops 1006632960 | bytes 9043968 | tf_op jit(solution)/shard_map/rows_grads/pallas_call | solution.py:190
  62.4 0.5 collective-permute-start.22
  62.9 0.1 add_convert_fusion.1
  63.1 0.1 collective-permute-start.20
  63.1 3.6 %weights_grads.2 = (bf16[1024,384]{1,0:T(8,128)(2,1)S(1)}, bf16[1024,384]{1,0:T(8,128)(2,1)S(1)}, bf16[384,1024]{1,0:T(8,128)(2,1)S(1)}) custom-call(bf16[136,1024]{1,0:T(8,128)(2,1)S(1)} %copy-done.3, bf16[136,1024]{1,0:T(8,128)(2,1)S(1)} %collective-permute-done.refs_1_, bf16[136,1024]{1,0:T(8,128)(2,1)S(1)} %collective-permute-done.1.refs_0_.refs_2_, ...), custom_call_target="tpu_custom_call" | custom-call | flops 1000 | bytes 1000 | tf_op jit(solution)/shard_map/weights_grads/pallas_call | solution.py:265
  66.7 0.1 collective-permute-start.24
  66.8 0.5 collective-permute-start.25
  67.3 0.0 collective-permute-done.11
  67.3 0.1 collective-permute-start.26
  67.4 0.1 add_convert_fusion.2
  67.4 1.6 %collective-permute-done.22 = bf16[136,1024]{1,0:T(8,128)(2,1)S(1)} collective-permute-done((bf16[136,1024]{1,0:T(8,128)(2,1)S(1)}, bf16[136,1024]{1,0:T(8,128)(2,1)S(1)}, u32[]{:S(2)}, u32[]{:S(2)}) %collective-permute-start.22) | collective-permute-done | bytes 278560 | tf_op jit(solution)/shard_map/ppermute | solution.py:352
  69.1 0.8 %collective-permute-start.12 = (bf16[136,1024]{1,0:T(8,128)(2,1)S(1)}, bf16[136,1024]{1,0:T(8,128)(2,1)S(1)}, u32[]{:S(2)}, u32[]{:S(2)}) collective-permute-start(bf16[136,1024]{1,0:T(8,128)(2,1)S(1)} %add_convert_fusion.2), channel_id=1, source_target_pairs={{0,2},{1,3},{2,0},{3,1},{4,6},{5,7},{6,4},{7,5},{8,10},{9,11},{10,... | collective-permute-start | bytes 835592 | tf_op jit(solution)/shard_map/ppermute | solution.py:352
  69.9 1.7 %collective-permute-done.20 = bf16[136,1024]{1,0:T(8,128)(2,1)S(1)} collective-permute-done((bf16[136,1024]{1,0:T(8,128)(2,1)S(1)}, bf16[136,1024]{1,0:T(8,128)(2,1)S(1)}, u32[]{:S(2)}, u32[]{:S(2)}) %collective-permute-start.20) | collective-permute-done | bytes 278560 | tf_op jit(solution)/shard_map/ppermute | solution.py:346
  71.6 0.1 add_convert_fusion
  71.7 0.0 copy-start.5
  71.7 0.0 copy-start.6
  71.8 0.1 collective-permute-start.23
  71.8 0.0 collective-permute-done.24.refs_20_
  71.8 0.0 collective-permute-done.25.refs_21_
  71.8 4.4 %weights_grads.3 = (bf16[1,1024,384]{2,1,0:T(8,128)(2,1)}, bf16[1,1024,384]{2,1,0:T(8,128)(2,1)}, bf16[1,384,1024]{2,1,0:T(8,128)(2,1)}) custom-call(bf16[136,1024]{1,0:T(8,128)(2,1)S(1)} %copy-done.3, bf16[136,1024]{1,0:T(8,128)(2,1)S(1)} %collective-permute-done.refs_1_, bf16[136,1024]{1,0:T(8,128)(2,1)S(1)} %collective-permute-done.1.refs_0_.refs_2_, ...), custom_call_target="tpu_custom_call" | custom-call | flops 1000 | bytes 1000 | tf_op jit(solution)/shard_map/weights_grads/pallas_call | solution.py:265
  76.3 0.2 collective-permute-done.12.refs_1_
  76.5 3.6 %collective-permute-done.23.refs_2_ = bf16[136,1024]{1,0:T(8,128)(2,1)S(1)} collective-permute-done((bf16[136,1024]{1,0:T(8,128)(2,1)S(1)}, bf16[136,1024]{1,0:T(8,128)(2,1)S(1)}, u32[]{:S(2)}, u32[]{:S(2)}) %collective-permute-start.23) | collective-permute-done | bytes 278560 | tf_op jit(solution)/shard_map/ppermute | solution.py:346
  80.2 0.8 finish.1
  (16 shorter events, 0.0 us)
Async XLA Ops:
  2.4 12.8 %collective-permute-start.1 = (bf16[136,1024]{1,0:T(8,128)(2,1)}, bf16[136,1024]{1,0:T(8,128)(2,1)S(1)}, u32[]{:S(2)}, u32[]{:S(2)}) collective-permute-start(bf16[136,1024]{1,0:T(8,128)(2,1)} %get-tuple-element.60.refs_0_), channel_id=1, source_target_pairs={{0,4},{1,5},{2,6},{3,7},{4,8},{5,9},{6,10},{7,11},{8,12},{9,13},{1... | collective-permute-start | bytes 835592 | tf_op jit(solution)/shard_map/ppermute | solution.py:346
  5.5 9.8 %collective-permute-start = (bf16[136,1024]{1,0:T(8,128)(2,1)}, bf16[136,1024]{1,0:T(8,128)(2,1)S(1)}, u32[]{:S(2)}, u32[]{:S(2)}) collective-permute-start(bf16[136,1024]{1,0:T(8,128)(2,1)} %get-tuple-element.60.refs_0_), channel_id=1, source_target_pairs={{0,2},{1,3},{2,0},{3,1},{4,6},{5,7},{6,4},{7,5},{8,10},{9,11},{10,... | collective-permute-start | bytes 835592 | tf_op jit(solution)/shard_map/ppermute | solution.py:352
  7.0 13.0 %collective-permute-start.5 = (bf16[128,1024]{1,0:T(8,128)(2,1)}, bf16[128,1024]{1,0:T(8,128)(2,1)S(1)}, u32[]{:S(2)}, u32[]{:S(2)}) collective-permute-start(bf16[128,1024]{1,0:T(8,128)(2,1)} %refs_8_.3), channel_id=1, source_target_pairs={{0,4},{1,5},{2,6},{3,7},{4,8},{5,9},{6,10},{7,11},{8,12},{9,13},{1... | collective-permute-start | bytes 786440 | tf_op jit(solution)/shard_map/ppermute | solution.py:346
  8.6 11.4 %collective-permute-start.4 = (bf16[128,1024]{1,0:T(8,128)(2,1)}, bf16[128,1024]{1,0:T(8,128)(2,1)S(1)}, u32[]{:S(2)}, u32[]{:S(2)}) collective-permute-start(bf16[128,1024]{1,0:T(8,128)(2,1)} %refs_8_.3), channel_id=1, source_target_pairs={{0,2},{1,3},{2,0},{3,1},{4,6},{5,7},{6,4},{7,5},{8,10},{9,11},{10,... | collective-permute-start | bytes 786440 | tf_op jit(solution)/shard_map/ppermute | solution.py:352
  9.1 6.7 %collective-permute-start.2 = (bf16[1024,384]{1,0:T(8,128)(2,1)}, bf16[1024,384]{1,0:T(8,128)(2,1)S(1)}, u32[]{:S(2)}, u32[]{:S(2)}) collective-permute-start(bf16[1024,384]{1,0:T(8,128)(2,1)} %bitcast.7), channel_id=1, source_target_pairs={{0,1},{1,0},{2,3},{3,2},{4,5},{5,4},{6,7},{7,6},{8,9},{9,8},{10,11... | collective-permute-start | bytes 2359304 | tf_op jit(solution)/shard_map/ppermute | solution.py:355
  15.2 2.5 %collective-permute-start.3 = (bf16[1024,384]{1,0:T(8,128)(2,1)}, bf16[1024,384]{1,0:T(8,128)(2,1)S(1)}, u32[]{:S(2)}, u32[]{:S(2)}) collective-permute-start(bf16[1024,384]{1,0:T(8,128)(2,1)} %bitcast.12), channel_id=1, source_target_pairs={{0,1},{1,0},{2,3},{3,2},{4,5},{5,4},{6,7},{7,6},{8,9},{9,8},{10,11... | collective-permute-start | bytes 2359304 | tf_op jit(solution)/shard_map/ppermute | solution.py:355
  15.3 7.3 %copy-start = (bf16[1,1024,384]{2,1,0:T(8,128)(2,1)S(1)}, bf16[1,1024,384]{2,1,0:T(8,128)(2,1)}, u32[]{:S(2)}) copy-start(bf16[1,1024,384]{2,1,0:T(8,128)(2,1)} %param.13) | copy-start | bytes 2359300
  15.3 7.3 %copy-start.1 = (bf16[1,1024,384]{2,1,0:T(8,128)(2,1)S(1)}, bf16[1,1024,384]{2,1,0:T(8,128)(2,1)}, u32[]{:S(2)}) copy-start(bf16[1,1024,384]{2,1,0:T(8,128)(2,1)} %param.14) | copy-start | bytes 2359300
  15.3 7.3 %copy-start.2 = (bf16[1,384,1024]{2,1,0:T(8,128)(2,1)S(1)}, bf16[1,384,1024]{2,1,0:T(8,128)(2,1)}, u32[]{:S(2)}) copy-start(bf16[1,384,1024]{2,1,0:T(8,128)(2,1)} %param.15) | copy-start | bytes 2359300
  15.3 7.3 %copy-start.3 = (bf16[136,1024]{1,0:T(8,128)(2,1)S(1)}, bf16[136,1024]{1,0:T(8,128)(2,1)}, u32[]{:S(2)}) copy-start(bf16[136,1024]{1,0:T(8,128)(2,1)} %get-tuple-element.60.refs_0_) | copy-start | bytes 835588
  15.3 7.3 %copy-start.4 = (bf16[128,1024]{1,0:T(8,128)(2,1)S(1)}, bf16[128,1024]{1,0:T(8,128)(2,1)}, u32[]{:S(2)}) copy-start(bf16[128,1024]{1,0:T(8,128)(2,1)} %refs_8_.3) | copy-start | bytes 786436
  15.3 4.7 %collective-permute-start.6 = (bf16[384,1024]{1,0:T(8,128)(2,1)}, bf16[384,1024]{1,0:T(8,128)(2,1)S(1)}, u32[]{:S(2)}, u32[]{:S(2)}) collective-permute-start(bf16[384,1024]{1,0:T(8,128)(2,1)} %bitcast.17), channel_id=1, source_target_pairs={{0,1},{1,0},{2,3},{3,2},{4,5},{5,4},{6,7},{7,6},{8,9},{9,8},{10,11... | collective-permute-start | bytes 2359304 | tf_op jit(solution)/shard_map/ppermute | solution.py:355
  17.7 11.3 %collective-permute-start.8 = (bf16[136,1024]{1,0:T(8,128)(2,1)S(1)}, bf16[136,1024]{1,0:T(8,128)(2,1)S(1)}, u32[]{:S(2)}, u32[]{:S(2)}) collective-permute-start(bf16[136,1024]{1,0:T(8,128)(2,1)S(1)} %collective-permute-done.1.refs_0_.refs_2_), channel_id=1, source_target_pairs={{0,4},{1,5},{2,6},{3,7},{4,8},{5,9},{6,10},{7,11},{8,12},{9,13},{1... | collective-permute-start | bytes 835592 | tf_op jit(solution)/shard_map/ppermute | solution.py:346
  17.7 11.3 %collective-permute-start.7 = (bf16[136,1024]{1,0:T(8,128)(2,1)S(1)}, bf16[136,1024]{1,0:T(8,128)(2,1)S(1)}, u32[]{:S(2)}, u32[]{:S(2)}) collective-permute-start(bf16[136,1024]{1,0:T(8,128)(2,1)S(1)} %collective-permute-done.1.refs_0_.refs_2_), channel_id=1, source_target_pairs={{0,2},{1,3},{2,0},{3,1},{4,6},{5,7},{6,4},{7,5},{8,10},{9,11},{10,... | collective-permute-start | bytes 835592 | tf_op jit(solution)/shard_map/ppermute | solution.py:352
  20.0 14.6 %collective-permute-start.10 = (bf16[128,1024]{1,0:T(8,128)(2,1)S(1)}, bf16[128,1024]{1,0:T(8,128)(2,1)S(1)}, u32[]{:S(2)}, u32[]{:S(2)}) collective-permute-start(bf16[128,1024]{1,0:T(8,128)(2,1)S(1)} %collective-permute-done.5.refs_2_.refs_10_), channel_id=1, source_target_pairs={{0,4},{1,5},{2,6},{3,7},{4,8},{5,9},{6,10},{7,11},{8,12},{9,13},{1... | collective-permute-start | bytes 786440 | tf_op jit(solution)/shard_map/ppermute | solution.py:346
  21.0 13.6 %collective-permute-start.9 = (bf16[128,1024]{1,0:T(8,128)(2,1)S(1)}, bf16[128,1024]{1,0:T(8,128)(2,1)S(1)}, u32[]{:S(2)}, u32[]{:S(2)}) collective-permute-start(bf16[128,1024]{1,0:T(8,128)(2,1)S(1)} %collective-permute-done.5.refs_2_.refs_10_), channel_id=1, source_target_pairs={{0,2},{1,3},{2,0},{3,1},{4,6},{5,7},{6,4},{7,5},{8,10},{9,11},{10,... | collective-permute-start | bytes 786440 | tf_op jit(solution)/shard_map/ppermute | solution.py:352
  29.0 11.6 %collective-permute-start.14 = (bf16[136,1024]{1,0:T(8,128)(2,1)S(1)}, bf16[136,1024]{1,0:T(8,128)(2,1)S(1)}, u32[]{:S(2)}, u32[]{:S(2)}) collective-permute-start(bf16[136,1024]{1,0:T(8,128)(2,1)S(1)} %collective-permute-done.8.refs_0_.refs_4_), channel_id=1, source_target_pairs={{0,4},{1,5},{2,6},{3,7},{4,8},{5,9},{6,10},{7,11},{8,12},{9,13},{1... | collective-permute-start | bytes 835592 | tf_op jit(solution)/shard_map/ppermute | solution.py:346
  29.0 11.6 %collective-permute-start.13 = (bf16[136,1024]{1,0:T(8,128)(2,1)S(1)}, bf16[136,1024]{1,0:T(8,128)(2,1)S(1)}, u32[]{:S(2)}, u32[]{:S(2)}) collective-permute-start(bf16[136,1024]{1,0:T(8,128)(2,1)S(1)} %collective-permute-done.8.refs_0_.refs_4_), channel_id=1, source_target_pairs={{0,2},{1,3},{2,0},{3,1},{4,6},{5,7},{6,4},{7,5},{8,10},{9,11},{10,... | collective-permute-start | bytes 835592 | tf_op jit(solution)/shard_map/ppermute | solution.py:352
  34.6 11.1 %collective-permute-start.16 = (bf16[128,1024]{1,0:T(8,128)(2,1)S(1)}, bf16[128,1024]{1,0:T(8,128)(2,1)S(1)}, u32[]{:S(2)}, u32[]{:S(2)}) collective-permute-start(bf16[128,1024]{1,0:T(8,128)(2,1)S(1)} %collective-permute-done.10.refs_2_.refs_12_), channel_id=1, source_target_pairs={{0,4},{1,5},{2,6},{3,7},{4,8},{5,9},{6,10},{7,11},{8,12},{9,13},{1... | collective-permute-start | bytes 786440 | tf_op jit(solution)/shard_map/ppermute | solution.py:346
  34.6 11.1 %collective-permute-start.15 = (bf16[128,1024]{1,0:T(8,128)(2,1)S(1)}, bf16[128,1024]{1,0:T(8,128)(2,1)S(1)}, u32[]{:S(2)}, u32[]{:S(2)}) collective-permute-start(bf16[128,1024]{1,0:T(8,128)(2,1)S(1)} %collective-permute-done.10.refs_2_.refs_12_), channel_id=1, source_target_pairs={{0,2},{1,3},{2,0},{3,1},{4,6},{5,7},{6,4},{7,5},{8,10},{9,11},{10,... | collective-permute-start | bytes 786440 | tf_op jit(solution)/shard_map/ppermute | solution.py:352
  40.6 18.7 %collective-permute-start.18 = (bf16[136,1024]{1,0:T(8,128)(2,1)S(1)}, bf16[136,1024]{1,0:T(8,128)(2,1)S(1)}, u32[]{:S(2)}, u32[]{:S(2)}) collective-permute-start(bf16[136,1024]{1,0:T(8,128)(2,1)S(1)} %collective-permute-done.14.refs_0_.refs_6_), channel_id=1, source_target_pairs={{0,2},{1,3},{2,0},{3,1},{4,6},{5,7},{6,4},{7,5},{8,10},{9,11},{10,... | collective-permute-start | bytes 835592 | tf_op jit(solution)/shard_map/ppermute | solution.py:352
  42.3 16.9 %collective-permute-start.17 = (bf16[136,1024]{1,0:T(8,128)(2,1)S(1)}, bf16[136,1024]{1,0:T(8,128)(2,1)S(1)}, u32[]{:S(2)}, u32[]{:S(2)}) collective-permute-start(bf16[136,1024]{1,0:T(8,128)(2,1)S(1)} %get-tuple-element.80), channel_id=1, source_target_pairs={{0,4},{1,5},{2,6},{3,7},{4,8},{5,9},{6,10},{7,11},{8,12},{9,13},{1... | collective-permute-start | bytes 835592 | tf_op jit(solution)/shard_map/ppermute | solution.py:346
  45.7 13.5 %collective-permute-start.21 = (bf16[128,1024]{1,0:T(8,128)(2,1)S(1)}, bf16[128,1024]{1,0:T(8,128)(2,1)S(1)}, u32[]{:S(2)}, u32[]{:S(2)}) collective-permute-start(bf16[128,1024]{1,0:T(8,128)(2,1)S(1)} %collective-permute-done.15.refs_3_.refs_13_), channel_id=1, source_target_pairs={{0,4},{1,5},{2,6},{3,7},{4,8},{5,9},{6,10},{7,11},{8,12},{9,13},{1... | collective-permute-start | bytes 786440 | tf_op jit(solution)/shard_map/ppermute | solution.py:346
  49.2 13.7 %collective-permute-start.19 = (bf16[136,1024]{1,0:T(8,128)(2,1)S(1)}, bf16[136,1024]{1,0:T(8,128)(2,1)S(1)}, u32[]{:S(2)}, u32[]{:S(2)}) collective-permute-start(bf16[136,1024]{1,0:T(8,128)(2,1)S(1)} %get-tuple-element.85), channel_id=1, source_target_pairs={{0,2},{1,3},{2,0},{3,1},{4,6},{5,7},{6,4},{7,5},{8,10},{9,11},{10,... | collective-permute-start | bytes 835592 | tf_op jit(solution)/shard_map/ppermute | solution.py:352
  51.2 16.1 %collective-permute-start.11 = (bf16[136,1024]{1,0:T(8,128)(2,1)S(1)}, bf16[136,1024]{1,0:T(8,128)(2,1)S(1)}, u32[]{:S(2)}, u32[]{:S(2)}) collective-permute-start(bf16[136,1024]{1,0:T(8,128)(2,1)S(1)} %get-tuple-element.73), channel_id=1, source_target_pairs={{0,12},{1,13},{2,14},{3,15},{4,0},{5,1},{6,2},{7,3},{8,4},{9,5},{1... | collective-permute-start | bytes 835592 | tf_op jit(solution)/shard_map/ppermute | solution.py:349
  62.4 6.6 %collective-permute-start.22 = (bf16[136,1024]{1,0:T(8,128)(2,1)S(1)}, bf16[136,1024]{1,0:T(8,128)(2,1)S(1)}, u32[]{:S(2)}, u32[]{:S(2)}) collective-permute-start(bf16[136,1024]{1,0:T(8,128)(2,1)S(1)} %get-tuple-element.90), channel_id=1, source_target_pairs={{0,2},{1,3},{2,0},{3,1},{4,6},{5,7},{6,4},{7,5},{8,10},{9,11},{10,... | collective-permute-start | bytes 835592 | tf_op jit(solution)/shard_map/ppermute | solution.py:352
  63.1 8.5 %collective-permute-start.20 = (bf16[136,1024]{1,0:T(8,128)(2,1)S(1)}, bf16[136,1024]{1,0:T(8,128)(2,1)S(1)}, u32[]{:S(2)}, u32[]{:S(2)}) collective-permute-start(bf16[136,1024]{1,0:T(8,128)(2,1)S(1)} %add_convert_fusion.1), channel_id=1, source_target_pairs={{0,4},{1,5},{2,6},{3,7},{4,8},{5,9},{6,10},{7,11},{8,12},{9,13},{1... | collective-permute-start | bytes 835592 | tf_op jit(solution)/shard_map/ppermute | solution.py:346
  66.7 5.1 %collective-permute-start.24 = (bf16[1024,384]{1,0:T(8,128)(2,1)S(1)}, bf16[1024,384]{1,0:T(8,128)(2,1)S(1)}, u32[]{:S(2)}, u32[]{:S(2)}) collective-permute-start(bf16[1024,384]{1,0:T(8,128)(2,1)S(1)} %get-tuple-element.95), channel_id=1, source_target_pairs={{0,1},{1,0},{2,3},{3,2},{4,5},{5,4},{6,7},{7,6},{8,9},{9,8},{10,11... | collective-permute-start | bytes 2359304 | tf_op jit(solution)/shard_map/ppermute | solution.py:355
  66.8 5.0 %collective-permute-start.25 = (bf16[1024,384]{1,0:T(8,128)(2,1)S(1)}, bf16[1024,384]{1,0:T(8,128)(2,1)S(1)}, u32[]{:S(2)}, u32[]{:S(2)}) collective-permute-start(bf16[1024,384]{1,0:T(8,128)(2,1)S(1)} %get-tuple-element.96), channel_id=1, source_target_pairs={{0,1},{1,0},{2,3},{3,2},{4,5},{5,4},{6,7},{7,6},{8,9},{9,8},{10,11... | collective-permute-start | bytes 2359304 | tf_op jit(solution)/shard_map/ppermute | solution.py:355
  67.3 4.6 %collective-permute-start.26 = (bf16[384,1024]{1,0:T(8,128)(2,1)S(1)}, bf16[384,1024]{1,0:T(8,128)(2,1)S(1)}, u32[]{:S(2)}, u32[]{:S(2)}) collective-permute-start(bf16[384,1024]{1,0:T(8,128)(2,1)S(1)} %get-tuple-element.97), channel_id=1, source_target_pairs={{0,1},{1,0},{2,3},{3,2},{4,5},{5,4},{6,7},{7,6},{8,9},{9,8},{10,11... | collective-permute-start | bytes 2359304 | tf_op jit(solution)/shard_map/ppermute | solution.py:355
  69.1 7.5 %collective-permute-start.12 = (bf16[136,1024]{1,0:T(8,128)(2,1)S(1)}, bf16[136,1024]{1,0:T(8,128)(2,1)S(1)}, u32[]{:S(2)}, u32[]{:S(2)}) collective-permute-start(bf16[136,1024]{1,0:T(8,128)(2,1)S(1)} %add_convert_fusion.2), channel_id=1, source_target_pairs={{0,2},{1,3},{2,0},{3,1},{4,6},{5,7},{6,4},{7,5},{8,10},{9,11},{10,... | collective-permute-start | bytes 835592 | tf_op jit(solution)/shard_map/ppermute | solution.py:352
  71.7 8.4 %copy-start.5 = (s32[128,8]{0,1:T(8,128)S(1)}, s32[128,8]{0,1:T(8,128)}, u32[]{:S(2)}) copy-start(s32[128,8]{0,1:T(8,128)} %param.11) | copy-start | bytes 12292
  71.7 8.4 %copy-start.6 = (f32[16,128]{1,0:T(8,128)S(1)}, f32[16,128]{1,0:T(8,128)}, u32[]{:S(2)}) copy-start(f32[16,128]{1,0:T(8,128)} %get-tuple-element.59.kept) | copy-start | bytes 24580
  71.8 8.4 %collective-permute-start.23 = (bf16[136,1024]{1,0:T(8,128)(2,1)S(1)}, bf16[136,1024]{1,0:T(8,128)(2,1)S(1)}, u32[]{:S(2)}, u32[]{:S(2)}) collective-permute-start(bf16[136,1024]{1,0:T(8,128)(2,1)S(1)} %add_convert_fusion), channel_id=1, source_target_pairs={{0,4},{1,5},{2,6},{3,7},{4,8},{5,9},{6,10},{7,11},{8,12},{9,13},{1... | collective-permute-start | bytes 835592 | tf_op jit(solution)/shard_map/ppermute | solution.py:346

commit v13 on v12

--- a/solution.py
+++ b/solution.py
@@ -416,7 +416,7 @@
             if inner > 1:
                 last[-1] = done.pop()
         if z == outer > 2:
-            first, xgs[z - 1] = together(send_z(dxs[1][0]), xgs[z - 1])
+            first = send_z(dxs[1][0])
         *dx, act = rows_grads(xgs[z - 1], dys[z - 1], weights)
         dxs.append(dx)
         acts.append(act)

time: 81.1 us -> 81.2 us (level)
  starting transfers between devices: 25 us -> 27.8 us
  waiting for transfers between devices: 31.4 us -> 28.7 us
    ppermute x10, starting transfers between devices: 13.9 us -> 15.7 us  [send_y(): lax.ppermute(v, 'expert', [(i, moved(i, 0, 1)) for i in range(devices)])]
    ppermute x10, waiting for transfers between devices: 27.6 us -> 25.8 us  [send_z(): lax.ppermute(v, 'expert', [(i, moved(i, 1, 0)) for i in range(devices)])]
    ppermute x10, starting transfers between devices: 6.11 us -> 7.05 us  [send_z(): lax.ppermute(v, 'expert', [(i, moved(i, 1, 0)) for i in range(devices)])]
    ppermute x10, waiting for transfers between devices: 1.92 us -> 1 us  [send_y(): lax.ppermute(v, 'expert', [(i, moved(i, 0, 1)) for i in range(devices)])]
  transfers between devices with their start and end apart: 27 -> 27, of which waited for: 13 -> 12; matrix products, arithmetic and copies ran while one was open for 0% -> 0% of each run, Pallas kernels for 26% -> 26%
where the time goes in v13:
time: 81.2 us; the launch traced here: 81 us
  waiting for transfers between devices  28.7 us (35%)
  starting transfers between devices  27.8 us (34%)
  Pallas kernels  23.4 us (29%)
  between operations  0.82 us (1%)
    ppermute x10, waiting for transfers between devices, send_z(): lax.ppermute(v, 'expert', [(i, moved(i, 1, 0)) for i in range(devices)])  25.8 us
    ppermute x10, starting transfers between devices, send_y(): lax.ppermute(v, 'expert', [(i, moved(i, 0, 1)) for i in range(devices)])  15.7 us
    pallas_call x4, Pallas kernels, rows_grads(): pl.pallas_call(functools.partial(rows_kernel, slots), out_shape=tuple((ja...  12.9 us
    pallas_call x2, Pallas kernels, weights_grads(): pl.pallas_call(functools.partial(weights_kernel, j, slots, steps, len(mor...  7.99 us
    ppermute x10, starting transfers between devices, send_z(): lax.ppermute(v, 'expert', [(i, moved(i, 1, 0)) for i in range(devices)])  7.05 us
    ppermute x1, starting transfers between devices, send_down(): lax.ppermute(v, 'expert', [(i, moved(i, -1, 0)) for i in range(devices)])  3.82 us
    ppermute x6, waiting for transfers between devices, send_core(): return lax.ppermute(v, 'expert', [(i, i ^ 1) for i in range(devices)])  1.89 us
    pallas_call x1, Pallas kernels, plan(): pl.pallas_call(functools.partial(plan_kernel, home_cap, rep_cap), out_sha...  1.74 us
  transfers between devices with their start and end apart: 27, of which 12 were waited for; matrix products, arithmetic and copies ran while one was open for 0% of the time, Pallas kernels for 26%

profile of v13, /device:TPU:0, one launch (start us, length us, event | category | flops | bytes accessed | tf_op | source)
XLA Modules:
  0.0 81.0 jit_solution(17094315644860174161)
XLA Ops:
  0.6 1.7 %plan.1 = (bf16[136,1024]{1,0:T(8,128)(2,1)}, f32[16,128]{1,0:T(8,128)}) custom-call(s32[1,16]{1,0:T(1,128)} %bitcast.25, s32[8,128]{1,0:T(8,128)} %bitcast.22, bf16[8,128]{1,0:T(8,128)(2,1)} %bitcast.24, bf16[128,1024]{1,0:T(8,128)(2,1)} %x_in.1), custom_call_target="tpu_custom_call" | custom-call | tf_op jit(solution)/shard_map/plan/pallas_call | solution.py:86
  2.4 3.1 %collective-permute-start.1 = (bf16[136,1024]{1,0:T(8,128)(2,1)}, bf16[136,1024]{1,0:T(8,128)(2,1)S(1)}, u32[]{:S(2)}, u32[]{:S(2)}) collective-permute-start(bf16[136,1024]{1,0:T(8,128)(2,1)} %get-tuple-element.57.refs_0_), channel_id=1, source_target_pairs={{0,4},{1,5},{2,6},{3,7},{4,8},{5,9},{6,10},{7,11},{8,12},{9,13},{1... | collective-permute-start | bytes 835592 | tf_op jit(solution)/shard_map/ppermute | solution.py:346
  5.5 1.5 %collective-permute-start = (bf16[136,1024]{1,0:T(8,128)(2,1)}, bf16[136,1024]{1,0:T(8,128)(2,1)S(1)}, u32[]{:S(2)}, u32[]{:S(2)}) collective-permute-start(bf16[136,1024]{1,0:T(8,128)(2,1)} %get-tuple-element.57.refs_0_), channel_id=1, source_target_pairs={{0,2},{1,3},{2,0},{3,1},{4,6},{5,7},{6,4},{7,5},{8,10},{9,11},{10,... | collective-permute-start | bytes 835592 | tf_op jit(solution)/shard_map/ppermute | solution.py:352
  7.0 1.6 %collective-permute-start.5 = (bf16[128,1024]{1,0:T(8,128)(2,1)}, bf16[128,1024]{1,0:T(8,128)(2,1)S(1)}, u32[]{:S(2)}, u32[]{:S(2)}) collective-permute-start(bf16[128,1024]{1,0:T(8,128)(2,1)} %refs_8_.3), channel_id=1, source_target_pairs={{0,4},{1,5},{2,6},{3,7},{4,8},{5,9},{6,10},{7,11},{8,12},{9,13},{1... | collective-permute-start | bytes 786440 | tf_op jit(solution)/shard_map/ppermute | solution.py:346
  8.6 0.5 collective-permute-start.4
  9.1 0.0 collective-permute-start.2
  9.1 6.1 %collective-permute-done.1.refs_0_.refs_2_ = bf16[136,1024]{1,0:T(8,128)(2,1)S(1)} collective-permute-done((bf16[136,1024]{1,0:T(8,128)(2,1)}, bf16[136,1024]{1,0:T(8,128)(2,1)S(1)}, u32[]{:S(2)}, u32[]{:S(2)}) %collective-permute-start.1) | collective-permute-done | bytes 278560 | tf_op jit(solution)/shard_map/ppermute | solution.py:346
  15.2 0.0 collective-permute-start.3
  15.2 0.1 collective-permute-done.refs_1_
  15.3 0.5 collective-permute-start.6
  15.8 0.0 collective-permute-done.2.refs_7_
  15.8 1.9 %collective-permute-done.3.refs_8_ = bf16[1024,384]{1,0:T(8,128)(2,1)S(1)} collective-permute-done((bf16[1024,384]{1,0:T(8,128)(2,1)}, bf16[1024,384]{1,0:T(8,128)(2,1)S(1)}, u32[]{:S(2)}, u32[]{:S(2)}) %collective-permute-start.3) | collective-permute-done | bytes 786464 | tf_op jit(solution)/shard_map/ppermute | solution.py:355
  17.7 0.0 collective-permute-start.8
  17.7 1.7 %collective-permute-start.7 = (bf16[136,1024]{1,0:T(8,128)(2,1)S(1)}, bf16[136,1024]{1,0:T(8,128)(2,1)S(1)}, u32[]{:S(2)}, u32[]{:S(2)}) collective-permute-start(bf16[136,1024]{1,0:T(8,128)(2,1)S(1)} %collective-permute-done.1.refs_0_.refs_2_), channel_id=1, source_target_pairs={{0,2},{1,3},{2,0},{3,1},{4,6},{5,7},{6,4},{7,5},{8,10},{9,11},{10,... | collective-permute-start | bytes 835592 | tf_op jit(solution)/shard_map/ppermute | solution.py:352
  19.4 0.5 collective-permute-done.5.refs_2_.refs_10_
  20.0 0.0 collective-permute-done.4.refs_3_.refs_9_
  20.0 0.0 collective-permute-done.6.refs_9_
  20.0 1.0 %collective-permute-start.10 = (bf16[128,1024]{1,0:T(8,128)(2,1)S(1)}, bf16[128,1024]{1,0:T(8,128)(2,1)S(1)}, u32[]{:S(2)}, u32[]{:S(2)}) collective-permute-start(bf16[128,1024]{1,0:T(8,128)(2,1)S(1)} %collective-permute-done.5.refs_2_.refs_10_), channel_id=1, source_target_pairs={{0,4},{1,5},{2,6},{3,7},{4,8},{5,9},{6,10},{7,11},{8,12},{9,13},{1... | collective-permute-start | bytes 786440 | tf_op jit(solution)/shard_map/ppermute | solution.py:346
  21.0 1.5 %collective-permute-start.9 = (bf16[128,1024]{1,0:T(8,128)(2,1)S(1)}, bf16[128,1024]{1,0:T(8,128)(2,1)S(1)}, u32[]{:S(2)}, u32[]{:S(2)}) collective-permute-start(bf16[128,1024]{1,0:T(8,128)(2,1)S(1)} %collective-permute-done.5.refs_2_.refs_10_), channel_id=1, source_target_pairs={{0,2},{1,3},{2,0},{3,1},{4,6},{5,7},{6,4},{7,5},{8,10},{9,11},{10,... | collective-permute-start | bytes 786440 | tf_op jit(solution)/shard_map/ppermute | solution.py:352
  22.5 3.2 %rows_grads.4 = (bf16[136,1024]{1,0:T(8,128)(2,1)S(1)}, bf16[136,1024]{1,0:T(8,128)(2,1)S(1)}, bf16[256,2304]{1,0:T(8,128)(2,1)S(1)}) custom-call(bf16[136,1024]{1,0:T(8,128)(2,1)S(1)} %copy-done.3, bf16[136,1024]{1,0:T(8,128)(2,1)S(1)} %collective-permute-done.refs_1_, bf16[128,1024]{1,0:T(8,128)(2,1)S(1)} %copy-done.4, ...), custom_call_target="tpu_custom_call" | custom-call | flops 1006632960 | bytes 9043968 | tf_op jit(solution)/shard_map/rows_grads/pallas_call | solution.py:190
  25.7 3.2 %collective-permute-done.8.refs_0_.refs_4_ = bf16[136,1024]{1,0:T(8,128)(2,1)S(1)} collective-permute-done((bf16[136,1024]{1,0:T(8,128)(2,1)S(1)}, bf16[136,1024]{1,0:T(8,128)(2,1)S(1)}, u32[]{:S(2)}, u32[]{:S(2)}) %collective-permute-start.8) | collective-permute-done | bytes 278560 | tf_op jit(solution)/shard_map/ppermute | solution.py:346
  29.0 0.0 collective-permute-done.7.refs_1_.refs_3_
  29.0 1.8 %collective-permute-start.13 = (bf16[136,1024]{1,0:T(8,128)(2,1)S(1)}, bf16[136,1024]{1,0:T(8,128)(2,1)S(1)}, u32[]{:S(2)}, u32[]{:S(2)}) collective-permute-start(bf16[136,1024]{1,0:T(8,128)(2,1)S(1)} %collective-permute-done.8.refs_0_.refs_4_), channel_id=1, source_target_pairs={{0,2},{1,3},{2,0},{3,1},{4,6},{5,7},{6,4},{7,5},{8,10},{9,11},{10,... | collective-permute-start | bytes 835592 | tf_op jit(solution)/shard_map/ppermute | solution.py:352
  30.7 3.8 %collective-permute-done.10.refs_2_.refs_12_ = bf16[128,1024]{1,0:T(8,128)(2,1)S(1)} collective-permute-done((bf16[128,1024]{1,0:T(8,128)(2,1)S(1)}, bf16[128,1024]{1,0:T(8,128)(2,1)S(1)}, u32[]{:S(2)}, u32[]{:S(2)}) %collective-permute-start.10) | collective-permute-done | bytes 262176 | tf_op jit(solution)/shard_map/ppermute | solution.py:346
  34.6 0.0 collective-permute-done.9.refs_3_.refs_11_
  34.6 0.0 collective-permute-start.16
  34.6 1.8 %collective-permute-start.15 = (bf16[128,1024]{1,0:T(8,128)(2,1)S(1)}, bf16[128,1024]{1,0:T(8,128)(2,1)S(1)}, u32[]{:S(2)}, u32[]{:S(2)}) collective-permute-start(bf16[128,1024]{1,0:T(8,128)(2,1)S(1)} %collective-permute-done.10.refs_2_.refs_12_), channel_id=1, source_target_pairs={{0,2},{1,3},{2,0},{3,1},{4,6},{5,7},{6,4},{7,5},{8,10},{9,11},{10,... | collective-permute-start | bytes 786440 | tf_op jit(solution)/shard_map/ppermute | solution.py:352
  36.4 3.2 %rows_grads.5 = (bf16[136,1024]{1,0:T(8,128)(2,1)S(1)}, bf16[136,1024]{1,0:T(8,128)(2,1)S(1)}, bf16[256,2304]{1,0:T(8,128)(2,1)S(1)}) custom-call(bf16[136,1024]{1,0:T(8,128)(2,1)S(1)} %collective-permute-done.1.refs_0_.refs_2_, bf16[136,1024]{1,0:T(8,128)(2,1)S(1)} %collective-permute-done.7.refs_1_.refs_3_, ...), custom_call_target="tpu_custom_call" | custom-call | flops 1006632960 | bytes 9043968 | tf_op jit(solution)/shard_map/rows_grads/pallas_call | solution.py:190
  39.6 1.2 %collective-permute-start.17 = (bf16[136,1024]{1,0:T(8,128)(2,1)S(1)}, bf16[136,1024]{1,0:T(8,128)(2,1)S(1)}, u32[]{:S(2)}, u32[]{:S(2)}) collective-permute-start(bf16[136,1024]{1,0:T(8,128)(2,1)S(1)} %get-tuple-element.77), channel_id=1, source_target_pairs={{0,4},{1,5},{2,6},{3,7},{4,8},{5,9},{6,10},{7,11},{8,12},{9,13},{1... | collective-permute-start | bytes 835592 | tf_op jit(solution)/shard_map/ppermute | solution.py:346
  40.8 0.0 collective-permute-done.14.refs_0_.refs_6_
  40.8 0.0 collective-permute-done.13.refs_1_.refs_5_
  40.8 1.5 %collective-permute-start.20 = (bf16[136,1024]{1,0:T(8,128)(2,1)S(1)}, bf16[136,1024]{1,0:T(8,128)(2,1)S(1)}, u32[]{:S(2)}, u32[]{:S(2)}) collective-permute-start(bf16[136,1024]{1,0:T(8,128)(2,1)S(1)} %collective-permute-done.14.refs_0_.refs_6_), channel_id=1, source_target_pairs={{0,2},{1,3},{2,0},{3,1},{4,6},{5,7},{6,4},{7,5},{8,10},{9,11},{10,... | collective-permute-start | bytes 835592 | tf_op jit(solution)/shard_map/ppermute | solution.py:352
  42.3 3.8 %collective-permute-done.16.refs_2_.refs_14_ = bf16[128,1024]{1,0:T(8,128)(2,1)S(1)} collective-permute-done((bf16[128,1024]{1,0:T(8,128)(2,1)S(1)}, bf16[128,1024]{1,0:T(8,128)(2,1)S(1)}, u32[]{:S(2)}, u32[]{:S(2)}) %collective-permute-start.16) | collective-permute-done | bytes 262176 | tf_op jit(solution)/shard_map/ppermute | solution.py:346
  46.2 0.0 collective-permute-done.15.refs_3_.refs_13_
  46.2 0.0 collective-permute-start.21
  46.2 3.2 %rows_grads.6 = (bf16[136,1024]{1,0:T(8,128)(2,1)S(1)}, bf16[136,1024]{1,0:T(8,128)(2,1)S(1)}, bf16[256,2304]{1,0:T(8,128)(2,1)S(1)}) custom-call(bf16[136,1024]{1,0:T(8,128)(2,1)S(1)} %collective-permute-done.8.refs_0_.refs_4_, bf16[136,1024]{1,0:T(8,128)(2,1)S(1)} %collective-permute-done.13.refs_1_.refs_5_, ...), custom_call_target="tpu_custom_call" | custom-call | flops 1006632960 | bytes 9043968 | tf_op jit(solution)/shard_map/rows_grads/pallas_call | solution.py:190
  49.4 1.8 %collective-permute-start.18 = (bf16[136,1024]{1,0:T(8,128)(2,1)S(1)}, bf16[136,1024]{1,0:T(8,128)(2,1)S(1)}, u32[]{:S(2)}, u32[]{:S(2)}) collective-permute-start(bf16[136,1024]{1,0:T(8,128)(2,1)S(1)} %get-tuple-element.78), channel_id=1, source_target_pairs={{0,2},{1,3},{2,0},{3,1},{4,6},{5,7},{6,4},{7,5},{8,10},{9,11},{10,... | collective-permute-start | bytes 835592 | tf_op jit(solution)/shard_map/ppermute | solution.py:352
  51.2 3.8 %collective-permute-start.11 = (bf16[136,1024]{1,0:T(8,128)(2,1)S(1)}, bf16[136,1024]{1,0:T(8,128)(2,1)S(1)}, u32[]{:S(2)}, u32[]{:S(2)}) collective-permute-start(bf16[136,1024]{1,0:T(8,128)(2,1)S(1)} %get-tuple-element.70), channel_id=1, source_target_pairs={{0,12},{1,13},{2,14},{3,15},{4,0},{5,1},{6,2},{7,3},{8,4},{9,5},{1... | collective-permute-start | bytes 835592 | tf_op jit(solution)/shard_map/ppermute | solution.py:349
  55.1 2.8 %collective-permute-done.21.refs_3_.refs_15_ = bf16[128,1024]{1,0:T(8,128)(2,1)S(1)} collective-permute-done((bf16[128,1024]{1,0:T(8,128)(2,1)S(1)}, bf16[128,1024]{1,0:T(8,128)(2,1)S(1)}, u32[]{:S(2)}, u32[]{:S(2)}) %collective-permute-start.21) | collective-permute-done | bytes 262176 | tf_op jit(solution)/shard_map/ppermute | solution.py:346
  57.8 3.2 %rows_grads.7 = (bf16[136,1024]{1,0:T(8,128)(2,1)S(1)}, bf16[136,1024]{1,0:T(8,128)(2,1)S(1)}, bf16[256,2304]{1,0:T(8,128)(2,1)S(1)}) custom-call(bf16[136,1024]{1,0:T(8,128)(2,1)S(1)} %collective-permute-done.14.refs_0_.refs_6_, bf16[136,1024]{1,0:T(8,128)(2,1)S(1)} %collective-permute-done.20.refs_1_.refs_7_, ...), custom_call_target="tpu_custom_call" | custom-call | flops 1006632960 | bytes 9043968 | tf_op jit(solution)/shard_map/rows_grads/pallas_call | solution.py:190
  61.0 1.8 %collective-permute-start.22 = (bf16[136,1024]{1,0:T(8,128)(2,1)S(1)}, bf16[136,1024]{1,0:T(8,128)(2,1)S(1)}, u32[]{:S(2)}, u32[]{:S(2)}) collective-permute-start(bf16[136,1024]{1,0:T(8,128)(2,1)S(1)} %get-tuple-element.84), channel_id=1, source_target_pairs={{0,2},{1,3},{2,0},{3,1},{4,6},{5,7},{6,4},{7,5},{8,10},{9,11},{10,... | collective-permute-start | bytes 835592 | tf_op jit(solution)/shard_map/ppermute | solution.py:352
  62.9 0.0 collective-permute-done.17
  62.9 0.0 collective-permute-done.18
  62.9 0.1 add_convert_fusion.1
  63.0 0.1 collective-permute-start.19
  63.1 3.6 %weights_grads.2 = (bf16[1024,384]{1,0:T(8,128)(2,1)S(1)}, bf16[1024,384]{1,0:T(8,128)(2,1)S(1)}, bf16[384,1024]{1,0:T(8,128)(2,1)S(1)}) custom-call(bf16[136,1024]{1,0:T(8,128)(2,1)S(1)} %copy-done.3, bf16[136,1024]{1,0:T(8,128)(2,1)S(1)} %collective-permute-done.refs_1_, bf16[136,1024]{1,0:T(8,128)(2,1)S(1)} %collective-permute-done.1.refs_0_.refs_2_, ...), custom_call_target="tpu_custom_call" | custom-call | flops 1000 | bytes 1000 | tf_op jit(solution)/shard_map/weights_grads/pallas_call | solution.py:265
  66.6 0.1 collective-permute-start.24
  66.7 0.5 collective-permute-start.25
  67.2 0.0 collective-permute-done.11
  67.2 0.1 collective-permute-start.26
  67.3 0.1 add_convert_fusion.2
  67.4 0.8 %collective-permute-done.22 = bf16[136,1024]{1,0:T(8,128)(2,1)S(1)} collective-permute-done((bf16[136,1024]{1,0:T(8,128)(2,1)S(1)}, bf16[136,1024]{1,0:T(8,128)(2,1)S(1)}, u32[]{:S(2)}, u32[]{:S(2)}) %collective-permute-start.22) | collective-permute-done | bytes 278560 | tf_op jit(solution)/shard_map/ppermute | solution.py:352
  68.2 1.7 %collective-permute-start.12 = (bf16[136,1024]{1,0:T(8,128)(2,1)S(1)}, bf16[136,1024]{1,0:T(8,128)(2,1)S(1)}, u32[]{:S(2)}, u32[]{:S(2)}) collective-permute-start(bf16[136,1024]{1,0:T(8,128)(2,1)S(1)} %add_convert_fusion.2), channel_id=1, source_target_pairs={{0,2},{1,3},{2,0},{3,1},{4,6},{5,7},{6,4},{7,5},{8,10},{9,11},{10,... | collective-permute-start | bytes 835592 | tf_op jit(solution)/shard_map/ppermute | solution.py:352
  69.9 1.7 %collective-permute-done.19 = bf16[136,1024]{1,0:T(8,128)(2,1)S(1)} collective-permute-done((bf16[136,1024]{1,0:T(8,128)(2,1)S(1)}, bf16[136,1024]{1,0:T(8,128)(2,1)S(1)}, u32[]{:S(2)}, u32[]{:S(2)}) %collective-permute-start.19) | collective-permute-done | bytes 278560 | tf_op jit(solution)/shard_map/ppermute | solution.py:346
  71.6 0.1 add_convert_fusion
  71.8 0.0 copy-start.5
  71.8 0.0 copy-start.6
  71.8 0.1 collective-permute-start.23
  71.9 0.0 collective-permute-done.24.refs_20_
  71.9 0.0 collective-permute-done.25.refs_21_
  71.9 4.4 %weights_grads.3 = (bf16[1,1024,384]{2,1,0:T(8,128)(2,1)}, bf16[1,1024,384]{2,1,0:T(8,128)(2,1)}, bf16[1,384,1024]{2,1,0:T(8,128)(2,1)}) custom-call(bf16[136,1024]{1,0:T(8,128)(2,1)S(1)} %copy-done.3, bf16[136,1024]{1,0:T(8,128)(2,1)S(1)} %collective-permute-done.refs_1_, bf16[136,1024]{1,0:T(8,128)(2,1)S(1)} %collective-permute-done.1.refs_0_.refs_2_, ...), custom_call_target="tpu_custom_call" | custom-call | flops 1000 | bytes 1000 | tf_op jit(solution)/shard_map/weights_grads/pallas_call | solution.py:265
  76.3 0.1 collective-permute-done.12.refs_1_
  76.4 3.8 %collective-permute-done.23.refs_2_ = bf16[136,1024]{1,0:T(8,128)(2,1)S(1)} collective-permute-done((bf16[136,1024]{1,0:T(8,128)(2,1)S(1)}, bf16[136,1024]{1,0:T(8,128)(2,1)S(1)}, u32[]{:S(2)}, u32[]{:S(2)}) %collective-permute-start.23) | collective-permute-done | bytes 278560 | tf_op jit(solution)/shard_map/ppermute | solution.py:346
  80.2 0.8 finish.1
  (16 shorter events, 0.0 us)
Async XLA Ops:
  2.4 12.8 %collective-permute-start.1 = (bf16[136,1024]{1,0:T(8,128)(2,1)}, bf16[136,1024]{1,0:T(8,128)(2,1)S(1)}, u32[]{:S(2)}, u32[]{:S(2)}) collective-permute-start(bf16[136,1024]{1,0:T(8,128)(2,1)} %get-tuple-element.57.refs_0_), channel_id=1, source_target_pairs={{0,4},{1,5},{2,6},{3,7},{4,8},{5,9},{6,10},{7,11},{8,12},{9,13},{1... | collective-permute-start | bytes 835592 | tf_op jit(solution)/shard_map/ppermute | solution.py:346
  5.5 9.8 %collective-permute-start = (bf16[136,1024]{1,0:T(8,128)(2,1)}, bf16[136,1024]{1,0:T(8,128)(2,1)S(1)}, u32[]{:S(2)}, u32[]{:S(2)}) collective-permute-start(bf16[136,1024]{1,0:T(8,128)(2,1)} %get-tuple-element.57.refs_0_), channel_id=1, source_target_pairs={{0,2},{1,3},{2,0},{3,1},{4,6},{5,7},{6,4},{7,5},{8,10},{9,11},{10,... | collective-permute-start | bytes 835592 | tf_op jit(solution)/shard_map/ppermute | solution.py:352
  7.0 13.0 %collective-permute-start.5 = (bf16[128,1024]{1,0:T(8,128)(2,1)}, bf16[128,1024]{1,0:T(8,128)(2,1)S(1)}, u32[]{:S(2)}, u32[]{:S(2)}) collective-permute-start(bf16[128,1024]{1,0:T(8,128)(2,1)} %refs_8_.3), channel_id=1, source_target_pairs={{0,4},{1,5},{2,6},{3,7},{4,8},{5,9},{6,10},{7,11},{8,12},{9,13},{1... | collective-permute-start | bytes 786440 | tf_op jit(solution)/shard_map/ppermute | solution.py:346
  8.6 11.4 %collective-permute-start.4 = (bf16[128,1024]{1,0:T(8,128)(2,1)}, bf16[128,1024]{1,0:T(8,128)(2,1)S(1)}, u32[]{:S(2)}, u32[]{:S(2)}) collective-permute-start(bf16[128,1024]{1,0:T(8,128)(2,1)} %refs_8_.3), channel_id=1, source_target_pairs={{0,2},{1,3},{2,0},{3,1},{4,6},{5,7},{6,4},{7,5},{8,10},{9,11},{10,... | collective-permute-start | bytes 786440 | tf_op jit(solution)/shard_map/ppermute | solution.py:352
  9.1 6.7 %collective-permute-start.2 = (bf16[1024,384]{1,0:T(8,128)(2,1)}, bf16[1024,384]{1,0:T(8,128)(2,1)S(1)}, u32[]{:S(2)}, u32[]{:S(2)}) collective-permute-start(bf16[1024,384]{1,0:T(8,128)(2,1)} %bitcast.7), channel_id=1, source_target_pairs={{0,1},{1,0},{2,3},{3,2},{4,5},{5,4},{6,7},{7,6},{8,9},{9,8},{10,11... | collective-permute-start | bytes 2359304 | tf_op jit(solution)/shard_map/ppermute | solution.py:355
  15.2 2.5 %collective-permute-start.3 = (bf16[1024,384]{1,0:T(8,128)(2,1)}, bf16[1024,384]{1,0:T(8,128)(2,1)S(1)}, u32[]{:S(2)}, u32[]{:S(2)}) collective-permute-start(bf16[1024,384]{1,0:T(8,128)(2,1)} %bitcast.12), channel_id=1, source_target_pairs={{0,1},{1,0},{2,3},{3,2},{4,5},{5,4},{6,7},{7,6},{8,9},{9,8},{10,11... | collective-permute-start | bytes 2359304 | tf_op jit(solution)/shard_map/ppermute | solution.py:355
  15.3 7.3 %copy-start = (bf16[1,1024,384]{2,1,0:T(8,128)(2,1)S(1)}, bf16[1,1024,384]{2,1,0:T(8,128)(2,1)}, u32[]{:S(2)}) copy-start(bf16[1,1024,384]{2,1,0:T(8,128)(2,1)} %param.13) | copy-start | bytes 2359300
  15.3 7.3 %copy-start.1 = (bf16[1,1024,384]{2,1,0:T(8,128)(2,1)S(1)}, bf16[1,1024,384]{2,1,0:T(8,128)(2,1)}, u32[]{:S(2)}) copy-start(bf16[1,1024,384]{2,1,0:T(8,128)(2,1)} %param.14) | copy-start | bytes 2359300
  15.3 7.3 %copy-start.2 = (bf16[1,384,1024]{2,1,0:T(8,128)(2,1)S(1)}, bf16[1,384,1024]{2,1,0:T(8,128)(2,1)}, u32[]{:S(2)}) copy-start(bf16[1,384,1024]{2,1,0:T(8,128)(2,1)} %param.15) | copy-start | bytes 2359300
  15.3 7.3 %copy-start.3 = (bf16[136,1024]{1,0:T(8,128)(2,1)S(1)}, bf16[136,1024]{1,0:T(8,128)(2,1)}, u32[]{:S(2)}) copy-start(bf16[136,1024]{1,0:T(8,128)(2,1)} %get-tuple-element.57.refs_0_) | copy-start | bytes 835588
  15.3 7.3 %copy-start.4 = (bf16[128,1024]{1,0:T(8,128)(2,1)S(1)}, bf16[128,1024]{1,0:T(8,128)(2,1)}, u32[]{:S(2)}) copy-start(bf16[128,1024]{1,0:T(8,128)(2,1)} %refs_8_.3) | copy-start | bytes 786436
  15.3 4.7 %collective-permute-start.6 = (bf16[384,1024]{1,0:T(8,128)(2,1)}, bf16[384,1024]{1,0:T(8,128)(2,1)S(1)}, u32[]{:S(2)}, u32[]{:S(2)}) collective-permute-start(bf16[384,1024]{1,0:T(8,128)(2,1)} %bitcast.17), channel_id=1, source_target_pairs={{0,1},{1,0},{2,3},{3,2},{4,5},{5,4},{6,7},{7,6},{8,9},{9,8},{10,11... | collective-permute-start | bytes 2359304 | tf_op jit(solution)/shard_map/ppermute | solution.py:355
  17.7 11.3 %collective-permute-start.8 = (bf16[136,1024]{1,0:T(8,128)(2,1)S(1)}, bf16[136,1024]{1,0:T(8,128)(2,1)S(1)}, u32[]{:S(2)}, u32[]{:S(2)}) collective-permute-start(bf16[136,1024]{1,0:T(8,128)(2,1)S(1)} %collective-permute-done.1.refs_0_.refs_2_), channel_id=1, source_target_pairs={{0,4},{1,5},{2,6},{3,7},{4,8},{5,9},{6,10},{7,11},{8,12},{9,13},{1... | collective-permute-start | bytes 835592 | tf_op jit(solution)/shard_map/ppermute | solution.py:346
  17.7 11.3 %collective-permute-start.7 = (bf16[136,1024]{1,0:T(8,128)(2,1)S(1)}, bf16[136,1024]{1,0:T(8,128)(2,1)S(1)}, u32[]{:S(2)}, u32[]{:S(2)}) collective-permute-start(bf16[136,1024]{1,0:T(8,128)(2,1)S(1)} %collective-permute-done.1.refs_0_.refs_2_), channel_id=1, source_target_pairs={{0,2},{1,3},{2,0},{3,1},{4,6},{5,7},{6,4},{7,5},{8,10},{9,11},{10,... | collective-permute-start | bytes 835592 | tf_op jit(solution)/shard_map/ppermute | solution.py:352
  20.0 14.6 %collective-permute-start.10 = (bf16[128,1024]{1,0:T(8,128)(2,1)S(1)}, bf16[128,1024]{1,0:T(8,128)(2,1)S(1)}, u32[]{:S(2)}, u32[]{:S(2)}) collective-permute-start(bf16[128,1024]{1,0:T(8,128)(2,1)S(1)} %collective-permute-done.5.refs_2_.refs_10_), channel_id=1, source_target_pairs={{0,4},{1,5},{2,6},{3,7},{4,8},{5,9},{6,10},{7,11},{8,12},{9,13},{1... | collective-permute-start | bytes 786440 | tf_op jit(solution)/shard_map/ppermute | solution.py:346
  21.0 13.6 %collective-permute-start.9 = (bf16[128,1024]{1,0:T(8,128)(2,1)S(1)}, bf16[128,1024]{1,0:T(8,128)(2,1)S(1)}, u32[]{:S(2)}, u32[]{:S(2)}) collective-permute-start(bf16[128,1024]{1,0:T(8,128)(2,1)S(1)} %collective-permute-done.5.refs_2_.refs_10_), channel_id=1, source_target_pairs={{0,2},{1,3},{2,0},{3,1},{4,6},{5,7},{6,4},{7,5},{8,10},{9,11},{10,... | collective-permute-start | bytes 786440 | tf_op jit(solution)/shard_map/ppermute | solution.py:352
  29.0 11.8 %collective-permute-start.14 = (bf16[136,1024]{1,0:T(8,128)(2,1)S(1)}, bf16[136,1024]{1,0:T(8,128)(2,1)S(1)}, u32[]{:S(2)}, u32[]{:S(2)}) collective-permute-start(bf16[136,1024]{1,0:T(8,128)(2,1)S(1)} %collective-permute-done.8.refs_0_.refs_4_), channel_id=1, source_target_pairs={{0,4},{1,5},{2,6},{3,7},{4,8},{5,9},{6,10},{7,11},{8,12},{9,13},{1... | collective-permute-start | bytes 835592 | tf_op jit(solution)/shard_map/ppermute | solution.py:346
  29.0 11.8 %collective-permute-start.13 = (bf16[136,1024]{1,0:T(8,128)(2,1)S(1)}, bf16[136,1024]{1,0:T(8,128)(2,1)S(1)}, u32[]{:S(2)}, u32[]{:S(2)}) collective-permute-start(bf16[136,1024]{1,0:T(8,128)(2,1)S(1)} %collective-permute-done.8.refs_0_.refs_4_), channel_id=1, source_target_pairs={{0,2},{1,3},{2,0},{3,1},{4,6},{5,7},{6,4},{7,5},{8,10},{9,11},{10,... | collective-permute-start | bytes 835592 | tf_op jit(solution)/shard_map/ppermute | solution.py:352
  34.6 11.6 %collective-permute-start.16 = (bf16[128,1024]{1,0:T(8,128)(2,1)S(1)}, bf16[128,1024]{1,0:T(8,128)(2,1)S(1)}, u32[]{:S(2)}, u32[]{:S(2)}) collective-permute-start(bf16[128,1024]{1,0:T(8,128)(2,1)S(1)} %collective-permute-done.10.refs_2_.refs_12_), channel_id=1, source_target_pairs={{0,4},{1,5},{2,6},{3,7},{4,8},{5,9},{6,10},{7,11},{8,12},{9,13},{1... | collective-permute-start | bytes 786440 | tf_op jit(solution)/shard_map/ppermute | solution.py:346
  34.6 11.6 %collective-permute-start.15 = (bf16[128,1024]{1,0:T(8,128)(2,1)S(1)}, bf16[128,1024]{1,0:T(8,128)(2,1)S(1)}, u32[]{:S(2)}, u32[]{:S(2)}) collective-permute-start(bf16[128,1024]{1,0:T(8,128)(2,1)S(1)} %collective-permute-done.10.refs_2_.refs_12_), channel_id=1, source_target_pairs={{0,2},{1,3},{2,0},{3,1},{4,6},{5,7},{6,4},{7,5},{8,10},{9,11},{10,... | collective-permute-start | bytes 786440 | tf_op jit(solution)/shard_map/ppermute | solution.py:352
  39.6 23.3 %collective-permute-start.17 = (bf16[136,1024]{1,0:T(8,128)(2,1)S(1)}, bf16[136,1024]{1,0:T(8,128)(2,1)S(1)}, u32[]{:S(2)}, u32[]{:S(2)}) collective-permute-start(bf16[136,1024]{1,0:T(8,128)(2,1)S(1)} %get-tuple-element.77), channel_id=1, source_target_pairs={{0,4},{1,5},{2,6},{3,7},{4,8},{5,9},{6,10},{7,11},{8,12},{9,13},{1... | collective-permute-start | bytes 835592 | tf_op jit(solution)/shard_map/ppermute | solution.py:346
  40.8 17.0 %collective-permute-start.20 = (bf16[136,1024]{1,0:T(8,128)(2,1)S(1)}, bf16[136,1024]{1,0:T(8,128)(2,1)S(1)}, u32[]{:S(2)}, u32[]{:S(2)}) collective-permute-start(bf16[136,1024]{1,0:T(8,128)(2,1)S(1)} %collective-permute-done.14.refs_0_.refs_6_), channel_id=1, source_target_pairs={{0,2},{1,3},{2,0},{3,1},{4,6},{5,7},{6,4},{7,5},{8,10},{9,11},{10,... | collective-permute-start | bytes 835592 | tf_op jit(solution)/shard_map/ppermute | solution.py:352
  46.2 11.6 %collective-permute-start.21 = (bf16[128,1024]{1,0:T(8,128)(2,1)S(1)}, bf16[128,1024]{1,0:T(8,128)(2,1)S(1)}, u32[]{:S(2)}, u32[]{:S(2)}) collective-permute-start(bf16[128,1024]{1,0:T(8,128)(2,1)S(1)} %collective-permute-done.15.refs_3_.refs_13_), channel_id=1, source_target_pairs={{0,4},{1,5},{2,6},{3,7},{4,8},{5,9},{6,10},{7,11},{8,12},{9,13},{1... | collective-permute-start | bytes 786440 | tf_op jit(solution)/shard_map/ppermute | solution.py:346
  49.4 13.5 %collective-permute-start.18 = (bf16[136,1024]{1,0:T(8,128)(2,1)S(1)}, bf16[136,1024]{1,0:T(8,128)(2,1)S(1)}, u32[]{:S(2)}, u32[]{:S(2)}) collective-permute-start(bf16[136,1024]{1,0:T(8,128)(2,1)S(1)} %get-tuple-element.78), channel_id=1, source_target_pairs={{0,2},{1,3},{2,0},{3,1},{4,6},{5,7},{6,4},{7,5},{8,10},{9,11},{10,... | collective-permute-start | bytes 835592 | tf_op jit(solution)/shard_map/ppermute | solution.py:352
  51.2 16.0 %collective-permute-start.11 = (bf16[136,1024]{1,0:T(8,128)(2,1)S(1)}, bf16[136,1024]{1,0:T(8,128)(2,1)S(1)}, u32[]{:S(2)}, u32[]{:S(2)}) collective-permute-start(bf16[136,1024]{1,0:T(8,128)(2,1)S(1)} %get-tuple-element.70), channel_id=1, source_target_pairs={{0,12},{1,13},{2,14},{3,15},{4,0},{5,1},{6,2},{7,3},{8,4},{9,5},{1... | collective-permute-start | bytes 835592 | tf_op jit(solution)/shard_map/ppermute | solution.py:349
  61.0 7.2 %collective-permute-start.22 = (bf16[136,1024]{1,0:T(8,128)(2,1)S(1)}, bf16[136,1024]{1,0:T(8,128)(2,1)S(1)}, u32[]{:S(2)}, u32[]{:S(2)}) collective-permute-start(bf16[136,1024]{1,0:T(8,128)(2,1)S(1)} %get-tuple-element.84), channel_id=1, source_target_pairs={{0,2},{1,3},{2,0},{3,1},{4,6},{5,7},{6,4},{7,5},{8,10},{9,11},{10,... | collective-permute-start | bytes 835592 | tf_op jit(solution)/shard_map/ppermute | solution.py:352
  63.0 8.6 %collective-permute-start.19 = (bf16[136,1024]{1,0:T(8,128)(2,1)S(1)}, bf16[136,1024]{1,0:T(8,128)(2,1)S(1)}, u32[]{:S(2)}, u32[]{:S(2)}) collective-permute-start(bf16[136,1024]{1,0:T(8,128)(2,1)S(1)} %add_convert_fusion.1), channel_id=1, source_target_pairs={{0,4},{1,5},{2,6},{3,7},{4,8},{5,9},{6,10},{7,11},{8,12},{9,13},{1... | collective-permute-start | bytes 835592 | tf_op jit(solution)/shard_map/ppermute | solution.py:346
  66.6 5.2 %collective-permute-start.24 = (bf16[1024,384]{1,0:T(8,128)(2,1)S(1)}, bf16[1024,384]{1,0:T(8,128)(2,1)S(1)}, u32[]{:S(2)}, u32[]{:S(2)}) collective-permute-start(bf16[1024,384]{1,0:T(8,128)(2,1)S(1)} %get-tuple-element.89), channel_id=1, source_target_pairs={{0,1},{1,0},{2,3},{3,2},{4,5},{5,4},{6,7},{7,6},{8,9},{9,8},{10,11... | collective-permute-start | bytes 2359304 | tf_op jit(solution)/shard_map/ppermute | solution.py:355
  66.7 5.2 %collective-permute-start.25 = (bf16[1024,384]{1,0:T(8,128)(2,1)S(1)}, bf16[1024,384]{1,0:T(8,128)(2,1)S(1)}, u32[]{:S(2)}, u32[]{:S(2)}) collective-permute-start(bf16[1024,384]{1,0:T(8,128)(2,1)S(1)} %get-tuple-element.90), channel_id=1, source_target_pairs={{0,1},{1,0},{2,3},{3,2},{4,5},{5,4},{6,7},{7,6},{8,9},{9,8},{10,11... | collective-permute-start | bytes 2359304 | tf_op jit(solution)/shard_map/ppermute | solution.py:355
  67.2 4.7 %collective-permute-start.26 = (bf16[384,1024]{1,0:T(8,128)(2,1)S(1)}, bf16[384,1024]{1,0:T(8,128)(2,1)S(1)}, u32[]{:S(2)}, u32[]{:S(2)}) collective-permute-start(bf16[384,1024]{1,0:T(8,128)(2,1)S(1)} %get-tuple-element.91), channel_id=1, source_target_pairs={{0,1},{1,0},{2,3},{3,2},{4,5},{5,4},{6,7},{7,6},{8,9},{9,8},{10,11... | collective-permute-start | bytes 2359304 | tf_op jit(solution)/shard_map/ppermute | solution.py:355
  68.2 8.3 %collective-permute-start.12 = (bf16[136,1024]{1,0:T(8,128)(2,1)S(1)}, bf16[136,1024]{1,0:T(8,128)(2,1)S(1)}, u32[]{:S(2)}, u32[]{:S(2)}) collective-permute-start(bf16[136,1024]{1,0:T(8,128)(2,1)S(1)} %add_convert_fusion.2), channel_id=1, source_target_pairs={{0,2},{1,3},{2,0},{3,1},{4,6},{5,7},{6,4},{7,5},{8,10},{9,11},{10,... | collective-permute-start | bytes 835592 | tf_op jit(solution)/shard_map/ppermute | solution.py:352
  71.8 8.4 %copy-start.5 = (s32[128,8]{0,1:T(8,128)S(1)}, s32[128,8]{0,1:T(8,128)}, u32[]{:S(2)}) copy-start(s32[128,8]{0,1:T(8,128)} %param.11) | copy-start | bytes 12292
  71.8 8.4 %copy-start.6 = (f32[16,128]{1,0:T(8,128)S(1)}, f32[16,128]{1,0:T(8,128)}, u32[]{:S(2)}) copy-start(f32[16,128]{1,0:T(8,128)} %get-tuple-element.56.kept) | copy-start | bytes 24580
  71.8 8.4 %collective-permute-start.23 = (bf16[136,1024]{1,0:T(8,128)(2,1)S(1)}, bf16[136,1024]{1,0:T(8,128)(2,1)S(1)}, u32[]{:S(2)}, u32[]{:S(2)}) collective-permute-start(bf16[136,1024]{1,0:T(8,128)(2,1)S(1)} %add_convert_fusion), channel_id=1, source_target_pairs={{0,4},{1,5},{2,6},{3,7},{4,8},{5,9},{6,10},{7,11},{8,12},{9,13},{1... | collective-permute-start | bytes 835592 | tf_op jit(solution)/shard_map/ppermute | solution.py:346

commit v14 on v12

--- a/solution.py
+++ b/solution.py
@@ -394,7 +394,7 @@
             if z < outer:
                 ahead = send_z(last[0])
             for y in range(1, inner):
-                if k and z == outer > 1 and y == inner - 1:
+                if k == 0 and z == outer > 1 and y == inner - 1:
                     last.append(send_z(stream[z - 2][y]))
                 else:
                     last.append(send_y(last[y - 1]))

time: 81.1 us -> 81.6 us (level)
    ppermute x1, starting transfers between devices: 3.82 us -> 0.96 us  [send_down(): lax.ppermute(v, 'expert', [(i, moved(i, -1, 0)) for i in range(devices)])]
    ppermute x10, starting transfers between devices: 6.11 us -> 8.09 us  [send_z(): lax.ppermute(v, 'expert', [(i, moved(i, 1, 0)) for i in range(devices)])]
    ppermute x10, waiting for transfers between devices: 1.92 us -> 3.07 us  [send_y(): lax.ppermute(v, 'expert', [(i, moved(i, 0, 1)) for i in range(devices)])]
  transfers between devices with their start and end apart: 27 -> 27, of which waited for: 13 -> 14; matrix products, arithmetic and copies ran while one was open for 0% -> 0% of each run, Pallas kernels for 26% -> 26%
where the time goes in v14:
time: 81.6 us; the launch traced here: 81.4 us
  waiting for transfers between devices  32.1 us (39%)
  starting transfers between devices  24.7 us (30%)
  Pallas kernels  23.4 us (29%)
  between operations  0.82 us (1%)
    ppermute x10, waiting for transfers between devices, send_z(): lax.ppermute(v, 'expert', [(i, moved(i, 1, 0)) for i in range(devices)])  27.2 us
    ppermute x10, starting transfers between devices, send_y(): lax.ppermute(v, 'expert', [(i, moved(i, 0, 1)) for i in range(devices)])  14.5 us
    pallas_call x4, Pallas kernels, rows_grads(): pl.pallas_call(functools.partial(rows_kernel, slots), out_shape=tuple((ja...  12.9 us
    ppermute x10, starting transfers between devices, send_z(): lax.ppermute(v, 'expert', [(i, moved(i, 1, 0)) for i in range(devices)])  8.09 us
    pallas_call x2, Pallas kernels, weights_grads(): pl.pallas_call(functools.partial(weights_kernel, j, slots, steps, len(mor...  7.98 us
    ppermute x10, waiting for transfers between devices, send_y(): lax.ppermute(v, 'expert', [(i, moved(i, 0, 1)) for i in range(devices)])  3.07 us
    ppermute x6, waiting for transfers between devices, send_core(): return lax.ppermute(v, 'expert', [(i, i ^ 1) for i in range(devices)])  1.89 us
    pallas_call x1, Pallas kernels, plan(): pl.pallas_call(functools.partial(plan_kernel, home_cap, rep_cap), out_sha...  1.74 us
  transfers between devices with their start and end apart: 27, of which 14 were waited for; matrix products, arithmetic and copies ran while one was open for 0% of the time, Pallas kernels for 26%

profile of v14, /device:TPU:0, one launch (start us, length us, event | category | flops | bytes accessed | tf_op | source)
XLA Modules:
  0.0 81.4 jit_solution(1105769512928971356)
XLA Ops:
  0.6 1.7 %plan.1 = (bf16[136,1024]{1,0:T(8,128)(2,1)}, f32[16,128]{1,0:T(8,128)}) custom-call(s32[1,16]{1,0:T(1,128)} %bitcast.25, s32[8,128]{1,0:T(8,128)} %bitcast.22, bf16[8,128]{1,0:T(8,128)(2,1)} %bitcast.24, bf16[128,1024]{1,0:T(8,128)(2,1)} %x_in.1), custom_call_target="tpu_custom_call" | custom-call | tf_op jit(solution)/shard_map/plan/pallas_call | solution.py:86
  2.4 3.1 %collective-permute-start.1 = (bf16[136,1024]{1,0:T(8,128)(2,1)}, bf16[136,1024]{1,0:T(8,128)(2,1)S(1)}, u32[]{:S(2)}, u32[]{:S(2)}) collective-permute-start(bf16[136,1024]{1,0:T(8,128)(2,1)} %get-tuple-element.60.refs_0_), channel_id=1, source_target_pairs={{0,4},{1,5},{2,6},{3,7},{4,8},{5,9},{6,10},{7,11},{8,12},{9,13},{1... | collective-permute-start | bytes 835592 | tf_op jit(solution)/shard_map/ppermute | solution.py:346
  5.5 1.5 %collective-permute-start = (bf16[136,1024]{1,0:T(8,128)(2,1)}, bf16[136,1024]{1,0:T(8,128)(2,1)S(1)}, u32[]{:S(2)}, u32[]{:S(2)}) collective-permute-start(bf16[136,1024]{1,0:T(8,128)(2,1)} %get-tuple-element.60.refs_0_), channel_id=1, source_target_pairs={{0,2},{1,3},{2,0},{3,1},{4,6},{5,7},{6,4},{7,5},{8,10},{9,11},{10,... | collective-permute-start | bytes 835592 | tf_op jit(solution)/shard_map/ppermute | solution.py:352
  7.0 1.6 %collective-permute-start.5 = (bf16[128,1024]{1,0:T(8,128)(2,1)}, bf16[128,1024]{1,0:T(8,128)(2,1)S(1)}, u32[]{:S(2)}, u32[]{:S(2)}) collective-permute-start(bf16[128,1024]{1,0:T(8,128)(2,1)} %refs_8_.3), channel_id=1, source_target_pairs={{0,4},{1,5},{2,6},{3,7},{4,8},{5,9},{6,10},{7,11},{8,12},{9,13},{1... | collective-permute-start | bytes 786440 | tf_op jit(solution)/shard_map/ppermute | solution.py:346
  8.6 0.5 collective-permute-start.4
  9.1 0.0 collective-permute-start.2
  9.1 6.1 %collective-permute-done.1.refs_0_.refs_2_ = bf16[136,1024]{1,0:T(8,128)(2,1)S(1)} collective-permute-done((bf16[136,1024]{1,0:T(8,128)(2,1)}, bf16[136,1024]{1,0:T(8,128)(2,1)S(1)}, u32[]{:S(2)}, u32[]{:S(2)}) %collective-permute-start.1) | collective-permute-done | bytes 278560 | tf_op jit(solution)/shard_map/ppermute | solution.py:346
  15.2 0.0 collective-permute-start.3
  15.2 0.1 collective-permute-done.refs_1_
  15.3 0.5 collective-permute-start.6
  15.8 0.0 collective-permute-done.2.refs_7_
  15.8 1.9 %collective-permute-done.3.refs_8_ = bf16[1024,384]{1,0:T(8,128)(2,1)S(1)} collective-permute-done((bf16[1024,384]{1,0:T(8,128)(2,1)}, bf16[1024,384]{1,0:T(8,128)(2,1)S(1)}, u32[]{:S(2)}, u32[]{:S(2)}) %collective-permute-start.3) | collective-permute-done | bytes 786464 | tf_op jit(solution)/shard_map/ppermute | solution.py:355
  17.7 0.0 collective-permute-start.8
  17.7 1.7 %collective-permute-start.7 = (bf16[136,1024]{1,0:T(8,128)(2,1)S(1)}, bf16[136,1024]{1,0:T(8,128)(2,1)S(1)}, u32[]{:S(2)}, u32[]{:S(2)}) collective-permute-start(bf16[136,1024]{1,0:T(8,128)(2,1)S(1)} %collective-permute-done.1.refs_0_.refs_2_), channel_id=1, source_target_pairs={{0,2},{1,3},{2,0},{3,1},{4,6},{5,7},{6,4},{7,5},{8,10},{9,11},{10,... | collective-permute-start | bytes 835592 | tf_op jit(solution)/shard_map/ppermute | solution.py:352
  19.4 0.5 collective-permute-done.5.refs_2_.refs_10_
  20.0 0.0 collective-permute-done.4.refs_3_.refs_9_
  20.0 0.0 collective-permute-done.6.refs_9_
  20.0 1.0 %collective-permute-start.10 = (bf16[128,1024]{1,0:T(8,128)(2,1)S(1)}, bf16[128,1024]{1,0:T(8,128)(2,1)S(1)}, u32[]{:S(2)}, u32[]{:S(2)}) collective-permute-start(bf16[128,1024]{1,0:T(8,128)(2,1)S(1)} %collective-permute-done.5.refs_2_.refs_10_), channel_id=1, source_target_pairs={{0,4},{1,5},{2,6},{3,7},{4,8},{5,9},{6,10},{7,11},{8,12},{9,13},{1... | collective-permute-start | bytes 786440 | tf_op jit(solution)/shard_map/ppermute | solution.py:346
  21.0 1.5 %collective-permute-start.9 = (bf16[128,1024]{1,0:T(8,128)(2,1)S(1)}, bf16[128,1024]{1,0:T(8,128)(2,1)S(1)}, u32[]{:S(2)}, u32[]{:S(2)}) collective-permute-start(bf16[128,1024]{1,0:T(8,128)(2,1)S(1)} %collective-permute-done.5.refs_2_.refs_10_), channel_id=1, source_target_pairs={{0,2},{1,3},{2,0},{3,1},{4,6},{5,7},{6,4},{7,5},{8,10},{9,11},{10,... | collective-permute-start | bytes 786440 | tf_op jit(solution)/shard_map/ppermute | solution.py:352
  22.5 3.2 %rows_grads.4 = (bf16[136,1024]{1,0:T(8,128)(2,1)S(1)}, bf16[136,1024]{1,0:T(8,128)(2,1)S(1)}, bf16[256,2304]{1,0:T(8,128)(2,1)S(1)}) custom-call(bf16[136,1024]{1,0:T(8,128)(2,1)S(1)} %copy-done.3, bf16[136,1024]{1,0:T(8,128)(2,1)S(1)} %collective-permute-done.refs_1_, bf16[128,1024]{1,0:T(8,128)(2,1)S(1)} %copy-done.4, ...), custom_call_target="tpu_custom_call" | custom-call | flops 1006632960 | bytes 9043968 | tf_op jit(solution)/shard_map/rows_grads/pallas_call | solution.py:190
  25.7 3.2 %collective-permute-done.8.refs_0_.refs_4_ = bf16[136,1024]{1,0:T(8,128)(2,1)S(1)} collective-permute-done((bf16[136,1024]{1,0:T(8,128)(2,1)S(1)}, bf16[136,1024]{1,0:T(8,128)(2,1)S(1)}, u32[]{:S(2)}, u32[]{:S(2)}) %collective-permute-start.8) | collective-permute-done | bytes 278560 | tf_op jit(solution)/shard_map/ppermute | solution.py:346
  29.0 0.0 collective-permute-done.7.refs_1_.refs_3_
  29.0 0.0 collective-permute-start.14
  29.0 1.8 %collective-permute-start.13 = (bf16[136,1024]{1,0:T(8,128)(2,1)S(1)}, bf16[136,1024]{1,0:T(8,128)(2,1)S(1)}, u32[]{:S(2)}, u32[]{:S(2)}) collective-permute-start(bf16[136,1024]{1,0:T(8,128)(2,1)S(1)} %collective-permute-done.8.refs_0_.refs_4_), channel_id=1, source_target_pairs={{0,2},{1,3},{2,0},{3,1},{4,6},{5,7},{6,4},{7,5},{8,10},{9,11},{10,... | collective-permute-start | bytes 835592 | tf_op jit(solution)/shard_map/ppermute | solution.py:352
  30.7 3.8 %collective-permute-done.10.refs_2_.refs_12_ = bf16[128,1024]{1,0:T(8,128)(2,1)S(1)} collective-permute-done((bf16[128,1024]{1,0:T(8,128)(2,1)S(1)}, bf16[128,1024]{1,0:T(8,128)(2,1)S(1)}, u32[]{:S(2)}, u32[]{:S(2)}) %collective-permute-start.10) | collective-permute-done | bytes 262176 | tf_op jit(solution)/shard_map/ppermute | solution.py:346
  34.6 0.0 collective-permute-done.9.refs_3_.refs_11_
  34.6 0.0 collective-permute-start.16
  34.6 1.8 %collective-permute-start.15 = (bf16[128,1024]{1,0:T(8,128)(2,1)S(1)}, bf16[128,1024]{1,0:T(8,128)(2,1)S(1)}, u32[]{:S(2)}, u32[]{:S(2)}) collective-permute-start(bf16[128,1024]{1,0:T(8,128)(2,1)S(1)} %collective-permute-done.10.refs_2_.refs_12_), channel_id=1, source_target_pairs={{0,2},{1,3},{2,0},{3,1},{4,6},{5,7},{6,4},{7,5},{8,10},{9,11},{10,... | collective-permute-start | bytes 786440 | tf_op jit(solution)/shard_map/ppermute | solution.py:352
  36.4 3.2 %rows_grads.5 = (bf16[136,1024]{1,0:T(8,128)(2,1)S(1)}, bf16[136,1024]{1,0:T(8,128)(2,1)S(1)}, bf16[256,2304]{1,0:T(8,128)(2,1)S(1)}) custom-call(bf16[136,1024]{1,0:T(8,128)(2,1)S(1)} %collective-permute-done.1.refs_0_.refs_2_, bf16[136,1024]{1,0:T(8,128)(2,1)S(1)} %collective-permute-done.7.refs_1_.refs_3_, ...), custom_call_target="tpu_custom_call" | custom-call | flops 1006632960 | bytes 9043968 | tf_op jit(solution)/shard_map/rows_grads/pallas_call | solution.py:190
  39.6 1.0 %collective-permute-done.14.refs_0_.refs_6_ = bf16[136,1024]{1,0:T(8,128)(2,1)S(1)} collective-permute-done((bf16[136,1024]{1,0:T(8,128)(2,1)S(1)}, bf16[136,1024]{1,0:T(8,128)(2,1)S(1)}, u32[]{:S(2)}, u32[]{:S(2)}) %collective-permute-start.14) | collective-permute-done | bytes 278560 | tf_op jit(solution)/shard_map/ppermute | solution.py:346
  40.6 0.0 collective-permute-done.13.refs_1_.refs_5_
  40.6 0.3 collective-permute-start.18
  40.8 2.0 %collective-permute-start.17 = (bf16[136,1024]{1,0:T(8,128)(2,1)S(1)}, bf16[136,1024]{1,0:T(8,128)(2,1)S(1)}, u32[]{:S(2)}, u32[]{:S(2)}) collective-permute-start(bf16[136,1024]{1,0:T(8,128)(2,1)S(1)} %get-tuple-element.80), channel_id=1, source_target_pairs={{0,4},{1,5},{2,6},{3,7},{4,8},{5,9},{6,10},{7,11},{8,12},{9,13},{1... | collective-permute-start | bytes 835592 | tf_op jit(solution)/shard_map/ppermute | solution.py:346
  42.8 3.3 %collective-permute-done.16.refs_2_.refs_14_ = bf16[128,1024]{1,0:T(8,128)(2,1)S(1)} collective-permute-done((bf16[128,1024]{1,0:T(8,128)(2,1)S(1)}, bf16[128,1024]{1,0:T(8,128)(2,1)S(1)}, u32[]{:S(2)}, u32[]{:S(2)}) %collective-permute-start.16) | collective-permute-done | bytes 262176 | tf_op jit(solution)/shard_map/ppermute | solution.py:346
  46.2 0.0 collective-permute-done.15.refs_3_.refs_13_
  46.2 1.8 %collective-permute-start.21 = (bf16[128,1024]{1,0:T(8,128)(2,1)S(1)}, bf16[128,1024]{1,0:T(8,128)(2,1)S(1)}, u32[]{:S(2)}, u32[]{:S(2)}) collective-permute-start(bf16[128,1024]{1,0:T(8,128)(2,1)S(1)} %collective-permute-done.16.refs_2_.refs_14_), channel_id=1, source_target_pairs={{0,2},{1,3},{2,0},{3,1},{4,6},{5,7},{6,4},{7,5},{8,10},{9,11},{10,... | collective-permute-start | bytes 786440 | tf_op jit(solution)/shard_map/ppermute | solution.py:352
  48.0 3.2 %rows_grads.6 = (bf16[136,1024]{1,0:T(8,128)(2,1)S(1)}, bf16[136,1024]{1,0:T(8,128)(2,1)S(1)}, bf16[256,2304]{1,0:T(8,128)(2,1)S(1)}) custom-call(bf16[136,1024]{1,0:T(8,128)(2,1)S(1)} %collective-permute-done.8.refs_0_.refs_4_, bf16[136,1024]{1,0:T(8,128)(2,1)S(1)} %collective-permute-done.13.refs_1_.refs_5_, ...), custom_call_target="tpu_custom_call" | custom-call | flops 1006632960 | bytes 9043968 | tf_op jit(solution)/shard_map/rows_grads/pallas_call | solution.py:190
  51.2 0.3 collective-permute-start.19
  51.5 1.0 %collective-permute-start.11 = (bf16[136,1024]{1,0:T(8,128)(2,1)S(1)}, bf16[136,1024]{1,0:T(8,128)(2,1)S(1)}, u32[]{:S(2)}, u32[]{:S(2)}) collective-permute-start(bf16[136,1024]{1,0:T(8,128)(2,1)S(1)} %get-tuple-element.73), channel_id=1, source_target_pairs={{0,12},{1,13},{2,14},{3,15},{4,0},{5,1},{6,2},{7,3},{8,4},{9,5},{1... | collective-permute-start | bytes 835592 | tf_op jit(solution)/shard_map/ppermute | solution.py:349
  52.5 2.1 %collective-permute-done.21.refs_3_.refs_15_ = bf16[128,1024]{1,0:T(8,128)(2,1)S(1)} collective-permute-done((bf16[128,1024]{1,0:T(8,128)(2,1)S(1)}, bf16[128,1024]{1,0:T(8,128)(2,1)S(1)}, u32[]{:S(2)}, u32[]{:S(2)}) %collective-permute-start.21) | collective-permute-done | bytes 262176 | tf_op jit(solution)/shard_map/ppermute | solution.py:352
  54.5 3.7 %collective-permute-done.17 = bf16[136,1024]{1,0:T(8,128)(2,1)S(1)} collective-permute-done((bf16[136,1024]{1,0:T(8,128)(2,1)S(1)}, bf16[136,1024]{1,0:T(8,128)(2,1)S(1)}, u32[]{:S(2)}, u32[]{:S(2)}) %collective-permute-start.17) | collective-permute-done | bytes 278560 | tf_op jit(solution)/shard_map/ppermute | solution.py:346
  58.2 3.2 %rows_grads.7 = (bf16[136,1024]{1,0:T(8,128)(2,1)S(1)}, bf16[136,1024]{1,0:T(8,128)(2,1)S(1)}, bf16[256,2304]{1,0:T(8,128)(2,1)S(1)}) custom-call(bf16[136,1024]{1,0:T(8,128)(2,1)S(1)} %collective-permute-done.14.refs_0_.refs_6_, bf16[136,1024]{1,0:T(8,128)(2,1)S(1)} %collective-permute-done.18.refs_1_.refs_7_, ...), custom_call_target="tpu_custom_call" | custom-call | flops 1006632960 | bytes 9043968 | tf_op jit(solution)/shard_map/rows_grads/pallas_call | solution.py:190
  61.4 1.8 %collective-permute-start.22 = (bf16[136,1024]{1,0:T(8,128)(2,1)S(1)}, bf16[136,1024]{1,0:T(8,128)(2,1)S(1)}, u32[]{:S(2)}, u32[]{:S(2)}) collective-permute-start(bf16[136,1024]{1,0:T(8,128)(2,1)S(1)} %get-tuple-element.90), channel_id=1, source_target_pairs={{0,2},{1,3},{2,0},{3,1},{4,6},{5,7},{6,4},{7,5},{8,10},{9,11},{10,... | collective-permute-start | bytes 835592 | tf_op jit(solution)/shard_map/ppermute | solution.py:352
  63.3 0.0 collective-permute-done.19
  63.3 0.1 add_convert_fusion.1
  63.4 0.1 collective-permute-start.20
  63.5 3.5 %weights_grads.2 = (bf16[1024,384]{1,0:T(8,128)(2,1)S(1)}, bf16[1024,384]{1,0:T(8,128)(2,1)S(1)}, bf16[384,1024]{1,0:T(8,128)(2,1)S(1)}) custom-call(bf16[136,1024]{1,0:T(8,128)(2,1)S(1)} %copy-done.3, bf16[136,1024]{1,0:T(8,128)(2,1)S(1)} %collective-permute-done.refs_1_, bf16[136,1024]{1,0:T(8,128)(2,1)S(1)} %collective-permute-done.1.refs_0_.refs_2_, ...), custom_call_target="tpu_custom_call" | custom-call | flops 1000 | bytes 1000 | tf_op jit(solution)/shard_map/weights_grads/pallas_call | solution.py:265
  67.0 0.1 collective-permute-start.24
  67.1 0.5 collective-permute-start.25
  67.6 0.1 collective-permute-start.26
  67.7 0.1 add_convert_fusion.2
  67.7 0.8 %collective-permute-done.22 = bf16[136,1024]{1,0:T(8,128)(2,1)S(1)} collective-permute-done((bf16[136,1024]{1,0:T(8,128)(2,1)S(1)}, bf16[136,1024]{1,0:T(8,128)(2,1)S(1)}, u32[]{:S(2)}, u32[]{:S(2)}) %collective-permute-start.22) | collective-permute-done | bytes 278560 | tf_op jit(solution)/shard_map/ppermute | solution.py:352
  68.6 1.7 %collective-permute-start.12 = (bf16[136,1024]{1,0:T(8,128)(2,1)S(1)}, bf16[136,1024]{1,0:T(8,128)(2,1)S(1)}, u32[]{:S(2)}, u32[]{:S(2)}) collective-permute-start(bf16[136,1024]{1,0:T(8,128)(2,1)S(1)} %add_convert_fusion.2), channel_id=1, source_target_pairs={{0,2},{1,3},{2,0},{3,1},{4,6},{5,7},{6,4},{7,5},{8,10},{9,11},{10,... | collective-permute-start | bytes 835592 | tf_op jit(solution)/shard_map/ppermute | solution.py:352
  70.3 1.7 %collective-permute-done.20 = bf16[136,1024]{1,0:T(8,128)(2,1)S(1)} collective-permute-done((bf16[136,1024]{1,0:T(8,128)(2,1)S(1)}, bf16[136,1024]{1,0:T(8,128)(2,1)S(1)}, u32[]{:S(2)}, u32[]{:S(2)}) %collective-permute-start.20) | collective-permute-done | bytes 278560 | tf_op jit(solution)/shard_map/ppermute | solution.py:346
  72.0 0.1 add_convert_fusion
  72.2 0.0 copy-start.5
  72.2 0.0 copy-start.6
  72.2 0.1 collective-permute-start.23
  72.3 0.0 collective-permute-done.24.refs_20_
  72.3 0.0 collective-permute-done.26.refs_22_
  72.3 4.4 %weights_grads.3 = (bf16[1,1024,384]{2,1,0:T(8,128)(2,1)}, bf16[1,1024,384]{2,1,0:T(8,128)(2,1)}, bf16[1,384,1024]{2,1,0:T(8,128)(2,1)}) custom-call(bf16[136,1024]{1,0:T(8,128)(2,1)S(1)} %copy-done.3, bf16[136,1024]{1,0:T(8,128)(2,1)S(1)} %collective-permute-done.refs_1_, bf16[136,1024]{1,0:T(8,128)(2,1)S(1)} %collective-permute-done.1.refs_0_.refs_2_, ...), custom_call_target="tpu_custom_call" | custom-call | flops 1000 | bytes 1000 | tf_op jit(solution)/shard_map/weights_grads/pallas_call | solution.py:265
  76.7 0.1 collective-permute-done.12.refs_1_
  76.8 3.8 %collective-permute-done.23.refs_2_ = bf16[136,1024]{1,0:T(8,128)(2,1)S(1)} collective-permute-done((bf16[136,1024]{1,0:T(8,128)(2,1)S(1)}, bf16[136,1024]{1,0:T(8,128)(2,1)S(1)}, u32[]{:S(2)}, u32[]{:S(2)}) %collective-permute-start.23) | collective-permute-done | bytes 278560 | tf_op jit(solution)/shard_map/ppermute | solution.py:346
  80.6 0.8 finish.1
  (16 shorter events, 0.0 us)
Async XLA Ops:
  2.4 12.8 %collective-permute-start.1 = (bf16[136,1024]{1,0:T(8,128)(2,1)}, bf16[136,1024]{1,0:T(8,128)(2,1)S(1)}, u32[]{:S(2)}, u32[]{:S(2)}) collective-permute-start(bf16[136,1024]{1,0:T(8,128)(2,1)} %get-tuple-element.60.refs_0_), channel_id=1, source_target_pairs={{0,4},{1,5},{2,6},{3,7},{4,8},{5,9},{6,10},{7,11},{8,12},{9,13},{1... | collective-permute-start | bytes 835592 | tf_op jit(solution)/shard_map/ppermute | solution.py:346
  5.5 9.8 %collective-permute-start = (bf16[136,1024]{1,0:T(8,128)(2,1)}, bf16[136,1024]{1,0:T(8,128)(2,1)S(1)}, u32[]{:S(2)}, u32[]{:S(2)}) collective-permute-start(bf16[136,1024]{1,0:T(8,128)(2,1)} %get-tuple-element.60.refs_0_), channel_id=1, source_target_pairs={{0,2},{1,3},{2,0},{3,1},{4,6},{5,7},{6,4},{7,5},{8,10},{9,11},{10,... | collective-permute-start | bytes 835592 | tf_op jit(solution)/shard_map/ppermute | solution.py:352
  7.0 13.0 %collective-permute-start.5 = (bf16[128,1024]{1,0:T(8,128)(2,1)}, bf16[128,1024]{1,0:T(8,128)(2,1)S(1)}, u32[]{:S(2)}, u32[]{:S(2)}) collective-permute-start(bf16[128,1024]{1,0:T(8,128)(2,1)} %refs_8_.3), channel_id=1, source_target_pairs={{0,4},{1,5},{2,6},{3,7},{4,8},{5,9},{6,10},{7,11},{8,12},{9,13},{1... | collective-permute-start | bytes 786440 | tf_op jit(solution)/shard_map/ppermute | solution.py:346
  8.6 11.4 %collective-permute-start.4 = (bf16[128,1024]{1,0:T(8,128)(2,1)}, bf16[128,1024]{1,0:T(8,128)(2,1)S(1)}, u32[]{:S(2)}, u32[]{:S(2)}) collective-permute-start(bf16[128,1024]{1,0:T(8,128)(2,1)} %refs_8_.3), channel_id=1, source_target_pairs={{0,2},{1,3},{2,0},{3,1},{4,6},{5,7},{6,4},{7,5},{8,10},{9,11},{10,... | collective-permute-start | bytes 786440 | tf_op jit(solution)/shard_map/ppermute | solution.py:352
  9.1 6.7 %collective-permute-start.2 = (bf16[1024,384]{1,0:T(8,128)(2,1)}, bf16[1024,384]{1,0:T(8,128)(2,1)S(1)}, u32[]{:S(2)}, u32[]{:S(2)}) collective-permute-start(bf16[1024,384]{1,0:T(8,128)(2,1)} %bitcast.7), channel_id=1, source_target_pairs={{0,1},{1,0},{2,3},{3,2},{4,5},{5,4},{6,7},{7,6},{8,9},{9,8},{10,11... | collective-permute-start | bytes 2359304 | tf_op jit(solution)/shard_map/ppermute | solution.py:355
  15.2 2.5 %collective-permute-start.3 = (bf16[1024,384]{1,0:T(8,128)(2,1)}, bf16[1024,384]{1,0:T(8,128)(2,1)S(1)}, u32[]{:S(2)}, u32[]{:S(2)}) collective-permute-start(bf16[1024,384]{1,0:T(8,128)(2,1)} %bitcast.12), channel_id=1, source_target_pairs={{0,1},{1,0},{2,3},{3,2},{4,5},{5,4},{6,7},{7,6},{8,9},{9,8},{10,11... | collective-permute-start | bytes 2359304 | tf_op jit(solution)/shard_map/ppermute | solution.py:355
  15.3 7.3 %copy-start = (bf16[1,1024,384]{2,1,0:T(8,128)(2,1)S(1)}, bf16[1,1024,384]{2,1,0:T(8,128)(2,1)}, u32[]{:S(2)}) copy-start(bf16[1,1024,384]{2,1,0:T(8,128)(2,1)} %param.13) | copy-start | bytes 2359300
  15.3 7.3 %copy-start.1 = (bf16[1,1024,384]{2,1,0:T(8,128)(2,1)S(1)}, bf16[1,1024,384]{2,1,0:T(8,128)(2,1)}, u32[]{:S(2)}) copy-start(bf16[1,1024,384]{2,1,0:T(8,128)(2,1)} %param.14) | copy-start | bytes 2359300
  15.3 7.3 %copy-start.2 = (bf16[1,384,1024]{2,1,0:T(8,128)(2,1)S(1)}, bf16[1,384,1024]{2,1,0:T(8,128)(2,1)}, u32[]{:S(2)}) copy-start(bf16[1,384,1024]{2,1,0:T(8,128)(2,1)} %param.15) | copy-start | bytes 2359300
  15.3 7.3 %copy-start.3 = (bf16[136,1024]{1,0:T(8,128)(2,1)S(1)}, bf16[136,1024]{1,0:T(8,128)(2,1)}, u32[]{:S(2)}) copy-start(bf16[136,1024]{1,0:T(8,128)(2,1)} %get-tuple-element.60.refs_0_) | copy-start | bytes 835588
  15.3 7.3 %copy-start.4 = (bf16[128,1024]{1,0:T(8,128)(2,1)S(1)}, bf16[128,1024]{1,0:T(8,128)(2,1)}, u32[]{:S(2)}) copy-start(bf16[128,1024]{1,0:T(8,128)(2,1)} %refs_8_.3) | copy-start | bytes 786436
  15.3 4.7 %collective-permute-start.6 = (bf16[384,1024]{1,0:T(8,128)(2,1)}, bf16[384,1024]{1,0:T(8,128)(2,1)S(1)}, u32[]{:S(2)}, u32[]{:S(2)}) collective-permute-start(bf16[384,1024]{1,0:T(8,128)(2,1)} %bitcast.17), channel_id=1, source_target_pairs={{0,1},{1,0},{2,3},{3,2},{4,5},{5,4},{6,7},{7,6},{8,9},{9,8},{10,11... | collective-permute-start | bytes 2359304 | tf_op jit(solution)/shard_map/ppermute | solution.py:355
  17.7 11.3 %collective-permute-start.8 = (bf16[136,1024]{1,0:T(8,128)(2,1)S(1)}, bf16[136,1024]{1,0:T(8,128)(2,1)S(1)}, u32[]{:S(2)}, u32[]{:S(2)}) collective-permute-start(bf16[136,1024]{1,0:T(8,128)(2,1)S(1)} %collective-permute-done.1.refs_0_.refs_2_), channel_id=1, source_target_pairs={{0,4},{1,5},{2,6},{3,7},{4,8},{5,9},{6,10},{7,11},{8,12},{9,13},{1... | collective-permute-start | bytes 835592 | tf_op jit(solution)/shard_map/ppermute | solution.py:346
  17.7 11.3 %collective-permute-start.7 = (bf16[136,1024]{1,0:T(8,128)(2,1)S(1)}, bf16[136,1024]{1,0:T(8,128)(2,1)S(1)}, u32[]{:S(2)}, u32[]{:S(2)}) collective-permute-start(bf16[136,1024]{1,0:T(8,128)(2,1)S(1)} %collective-permute-done.1.refs_0_.refs_2_), channel_id=1, source_target_pairs={{0,2},{1,3},{2,0},{3,1},{4,6},{5,7},{6,4},{7,5},{8,10},{9,11},{10,... | collective-permute-start | bytes 835592 | tf_op jit(solution)/shard_map/ppermute | solution.py:352
  20.0 14.6 %collective-permute-start.10 = (bf16[128,1024]{1,0:T(8,128)(2,1)S(1)}, bf16[128,1024]{1,0:T(8,128)(2,1)S(1)}, u32[]{:S(2)}, u32[]{:S(2)}) collective-permute-start(bf16[128,1024]{1,0:T(8,128)(2,1)S(1)} %collective-permute-done.5.refs_2_.refs_10_), channel_id=1, source_target_pairs={{0,4},{1,5},{2,6},{3,7},{4,8},{5,9},{6,10},{7,11},{8,12},{9,13},{1... | collective-permute-start | bytes 786440 | tf_op jit(solution)/shard_map/ppermute | solution.py:346
  21.0 13.6 %collective-permute-start.9 = (bf16[128,1024]{1,0:T(8,128)(2,1)S(1)}, bf16[128,1024]{1,0:T(8,128)(2,1)S(1)}, u32[]{:S(2)}, u32[]{:S(2)}) collective-permute-start(bf16[128,1024]{1,0:T(8,128)(2,1)S(1)} %collective-permute-done.5.refs_2_.refs_10_), channel_id=1, source_target_pairs={{0,2},{1,3},{2,0},{3,1},{4,6},{5,7},{6,4},{7,5},{8,10},{9,11},{10,... | collective-permute-start | bytes 786440 | tf_op jit(solution)/shard_map/ppermute | solution.py:352
  29.0 11.6 %collective-permute-start.14 = (bf16[136,1024]{1,0:T(8,128)(2,1)S(1)}, bf16[136,1024]{1,0:T(8,128)(2,1)S(1)}, u32[]{:S(2)}, u32[]{:S(2)}) collective-permute-start(bf16[136,1024]{1,0:T(8,128)(2,1)S(1)} %collective-permute-done.8.refs_0_.refs_4_), channel_id=1, source_target_pairs={{0,4},{1,5},{2,6},{3,7},{4,8},{5,9},{6,10},{7,11},{8,12},{9,13},{1... | collective-permute-start | bytes 835592 | tf_op jit(solution)/shard_map/ppermute | solution.py:346
  29.0 11.6 %collective-permute-start.13 = (bf16[136,1024]{1,0:T(8,128)(2,1)S(1)}, bf16[136,1024]{1,0:T(8,128)(2,1)S(1)}, u32[]{:S(2)}, u32[]{:S(2)}) collective-permute-start(bf16[136,1024]{1,0:T(8,128)(2,1)S(1)} %collective-permute-done.8.refs_0_.refs_4_), channel_id=1, source_target_pairs={{0,2},{1,3},{2,0},{3,1},{4,6},{5,7},{6,4},{7,5},{8,10},{9,11},{10,... | collective-permute-start | bytes 835592 | tf_op jit(solution)/shard_map/ppermute | solution.py:352
  34.6 11.6 %collective-permute-start.16 = (bf16[128,1024]{1,0:T(8,128)(2,1)S(1)}, bf16[128,1024]{1,0:T(8,128)(2,1)S(1)}, u32[]{:S(2)}, u32[]{:S(2)}) collective-permute-start(bf16[128,1024]{1,0:T(8,128)(2,1)S(1)} %collective-permute-done.10.refs_2_.refs_12_), channel_id=1, source_target_pairs={{0,4},{1,5},{2,6},{3,7},{4,8},{5,9},{6,10},{7,11},{8,12},{9,13},{1... | collective-permute-start | bytes 786440 | tf_op jit(solution)/shard_map/ppermute | solution.py:346
  34.6 11.6 %collective-permute-start.15 = (bf16[128,1024]{1,0:T(8,128)(2,1)S(1)}, bf16[128,1024]{1,0:T(8,128)(2,1)S(1)}, u32[]{:S(2)}, u32[]{:S(2)}) collective-permute-start(bf16[128,1024]{1,0:T(8,128)(2,1)S(1)} %collective-permute-done.10.refs_2_.refs_12_), channel_id=1, source_target_pairs={{0,2},{1,3},{2,0},{3,1},{4,6},{5,7},{6,4},{7,5},{8,10},{9,11},{10,... | collective-permute-start | bytes 786440 | tf_op jit(solution)/shard_map/ppermute | solution.py:352
  40.6 14.0 %collective-permute-start.18 = (bf16[136,1024]{1,0:T(8,128)(2,1)S(1)}, bf16[136,1024]{1,0:T(8,128)(2,1)S(1)}, u32[]{:S(2)}, u32[]{:S(2)}) collective-permute-start(bf16[136,1024]{1,0:T(8,128)(2,1)S(1)} %collective-permute-done.13.refs_1_.refs_5_), channel_id=1, source_target_pairs={{0,4},{1,5},{2,6},{3,7},{4,8},{5,9},{6,10},{7,11},{8,12},{9,13},{1... | collective-permute-start | bytes 835592 | tf_op jit(solution)/shard_map/ppermute | solution.py:346
  40.8 17.4 %collective-permute-start.17 = (bf16[136,1024]{1,0:T(8,128)(2,1)S(1)}, bf16[136,1024]{1,0:T(8,128)(2,1)S(1)}, u32[]{:S(2)}, u32[]{:S(2)}) collective-permute-start(bf16[136,1024]{1,0:T(8,128)(2,1)S(1)} %get-tuple-element.80), channel_id=1, source_target_pairs={{0,4},{1,5},{2,6},{3,7},{4,8},{5,9},{6,10},{7,11},{8,12},{9,13},{1... | collective-permute-start | bytes 835592 | tf_op jit(solution)/shard_map/ppermute | solution.py:346
  46.2 8.3 %collective-permute-start.21 = (bf16[128,1024]{1,0:T(8,128)(2,1)S(1)}, bf16[128,1024]{1,0:T(8,128)(2,1)S(1)}, u32[]{:S(2)}, u32[]{:S(2)}) collective-permute-start(bf16[128,1024]{1,0:T(8,128)(2,1)S(1)} %collective-permute-done.16.refs_2_.refs_14_), channel_id=1, source_target_pairs={{0,2},{1,3},{2,0},{3,1},{4,6},{5,7},{6,4},{7,5},{8,10},{9,11},{10,... | collective-permute-start | bytes 786440 | tf_op jit(solution)/shard_map/ppermute | solution.py:352
  51.2 12.1 %collective-permute-start.19 = (bf16[136,1024]{1,0:T(8,128)(2,1)S(1)}, bf16[136,1024]{1,0:T(8,128)(2,1)S(1)}, u32[]{:S(2)}, u32[]{:S(2)}) collective-permute-start(bf16[136,1024]{1,0:T(8,128)(2,1)S(1)} %get-tuple-element.85), channel_id=1, source_target_pairs={{0,2},{1,3},{2,0},{3,1},{4,6},{5,7},{6,4},{7,5},{8,10},{9,11},{10,... | collective-permute-start | bytes 835592 | tf_op jit(solution)/shard_map/ppermute | solution.py:352
  51.5 16.1 %collective-permute-start.11 = (bf16[136,1024]{1,0:T(8,128)(2,1)S(1)}, bf16[136,1024]{1,0:T(8,128)(2,1)S(1)}, u32[]{:S(2)}, u32[]{:S(2)}) collective-permute-start(bf16[136,1024]{1,0:T(8,128)(2,1)S(1)} %get-tuple-element.73), channel_id=1, source_target_pairs={{0,12},{1,13},{2,14},{3,15},{4,0},{5,1},{6,2},{7,3},{8,4},{9,5},{1... | collective-permute-start | bytes 835592 | tf_op jit(solution)/shard_map/ppermute | solution.py:349
  61.4 7.2 %collective-permute-start.22 = (bf16[136,1024]{1,0:T(8,128)(2,1)S(1)}, bf16[136,1024]{1,0:T(8,128)(2,1)S(1)}, u32[]{:S(2)}, u32[]{:S(2)}) collective-permute-start(bf16[136,1024]{1,0:T(8,128)(2,1)S(1)} %get-tuple-element.90), channel_id=1, source_target_pairs={{0,2},{1,3},{2,0},{3,1},{4,6},{5,7},{6,4},{7,5},{8,10},{9,11},{10,... | collective-permute-start | bytes 835592 | tf_op jit(solution)/shard_map/ppermute | solution.py:352
  63.4 8.7 %collective-permute-start.20 = (bf16[136,1024]{1,0:T(8,128)(2,1)S(1)}, bf16[136,1024]{1,0:T(8,128)(2,1)S(1)}, u32[]{:S(2)}, u32[]{:S(2)}) collective-permute-start(bf16[136,1024]{1,0:T(8,128)(2,1)S(1)} %add_convert_fusion.1), channel_id=1, source_target_pairs={{0,4},{1,5},{2,6},{3,7},{4,8},{5,9},{6,10},{7,11},{8,12},{9,13},{1... | collective-permute-start | bytes 835592 | tf_op jit(solution)/shard_map/ppermute | solution.py:346
  67.0 5.3 %collective-permute-start.24 = (bf16[1024,384]{1,0:T(8,128)(2,1)S(1)}, bf16[1024,384]{1,0:T(8,128)(2,1)S(1)}, u32[]{:S(2)}, u32[]{:S(2)}) collective-permute-start(bf16[1024,384]{1,0:T(8,128)(2,1)S(1)} %get-tuple-element.95), channel_id=1, source_target_pairs={{0,1},{1,0},{2,3},{3,2},{4,5},{5,4},{6,7},{7,6},{8,9},{9,8},{10,11... | collective-permute-start | bytes 2359304 | tf_op jit(solution)/shard_map/ppermute | solution.py:355
  67.1 5.2 %collective-permute-start.25 = (bf16[1024,384]{1,0:T(8,128)(2,1)S(1)}, bf16[1024,384]{1,0:T(8,128)(2,1)S(1)}, u32[]{:S(2)}, u32[]{:S(2)}) collective-permute-start(bf16[1024,384]{1,0:T(8,128)(2,1)S(1)} %get-tuple-element.96), channel_id=1, source_target_pairs={{0,1},{1,0},{2,3},{3,2},{4,5},{5,4},{6,7},{7,6},{8,9},{9,8},{10,11... | collective-permute-start | bytes 2359304 | tf_op jit(solution)/shard_map/ppermute | solution.py:355
  67.6 4.7 %collective-permute-start.26 = (bf16[384,1024]{1,0:T(8,128)(2,1)S(1)}, bf16[384,1024]{1,0:T(8,128)(2,1)S(1)}, u32[]{:S(2)}, u32[]{:S(2)}) collective-permute-start(bf16[384,1024]{1,0:T(8,128)(2,1)S(1)} %get-tuple-element.97), channel_id=1, source_target_pairs={{0,1},{1,0},{2,3},{3,2},{4,5},{5,4},{6,7},{7,6},{8,9},{9,8},{10,11... | collective-permute-start | bytes 2359304 | tf_op jit(solution)/shard_map/ppermute | solution.py:355
  68.6 8.2 %collective-permute-start.12 = (bf16[136,1024]{1,0:T(8,128)(2,1)S(1)}, bf16[136,1024]{1,0:T(8,128)(2,1)S(1)}, u32[]{:S(2)}, u32[]{:S(2)}) collective-permute-start(bf16[136,1024]{1,0:T(8,128)(2,1)S(1)} %add_convert_fusion.2), channel_id=1, source_target_pairs={{0,2},{1,3},{2,0},{3,1},{4,6},{5,7},{6,4},{7,5},{8,10},{9,11},{10,... | collective-permute-start | bytes 835592 | tf_op jit(solution)/shard_map/ppermute | solution.py:352
  72.2 8.4 %copy-start.5 = (s32[128,8]{0,1:T(8,128)S(1)}, s32[128,8]{0,1:T(8,128)}, u32[]{:S(2)}) copy-start(s32[128,8]{0,1:T(8,128)} %param.11) | copy-start | bytes 12292
  72.2 8.4 %copy-start.6 = (f32[16,128]{1,0:T(8,128)S(1)}, f32[16,128]{1,0:T(8,128)}, u32[]{:S(2)}) copy-start(f32[16,128]{1,0:T(8,128)} %get-tuple-element.59.kept) | copy-start | bytes 24580
  72.2 8.4 %collective-permute-start.23 = (bf16[136,1024]{1,0:T(8,128)(2,1)S(1)}, bf16[136,1024]{1,0:T(8,128)(2,1)S(1)}, u32[]{:S(2)}, u32[]{:S(2)}) collective-permute-start(bf16[136,1024]{1,0:T(8,128)(2,1)S(1)} %add_convert_fusion), channel_id=1, source_target_pairs={{0,4},{1,5},{2,6},{3,7},{4,8},{5,9},{6,10},{7,11},{8,12},{9,13},{1... | collective-permute-start | bytes 835592 | tf_op jit(solution)/shard_map/ppermute | solution.py:346
